TPU v7x, 32 devices: a whole 2x2x4 slice. The times are simulated.
32 devices in a mesh: dp: 8 (over z, x), tensor: 4 (over y, core).
Axes of the slice: x: 2, y: 2, z: 4, core: 2. Of those that a mesh axis runs over, the one named last changes fastest.
Arguments:
- tokens: bfloat16 [7680, 1024], P(('dp', 'tensor')), may hold values from -6 to 6
- keep_mask: int32 [24, 320], P('dp'), may hold values from 0 to 1, as said below
- grad_out: bfloat16 [7680, 1024], P(('dp', 'tensor')), may hold values from -12 to 12
- in_weight: bfloat16 [1024, 3072], P(None, 'tensor'), may hold values from -0.1875 to 0.1875
- in_bias: float32 [2048], P('tensor'), may hold values from -3 to 3
- out_weight: bfloat16 [1024, 1024], P('tensor'), may hold values from -0.75 to 0.75
- out_bias: float32 [1024], replicated, may hold values from -2 to 2
- up_weight: bfloat16 [1024, 4096], P(None, 'tensor'), may hold values from -0.1875 to 0.1875
- up_bias: float32 [4096], P('tensor'), may hold values from -3 to 3
- down_weight: bfloat16 [4096, 1024], P('tensor'), may hold values from -0.09375 to 0.09375
- down_bias: float32 [1024], replicated, may hold values from -2 to 2
- gain_one: float32 [1024], replicated, may hold values from 0.25 to 1.75
- shift_one: float32 [1024], replicated, may hold values from -2 to 2
- gain_two: float32 [1024], replicated, may hold values from 0.25 to 1.75
- shift_two: float32 [1024], replicated, may hold values from -2 to 2
Outputs:
- output: bfloat16 [7680, 1024], P(('dp', 'tensor'))
- tokens_grad: float32 [7680, 1024], P(('dp', 'tensor'))
- in_weight_grad: float32 [1024, 3072], P(None, 'tensor')
- in_bias_grad: float32 [2048], P('tensor')
- out_weight_grad: float32 [1024, 1024], P('tensor')
- out_bias_grad: float32 [1024], replicated
- up_weight_grad: float32 [1024, 4096], P(None, 'tensor')
- up_bias_grad: float32 [4096], P('tensor')
- down_weight_grad: float32 [4096, 1024], P('tensor')
- down_bias_grad: float32 [1024], replicated
- gain_one_grad: float32 [1024], replicated
- shift_one_grad: float32 [1024], replicated
- gain_two_grad: float32 [1024], replicated
- shift_two_grad: float32 [1024], replicated
Inputs may be any that keep to these rules, and one draw needn't show every extreme that they name: `keep_mask`: 1 in the first 64 slots of every image and in at least one of its other 256 slots.
All inputs are finite; a program needn't handle non-finite values.
Results may differ from a plain program's by a relative error of at most 0.012.
The roundings to bfloat16 on the way count: a program that leaves them out, or rounds other values in their place, can miss the bound.
Values may be sent and summed in bfloat16 or wider, within the bound.
No kernel may reach another device: no remote copies, remote signals or barrier semaphores. Data moves between devices by JAX's collectives and lax.ppermute only.
A program may use at most 128 MiB of HBM per device.

v0:
```python
import jax
import jax.numpy as jnp
from jax import lax
from jax.sharding import PartitionSpec as P

HD = 64
SLOTS = 320


EPSILON = 1e-06


def layer_norm(values, gain, shift):
    average = jnp.mean(values, axis=-1, keepdims=True)
    centred = values - average
    variance = jnp.mean(centred * centred, axis=-1, keepdims=True)
    return centred * lax.rsqrt(variance + EPSILON) * gain + shift


def gelu_exact(values):
    return jax.nn.gelu(values, approximate=False)


def over_rows(left, right):
    return lax.dot_general(
        left, right, (((0,), (0,)), ((), ())), preferred_element_type=jnp.float32
    )


def over_cols(left, right):
    return lax.dot_general(
        left, right, (((1,), (1,)), ((), ())), preferred_element_type=jnp.float32
    )


def masked_scores(query_rows, key_rows, key_live):
    scores = jnp.einsum(
        "ishd,ithd->ihst", query_rows, key_rows, preferred_element_type=jnp.float32
    ) * HD ** (-0.5)
    return jnp.where(key_live, scores, -1000000000.0)


def forward_pass(tokens, keep_mask, keep_local, params):
    (
        in_weight,
        in_bias,
        out_weight,
        out_bias,
        up_weight,
        up_bias,
        down_weight,
        down_bias,
        gain_one,
        shift_one,
        gain_two,
        shift_two,
    ) = params
    token_values = tokens.astype(jnp.float32)
    first_normed = lax.all_gather(
        layer_norm(token_values, gain_one, shift_one).astype(jnp.bfloat16),
        "tensor",
        axis=0,
        tiled=True,
    )
    row_count = first_normed.shape[0]
    images = row_count // SLOTS
    head_count = in_weight.shape[1] // (3 * HD)
    projected = jnp.dot(first_normed, in_weight, preferred_element_type=jnp.float32)
    projected = projected.reshape(row_count, head_count, 3, HD)
    bias_pair = in_bias.reshape(head_count, 2, HD)
    bias_full = jnp.concatenate(
        [bias_pair[:, :1], jnp.zeros((head_count, 1, HD), jnp.float32), bias_pair[:, 1:]], axis=1
    )
    packed = (projected + bias_full).astype(jnp.bfloat16).reshape(images, SLOTS, head_count, 3, HD)
    query_rows = packed[:, :, :, 0]
    key_rows = packed[:, :, :, 1]
    value_rows = packed[:, :, :, 2]
    key_live = keep_mask.reshape(images, 1, 1, SLOTS) > 0
    scores = masked_scores(query_rows, key_rows, key_live)
    maximum = jnp.max(scores, axis=-1, keepdims=True)
    exponent = jnp.exp(scores - maximum)
    totals = jnp.sum(exponent, axis=-1, keepdims=True)
    log_total = maximum + jnp.log(totals)
    attention = (exponent / totals).astype(jnp.bfloat16)
    heads_out = jnp.einsum(
        "ihst,ithd->ishd", attention, value_rows, preferred_element_type=jnp.float32
    )
    heads_out = heads_out.astype(jnp.bfloat16).reshape(row_count, head_count * HD)
    attention_rows = lax.psum_scatter(
        jnp.dot(heads_out, out_weight, preferred_element_type=jnp.float32),
        "tensor",
        scatter_dimension=0,
        tiled=True,
    )
    middle = token_values + attention_rows + out_bias
    second = lax.all_gather(
        layer_norm(middle, gain_two, shift_two).astype(jnp.bfloat16), "tensor", axis=0, tiled=True
    )
    pre_act = jnp.dot(second, up_weight, preferred_element_type=jnp.float32) + up_bias
    act_low = gelu_exact(pre_act).astype(jnp.bfloat16)
    feed_rows = lax.psum_scatter(
        jnp.dot(act_low, down_weight, preferred_element_type=jnp.float32).astype(jnp.bfloat16),
        "tensor",
        scatter_dimension=0,
        tiled=True,
    ).astype(jnp.float32)
    output = (keep_local[:, None] * (middle + feed_rows + down_bias)).astype(jnp.bfloat16)
    saved = (
        token_values,
        first_normed,
        query_rows,
        key_rows,
        value_rows,
        key_live,
        log_total,
        heads_out,
        middle,
        second,
        pre_act,
        act_low,
    )
    return (output, saved)


def on_device(
    tokens,
    keep_mask,
    grad_out,
    in_weight,
    in_bias,
    out_weight,
    out_bias,
    up_weight,
    up_bias,
    down_weight,
    down_bias,
    gain_one,
    shift_one,
    gain_two,
    shift_two,
):
    params = (
        in_weight,
        in_bias,
        out_weight,
        out_bias,
        up_weight,
        up_bias,
        down_weight,
        down_bias,
        gain_one,
        shift_one,
        gain_two,
        shift_two,
    )
    local_rows = tokens.shape[0]
    keep_flat = keep_mask.reshape(-1)
    offset = lax.axis_index("tensor") * local_rows
    keep_local = lax.dynamic_slice_in_dim(keep_flat, offset, local_rows).astype(jnp.float32)
    output, saved = forward_pass(tokens, keep_mask, keep_local, params)
    (
        token_values,
        first_normed,
        query_rows,
        key_rows,
        value_rows,
        key_live,
        log_total,
        heads_out,
        middle,
        second,
        pre_act,
        act_low,
    ) = saved
    row_count = first_normed.shape[0]
    images = row_count // SLOTS
    head_count = in_weight.shape[1] // (3 * HD)
    cot_rows = grad_out.astype(jnp.float32) * keep_local[:, None]
    down_bias_grad = jnp.sum(cot_rows, axis=0)
    cot_all = lax.all_gather(cot_rows.astype(jnp.bfloat16), "tensor", axis=0, tiled=True)
    down_weight_grad = over_rows(act_low, cot_all)
    act_grad = over_cols(cot_all, down_weight)
    pre_grad = jax.vjp(gelu_exact, pre_act)[1](act_grad)[0]
    up_bias_grad = jnp.sum(pre_grad, axis=0)
    pre_low = pre_grad.astype(jnp.bfloat16)
    up_weight_grad = over_rows(second, pre_low)
    second_rows = lax.psum_scatter(
        over_cols(pre_low, up_weight), "tensor", scatter_dimension=0, tiled=True
    )
    middle_norm_grad, gain_two_grad, shift_two_grad = jax.vjp(
        layer_norm, middle, gain_two, shift_two
    )[1](second_rows)
    middle_grad = cot_rows + middle_norm_grad
    out_bias_grad = jnp.sum(middle_grad, axis=0)
    middle_all = lax.all_gather(middle_grad.astype(jnp.bfloat16), "tensor", axis=0, tiled=True)
    out_weight_grad = over_rows(heads_out, middle_all)
    heads_grad = (
        over_cols(middle_all, out_weight)
        .astype(jnp.bfloat16)
        .reshape(images, SLOTS, head_count, HD)
    )
    scores = masked_scores(query_rows, key_rows, key_live)
    attention = jnp.exp(scores - log_total)
    value_grad = jnp.einsum(
        "ihst,ishd->ithd",
        attention.astype(jnp.bfloat16),
        heads_grad,
        preferred_element_type=jnp.float32,
    )
    prob_grad = jnp.einsum(
        "ishd,ithd->ihst", heads_grad, value_rows, preferred_element_type=jnp.float32
    )
    row_delta = jnp.sum(attention * prob_grad, axis=-1, keepdims=True)
    score_grad = (attention * (prob_grad - row_delta) * HD ** (-0.5)).astype(jnp.bfloat16)
    query_grad = jnp.einsum(
        "ihst,ithd->ishd", score_grad, key_rows, preferred_element_type=jnp.float32
    )
    key_grad = jnp.einsum(
        "ihst,ishd->ithd", score_grad, query_rows, preferred_element_type=jnp.float32
    )
    in_bias_grad = jnp.sum(jnp.stack([query_grad, value_grad], axis=3), axis=(0, 1)).reshape(-1)
    stacked_low = jnp.stack([query_grad, key_grad, value_grad], axis=3).reshape(
        row_count, head_count * 3 * HD
    )
    stacked_low = stacked_low.astype(jnp.bfloat16)
    in_weight_grad = over_rows(first_normed, stacked_low)
    first_rows = lax.psum_scatter(
        over_cols(stacked_low, in_weight), "tensor", scatter_dimension=0, tiled=True
    )
    token_norm_grad, gain_one_grad, shift_one_grad = jax.vjp(
        layer_norm, token_values, gain_one, shift_one
    )[1](first_rows)
    tokens_grad = middle_grad + token_norm_grad
    small_sums = lax.psum(
        (
            out_bias_grad,
            down_bias_grad,
            gain_one_grad,
            shift_one_grad,
            gain_two_grad,
            shift_two_grad,
        ),
        ("dp", "tensor"),
    )
    in_weight_sum, in_bias_sum, out_weight_sum, up_weight_sum, up_bias_sum, down_weight_sum = (
        lax.psum(
            (
                in_weight_grad,
                in_bias_grad,
                out_weight_grad,
                up_weight_grad,
                up_bias_grad,
                down_weight_grad,
            ),
            "dp",
        )
    )
    return (
        output,
        tokens_grad,
        in_weight_sum,
        in_bias_sum,
        out_weight_sum,
        small_sums[0],
        up_weight_sum,
        up_bias_sum,
        down_weight_sum,
        small_sums[1],
        small_sums[2],
        small_sums[3],
        small_sums[4],
        small_sums[5],
    )


def solution(mesh):
    placed = (
        P(("dp", "tensor"), None),
        P("dp", None),
        P(("dp", "tensor"), None),
        P(None, "tensor"),
        P("tensor"),
        P("tensor", None),
        P(),
        P(None, "tensor"),
        P("tensor"),
        P("tensor", None),
        P(),
        P(),
        P(),
        P(),
        P(),
    )
    return jax.shard_map(
        on_device,
        mesh=mesh,
        in_specs=placed,
        out_specs=(
            P(("dp", "tensor"), None),
            P(("dp", "tensor"), None),
            P(None, "tensor"),
            P("tensor"),
            P("tensor", None),
            P(),
            P(None, "tensor"),
            P("tensor"),
            P("tensor", None),
            P(),
            P(),
            P(),
            P(),
            P(),
        ),
        check_vma=False,
    )
```

profile of v0, /device:TPU:0, one launch (start us, length us, event | category | flops | bytes accessed | tf_op | source)
XLA Modules:
  0.0 796.6 jit_solution(16270902399068437149)
XLA Ops:
  13.7 23.1 %all-gather.5.cloned.1.call-done = bf16[960,1024]{1,0:T(8,128)(2,1)} async-done(((bf16[240,1024]{1,0:T(8,128)(2,1)}), bf16[960,1024]{1,0:T(8,128)(2,1)}) %all-gather.5.cloned.1.call-update) | async-done | bytes 1966096 | tf_op jit(solution)/shard_map/all_gather | solution.py:59
  36.8 5.5 fusion.83
  42.3 6.2 reshape.134
  48.5 2.6 fusion.12
  56.4 3.9 fusion.84
  60.4 43.0 %reduce-scatter.5.cloned.1.call-done = f32[240,1024]{1,0:T(8,128)} async-done(((f32[960,1024]{1,0:T(8,128)}), f32[240,1024]{1,0:T(8,128)}) %reduce-scatter.5.cloned.1.call-update) | async-done | bytes 983056 | tf_op jit(solution)/shard_map/reduce_scatter | solution.py:89
  108.7 19.6 %all-gather.7.cloned.1.call-done = bf16[960,1024]{1,0:T(8,128)(2,1)} async-done(((bf16[240,1024]{1,0:T(8,128)(2,1)}), bf16[960,1024]{1,0:T(8,128)(2,1)}) %all-gather.7.cloned.1.call-update) | async-done | bytes 1966096 | tf_op jit(solution)/shard_map/all_gather | solution.py:96
  128.3 6.3 fusion.85
  134.6 17.7 %all-gather.9.cloned.1.call-done = bf16[960,1024]{1,0:T(8,128)(2,1)} async-done(((bf16[240,1024]{1,0:T(8,128)(2,1)}), bf16[960,1024]{1,0:T(8,128)(2,1)}) %all-gather.9.cloned.1.call-update) | async-done | bytes 1966096 | tf_op jit(solution)/shard_map/all_gather | solution.py:180
  152.2 14.0 %fusion.72 = (f32[1024]{0:T(1024)S(1)}, bf16[960,1024]{1,0:T(8,128)(2,1)S(1)}, f32[960,1024]{1,0:T(8,128)}) fusion(f32[960,1024]{1,0:T(8,128)} %fusion.85, f32[1024]{0:T(1024)S(1)} %copy-done.22, bf16[960,1024]{1,0:T(8,128)(2,1)} %all-gather.9.cloned.1.call-done, bf16[1024,1024]{1,0:T(8,128)(2,1)S(1)} %copy-done), kind=kOutput, calls=%fused_computation.105 | convolution fusion | flops 2086009856 | bytes 13901824 | tf_op jit(solution)/shard_map/dot_general | solution.py:31
  167.5 4.1 fusion.57
  171.7 4.4 multiply_convert_fusion.1
  177.4 3.5 convolution_convert_fusion
  180.9 33.8 %reduce-scatter.9.cloned.1.call-done = f32[240,1024]{1,0:T(8,128)} async-done(((f32[960,1024]{1,0:T(8,128)}), f32[240,1024]{1,0:T(8,128)}) %reduce-scatter.9.cloned.1.call-update) | async-done | bytes 983056 | tf_op jit(solution)/shard_map/reduce_scatter | solution.py:187
  216.3 32.1 %reduce-scatter.7.cloned.1.call-done = bf16[240,1024]{1,0:T(8,128)(2,1)} async-done(((bf16[960,1024]{1,0:T(8,128)(2,1)}), bf16[240,1024]{1,0:T(8,128)(2,1)}) %reduce-scatter.7.cloned.1.call-update) | async-done | bytes 491536 | tf_op jit(solution)/shard_map/reduce_scatter | solution.py:101
  248.4 2.6 fusion.74
  253.2 21.7 %all-gather.11.cloned.1.call-done = bf16[960,1024]{1,0:T(8,128)(2,1)} async-done(((bf16[240,1024]{1,0:T(8,128)(2,1)}), bf16[960,1024]{1,0:T(8,128)(2,1)}) %all-gather.11.cloned.1.call-update) | async-done | bytes 1966096 | tf_op jit(solution)/shard_map/all_gather | solution.py:195
  281.0 4.5 fusion.61
  285.5 12.1 %fusion.80 = (bf16[3,320,4,1,64]{1,4,2,0,3:T(8,128)(2,1)S(1)}, f32[3,320,4,1,64]{1,4,2,0,3:T(8,128)}) fusion(f32[3,4,320,320]{2,3,1,0:T(8,128)} %fusion.61, f32[3,4,320,320]{2,3,1,0:T(8,128)} %copy-done.1, f32[3,4,320]{2,1,0:T(4,128)S(1)} %log_add_fusion, bf16[3,320,4,3,64]{1,4,2,0,3:T(8,128)(2,1)} %copy-done.6), kind=kOutput, calls=%fused_computation.111 | convolution fusion | flops 166137920 | bytes 25694208 | tf_op jit(solution)/shard_map/ihst,ithd->ishd/dot_general | solution.py:215
  297.6 11.7 %fusion.43 = bf16[3,320,4,1,64]{1,4,2,0,3:T(8,128)(2,1)} fusion(f32[3,4,320,320]{2,3,1,0:T(8,128)} %fusion.61, f32[3,4,320,320]{2,3,1,0:T(8,128)} %copy-done.1, f32[3,4,320]{2,1,0:T(4,128)S(1)} %log_add_fusion, bf16[3,320,4,3,64]{1,4,2,0,3:T(8,128)(2,1)} %copy-done.6), kind=kOutput, calls=%fused_computation.55 | convolution fusion | flops 166137920 | bytes 24711168 | tf_op jit(solution)/shard_map/ihst,ishd->ithd/dot_general | solution.py:218
  309.3 4.8 fusion.79
  314.5 2.9 copy.71
  317.4 5.4 convert_element_type.81
  322.8 5.7 fusion.86
  328.9 6.7 fusion.55
  335.7 4.4 fusion.89
  341.8 3.6 fusion.87
  347.4 22.1 %all-reduce.1 = (f32[512]{0:T(512)}, f32[1024]{0:T(1024)}) all-reduce(f32[512]{0:T(512)S(1)} %reshape.138, f32[1024]{0:T(1024)S(1)} %get-tuple-element.35), channel_id=1, replica_groups=mesh['dp'=8,'tensor'=4] {'dp'}, use_global_device_ids=true, to_apply=%region_17.18 | all-reduce | flops 1536 | bytes 12288 | tf_op jit(solution)/shard_map/psum | solution.py:246
  374.9 3.0 fusion.59
  378.0 43.7 %all-reduce = (f32[1024]{0:T(1024)}, f32[1024]{0:T(1024)}, f32[1024]{0:T(1024)}, f32[1024]{0:T(1024)}, f32[1024]{0:T(1024)}, /*index=5*/f32[1024]{0:T(1024)}) all-reduce(f32[1024]{0:T(1024)S(1)} %get-tuple-element.22, f32[1024]{0:T(1024)S(1)} %get-tuple-element.21, ...), channel_id=1, replica_groups=mesh['dp'=8,'tensor'=4] {'dp','tensor'}, use_global_device_ids=true, to_apply=%region_20.21 | all-reduce | flops 6144 | bytes 49152 | tf_op jit(solution)/shard_map/psum | solution.py:234
  421.6 357.4 %all-reduce.5.cloned.1.call-done = (f32[1024,768]{1,0:T(8,128)}, f32[256,1024]{1,0:T(8,128)}, f32[1024,1024]{1,0:T(8,128)}, f32[1024,1024]{1,0:T(8,128)}) async-done(((f32[1024,768]{1,0:T(8,128)}, f32[256,1024]{1,0:T(8,128)}, f32[1024,1024]{1,0:T(8,128)}, f32[1024,1024]{1,0:T(8,128)}), (f32[1024,768]{1,0:T(8,128)}, f32[256,1024]{1,0:T(8,128)}, f32[1024,1024]{1,0:T(8,128)}, ...) | async-done | bytes 12582928 | tf_op jit(solution)/shard_map/psum | solution.py:246
  779.0 3.9 copy.87
  (119 shorter events, 46.0 us)
Async XLA Ops:
  7.2 145.1 %copy-start = (bf16[1024,1024]{1,0:T(8,128)(2,1)S(1)}, bf16[1024,1024]{1,0:T(8,128)(2,1)}, u32[]{:S(2)}) copy-start(bf16[1024,1024]{1,0:T(8,128)(2,1)} %param.24) | copy-start | bytes 6291460
  7.2 29.6 %all-gather.5.cloned.1.call-start = ((), (), s32[]{:S(2)}) async-start(), calls=%async_computation.4 | async-start | bytes 2457600 | tf_op jit(solution)/shard_map/all_gather | solution.py:59
  12.0 91.3 %reduce-scatter.5.cloned.1.call-start = ((), (), s32[]{:S(2)}) async-start(), calls=%async_computation.5 | async-start | bytes 4915200 | tf_op jit(solution)/shard_map/reduce_scatter | solution.py:89
  56.4 3.9 copy-start.4
  60.3 43.1 %copy-start.20 = (f32[1024]{0:T(1024)S(1)}, f32[1024]{0:T(1024)}, u32[]{:S(2)}) copy-start(f32[1024]{0:T(1024)} %param.21) | copy-start | bytes 12292
  60.3 44.9 %copy-start.18 = (f32[1024]{0:T(1024)S(1)}, f32[1024]{0:T(1024)}, u32[]{:S(2)}) copy-start(f32[1024]{0:T(1024)} %param.28) | copy-start | bytes 12292
  60.3 44.9 %copy-start.21 = (f32[1024]{0:T(1024)S(1)}, f32[1024]{0:T(1024)}, u32[]{:S(2)}) copy-start(f32[1024]{0:T(1024)} %param.29) | copy-start | bytes 12292
  60.3 46.0 %copy-start.19 = (s32[3,320]{1,0:T(4,128)S(1)}, s32[3,320]{1,0:T(4,128)}, u32[]{:S(2)}) copy-start(s32[3,320]{1,0:T(4,128)} %param.16) | copy-start | bytes 11524
  60.3 67.9 %all-gather.7.cloned.1.call-start = ((), (), s32[]{:S(2)}) async-start(), calls=%async_computation.6 | async-start | bytes 2457600 | tf_op jit(solution)/shard_map/all_gather | solution.py:96
  106.3 46.0 %all-gather.9.cloned.1.call-start = ((), (), s32[]{:S(2)}) async-start(), calls=%async_computation.8 | async-start | bytes 2457600 | tf_op jit(solution)/shard_map/all_gather | solution.py:180
  108.5 43.8 %copy-start.22 = (f32[1024]{0:T(1024)S(1)}, f32[1024]{0:T(1024)}, u32[]{:S(2)}) copy-start(f32[1024]{0:T(1024)} %param.23) | copy-start | bytes 12292
  108.5 106.2 %reduce-scatter.9.cloned.1.call-start = ((), (), s32[]{:S(2)}) async-start(), calls=%async_computation.9 | async-start | bytes 4915200 | tf_op jit(solution)/shard_map/reduce_scatter | solution.py:187
  152.2 15.3 %copy-start.24 = (bf16[1024,1024]{1,0:T(8,128)(2,1)S(1)}, bf16[1024,1024]{1,0:T(8,128)(2,1)}, u32[]{:S(2)}) copy-start(bf16[1024,1024]{1,0:T(8,128)(2,1)} %param.22) | copy-start | bytes 6291460
  171.7 76.7 %reduce-scatter.7.cloned.1.call-start = ((), (), s32[]{:S(2)}) async-start(), calls=%async_computation.7 | async-start | bytes 2457600 | tf_op jit(solution)/shard_map/reduce_scatter | solution.py:101
  180.8 67.5 %copy-start.23 = (f32[1024]{0:T(1024)S(1)}, f32[1024]{0:T(1024)}, u32[]{:S(2)}) copy-start(f32[1024]{0:T(1024)} %param.25) | copy-start | bytes 12292
  180.9 94.1 %all-gather.11.cloned.1.call-start = ((), (), s32[]{:S(2)}) async-start(), calls=%async_computation.10 | async-start | bytes 2457600 | tf_op jit(solution)/shard_map/all_gather | solution.py:195
  248.4 3.6 copy-start.7
  252.9 118.7 %reduce-scatter.11.cloned.1.call-start = ((), (), s32[]{:S(2)}) async-start(), calls=%async_computation.11 | async-start | bytes 4915200 | tf_op jit(solution)/shard_map/reduce_scatter | solution.py:227
  309.3 4.8 copy-start.16
  328.6 450.4 %all-reduce.5.cloned.1.call-start = ((), (), s32[]{:S(2)}) async-start(), calls=%async_computation.12 | async-start | bytes 25165824 | tf_op jit(solution)/shard_map/psum | solution.py:246
  328.9 6.7 copy-start.13
  328.9 6.7 copy-start.26
  335.6 4.5 copy-start.5
  335.6 4.5 copy-start.11
  335.6 6.2 copy-start.14
  335.7 6.1 copy-start.25
  345.4 26.3 %copy-start.2 = (bf16[240,1024]{1,0:T(8,128)(2,1)S(1)}, bf16[240,1024]{1,0:T(8,128)(2,1)}, u32[]{:S(2)}) copy-start(bf16[240,1024]{1,0:T(8,128)(2,1)} %param.15) | copy-start | bytes 1474564
  345.4 26.3 %copy-start.17 = (f32[1024]{0:T(1024)S(1)}, f32[1024]{0:T(1024)}, u32[]{:S(2)}) copy-start(f32[1024]{0:T(1024)} %param.26) | copy-start | bytes 12292
  345.4 29.5 %copy-start.8 = (bf16[240,1024]{1,0:T(8,128)(2,1)S(1)}, bf16[240,1024]{1,0:T(8,128)(2,1)}, u32[]{:S(2)}) copy-start(bf16[240,1024]{1,0:T(8,128)(2,1)} %param.17) | copy-start | bytes 1474564
  779.0 3.9 copy-start.15
  779.0 4.9 copy-start.10
  783.9 3.7 copy-start.9
  (5 other events, 8.5 us)
Sparse Core Ops, SparseCore 0:
  12.2 24.5 all-gather.4
  60.4 42.8 reduce-scatter.4
  106.4 21.8 all-gather.6
  130.3 21.8 all-gather.8
  171.8 42.8 reduce-scatter.8
  217.7 30.6 reduce-scatter.6
  253.1 21.8 all-gather.10
  328.7 42.8 reduce-scatter.10
  377.6 401.4 all-reduce.4
where the time goes:
time: 804 us; the launch traced here: 797 us
  waiting for transfers between devices  551 us (69%)
  matrix products  97.6 us (12%)
  blocking collectives  65.8 us (8%)
  local copies, waits for them, and re-layouts  35 us (4%)
  other arithmetic  32 us (4%)
  between operations  14.6 us (2%)
    psum x1, waiting for transfers between devices, on_device(): lax.psum((in_weight_grad, in_bias_grad, out_weight_grad, up_weight_grad,...  357 us
    psum x1, blocking collectives, on_device(): lax.psum((out_bias_grad, down_bias_grad, gain_one_grad, shift_one_grad, g...  43.7 us
    reduce_scatter x1, waiting for transfers between devices, forward_pass(): lax.psum_scatter(jnp.dot(heads_out, out_weight, preferred_element_type=jn...  43 us
    reduce_scatter x1, waiting for transfers between devices, on_device(): lax.psum_scatter(over_cols(pre_low, up_weight), 'tensor', scatter_dimensi...  33.8 us
    reduce_scatter x1, waiting for transfers between devices, forward_pass(): lax.psum_scatter(jnp.dot(act_low, down_weight, preferred_element_type=jnp...  32.1 us
    dot_general x4, matrix products, over_cols(): lax.dot_general(left, right, (((1,), (1,)), ((), ())), preferred_element_...  26.2 us
    all_gather x1, waiting for transfers between devices, forward_pass(): lax.all_gather(layer_norm(token_values, gain_one, shift_one).astype(jnp.b...  23.1 us
    psum x1, blocking collectives, on_device(): lax.psum((in_weight_grad, in_bias_grad, out_weight_grad, up_weight_grad,...  22.1 us
  transfers between devices with their start and end apart: 9, of which 9 were waited for; matrix products, arithmetic and copies ran while one was open for 6% of the time, Pallas kernels for 0%

commit v1 on v0

v1 whole, which is shorter than its diff:
```python
import jax
import jax.numpy as jnp
from jax import lax
from jax.sharding import PartitionSpec as P

HD = 64
SLOTS = 320
EPSILON = 1e-06
BF = jnp.bfloat16
F32 = jnp.float32


def gelu_exact(values):
    return jax.nn.gelu(values, approximate=False)


def mm(left, right, dims):
    return lax.dot_general(left, right, (dims, ((), ())), preferred_element_type=F32)


def swap(values, axis, bit):
    count = lax.axis_size(axis)
    return lax.ppermute(values, axis, [(i, i ^ bit) for i in range(count)])


def gather_rows(own):
    core = swap(own, "tensor", 1)
    far = swap(own, "tensor", 2)
    return own, core, far, swap(far, "tensor", 1)


def scatter_rows(blocks):
    far = blocks[2] + swap(blocks[3].astype(BF), "tensor", 1).astype(F32)
    near = blocks[0] + swap(blocks[1].astype(BF), "tensor", 1).astype(F32)
    return near + swap(far.astype(BF), "tensor", 2).astype(F32)


def reorder(blocks):
    me = lax.axis_index("tensor")
    core = (me & 1) > 0
    far = (me & 2) > 0
    a, b, c, d = blocks
    a, b = jnp.where(core, b, a), jnp.where(core, a, b)
    c, d = jnp.where(core, d, c), jnp.where(core, c, d)
    return (
        jnp.where(far, c, a),
        jnp.where(far, d, b),
        jnp.where(far, a, c),
        jnp.where(far, b, d),
    )


def split_rows(values, count):
    rows = values.shape[0] // count
    return tuple(values[i * rows : (i + 1) * rows] for i in range(count))


def add_small(own, other_packed):
    high, low = unpack(own)
    other_high, other_low = unpack(other_packed)
    return pack((high + low) + (other_high + other_low))


def pack(values):
    high = values.astype(BF)
    low = (values - high.astype(F32)).astype(BF)
    return jnp.concatenate([high, low], axis=0)


def unpack(packed):
    half = packed.shape[0] // 2
    return packed[:half].astype(F32), packed[half:].astype(F32)


def sum_over_data(values, order, small=None):
    count = lax.axis_size("dp")
    me = lax.axis_index("dp")
    bits = [1 << i for i in range(count.bit_length() - 1)]
    halved = [bits[i] for i in order if i < len(bits)]
    rest = bits[len(halved) :]
    for bit in halved:
        low, high = split_rows(values, 2)
        mine = (me & bit) > 0
        sent = jnp.where(mine, low, high).astype(BF)
        values = jnp.where(mine, high, low) + swap(sent, "dp", bit).astype(F32)
    values = values.astype(BF)
    for bit in rest:
        values = (values.astype(F32) + swap(values, "dp", bit).astype(F32)).astype(BF)
        if small is not None:
            small = add_small(small, swap(small, "dp", bit))
    for bit in reversed(halved):
        rows = values.shape[0]
        mine = (me & bit) > 0
        if small is None:
            other = swap(values, "dp", bit)
        else:
            other = swap(jnp.concatenate([values, small], axis=0), "dp", bit)
            small = add_small(small, other[rows:])
            other = other[:rows]
        values = jnp.concatenate(
            [jnp.where(mine, other, values), jnp.where(mine, values, other)], axis=0
        )
    return (values.astype(F32), small)


def normalise(values):
    average = jnp.mean(values, axis=-1, keepdims=True)
    centred = values - average
    factor = lax.rsqrt(jnp.mean(centred * centred, axis=-1, keepdims=True) + EPSILON)
    return centred * factor, factor


def norm_back(grad, gain, z, factor):
    s = grad * gain
    return factor * (
        s - jnp.mean(s, axis=-1, keepdims=True) - z * jnp.mean(s * z, axis=-1, keepdims=True)
    )


def on_device(
    tokens,
    keep_mask,
    grad_out,
    in_weight,
    in_bias,
    out_weight,
    out_bias,
    up_weight,
    up_bias,
    down_weight,
    down_bias,
    gain_one,
    shift_one,
    gain_two,
    shift_two,
):
    rows = tokens.shape[0]
    me = lax.axis_index("tensor")
    keep_flat = keep_mask.reshape(-1)
    keep_blocks = tuple(
        lax.dynamic_slice_in_dim(keep_flat, (me ^ i) * rows, rows)[:, None] for i in range(4)
    )
    keep_own = keep_blocks[0].astype(F32)
    images = keep_mask.shape[0]
    heads = in_weight.shape[1] // (3 * HD)

    token_values = tokens.astype(F32)
    z_one, factor_one = normalise(token_values)
    normed_one = reorder(gather_rows((z_one * gain_one + shift_one).astype(BF)))
    normed_one = jnp.concatenate(normed_one, axis=0)
    cot_own = grad_out.astype(F32) * keep_own
    cot_all = jnp.concatenate(gather_rows(cot_own.astype(BF)), axis=0)
    projected = mm(normed_one, in_weight, ((1,), (0,))).reshape(-1, heads, 3, HD)
    bias_pair = in_bias.reshape(heads, 2, HD)
    bias_full = jnp.concatenate(
        [bias_pair[:, :1], jnp.zeros((heads, 1, HD), F32), bias_pair[:, 1:]], axis=1
    )
    packed = (projected + bias_full).astype(BF).reshape(images, SLOTS, heads, 3, HD)
    q, k, v = packed[:, :, :, 0], packed[:, :, :, 1], packed[:, :, :, 2]
    live = keep_mask.reshape(images, 1, 1, SLOTS) > 0
    scores = jnp.einsum("ishd,ithd->ihst", q, k, preferred_element_type=F32) * HD ** (-0.5)
    scores = jnp.where(live, scores, -1000000000.0)
    maximum = jnp.max(scores, axis=-1, keepdims=True)
    exponent = jnp.exp(scores - maximum)
    probs = exponent / jnp.sum(exponent, axis=-1, keepdims=True)
    heads_out = jnp.einsum("ihst,ithd->ishd", probs.astype(BF), v, preferred_element_type=F32)
    heads_out = heads_out.astype(BF).reshape(images * SLOTS, heads * HD)
    partial = reorder(split_rows(mm(heads_out, out_weight, ((1,), (0,))), 4))
    middle = token_values + scatter_rows(partial) + out_bias
    z_two, factor_two = normalise(middle)
    second = jnp.concatenate(
        gather_rows((z_two * gain_two + shift_two).astype(BF)), axis=0
    )
    pre_act = mm(second, up_weight, ((1,), (0,))) + up_bias
    act_low = gelu_exact(pre_act).astype(BF)

    act_grad = mm(cot_all, down_weight, ((1,), (1,)))
    pre_grad = jax.vjp(gelu_exact, pre_act)[1](act_grad)[0]
    pre_low = pre_grad.astype(BF)
    second_grad = scatter_rows(split_rows(mm(pre_low, up_weight, ((1,), (1,))), 4))
    down_weight_grad = mm(act_low, cot_all, ((0,), (0,)))
    up_weight_grad = mm(second, pre_low, ((0,), (0,)))
    up_bias_grad = jnp.sum(pre_grad, axis=0)
    feed = scatter_rows(split_rows(mm(act_low, down_weight, ((1,), (0,))), 4))
    output = (keep_own * (middle + feed + down_bias)).astype(BF)
    down_sum, _ = sum_over_data(down_weight_grad, (0, 1, 2))
    up_sum, _ = sum_over_data(up_weight_grad, (1, 0, 2))

    middle_grad = cot_own + norm_back(second_grad, gain_two, z_two, factor_two)
    middle_all = jnp.concatenate(reorder(gather_rows(middle_grad.astype(BF))), axis=0)
    out_weight_grad = mm(heads_out, middle_all, ((0,), (0,)))
    heads_grad = (
        mm(middle_all, out_weight, ((1,), (1,))).astype(BF).reshape(images, SLOTS, heads, HD)
    )
    value_grad = jnp.einsum(
        "ihst,ishd->ithd", probs.astype(BF), heads_grad, preferred_element_type=F32
    )
    prob_grad = jnp.einsum("ishd,ithd->ihst", heads_grad, v, preferred_element_type=F32)
    delta = jnp.sum(probs * prob_grad, axis=-1, keepdims=True)
    score_grad = (probs * (prob_grad - delta) * HD ** (-0.5)).astype(BF)
    query_grad = jnp.einsum("ihst,ithd->ishd", score_grad, k, preferred_element_type=F32)
    key_grad = jnp.einsum("ihst,ishd->ithd", score_grad, q, preferred_element_type=F32)
    in_bias_grad = jnp.sum(jnp.stack([query_grad, value_grad], axis=3), axis=(0, 1)).reshape(-1)
    stacked = jnp.stack([query_grad, key_grad, value_grad], axis=3)
    stacked = stacked.reshape(images * SLOTS, heads * 3 * HD).astype(BF)
    first_grad = scatter_rows(
        reorder(split_rows(mm(stacked, in_weight, ((1,), (1,))), 4))
    )
    in_weight_grad = mm(normed_one, stacked, ((0,), (0,)))
    tokens_grad = middle_grad + norm_back(first_grad, gain_one, z_one, factor_one)

    small = jnp.stack(
        [
            jnp.sum(middle_grad, axis=0),
            jnp.sum(cot_own, axis=0),
            jnp.sum(first_grad * z_one, axis=0),
            jnp.sum(first_grad, axis=0),
            jnp.sum(second_grad * z_two, axis=0),
            jnp.sum(second_grad, axis=0),
        ]
    )
    small = pack(small)
    for bit in (1, 2):
        small = add_small(small, swap(small, "tensor", bit))
    shared = sum(unpack(small))
    own_small = jnp.stack([up_bias_grad, jnp.pad(in_bias_grad, (0, up_bias_grad.shape[0] - in_bias_grad.shape[0]))])
    small = pack(jnp.concatenate([shared, own_small], axis=0))
    mixed = jnp.concatenate(
        [
            in_weight_grad,
            jnp.concatenate(
                [out_weight_grad[:, i * 256 : (i + 1) * 256] for i in range(4)], axis=0
            ),
        ],
        axis=1,
    )
    half = mixed.shape[0] // 2
    first_half, small = sum_over_data(mixed[:half], (0, 1, 2), small)
    second_half, _ = sum_over_data(mixed[half:], (1, 0, 2))
    mixed = jnp.concatenate([first_half, second_half], axis=0)
    columns = in_weight.shape[1]
    small = sum(unpack(small))
    out_sum = jnp.concatenate(split_rows(mixed[:, columns:], 4), axis=1)
    return (
        output,
        tokens_grad,
        mixed[:, :columns],
        small[7, : in_bias.shape[0]],
        out_sum,
        small[0],
        up_sum,
        small[6],
        down_sum,
        small[1],
        small[2],
        small[3],
        small[4],
        small[5],
    )


def solution(mesh):
    rows = P(("dp", "tensor"), None)
    placed = (
        rows,
        P("dp", None),
        rows,
        P(None, "tensor"),
        P("tensor"),
        P("tensor", None),
        P(),
        P(None, "tensor"),
        P("tensor"),
        P("tensor", None),
        P(),
        P(),
        P(),
        P(),
        P(),
    )
    given = (
        rows,
        rows,
        P(None, "tensor"),
        P("tensor"),
        P("tensor", None),
        P(),
        P(None, "tensor"),
        P("tensor"),
        P("tensor", None),
        P(),
        P(),
        P(),
        P(),
        P(),
    )
    return jax.shard_map(on_device, mesh=mesh, in_specs=placed, out_specs=given, check_vma=False)
```

time: 804 us -> 379 us (0.47)
  waiting for transfers between devices: 551 us -> 154 us
  blocking collectives: 65.8 us -> 0 us
  starting transfers between devices: 1.01 us -> 53.2 us
  other arithmetic: 32 us -> 54.7 us
  between operations: 14.6 us -> 2.06 us
  matrix products: 97.6 us -> 86.6 us
  local copies, waits for them, and re-layouts: 35 us -> 24.7 us
    psum x1 -> x0, waiting for transfers between devices: 357 us -> none  [on_device(): lax.psum((in_weight_grad, in_bias_grad, out_weight_grad, up_weight_grad,...]
    ppermute x0 -> x50, waiting for transfers between devices: none -> 154 us  [swap(): return lax.ppermute(values, axis, [(i, i ^ bit) for i in range(count)])]
    reduce_scatter x4 -> x0, waiting for transfers between devices: 111 us -> none  [the longest x1 43 us: forward_pass(): lax.psum_scatter(jnp.dot(heads_out, out_weight, preferred_element_type=jn...]
    all_gather x4 -> x0, waiting for transfers between devices: 82.1 us -> none  [the longest x1 23.1 us: forward_pass(): lax.all_gather(layer_norm(token_values, gain_one, shift_one).astype(jnp.b...]
    psum x2 -> x0, blocking collectives: 65.8 us -> none  [the longest x1 43.7 us: on_device(): lax.psum((out_bias_grad, down_bias_grad, gain_one_grad, shift_one_grad, g...]
    ppermute x0 -> x50, starting transfers between devices: none -> 53.2 us  [swap(): return lax.ppermute(values, axis, [(i, i ^ bit) for i in range(count)])]
    dot_general x18 -> x17, matrix products: 97.6 us -> 80.5 us  [the longest x12 46.4 us: mm(): lax.dot_general(left, right, (dims, ((), ())), preferred_element_type=F32)]
    unnamed x60 -> x94, local copies, waits for them, and re-layouts: 14.6 us -> 4.7 us
  transfers between devices with their start and end apart: 9 -> 50, of which waited for: 9 -> 23; matrix products, arithmetic and copies ran while one was open for 6% -> 30% of each run, Pallas kernels for 0% -> 0%
where the time goes in v1:
time: 379 us; the launch traced here: 375 us
  waiting for transfers between devices  154 us (41%)
  matrix products  86.6 us (23%)
  other arithmetic  54.7 us (14%)
  starting transfers between devices  53.2 us (14%)
  local copies, waits for them, and re-layouts  24.7 us (7%)
    ppermute x50, waiting for transfers between devices, swap(): return lax.ppermute(values, axis, [(i, i ^ bit) for i in range(count)])  154 us
    ppermute x50, starting transfers between devices, swap(): return lax.ppermute(values, axis, [(i, i ^ bit) for i in range(count)])  53.2 us
    dot_general x12, matrix products, mm(): lax.dot_general(left, right, (dims, ((), ())), preferred_element_type=F32)  46.4 us
    dot_general x1, matrix products, on_device(): jnp.einsum('ihst,ithd->ishd', score_grad, k, preferred_element_type=F32)  10.7 us
    dot_general x1, matrix products, on_device(): jnp.einsum('ihst,ishd->ithd', score_grad, q, preferred_element_type=F32)  10.6 us
  transfers between devices with their start and end apart: 50, of which 23 were waited for; matrix products, arithmetic and copies ran while one was open for 30% of the time, Pallas kernels for 0%

profile of v1, /device:TPU:0, one launch (start us, length us, event | category | flops | bytes accessed | tf_op | source)
XLA Modules:
  0.0 374.8 jit_solution(812215940370951090)
XLA Ops:
  9.2 10.7 %collective-permute-done = bf16[240,1024]{1,0:T(8,128)(2,1)S(1)} collective-permute-done((bf16[240,1024]{1,0:T(8,128)(2,1)}, bf16[240,1024]{1,0:T(8,128)(2,1)S(1)}, u32[]{:S(2)}, u32[]{:S(2)}) %collective-permute-start) | collective-permute-done | bytes 491552 | tf_op jit(solution)/shard_map/ppermute | solution.py:23
  28.2 6.7 %reshape.107 = f32[3,320,4,3,64]{1,0,4,3,2:T(4,128)} reshape(f32[960,768]{0,1:T(8,128)} %fusion.83) | data formatting | bytes 5898240 | tf_op jit(solution)/shard_map/reshape | solution.py:153
  34.9 3.9 %fusion.14 = bf16[3,320,4,3,64]{1,4,2,0,3:T(8,128)(2,1)} fusion(f32[3,320,4,3,64]{1,0,4,3,2:T(4,128)} %reshape.107, f32[4,3,64]{2,0,1:T(4,128)S(1)} %copy.146), kind=kLoop, calls=%fused_computation.28 | loop fusion | flops 1474560 | bytes 4426752 | tf_op jit(solution)/shard_map/convert_element_type | solution.py:158
  38.8 6.1 %fusion.131 = (f32[3,4,320]{2,1,0:T(4,128)S(1)}, f32[3,4,320,320]{2,3,1,0:T(8,128)}) fusion(pred[3,320]{1,0:T(4,128)(4,1)S(1)} %broadcast_compare_fusion, bf16[3,320,4,3,64]{1,4,2,0,3:T(8,128)(2,1)} %fusion.14), kind=kOutput, calls=%fused_computation.273 | convolution fusion | flops 162201920 | bytes 6111168 | tf_op jit(solution)/shard_map/sub | solution.py:164
  44.9 3.5 fusion.45
  56.1 11.5 %collective-permute-done.5 = bf16[240,1024]{1,0:T(8,128)(2,1)S(1)} collective-permute-done((bf16[240,1024]{1,0:T(8,128)(2,1)S(1)}, bf16[240,1024]{1,0:T(8,128)(2,1)S(1)}, u32[]{:S(2)}, u32[]{:S(2)}) %collective-permute-start.5) | collective-permute-done | bytes 491552 | tf_op jit(solution)/shard_map/ppermute | solution.py:23
  73.6 10.3 %collective-permute-done.7 = bf16[240,1024]{1,0:T(8,128)(2,1)} collective-permute-done((bf16[240,1024]{1,0:T(8,128)(2,1)}, bf16[240,1024]{1,0:T(8,128)(2,1)}, u32[]{:S(2)}, u32[]{:S(2)}) %collective-permute-start.7) | collective-permute-done | bytes 491552 | tf_op jit(solution)/shard_map/ppermute | solution.py:23
  84.4 8.3 %collective-permute-done.13 = bf16[240,1024]{1,0:T(8,128)(2,1)} collective-permute-done((bf16[240,1024]{1,0:T(8,128)(2,1)}, bf16[240,1024]{1,0:T(8,128)(2,1)}, u32[]{:S(2)}, u32[]{:S(2)}) %collective-permute-start.13) | collective-permute-done | bytes 491552 | tf_op jit(solution)/shard_map/ppermute | solution.py:23
  92.8 13.4 %multiply_convert_fusion.1 = (bf16[960,1024]{1,0:T(8,128)(2,1)S(1)}, f32[960,1024]{1,0:T(8,128)S(1)}, f32[960,1024]{1,0:T(8,128)S(1)}) fusion(f32[1024]{0:T(1024)S(1)} %copy-done.44, bf16[1024,1024]{1,0:T(8,128)(2,1)S(1)} %copy-done, bf16[240,1024]{1,0:T(8,128)(2,1)} %collective-permute-done.8, bf16[240,1024]{1,0:T(8,128)(2,1)} %collective-permute-done.7, ...), kind=kOutput, calls=%fused_computation.13 | convolution fusion | flops 2086010880 | bytes 13897728 | tf_op jit(solution)/shard_map/dot_general | solution.py:18
  106.2 5.5 %fusion.138 = (f32[1024]{0:T(1024)}, bf16[960,1024]{1,0:T(8,128)(2,1)S(1)}) fusion(f32[960,1024]{1,0:T(8,128)S(1)} %get-tuple-element.93, bf16[1024,1024]{1,0:T(8,128)(2,1)S(1)} %copy-done.42, bf16[240,1024]{1,0:T(8,128)(2,1)S(1)} %collective-permute-done.14, bf16[240,1024]{1,0:T(8,128)(2,1)} %collective-permute-done.13, ...), kind=kOutput, calls=%fused_computation.278 | convolution fusion | flops 2036857856 | bytes 13901824 | tf_op jit(solution)/shard_map/dot_general | solution.py:18
  117.6 3.9 %fusion.71 = f32[1024,1024]{1,0:T(8,128)S(1)} fusion(bf16[960,1024]{1,0:T(8,128)(2,1)S(1)} %get-tuple-element.171, bf16[240,1024]{1,0:T(8,128)(2,1)} %collective-permute-done.8, bf16[240,1024]{1,0:T(8,128)(2,1)} %collective-permute-done.7, bf16[240,1024]{1,0:T(8,128)(2,1)} %collective-permute-done.6, bf16[240,1024]{1,0:T(8,128)(2,1)} %add_convert_fusion.1), kind=kOutput, calls=%fused_computation.115 | convolution fusion | flops 2021130240 | bytes 8126464 | tf_op jit(solution)/shard_map/dot_general | solution.py:18
  123.5 3.8 %fusion.79 = f32[1024,1024]{1,0:T(8,128)S(1)} fusion(bf16[960,1024]{1,0:T(8,128)(2,1)S(1)} %get-tuple-element.92, bf16[240,1024]{1,0:T(8,128)(2,1)S(1)} %collective-permute-done.14, bf16[240,1024]{1,0:T(8,128)(2,1)} %collective-permute-done.13, bf16[240,1024]{1,0:T(8,128)(2,1)} %collective-permute-done.12, bf16[240,1024]{1,0:T(8,128)(2,1)} %fusion.76), kind=kOutput, calls=%fused_computation.180 | convolution fusion | flops 2021130240 | bytes 8126464 | tf_op jit(solution)/shard_map/dot_general | solution.py:18
  131.9 9.7 %collective-permute-done.17 = bf16[240,1024]{1,0:T(8,128)(2,1)S(1)} collective-permute-done((bf16[240,1024]{1,0:T(8,128)(2,1)S(1)}, bf16[240,1024]{1,0:T(8,128)(2,1)S(1)}, u32[]{:S(2)}, u32[]{:S(2)}) %collective-permute-start.17) | collective-permute-done | bytes 491552 | tf_op jit(solution)/shard_map/ppermute | solution.py:23
  142.2 9.1 %collective-permute-done.11 = bf16[240,1024]{1,0:T(8,128)(2,1)S(1)} collective-permute-done((bf16[240,1024]{1,0:T(8,128)(2,1)S(1)}, bf16[240,1024]{1,0:T(8,128)(2,1)S(1)}, u32[]{:S(2)}, u32[]{:S(2)}) %collective-permute-start.11) | collective-permute-done | bytes 491552 | tf_op jit(solution)/shard_map/ppermute | solution.py:23
  158.9 10.0 %collective-permute-done.39 = bf16[256,1024]{1,0:T(8,128)(2,1)S(1)} collective-permute-done((bf16[256,1024]{1,0:T(8,128)(2,1)S(1)}, bf16[256,1024]{1,0:T(8,128)(2,1)S(1)}, u32[]{:S(2)}, u32[]{:S(2)}) %collective-permute-start.39) | collective-permute-done | bytes 524320 | tf_op jit(solution)/shard_map/ppermute | solution.py:23
  172.2 4.1 %collective-permute-start.46 = (bf16[128,1024]{1,0:T(8,128)(2,1)S(1)}, bf16[128,1024]{1,0:T(8,128)(2,1)S(1)}, u32[]{:S(2)}, u32[]{:S(2)}) collective-permute-start(bf16[128,1024]{1,0:T(8,128)(2,1)S(1)} %select_convert_fusion.10), channel_id=1, source_target_pairs={{0,16},{4,20},{8,24},{12,28},{16,0},{20,4},{24,8},{28,12},{1,17},{... | collective-permute-start | bytes 786440 | tf_op jit(solution)/shard_map/ppermute | solution.py:23
  176.8 12.4 %collective-permute-done.40 = bf16[128,1024]{1,0:T(8,128)(2,1)S(1)} collective-permute-done((bf16[128,1024]{1,0:T(8,128)(2,1)S(1)}, bf16[128,1024]{1,0:T(8,128)(2,1)S(1)}, u32[]{:S(2)}, u32[]{:S(2)}) %collective-permute-start.40) | collective-permute-done | bytes 262176 | tf_op jit(solution)/shard_map/ppermute | solution.py:23
  190.0 10.4 %collective-permute-done.46 = bf16[128,1024]{1,0:T(8,128)(2,1)S(1)} collective-permute-done((bf16[128,1024]{1,0:T(8,128)(2,1)S(1)}, bf16[128,1024]{1,0:T(8,128)(2,1)S(1)}, u32[]{:S(2)}, u32[]{:S(2)}) %collective-permute-start.46) | collective-permute-done | bytes 262176 | tf_op jit(solution)/shard_map/ppermute | solution.py:23
  204.0 4.8 %fusion.134 = (bf16[3,320,4,1,64]{1,4,2,0,3:T(8,128)(2,1)S(1)}, f32[3,320,4,1,64]{1,4,2,0,3:T(8,128)}) fusion(bf16[3,320,4,64]{1,3,2,0:T(8,128)(2,1)S(1)} %copy.151, f32[3,4,320,320]{2,3,1,0:T(8,128)} %get-tuple-element.160, f32[3,4,320]{2,1,0:T(4,128)S(1)} %copy-done.46), kind=kOutput, calls=%fused_computation.276 | convolution fusion | flops 159989760 | bytes 6896640 | tf_op jit(solution)/shard_map/ihst,ishd->ithd/dot_general | solution.py:195
  208.8 4.5 %fusion.77 = f32[3,4,320,320]{2,3,1,0:T(8,128)} fusion(bf16[3,320,4,64]{1,3,2,0:T(8,128)(2,1)S(1)} %copy.151, bf16[3,320,4,3,64]{1,4,2,0,3:T(8,128)(2,1)} %fusion.14), kind=kOutput, calls=%fused_computation.162 | convolution fusion | flops 157286400 | bytes 5996544 | tf_op jit(solution)/shard_map/ishd,ithd->ihst/dot_general | solution.py:198
  213.3 10.6 %fusion.42 = bf16[3,320,4,1,64]{1,4,2,0,3:T(8,128)(2,1)} fusion(f32[3,4,320,320]{2,3,1,0:T(8,128)} %fusion.77, bf16[3,320,4,3,64]{1,4,2,0,3:T(8,128)(2,1)} %fusion.14, f32[3,4,320,320]{2,3,1,0:T(8,128)} %get-tuple-element.160, f32[3,4,320]{2,1,0:T(4,128)S(1)} %copy-done.46), kind=kOutput, calls=%fused_computation.62 | convolution fusion | flops 166137920 | bytes 24711168 | tf_op jit(solution)/shard_map/ihst,ishd->ithd/dot_general | solution.py:202
  224.0 10.7 %fusion.135 = (bf16[3,320,4,1,64]{1,4,2,0,3:T(8,128)(2,1)}, f32[3,320,4,1,64]{1,4,2,0,3:T(8,128)S(1)}) fusion(f32[3,4,320,320]{2,3,1,0:T(8,128)} %fusion.77, f32[3,4,320,320]{2,3,1,0:T(8,128)} %get-tuple-element.160, f32[3,4,320]{2,1,0:T(4,128)} %copy-done.45, bf16[3,320,4,3,64]{1,4,2,0,3:T(8,128)(2,1)} %fusion.14), kind=kOutput, calls=%fused_computation.277 | convolution fusion | flops 166137920 | bytes 25694208 | tf_op jit(solution)/shard_map/ihst,ithd->ishd/dot_general | solution.py:201
  241.2 5.6 %convert_element_type.368 = bf16[960,768]{0,1:T(8,128)(2,1)} reshape(bf16[3,320,4,3,64]{1,0,4,3,2:T(4,128)(2,1)} %copy.156) | data formatting | bytes 2949120 | tf_op jit(solution)/shard_map/convert_element_type | solution.py:205
  246.8 4.0 %fusion.140 = f32[960,1024]{1,0:T(8,128)S(1)} fusion(bf16[960,768]{0,1:T(8,128)(2,1)} %convert_element_type.368, bf16[1024,768]{1,0:T(8,128)(2,1)} %param.18), kind=kOutput, calls=%fused_computation.280 | convolution fusion | flops 1509949440 | bytes 6979584 | tf_op jit(solution)/shard_map/dot_general | solution.py:18
  260.0 5.7 %collective-permute-start.32 = (bf16[256,1024]{1,0:T(8,128)(2,1)S(1)}, bf16[256,1024]{1,0:T(8,128)(2,1)S(1)}, u32[]{:S(2)}, u32[]{:S(2)}) collective-permute-start(bf16[256,1024]{1,0:T(8,128)(2,1)S(1)} %get-tuple-element.99), channel_id=1, source_target_pairs={{0,8},{4,12},{8,0},{12,4},{16,24},{20,28},{24,16},{28,20},{1,9},{5... | collective-permute-start | bytes 1572872 | tf_op jit(solution)/shard_map/ppermute | solution.py:23
  273.9 4.6 %collective-permute-done.32 = bf16[256,1024]{1,0:T(8,128)(2,1)S(1)} collective-permute-done((bf16[256,1024]{1,0:T(8,128)(2,1)S(1)}, bf16[256,1024]{1,0:T(8,128)(2,1)S(1)}, u32[]{:S(2)}, u32[]{:S(2)}) %collective-permute-start.32) | collective-permute-done | bytes 524320 | tf_op jit(solution)/shard_map/ppermute | solution.py:23
  284.5 5.6 %collective-permute-start.25 = (bf16[128,1024]{1,0:T(8,128)(2,1)S(1)}, bf16[128,1024]{1,0:T(8,128)(2,1)S(1)}, u32[]{:S(2)}, u32[]{:S(2)}) collective-permute-start(bf16[128,1024]{1,0:T(8,128)(2,1)S(1)} %select_convert_fusion.13), channel_id=1, source_target_pairs={{0,8},{4,12},{8,0},{12,4},{16,24},{20,28},{24,16},{28,20},{1,9},{5... | collective-permute-start | bytes 786440 | tf_op jit(solution)/shard_map/ppermute | solution.py:23
  294.3 4.4 %collective-permute-done.25 = bf16[128,1024]{1,0:T(8,128)(2,1)S(1)} collective-permute-done((bf16[128,1024]{1,0:T(8,128)(2,1)S(1)}, bf16[128,1024]{1,0:T(8,128)(2,1)S(1)}, u32[]{:S(2)}, u32[]{:S(2)}) %collective-permute-start.25) | collective-permute-done | bytes 262176 | tf_op jit(solution)/shard_map/ppermute | solution.py:23
  298.8 20.4 %collective-permute-done.34 = bf16[64,1024]{1,0:T(8,128)(2,1)S(1)} collective-permute-done((bf16[64,1024]{1,0:T(8,128)(2,1)S(1)}, bf16[64,1024]{1,0:T(8,128)(2,1)S(1)}, u32[]{:S(2)}, u32[]{:S(2)}) %collective-permute-start.34) | collective-permute-done | bytes 131104 | tf_op jit(solution)/shard_map/ppermute | solution.py:23
  322.6 6.8 %collective-permute-done.26 = bf16[64,1024]{1,0:T(8,128)(2,1)S(1)} collective-permute-done((bf16[64,1024]{1,0:T(8,128)(2,1)S(1)}, bf16[64,1024]{1,0:T(8,128)(2,1)S(1)}, u32[]{:S(2)}, u32[]{:S(2)}) %collective-permute-start.26) | collective-permute-done | bytes 131104 | tf_op jit(solution)/shard_map/ppermute | solution.py:23
  343.6 3.5 collective-permute-done.29
  349.5 7.6 %collective-permute-done.30 = bf16[144,1024]{1,0:T(8,128)(2,1)S(1)} collective-permute-done((bf16[144,1024]{1,0:T(8,128)(2,1)S(1)}, bf16[144,1024]{1,0:T(8,128)(2,1)S(1)}, u32[]{:S(2)}, u32[]{:S(2)}) %collective-permute-start.30) | collective-permute-done | bytes 294944 | tf_op jit(solution)/shard_map/ppermute | solution.py:23
  (295 shorter events, 130.7 us)
Async XLA Ops:
  5.5 14.4 %collective-permute-start = (bf16[240,1024]{1,0:T(8,128)(2,1)}, bf16[240,1024]{1,0:T(8,128)(2,1)S(1)}, u32[]{:S(2)}, u32[]{:S(2)}) collective-permute-start(bf16[240,1024]{1,0:T(8,128)(2,1)} %fusion.55), channel_id=1, source_target_pairs={{0,2},{1,3},{2,0},{3,1},{4,6},{5,7},{6,4},{7,5},{8,10},{9,11},{10,... | collective-permute-start | bytes 1474568 | tf_op jit(solution)/shard_map/ppermute | solution.py:23
  69.4 14.5 %collective-permute-start.7 = (bf16[240,1024]{1,0:T(8,128)(2,1)}, bf16[240,1024]{1,0:T(8,128)(2,1)}, u32[]{:S(2)}, u32[]{:S(2)}) collective-permute-start(bf16[240,1024]{1,0:T(8,128)(2,1)} %add_convert_fusion.1), channel_id=1, source_target_pairs={{0,2},{1,3},{2,0},{3,1},{4,6},{5,7},{6,4},{7,5},{8,10},{9,11},{10,... | collective-permute-start | bytes 1474568 | tf_op jit(solution)/shard_map/ppermute | solution.py:23
  73.3 19.4 %collective-permute-start.13 = (bf16[240,1024]{1,0:T(8,128)(2,1)}, bf16[240,1024]{1,0:T(8,128)(2,1)}, u32[]{:S(2)}, u32[]{:S(2)}) collective-permute-start(bf16[240,1024]{1,0:T(8,128)(2,1)} %fusion.76), channel_id=1, source_target_pairs={{0,2},{1,3},{2,0},{3,1},{4,6},{5,7},{6,4},{7,5},{8,10},{9,11},{10,... | collective-permute-start | bytes 1474568 | tf_op jit(solution)/shard_map/ppermute | solution.py:23
  73.6 19.1 %collective-permute-start.6 = (bf16[240,1024]{1,0:T(8,128)(2,1)}, bf16[240,1024]{1,0:T(8,128)(2,1)}, u32[]{:S(2)}, u32[]{:S(2)}) collective-permute-start(bf16[240,1024]{1,0:T(8,128)(2,1)} %add_convert_fusion.1), channel_id=1, source_target_pairs={{0,1},{1,0},{2,3},{3,2},{4,5},{5,4},{6,7},{7,6},{8,9},{9,8},{10,11... | collective-permute-start | bytes 1474568 | tf_op jit(solution)/shard_map/ppermute | solution.py:23
  83.9 22.3 %collective-permute-start.12 = (bf16[240,1024]{1,0:T(8,128)(2,1)}, bf16[240,1024]{1,0:T(8,128)(2,1)}, u32[]{:S(2)}, u32[]{:S(2)}) collective-permute-start(bf16[240,1024]{1,0:T(8,128)(2,1)} %fusion.76), channel_id=1, source_target_pairs={{0,1},{1,0},{2,3},{3,2},{4,5},{5,4},{6,7},{7,6},{8,9},{9,8},{10,11... | collective-permute-start | bytes 1474568 | tf_op jit(solution)/shard_map/ppermute | solution.py:23
  92.7 13.5 %collective-permute-start.14 = (bf16[240,1024]{1,0:T(8,128)(2,1)}, bf16[240,1024]{1,0:T(8,128)(2,1)S(1)}, u32[]{:S(2)}, u32[]{:S(2)}) collective-permute-start(bf16[240,1024]{1,0:T(8,128)(2,1)} %collective-permute-done.13), channel_id=1, source_target_pairs={{0,1},{1,0},{2,3},{3,2},{4,5},{5,4},{6,7},{7,6},{8,9},{9,8},{10,11... | collective-permute-start | bytes 1474568 | tf_op jit(solution)/shard_map/ppermute | solution.py:23
  114.6 16.7 %collective-permute-start.15 = (bf16[240,1024]{1,0:T(8,128)(2,1)S(1)}, bf16[240,1024]{1,0:T(8,128)(2,1)S(1)}, u32[]{:S(2)}, u32[]{:S(2)}) collective-permute-start(bf16[240,1024]{1,0:T(8,128)(2,1)S(1)} %get-tuple-element.116), channel_id=1, source_target_pairs={{0,1},{1,0},{2,3},{3,2},{4,5},{5,4},{6,7},{7,6},{8,9},{9,8},{10,11... | collective-permute-start | bytes 1474568 | tf_op jit(solution)/shard_map/ppermute | solution.py:23
  117.5 24.7 %collective-permute-start.9 = (bf16[240,1024]{1,0:T(8,128)(2,1)S(1)}, bf16[240,1024]{1,0:T(8,128)(2,1)S(1)}, u32[]{:S(2)}, u32[]{:S(2)}) collective-permute-start(bf16[240,1024]{1,0:T(8,128)(2,1)S(1)} %get-tuple-element.118), channel_id=1, source_target_pairs={{0,1},{1,0},{2,3},{3,2},{4,5},{5,4},{6,7},{7,6},{8,9},{9,8},{10,11... | collective-permute-start | bytes 1474568 | tf_op jit(solution)/shard_map/ppermute | solution.py:23
  121.6 33.5 %collective-permute-start.38 = (bf16[512,1024]{1,0:T(8,128)(2,1)S(1)}, bf16[512,1024]{1,0:T(8,128)(2,1)S(1)}, u32[]{:S(2)}, u32[]{:S(2)}) collective-permute-start(bf16[512,1024]{1,0:T(8,128)(2,1)S(1)} %select_convert_fusion.1), channel_id=1, source_target_pairs={{0,8},{4,12},{8,0},{12,4},{16,24},{20,28},{24,16},{28,20},{1,9},{5... | collective-permute-start | bytes 3145736 | tf_op jit(solution)/shard_map/ppermute | solution.py:23
  127.5 14.1 %collective-permute-start.17 = (bf16[240,1024]{1,0:T(8,128)(2,1)S(1)}, bf16[240,1024]{1,0:T(8,128)(2,1)S(1)}, u32[]{:S(2)}, u32[]{:S(2)}) collective-permute-start(bf16[240,1024]{1,0:T(8,128)(2,1)S(1)} %fusion.63), channel_id=1, source_target_pairs={{0,2},{1,3},{2,0},{3,1},{4,6},{5,7},{6,4},{7,5},{8,10},{9,11},{10,... | collective-permute-start | bytes 1474568 | tf_op jit(solution)/shard_map/ppermute | solution.py:23
  129.2 28.3 %collective-permute-start.44 = (bf16[512,1024]{1,0:T(8,128)(2,1)S(1)}, bf16[512,1024]{1,0:T(8,128)(2,1)S(1)}, u32[]{:S(2)}, u32[]{:S(2)}) collective-permute-start(bf16[512,1024]{1,0:T(8,128)(2,1)S(1)} %select_convert_fusion), channel_id=1, source_target_pairs={{0,4},{4,0},{8,12},{12,8},{16,20},{20,16},{24,28},{28,24},{1,5},{5... | collective-permute-start | bytes 3145736 | tf_op jit(solution)/shard_map/ppermute | solution.py:23
  131.4 20.0 %collective-permute-start.11 = (bf16[240,1024]{1,0:T(8,128)(2,1)S(1)}, bf16[240,1024]{1,0:T(8,128)(2,1)S(1)}, u32[]{:S(2)}, u32[]{:S(2)}) collective-permute-start(bf16[240,1024]{1,0:T(8,128)(2,1)S(1)} %fusion.65), channel_id=1, source_target_pairs={{0,2},{1,3},{2,0},{3,1},{4,6},{5,7},{6,4},{7,5},{8,10},{9,11},{10,... | collective-permute-start | bytes 1474568 | tf_op jit(solution)/shard_map/ppermute | solution.py:23
  153.5 22.8 %collective-permute-start.18 = (bf16[240,1024]{1,0:T(8,128)(2,1)S(1)}, bf16[240,1024]{1,0:T(8,128)(2,1)S(1)}, u32[]{:S(2)}, u32[]{:S(2)}) collective-permute-start(bf16[240,1024]{1,0:T(8,128)(2,1)S(1)} %convert_element_type.365), channel_id=1, source_target_pairs={{0,2},{1,3},{2,0},{3,1},{4,6},{5,7},{6,4},{7,5},{8,10},{9,11},{10,... | collective-permute-start | bytes 1474568 | tf_op jit(solution)/shard_map/ppermute | solution.py:23
  158.4 13.5 %collective-permute-start.45 = (bf16[256,1024]{1,0:T(8,128)(2,1)S(1)}, bf16[256,1024]{1,0:T(8,128)(2,1)S(1)}, u32[]{:S(2)}, u32[]{:S(2)}) collective-permute-start(bf16[256,1024]{1,0:T(8,128)(2,1)S(1)} %select_convert_fusion.2), channel_id=1, source_target_pairs={{0,8},{4,12},{8,0},{12,4},{16,24},{20,28},{24,16},{28,20},{1,9},{5... | collective-permute-start | bytes 1572872 | tf_op jit(solution)/shard_map/ppermute | solution.py:23
  169.2 20.0 %collective-permute-start.40 = (bf16[128,1024]{1,0:T(8,128)(2,1)S(1)}, bf16[128,1024]{1,0:T(8,128)(2,1)S(1)}, u32[]{:S(2)}, u32[]{:S(2)}) collective-permute-start(bf16[128,1024]{1,0:T(8,128)(2,1)S(1)} %select_convert_fusion.11), channel_id=1, source_target_pairs={{0,16},{4,20},{8,24},{12,28},{16,0},{20,4},{24,8},{28,12},{1,17},{... | collective-permute-start | bytes 786440 | tf_op jit(solution)/shard_map/ppermute | solution.py:23
  172.2 28.3 %collective-permute-start.46 = (bf16[128,1024]{1,0:T(8,128)(2,1)S(1)}, bf16[128,1024]{1,0:T(8,128)(2,1)S(1)}, u32[]{:S(2)}, u32[]{:S(2)}) collective-permute-start(bf16[128,1024]{1,0:T(8,128)(2,1)S(1)} %select_convert_fusion.10), channel_id=1, source_target_pairs={{0,16},{4,20},{8,24},{12,28},{16,0},{20,4},{24,8},{28,12},{1,17},{... | collective-permute-start | bytes 786440 | tf_op jit(solution)/shard_map/ppermute | solution.py:23
  176.3 24.4 %collective-permute-start.20 = (bf16[240,1024]{1,0:T(8,128)(2,1)S(1)}, bf16[240,1024]{1,0:T(8,128)(2,1)S(1)}, u32[]{:S(2)}, u32[]{:S(2)}) collective-permute-start(bf16[240,1024]{1,0:T(8,128)(2,1)S(1)} %convert_element_type.365), channel_id=1, source_target_pairs={{0,1},{1,0},{2,3},{3,2},{4,5},{5,4},{6,7},{7,6},{8,9},{9,8},{10,11... | collective-permute-start | bytes 1474568 | tf_op jit(solution)/shard_map/ppermute | solution.py:23
  176.3 24.4 %collective-permute-start.19 = (bf16[240,1024]{1,0:T(8,128)(2,1)S(1)}, bf16[240,1024]{1,0:T(8,128)(2,1)S(1)}, u32[]{:S(2)}, u32[]{:S(2)}) collective-permute-start(bf16[240,1024]{1,0:T(8,128)(2,1)S(1)} %collective-permute-done.18), channel_id=1, source_target_pairs={{0,1},{1,0},{2,3},{3,2},{4,5},{5,4},{6,7},{7,6},{8,9},{9,8},{10,11... | collective-permute-start | bytes 1474568 | tf_op jit(solution)/shard_map/ppermute | solution.py:23
  190.0 70.0 %collective-permute-start.41 = (bf16[128,1024]{1,0:T(8,128)(2,1)}, bf16[128,1024]{1,0:T(8,128)(2,1)}, u32[]{:S(2)}, u32[]{:S(2)}) collective-permute-start(bf16[128,1024]{1,0:T(8,128)(2,1)} %add_convert_fusion.4), channel_id=1, source_target_pairs={{0,16},{4,20},{8,24},{12,28},{16,0},{20,4},{24,8},{28,12},{1,17},{... | collective-permute-start | bytes 786440 | tf_op jit(solution)/shard_map/ppermute | solution.py:23
  200.6 66.2 %collective-permute-start.47 = (bf16[128,1024]{1,0:T(8,128)(2,1)S(1)}, bf16[128,1024]{1,0:T(8,128)(2,1)}, u32[]{:S(2)}, u32[]{:S(2)}) collective-permute-start(bf16[128,1024]{1,0:T(8,128)(2,1)S(1)} %add_convert_fusion.3), channel_id=1, source_target_pairs={{0,16},{4,20},{8,24},{12,28},{16,0},{20,4},{24,8},{28,12},{1,17},{... | collective-permute-start | bytes 786440 | tf_op jit(solution)/shard_map/ppermute | solution.py:23
  254.0 14.8 %collective-permute-start.22 = (bf16[240,1024]{1,0:T(8,128)(2,1)}, bf16[240,1024]{1,0:T(8,128)(2,1)}, u32[]{:S(2)}, u32[]{:S(2)}) collective-permute-start(bf16[240,1024]{1,0:T(8,128)(2,1)} %get-tuple-element.101), channel_id=1, source_target_pairs={{0,1},{1,0},{2,3},{3,2},{4,5},{5,4},{6,7},{7,6},{8,9},{9,8},{10,11... | collective-permute-start | bytes 1474568 | tf_op jit(solution)/shard_map/ppermute | solution.py:23
  254.0 75.5 %collective-permute-start.21 = (bf16[240,1024]{1,0:T(8,128)(2,1)}, bf16[240,1024]{1,0:T(8,128)(2,1)}, u32[]{:S(2)}, u32[]{:S(2)}) collective-permute-start(bf16[240,1024]{1,0:T(8,128)(2,1)} %get-tuple-element.100), channel_id=1, source_target_pairs={{0,1},{1,0},{2,3},{3,2},{4,5},{5,4},{6,7},{7,6},{8,9},{9,8},{10,11... | collective-permute-start | bytes 1474568 | tf_op jit(solution)/shard_map/ppermute | solution.py:23
  258.2 15.1 %collective-permute-start.24 = (bf16[256,1024]{1,0:T(8,128)(2,1)}, bf16[256,1024]{1,0:T(8,128)(2,1)}, u32[]{:S(2)}, u32[]{:S(2)}) collective-permute-start(bf16[256,1024]{1,0:T(8,128)(2,1)} %get-tuple-element.98), channel_id=1, source_target_pairs={{0,4},{4,0},{8,12},{12,8},{16,20},{20,16},{24,28},{28,24},{1,5},{5... | collective-permute-start | bytes 1572872 | tf_op jit(solution)/shard_map/ppermute | solution.py:23
  260.0 18.4 %collective-permute-start.32 = (bf16[256,1024]{1,0:T(8,128)(2,1)S(1)}, bf16[256,1024]{1,0:T(8,128)(2,1)S(1)}, u32[]{:S(2)}, u32[]{:S(2)}) collective-permute-start(bf16[256,1024]{1,0:T(8,128)(2,1)S(1)} %get-tuple-element.99), channel_id=1, source_target_pairs={{0,8},{4,12},{8,0},{12,4},{16,24},{20,28},{24,16},{28,20},{1,9},{5... | collective-permute-start | bytes 1572872 | tf_op jit(solution)/shard_map/ppermute | solution.py:23
  266.8 17.7 %collective-permute-start.42 = (bf16[256,1024]{1,0:T(8,128)(2,1)S(1)}, bf16[256,1024]{1,0:T(8,128)(2,1)S(1)}, u32[]{:S(2)}, u32[]{:S(2)}) collective-permute-start(bf16[256,1024]{1,0:T(8,128)(2,1)S(1)} %pad_maximum_fusion.12), channel_id=1, source_target_pairs={{0,4},{4,0},{8,12},{12,8},{16,20},{20,16},{24,28},{28,24},{1,5},{5... | collective-permute-start | bytes 1572872 | tf_op jit(solution)/shard_map/ppermute | solution.py:23
  268.8 22.5 %collective-permute-start.48 = (bf16[256,1024]{1,0:T(8,128)(2,1)S(1)}, bf16[256,1024]{1,0:T(8,128)(2,1)S(1)}, u32[]{:S(2)}, u32[]{:S(2)}) collective-permute-start(bf16[256,1024]{1,0:T(8,128)(2,1)S(1)} %pad_maximum_fusion.13), channel_id=1, source_target_pairs={{0,8},{4,12},{8,0},{12,4},{16,24},{20,28},{24,16},{28,20},{1,9},{5... | collective-permute-start | bytes 1572872 | tf_op jit(solution)/shard_map/ppermute | solution.py:23
  273.3 56.1 %collective-permute-start.23 = (bf16[240,1024]{1,0:T(8,128)(2,1)S(1)}, bf16[240,1024]{1,0:T(8,128)(2,1)S(1)}, u32[]{:S(2)}, u32[]{:S(2)}) collective-permute-start(bf16[240,1024]{1,0:T(8,128)(2,1)S(1)} %add_convert_fusion), channel_id=1, source_target_pairs={{0,2},{1,3},{2,0},{3,1},{4,6},{5,7},{6,4},{7,5},{8,10},{9,11},{10,... | collective-permute-start | bytes 1474568 | tf_op jit(solution)/shard_map/ppermute | solution.py:23
  284.5 14.2 %collective-permute-start.25 = (bf16[128,1024]{1,0:T(8,128)(2,1)S(1)}, bf16[128,1024]{1,0:T(8,128)(2,1)S(1)}, u32[]{:S(2)}, u32[]{:S(2)}) collective-permute-start(bf16[128,1024]{1,0:T(8,128)(2,1)S(1)} %select_convert_fusion.13), channel_id=1, source_target_pairs={{0,8},{4,12},{8,0},{12,4},{16,24},{20,28},{24,16},{28,20},{1,9},{5... | collective-permute-start | bytes 786440 | tf_op jit(solution)/shard_map/ppermute | solution.py:23
  291.3 67.6 %collective-permute-start.43 = (bf16[512,1024]{1,0:T(8,128)(2,1)}, bf16[512,1024]{1,0:T(8,128)(2,1)}, u32[]{:S(2)}, u32[]{:S(2)}) collective-permute-start(bf16[512,1024]{1,0:T(8,128)(2,1)} %pad_maximum_fusion.7), channel_id=1, source_target_pairs={{0,8},{4,12},{8,0},{12,4},{16,24},{20,28},{24,16},{28,20},{1,9},{5... | collective-permute-start | bytes 3145736 | tf_op jit(solution)/shard_map/ppermute | solution.py:23
  292.6 70.5 %collective-permute-start.49 = (bf16[512,1024]{1,0:T(8,128)(2,1)}, bf16[512,1024]{1,0:T(8,128)(2,1)}, u32[]{:S(2)}, u32[]{:S(2)}) collective-permute-start(bf16[512,1024]{1,0:T(8,128)(2,1)} %pad_maximum_fusion.8), channel_id=1, source_target_pairs={{0,4},{4,0},{8,12},{12,8},{16,20},{20,16},{24,28},{28,24},{1,5},{5... | collective-permute-start | bytes 3145736 | tf_op jit(solution)/shard_map/ppermute | solution.py:23
  298.7 20.6 %collective-permute-start.34 = (bf16[64,1024]{1,0:T(8,128)(2,1)S(1)}, bf16[64,1024]{1,0:T(8,128)(2,1)S(1)}, u32[]{:S(2)}, u32[]{:S(2)}) collective-permute-start(bf16[64,1024]{1,0:T(8,128)(2,1)S(1)} %select_convert_fusion.14), channel_id=1, source_target_pairs={{0,16},{4,20},{8,24},{12,28},{16,0},{20,4},{24,8},{28,12},{1,17},{... | collective-permute-start | bytes 393224 | tf_op jit(solution)/shard_map/ppermute | solution.py:23
  349.2 18.1 %collective-permute-start.37 = (bf16[256,1024]{1,0:T(8,128)(2,1)S(1)}, bf16[256,1024]{1,0:T(8,128)(2,1)S(1)}, u32[]{:S(2)}, u32[]{:S(2)}) collective-permute-start(bf16[256,1024]{1,0:T(8,128)(2,1)S(1)} %pad_maximum_fusion.11), channel_id=1, source_target_pairs={{0,8},{4,12},{8,0},{12,4},{16,24},{20,28},{24,16},{28,20},{1,9},{5... | collective-permute-start | bytes 1572872 | tf_op jit(solution)/shard_map/ppermute | solution.py:23
  (65 other events, 839.6 us)

commit v2 on v1

v2 whole, which is shorter than its diff:
```python
import functools

import jax
import jax.numpy as jnp
from jax import lax
from jax.experimental import pallas as pl
from jax.experimental.pallas import tpu as pltpu
from jax.sharding import PartitionSpec as P

HD = 64
SLOTS = 320
HALF = SLOTS // 2
PIECES = 8
EPSILON = 1e-06
BF = jnp.bfloat16
F32 = jnp.float32
MIB = 1 << 20


def mm(left, right, dims=((1,), (0,))):
    return lax.dot_general(left, right, (dims, ((), ())), preferred_element_type=F32)


NT = ((1,), (1,))
TN = ((0,), (0,))


def swap(values, axis, bit):
    count = lax.axis_size(axis)
    return lax.ppermute(values, axis, [(i, i ^ bit) for i in range(count)])


def after(values, *earlier):
    return lax.optimization_barrier((values, *earlier))[0]


def shape(dims, kind=F32):
    return jax.ShapeDtypeStruct(dims, kind)


def whole(dims):
    return pl.BlockSpec(dims, lambda *_: (0,) * len(dims))


def held(dims, kind):
    rows = -(-dims[-2] // 16) * 16 if len(dims) > 1 else 16
    count = rows * (-(-dims[-1] // 128) * 128)
    for size in dims[:-2]:
        count *= size
    return count * jnp.dtype(kind).itemsize


def run(body, operands, outs, grid=(1,), ins=None, out_specs=None, scratch=(), flops=0, room=6):
    ins = ins or [whole(x.shape) for x in operands[1:]]
    out_specs = out_specs or [whole(x.shape) for x in outs]
    arrays = [*operands[1:], *outs]
    moved = sum(x.size * x.dtype.itemsize for x in arrays)
    limit = room * MIB
    for spec, x in zip([*ins, *out_specs], arrays, strict=True):
        limit += (1 if spec.block_shape == x.shape else 2) * held(spec.block_shape, x.dtype)
    for x in scratch:
        limit += held(x.shape, x.dtype)
    ins = [
        pl.BlockSpec(x.block_shape, x.index_map, pipeline_mode=pl.Buffered(1))
        if x.block_shape == y.shape
        else x
        for x, y in zip(ins, operands[1:], strict=True)
    ]
    return pl.pallas_call(
        body,
        out_shape=outs,
        grid_spec=pltpu.PrefetchScalarGridSpec(
            num_scalar_prefetch=1,
            grid=grid,
            in_specs=ins,
            out_specs=out_specs,
            scratch_shapes=scratch,
        ),
        compiler_params=pltpu.CompilerParams(vmem_limit_bytes=limit),
        cost_estimate=pl.CostEstimate(
            flops=int(flops), bytes_accessed=int(moved), transcendentals=0
        ),
    )(*operands)


def row_tiles(rows, size, step):
    def one(i, carry):
        step(pl.ds(pl.multiple_of(i * size, size), size))
        return carry

    lax.fori_loop(0, rows // size, one, 0)


def normalise(values):
    average = jnp.mean(values, axis=-1, keepdims=True)
    centred = values - average
    factor = lax.rsqrt(jnp.mean(centred * centred, axis=-1, keepdims=True) + EPSILON)
    return centred * factor, factor


def norm_back(grad, gain, z, factor):
    s = grad * gain
    return factor * (
        s - jnp.mean(s, axis=-1, keepdims=True) - z * jnp.mean(s * z, axis=-1, keepdims=True)
    )


def fold(values):
    return functools.reduce(
        lambda a, b: a + b, [values[i : i + 8] for i in range(0, values.shape[0], 8)]
    )


def project_side(blocks, gain, shift, weight, bias, normed, put):
    rows = blocks[0].shape[0]
    for i, block in enumerate(blocks):

        def step(at, block=block, i=i):
            z, _ = normalise(block[at, :].astype(F32))
            tile = pl.ds(pl.multiple_of(at.start + i * rows, 16), at.size)
            normed[tile, :] = (z * gain[...] + shift[...]).astype(BF)

        row_tiles(rows, 48, step)
        put(i, (mm(normed[i * rows : (i + 1) * rows, :], weight[...]) + bias[...]).astype(BF))


def project_local(me, tok_a, tok_b, gain, shift, weight, bias, normed, proj):
    rows = tok_a.shape[0]

    def put(i, values):
        proj[i * rows : (i + 1) * rows, :] = values

    project_side((tok_a, tok_b), gain, shift, weight, bias, normed, put)


def attend(side, qkv, keep, probs, heads_out):
    half_lane = lax.broadcasted_iota(jnp.int32, (1, 2 * HD), 1) // HD
    width = qkv.shape[1] // 3

    def one(j, carry):
        place = 3 * side + j
        image = place // 2
        queries = pl.ds(pl.multiple_of(place * HALF, 16), HALF)
        keys = pl.ds(pl.multiple_of(image * SLOTS, 16), SLOTS)
        live = keep[pl.ds(image, 1), :] > 0
        for pair in range(width // (2 * HD)):
            lanes = pl.ds(pair * 2 * HD, 2 * HD)
            q = qkv[queries, lanes] * 0.125
            k = qkv[keys, pl.ds(width + pair * 2 * HD, 2 * HD)]
            v = qkv[keys, pl.ds(2 * width + pair * 2 * HD, 2 * HD)]
            outs = []
            for e in range(2):
                scores = mm(jnp.where(half_lane == e, q, jnp.zeros_like(q)), k, NT)
                scores = jnp.where(live, scores, -1000000000.0)
                power = jnp.exp(scores - jnp.max(scores, axis=-1, keepdims=True))
                p = (power / jnp.sum(power, axis=-1, keepdims=True)).astype(BF)
                probs[j * 4 + pair * 2 + e] = p
                outs.append(mm(p, v))
            heads_out[pl.ds(pl.multiple_of(j * HALF, 16), HALF), lanes] = jnp.where(
                half_lane == 0, outs[0], outs[1]
            ).astype(BF)
        return carry

    lax.fori_loop(0, 3, one, 0)


def out_project(core, heads_out, weight, send, hold):
    rows = send.shape[0]
    send[...] = mm(
        heads_out[pl.ds(pl.multiple_of((1 - core) * rows, 16), rows), :], weight[...]
    ).astype(BF)
    hold[...] = mm(heads_out[pl.ds(pl.multiple_of(core * rows, 16), rows), :], weight[...])


def attend_far(
    me, near, tok_a, tok_b, gain, shift, weight, bias, keep, out_w,
    normed, qkv, probs, heads_out, send, hold,
):
    rows = tok_a.shape[0]
    core, far = me[0] & 1, me[0] >> 1
    for i in range(2):
        at = pl.multiple_of((2 * far + (core ^ i)) * rows, 16)
        qkv[pl.ds(at, rows), :] = near[i * rows : (i + 1) * rows, :]

    def put(i, values):
        at = pl.multiple_of((2 * (1 - far) + (core ^ i)) * rows, 16)
        qkv[pl.ds(at, rows), :] = values

    project_side((tok_a, tok_b), gain, shift, weight, bias, normed, put)
    attend(1 - far, qkv, keep, probs, heads_out)
    out_project(core, heads_out, out_w, send, hold)


def attend_near(me, qkv, keep, out_w, probs, heads_out, send, hold):
    core, far = me[0] & 1, me[0] >> 1
    attend(far, qkv, keep, probs, heads_out)
    out_project(core, heads_out, out_w, send, hold)


def second_norm(me, tok, hold, near, far, bias, gain, shift, middle, second):
    def step(at):
        total = hold[at, :] + near[at, :].astype(F32) + far[at, :].astype(F32)
        values = tok[at, :].astype(F32) + total + bias[...]
        middle[at, :] = values
        z, _ = normalise(values)
        second[at, :] = (z * gain[...] + shift[...]).astype(BF)

    row_tiles(tok.shape[0], 48, step)


def act_back(me, grad_a, grad_b, keep, down, cot, act_grad):
    rows = grad_a.shape[0]

    @pl.when(pl.program_id(0) == 0)
    def _():
        for i, block in enumerate((grad_a, grad_b)):
            at = pl.ds(i * rows, rows)
            cot[at, :] = (block[...].astype(F32) * keep[at, :]).astype(BF)

    act_grad[...] = mm(cot[...], down[...], NT)


def feed_forward(
    me, norm_a, norm_b, up, bias, act_grad, act, pre_low, bias_grad, send, hold, total, pre
):
    step = pl.program_id(0)
    rows = norm_a.shape[0]
    for i, block in enumerate((norm_a, norm_b)):
        pre[pl.ds(i * rows, rows), :] = mm(block[...], up[...])

    def one(i, sums):
        at = pl.ds(pl.multiple_of(i * 32, 32), 32)
        x = pre[at, :] + bias[...]
        share = 0.5 + 0.5 * lax.erf(x * 0.7071067811865476)
        slope = share + x * (0.3989422804014327 * jnp.exp(-0.5 * x * x))
        act[at, :] = (x * share).astype(BF)
        grad = act_grad[at, :] * slope
        pre_low[at, :] = grad.astype(BF)
        return sums + fold(grad)

    sums = lax.fori_loop(0, 2 * rows // 32, one, jnp.zeros((8, pre.shape[1]), F32))
    bias_grad[...] = jnp.sum(sums, axis=0, keepdims=True)
    part = mm(pre_low[...], up[...], NT)

    @pl.when(step == 0)
    def _():
        total[...] = part

    @pl.when(step > 0)
    def _():
        total[...] += part

    @pl.when(step == pl.num_programs(0) - 1)
    def _():
        hold[...] = total[:rows, :]
        send[...] = total[rows:, :].astype(BF)


def feed_out(me, act, down, send, hold):
    rows = send.shape[0]
    send[...] = mm(act[rows:, :], down[...]).astype(BF)
    hold[...] = mm(act[:rows, :], down[...])


def weight_piece(me, left_a, left_b, right_a, right_b, out):
    out[...] = (
        mm(left_a[...], right_a[...], TN) + mm(left_b[...], right_b[...], TN)
    ).astype(out.dtype)


def middle_back(
    me, hold, near, far, middle, grad, keep, gain, middle_grad, middle_low, sums, parts
):
    parts[...] = jnp.zeros_like(parts)

    def step(at):
        second = hold[at, :] + near[at, :].astype(F32) + far[at, :].astype(F32)
        z, factor = normalise(middle[at, :])
        cot = grad[at, :].astype(F32) * keep[at, :]
        total = cot + norm_back(second, gain[...], z, factor)
        middle_grad[at, :] = total
        middle_low[at, :] = total.astype(BF)
        parts[0] += fold(total)
        parts[1] += fold(cot)
        parts[2] += fold(second * z)
        parts[3] += fold(second)

    row_tiles(hold.shape[0], 48, step)
    for i in range(4):
        sums[i : i + 1, :] = jnp.sum(parts[i], axis=0, keepdims=True)


def attend_back(side, mid_blocks, core, qkv, probs, out_w, grads, pg_q, keys_grad):
    rows = mid_blocks[0].shape[0]
    half_lane = lax.broadcasted_iota(jnp.int32, (1, 2 * HD), 1) // HD
    width = qkv.shape[1] // 3
    for i, block in enumerate(mid_blocks):
        at = pl.multiple_of((core ^ i) * rows, 16)
        grads[pl.ds(at, rows), :] = mm(block[...], out_w[...], NT).astype(BF)

    def one(j, carry):
        place = 3 * side + j
        image = place // 2
        inside = pl.ds(pl.multiple_of(j * HALF, 16), HALF)
        queries = pl.ds(pl.multiple_of(place * HALF, 16), HALF)
        keys = pl.ds(pl.multiple_of(image * SLOTS, 16), SLOTS)
        for pair in range(width // (2 * HD)):
            lanes = pl.ds(pair * 2 * HD, 2 * HD)
            q = qkv[queries, lanes]
            k = qkv[keys, pl.ds(width + pair * 2 * HD, 2 * HD)]
            v = qkv[keys, pl.ds(2 * width + pair * 2 * HD, 2 * HD)]
            g = grads[inside, lanes]
            found = []
            for e in range(2):
                p = probs[j * 4 + pair * 2 + e]
                wide = p.astype(F32)
                prob_grad = mm(jnp.where(half_lane == e, g, jnp.zeros_like(g)), v, NT)
                delta = jnp.sum(wide * prob_grad, axis=-1, keepdims=True)
                score_grad = (wide * (prob_grad - delta) * 0.125).astype(BF)
                found.append(
                    (mm(score_grad, k), mm(score_grad, q, TN), mm(p, g, TN))
                )
            q_grad, k_grad, v_grad = (
                jnp.where(half_lane == 0, a, b) for a, b in zip(*found, strict=True)
            )
            pg_q[inside, lanes] = q_grad
            keys_grad[keys, lanes] += k_grad
            keys_grad[keys, pl.ds(width + pair * 2 * HD, 2 * HD)] += v_grad
        return carry

    lax.fori_loop(0, 3, one, 0)


def back_near(me, mid_a, mid_b, qkv, probs, out_w, pg_q, keys_grad, grads):
    core, far = me[0] & 1, me[0] >> 1
    keys_grad[...] = jnp.zeros_like(keys_grad)
    attend_back(far, (mid_a, mid_b), core, qkv, probs, out_w, grads, pg_q, keys_grad)


def back_far(
    me, mid_a, mid_b, qkv, probs, out_w, near_q, near_keys, in_w,
    proj_near, proj_far, flat_near, flat_far, bias_grad, send, hold, grads, far_q, keys_grad,
):
    core, far = me[0] & 1, me[0] >> 1
    rows = mid_a.shape[0]
    width = far_q.shape[1]
    keys_grad[...] = near_keys[...]
    attend_back(1 - far, (mid_a, mid_b), core, qkv, probs, out_w, grads, far_q, keys_grad)
    bias_grad[...] = jnp.concatenate(
        [
            jnp.sum(far_q[...], axis=0, keepdims=True) + jnp.sum(near_q[...], axis=0, keepdims=True),
            jnp.sum(keys_grad[:, width:], axis=0, keepdims=True),
        ],
        axis=1,
    )
    sides = ((proj_near, flat_near, near_q), (proj_far, flat_far, far_q))
    for side, (out, flat, q_part) in enumerate(sides):
        for i in range(2):
            inside = pl.multiple_of((core ^ i) * rows, 16)
            place = pl.multiple_of((2 * (far ^ side) + (core ^ i)) * rows, 16)
            to = pl.ds(i * rows, rows)
            out[to, :width] = q_part[pl.ds(inside, rows), :].astype(BF)
            out[to, width:] = keys_grad[pl.ds(place, rows), :].astype(BF)
        for head in range(width // HD):
            for kind in range(3):
                at = (head * 3 + kind) * HD
                flat[:, at : at + HD] = out[:, kind * width + head * HD :][:, :HD]
    send[...] = mm(proj_far[rows:, :], in_w[...], NT).astype(BF)
    hold[...] = mm(proj_far[:rows, :], in_w[...], NT)


def first_back(me, proj, in_w, send, hold):
    rows = send.shape[0]
    send[...] = mm(proj[rows:, :], in_w[...], NT).astype(BF)
    hold[...] = mm(proj[:rows, :], in_w[...], NT)


def mixed_piece(me, norm_a, norm_b, proj_a, proj_b, heads_a, heads_b, mid_a, mid_b, out):
    width = proj_a.shape[1]
    out[:, :width] = (
        mm(norm_a[...], proj_a[...], TN) + mm(norm_b[...], proj_b[...], TN)
    ).astype(out.dtype)
    both = mm(heads_a[...], mid_a[...], TN) + mm(heads_b[...], mid_b[...], TN)
    half = both.shape[0] // 2
    out[:, width : width + half] = both[:half].astype(out.dtype)
    out[:, width + half :] = both[half:].astype(out.dtype)


def token_back(me, hold, near, far, tok, middle_grad, gain, tokens_grad, sums, parts):
    parts[...] = jnp.zeros_like(parts)

    def step(at):
        first = hold[at, :] + near[at, :].astype(F32) + far[at, :].astype(F32)
        z, factor = normalise(tok[at, :].astype(F32))
        tokens_grad[at, :] = middle_grad[at, :] + norm_back(first, gain[...], z, factor)
        parts[0] += fold(first * z)
        parts[1] += fold(first)

    row_tiles(hold.shape[0], 48, step)
    for i in range(2):
        sums[i : i + 1, :] = jnp.sum(parts[i], axis=0, keepdims=True)


def place_pieces(me, gathered, out):
    out[...] = gathered[...].astype(F32)


def place_mixed(me, first, second, in_out, out_out):
    in_out[:, : first.shape[1]] = first[...].astype(F32)
    rest = in_out.shape[1] - first.shape[1]
    in_out[:, first.shape[1] :] = second[:, :rest].astype(F32)
    half = out_out.shape[0] // 2
    out_out[:half, :] = second[:, rest : rest + half].astype(F32)
    out_out[half:, :] = second[:, rest + half :].astype(F32)


def piece_of(position, order, me):
    relative = 0
    for step, bit in enumerate(order):
        relative = relative | (((position >> (len(order) - 1 - step)) & 1) << bit)
    return relative ^ (me & (PIECES - 1))


def position_of(piece, order, me):
    relative = piece ^ (me & (PIECES - 1))
    place = 0
    for step, bit in enumerate(order):
        place = place | (((relative >> bit) & 1) << (len(order) - 1 - step))
    return place


def pack(values):
    high = values.astype(BF)
    return jnp.concatenate([high, (values - high.astype(F32)).astype(BF)], axis=0)


def unpack(packed):
    half = packed.shape[0] // 2
    return packed[:half].astype(F32) + packed[half:].astype(F32)


class Reduction:
    def __init__(self, send, order):
        self.send, self.order = send, order
        self.count = lax.axis_size("dp").bit_length() - 1
        self.bits = [*order, *range(len(order), self.count), *reversed(order)]
        self.values, self.small, self.came, self.at = None, None, None, 0

    def take(self, *earlier):
        self.came = swap(self.send, "dp", 1 << self.bits[self.at])
        if earlier:
            self.came = after(self.came, *earlier)
        return self.came

    def arrive(self, *earlier):
        if self.came is None:
            self.take()
        arrived = after(self.came, *earlier)
        self.came = None
        self.at += 1
        halving = len(self.order)
        if self.at < halving:
            middle = self.values.shape[0] // 2
            self.send = (self.values[middle:] + arrived[middle:].astype(F32)).astype(BF)
            self.values = self.values[:middle] + arrived[:middle].astype(F32)
        elif self.at == halving:
            self.values = (self.values + arrived.astype(F32)).astype(BF)
            self.send = self.values
        elif self.at <= self.count:
            self.values = (self.values.astype(F32) + arrived.astype(F32)).astype(BF)
            self.send = self.values
        else:
            rows = self.values.shape[0]
            if self.small is not None:
                self.small = pack(unpack(self.small) + unpack(arrived[rows:]))
            self.values = jnp.concatenate([self.values, arrived[:rows]], axis=0)
            self.send = self.values
            if self.small is not None and self.at < len(self.bits):
                self.send = jnp.concatenate([self.values, self.small], axis=0)
        return self.values

    def join(self, small):
        for bit in range(len(self.order), self.count):
            small = pack(unpack(small) + unpack(swap(small, "dp", 1 << bit)))
        self.small = small
        self.send = jnp.concatenate([self.values, small], axis=0)


ORDER_A = (0, 1, 2)
ORDER_B = (1, 0, 2)


def weight_grad(me, lefts, rights, order, kept):
    rows, columns = lefts[0].shape[0], lefts[0].shape[1]
    wide = rights[0].shape[1]
    piece = columns // PIECES
    half = PIECES // 2
    base = 0 if kept else half

    def index(i, scalars):
        return (0, piece_of(base + i, order, scalars[1]))

    return run(
        weight_piece,
        (me, *lefts, *rights),
        [shape((piece * half, wide), F32 if kept else BF)],
        grid=(half,),
        ins=[pl.BlockSpec((rows, piece), index)] * 2 + [whole(x.shape) for x in rights],
        out_specs=[pl.BlockSpec((piece, wide), lambda i, s: (i, 0))],
        flops=2 * 2 * rows * columns * wide // 2,
    )[0]


def mixed_grad(me, normed, proj, heads, mids, order, kept):
    rows, columns = normed[0].shape
    piece = columns // PIECES
    half = PIECES // 2
    base = 0 if kept else half
    wide = proj[0].shape[1] + heads[0].shape[1]

    def index(i, scalars):
        return (0, piece_of(base + i, order, scalars[1]))

    return run(
        mixed_piece,
        (me, *normed, *proj, *heads, *mids),
        [shape((piece * half, wide), F32 if kept else BF)],
        grid=(half,),
        ins=[pl.BlockSpec((rows, piece), index)] * 2
        + [whole(x.shape) for x in (*proj, *heads)]
        + [pl.BlockSpec((rows, piece), index)] * 2,
        out_specs=[pl.BlockSpec((piece, wide), lambda i, s: (i, 0))],
        flops=2 * 2 * rows * columns * wide // 2,
    )[0]


def place(me, gathered, order):
    piece = gathered.shape[0] // PIECES
    wide = gathered.shape[1]
    return run(
        place_pieces,
        (me, gathered),
        [shape(gathered.shape)],
        grid=(PIECES,),
        ins=[pl.BlockSpec((piece, wide), lambda i, s: (position_of(i, order, s[1]), 0))],
        out_specs=[pl.BlockSpec((piece, wide), lambda i, s: (i, 0))],
    )[0]


def on_device(
    tokens,
    keep_mask,
    grad_out,
    in_weight,
    in_bias,
    out_weight,
    out_bias,
    up_weight,
    up_bias,
    down_weight,
    down_bias,
    gain_one,
    shift_one,
    gain_two,
    shift_two,
):
    rows, model = tokens.shape
    me = jnp.stack([lax.axis_index("tensor"), lax.axis_index("dp")]).astype(jnp.int32)
    images = keep_mask.shape[0]
    heads = in_weight.shape[1] // (3 * HD)
    width = heads * HD
    hidden = up_weight.shape[1]

    def line(values):
        return values.reshape(1, -1)

    side = 2 * rows
    block = 256
    steps = hidden // block
    project_flops = 2 * side * model * 3 * width
    attend_flops = 3 * heads * 4 * HALF * SLOTS * 128 + 2 * side * width * model
    back_flops = 3 * heads * 10 * HALF * SLOTS * 128 + 2 * side * width * model

    def act_grad_of(one, other, keep):
        return run(
            act_back,
            (me, one, other, keep, down_weight),
            [shape((side, model), BF), shape((side, hidden))],
            grid=(steps,),
            ins=[
                whole(one.shape),
                whole(one.shape),
                whole(keep.shape),
                pl.BlockSpec((block, model), lambda i, s: (i, 0)),
            ],
            out_specs=[whole((side, model)), pl.BlockSpec((side, block), lambda i, s: (0, i))],
            flops=2 * side * model * hidden,
        )

    def feed(one, other, act_grad):
        column = pl.BlockSpec((side, block), lambda i, s: (0, i))
        single = pl.BlockSpec((1, block), lambda i, s: (0, i))
        return run(
            feed_forward,
            (me, one, other, up_weight, line(up_bias), act_grad),
            [
                shape((side, hidden), BF),
                shape((side, hidden), BF),
                shape((1, hidden)),
                shape((rows, model), BF),
                shape((rows, model)),
            ],
            grid=(steps,),
            ins=[
                whole(one.shape),
                whole(one.shape),
                pl.BlockSpec((model, block), lambda i, s: (0, i)),
                single,
                column,
            ],
            out_specs=[
                column,
                column,
                single,
                whole((rows, model)),
                whole((rows, model)),
            ],
            scratch=[pltpu.VMEM((side, model), F32), pltpu.VMEM((side, block), F32)],
            flops=4 * side * model * hidden,
        )

    def feed_back(act):
        return run(
            feed_out,
            (me, act, down_weight),
            [shape((rows, model), BF), shape((rows, model))],
            flops=2 * side * model * hidden,
        )

    tok_far = swap(tokens, "tensor", 2)
    tok_core = swap(tokens, "tensor", 1)
    grad_core = swap(grad_out, "tensor", 1)
    keep_flat = keep_mask.reshape(-1).astype(F32)
    keeps = [
        lax.dynamic_slice_in_dim(keep_flat, (me[0] ^ i) * rows, rows) for i in range(4)
    ]
    keep_near = jnp.concatenate(keeps[:2])[:, None]
    keep_far = jnp.concatenate(keeps[2:])[:, None]
    in_grouped = in_weight.reshape(model, heads, 3, HD).transpose(0, 2, 1, 3)
    in_grouped = in_grouped.reshape(model, 3 * width)
    pair = in_bias.reshape(heads, 2, HD).transpose(1, 0, 2).reshape(2, width)
    bias_full = jnp.concatenate([pair[:1], jnp.zeros((1, width), F32), pair[1:]], axis=1)
    norm_near, proj_near = run(
        project_local,
        (me, tokens, tok_core, line(gain_one), line(shift_one), in_grouped, bias_full),
        [shape((side, model), BF), shape((side, 3 * width), BF)],
        flops=project_flops,
    )
    tok_far = after(tok_far, proj_near, keep_near, keep_far)

    tok_both = swap(tok_far, "tensor", 1)
    grad_far = swap(after(grad_out, tok_far), "tensor", 2)
    attend_outs = [
        shape((3 * heads, HALF, SLOTS), BF),
        shape((side, width), BF),
        shape((rows, model), BF),
        shape((rows, model), F32),
    ]
    norm_far, qkv, probs_far, heads_far, send, far_hold = run(
        attend_far,
        (
            me, proj_near, tok_far, tok_both, line(gain_one), line(shift_one), in_grouped,
            bias_full, keep_mask, out_weight,
        ),
        [shape((side, model), BF), shape((2 * side, 3 * width), BF), *attend_outs],
        flops=project_flops + attend_flops,
    )
    arrived = after(swap(send, "tensor", 1), grad_far)
    far_sum = (far_hold + arrived.astype(F32)).astype(BF)
    grad_far = after(grad_far, far_sum)
    grad_both = swap(grad_far, "tensor", 1)
    arrived_far = swap(far_sum, "tensor", 2)
    probs_near, heads_near, send, hold = run(
        attend_near,
        (me, after(qkv, far_sum), keep_mask, out_weight),
        attend_outs,
        flops=attend_flops,
    )
    cot_near, act_grad_near = act_grad_of(after(grad_out, hold), grad_core, keep_near)
    arrived_near = after(swap(send, "tensor", 1), arrived_far)
    middle, second = run(
        second_norm,
        (
            me, tokens, after(hold, cot_near), arrived_near, arrived_far, line(out_bias),
            line(gain_two), line(shift_two),
        ),
        [shape((rows, model)), shape((rows, model), BF)],
    )

    second_far = swap(second, "tensor", 2)
    second_core = swap(second, "tensor", 1)
    act_near, pre_near, up_bias_near, near_send, near_hold = feed(
        second, second_core, act_grad_near
    )
    cot_far, act_grad_far = act_grad_of(after(grad_far, near_hold), grad_both, keep_far)
    second_far = after(second_far, cot_far)
    second_both = swap(second_far, "tensor", 1)
    act_far, pre_far, up_bias_far, far_send, far_hold = feed(
        second_far, second_both, act_grad_far
    )
    far_sum = (far_hold + swap(far_send, "tensor", 1).astype(F32)).astype(BF)
    arrived_far = swap(far_sum, "tensor", 2)
    arrived_near = swap(near_send, "tensor", 1)
    acts, cots = (act_near, act_far), (after(cot_near, far_sum), cot_far)
    down_send = weight_grad(me, acts, cots, ORDER_A, False)
    down = Reduction(down_send, ORDER_A)
    seconds, pres = ((second, second_core), (second_far, second_both)), (pre_near, pre_far)
    seconds = tuple(jnp.concatenate(x, axis=0) for x in seconds)
    pres = (after(pre_near, down_send), pre_far)
    up_send = weight_grad(me, seconds, pres, ORDER_B, False)
    up = Reduction(up_send, ORDER_B)
    feed_send, feed_hold = feed_back(after(act_far, up_send))
    feed_far = (feed_hold + swap(feed_send, "tensor", 1).astype(F32)).astype(BF)
    middle_grad, middle_low, middle_sums = run(
        middle_back,
        (
            me, after(near_hold, feed_hold), arrived_near, arrived_far, middle, grad_out,
            keep_near[:rows], line(gain_two),
        ),
        [shape((rows, model)), shape((rows, model), BF), shape((4, model))],
        scratch=[pltpu.VMEM((4, 8, model), F32)],
    )

    mid_far = swap(middle_low, "tensor", 2)
    mid_core = swap(middle_low, "tensor", 1)
    grads = pltpu.VMEM((side, width), BF)
    down.values = weight_grad(me, (after(act_near, middle_low), act_far), cots, ORDER_A, True)
    near_q, near_keys = run(
        back_near,
        (me, after(middle_low, down.values), mid_core, qkv, probs_near, out_weight),
        [shape((side, width)), shape((2 * side, 2 * width))],
        scratch=[grads],
        flops=back_flops,
    )
    up.values = weight_grad(me, seconds, (after(pre_near, near_q), pre_far), ORDER_B, True)
    mid_far = after(mid_far, up.values)
    mid_both = swap(mid_far, "tensor", 1)
    feed_far = swap(after(feed_far, mid_far), "tensor", 2)
    down.arrive(mid_far)
    up.arrive(mid_far)
    proj_near, proj_far, flat_near, flat_far, bias_grad, far_send, far_hold = run(
        back_far,
        (
            me, mid_far, mid_both, after(qkv, down.send, up.send), probs_far, out_weight, near_q,
            near_keys, in_grouped,
        ),
        [
            shape((side, 3 * width), BF),
            shape((side, 3 * width), BF),
            shape((side, 3 * width), BF),
            shape((side, 3 * width), BF),
            shape((1, 2 * width)),
            shape((rows, model), BF),
            shape((rows, model)),
        ],
        scratch=[
            grads,
            pltpu.VMEM((side, width), F32),
            pltpu.VMEM((2 * side, 2 * width), F32),
        ],
        flops=back_flops + project_flops,
    )
    down.take(bias_grad)
    up.take(bias_grad)
    arrived = after(swap(far_send, "tensor", 1), feed_far, down.came, up.came)
    far_sum = (far_hold + arrived.astype(F32)).astype(BF)
    arrived_far = swap(far_sum, "tensor", 2)

    def mix_heads(values):
        core = (me[0] & 1) > 0
        return jnp.where(core, jnp.concatenate([values[rows:], values[:rows]], axis=0), values)

    down.arrive(far_sum)
    up.arrive(far_sum)
    normed = (after(norm_near, down.send, up.send), norm_far)
    split = (3 * width + width) // 2
    first_proj = tuple(x[:, :split] for x in (flat_near, flat_far))
    second_proj = tuple(x[:, split:] for x in (flat_near, flat_far))
    head_rows = (mix_heads(heads_near), mix_heads(heads_far))
    mids = (
        jnp.concatenate([middle_low, mid_core], axis=0),
        jnp.concatenate([mid_far, mid_both], axis=0),
    )
    first_send = weight_grad(me, normed, first_proj, ORDER_A, False)
    first = Reduction(first_send, ORDER_A)
    second_proj = (after(second_proj[0], first_send), second_proj[1])
    mixed_send = mixed_grad(me, normed, second_proj, head_rows, mids, ORDER_A, False)
    mixed = Reduction(mixed_send, ORDER_A)
    down.take(mixed_send)
    up.take(mixed_send)
    near_send, hold = run(
        first_back,
        (me, after(proj_near, mixed_send), in_grouped),
        [shape((rows, model), BF), shape((rows, model))],
        flops=project_flops,
    )
    arrived_near = swap(near_send, "tensor", 1)
    normed = (after(norm_near, hold), norm_far)
    first.values = weight_grad(me, normed, first_proj, ORDER_A, True)
    normed = (after(norm_near, first.values), norm_far)
    mixed.values = mixed_grad(me, normed, second_proj, head_rows, mids, ORDER_A, True)
    down.arrive(mixed.values)
    up.arrive(mixed.values)
    first.arrive(down.values)
    mixed.arrive(up.values)
    tokens_grad, token_sums = run(
        token_back,
        (
            me, after(hold, first.send, mixed.send), arrived_near, arrived_far, tokens,
            middle_grad, line(gain_one),
        ),
        [shape((rows, model)), shape((2, model))],
        scratch=[pltpu.VMEM((2, 8, model), F32)],
    )
    feed_send, feed_hold = feed_back(after(act_near, token_sums))
    feed_rows = feed_hold + swap(feed_send, "tensor", 1).astype(F32) + feed_far.astype(F32)
    output = (keep_near[:rows] * (middle + feed_rows + down_bias)).astype(BF)

    shared = pack(jnp.concatenate([middle_sums, token_sums], axis=0))
    for bit in (1, 2):
        shared = pack(unpack(shared) + unpack(swap(shared, "tensor", bit)))
    own = jnp.concatenate(
        [up_bias_near + up_bias_far, jnp.pad(bias_grad, ((0, 0), (0, hidden - 2 * width)))], axis=0
    )
    small = jnp.concatenate([unpack(shared), own], axis=0)
    small = pack(jnp.concatenate([small[:, :split], small[:, split:]], axis=0))
    first.arrive(output)
    mixed.arrive(output)
    down.arrive(first.send)
    up.arrive(mixed.send)
    first.arrive(down.send)
    mixed.arrive(up.send)
    while first.at < first.count:
        first.arrive()
    first.join(small)
    first.arrive(mixed.send)
    mixed.arrive(first.send)
    down.arrive(first.send)
    up.arrive(mixed.send)
    while first.at < len(first.bits):
        first.arrive()
        mixed.arrive()
    while down.at < len(down.bits):
        down.arrive()
        up.arrive()
    small = unpack(first.small)
    small = jnp.concatenate([small[:8], small[8:]], axis=1)
    piece = model // PIECES
    down_sum = place(me, down.values, ORDER_A)
    up_sum = place(me, up.values, ORDER_B)
    in_sum, out_sum = run(
        place_mixed,
        (me, first.values, mixed.values),
        [shape((model, 3 * width)), shape((width, model))],
        grid=(PIECES,),
        ins=[
            pl.BlockSpec((piece, split), lambda i, s: (position_of(i, ORDER_A, s[1]), 0)),
            pl.BlockSpec((piece, split), lambda i, s: (position_of(i, ORDER_A, s[1]), 0)),
        ],
        out_specs=[
            pl.BlockSpec((piece, 3 * width), lambda i, s: (i, 0)),
            pl.BlockSpec((width, piece), lambda i, s: (0, i)),
        ],
    )
    in_bias_sum = small[7, : 2 * width].reshape(2, heads, HD).transpose(1, 0, 2).reshape(-1)
    return (
        output,
        tokens_grad,
        in_sum,
        in_bias_sum,
        out_sum,
        small[0],
        up_sum,
        small[6],
        down_sum,
        small[1],
        small[4],
        small[5],
        small[2],
        small[3],
    )


def solution(mesh):
    rows = P(("dp", "tensor"), None)
    placed = (
        rows,
        P("dp", None),
        rows,
        P(None, "tensor"),
        P("tensor"),
        P("tensor", None),
        P(),
        P(None, "tensor"),
        P("tensor"),
        P("tensor", None),
        P(),
        P(),
        P(),
        P(),
        P(),
    )
    given = (
        rows,
        rows,
        P(None, "tensor"),
        P("tensor"),
        P("tensor", None),
        P(),
        P(None, "tensor"),
        P("tensor"),
        P("tensor", None),
        P(),
        P(),
        P(),
        P(),
        P(),
    )
    return jax.shard_map(on_device, mesh=mesh, in_specs=placed, out_specs=given, check_vma=False)
```

time: 379 us -> 306 us (0.81)
  Pallas kernels: 0 us -> 108 us
  matrix products: 86.6 us -> 0 us
  waiting for transfers between devices: 154 us -> 96.5 us
  other arithmetic: 54.7 us -> 12.1 us
  local copies, waits for them, and re-layouts: 24.7 us -> 45.7 us
  starting transfers between devices: 53.2 us -> 40.9 us
    pallas_call x0 -> x26, Pallas kernels: none -> 108 us  [run(): pl.pallas_call(body, out_shape=outs, grid_spec=pltpu.PrefetchScalarGridSp...]
    dot_general x17 -> x0, matrix products: 80.5 us -> none  [the longest x12 46.4 us: mm(): lax.dot_general(left, right, (dims, ((), ())), preferred_element_type=F32)]
    ppermute x50, waiting for transfers between devices: 154 us -> 96.5 us  [swap(): return lax.ppermute(values, axis, [(i, i ^ bit) for i in range(count)])]
    unnamed x94 -> x129, local copies, waits for them, and re-layouts: 4.7 us -> 32 us
    convert_element_type x36 -> x18, other arithmetic: 21.8 us -> 2.89 us  [the longest x1 1.08 us: on_device(): output = (keep_near[:rows] * (middle + feed_rows + down_bias)).astype(BF)]
    ppermute x50, starting transfers between devices: 53.2 us -> 40.9 us  [swap(): return lax.ppermute(values, axis, [(i, i ^ bit) for i in range(count)])]
    reduce_sum x8 -> x0, other arithmetic: 9.55 us -> none  [the longest x1 3.24 us: on_device(): jnp.sum(first_grad * z_one, axis=0)]
    select_n x14 -> x2, other arithmetic: 8.9 us -> 0.13 us  [mix_heads(): jnp.where(core, jnp.concatenate([values[rows:], values[:rows]], axis=0),...]
  transfers between devices with their start and end apart: 50 -> 50, of which waited for: 23 -> 24; matrix products, arithmetic and copies ran while one was open for 30% -> 9% of each run, Pallas kernels for 0% -> 29%
where the time goes in v2:
time: 306 us; the launch traced here: 305 us
  Pallas kernels  108 us (35%)
  waiting for transfers between devices  96.5 us (32%)
  local copies, waits for them, and re-layouts  45.7 us (15%)
  starting transfers between devices  40.9 us (13%)
  other arithmetic  12.1 us (4%)
    pallas_call x26, Pallas kernels, run(): pl.pallas_call(body, out_shape=outs, grid_spec=pltpu.PrefetchScalarGridSp...  108 us
    ppermute x50, waiting for transfers between devices, swap(): return lax.ppermute(values, axis, [(i, i ^ bit) for i in range(count)])  96.5 us
    ppermute x50, starting transfers between devices, swap(): return lax.ppermute(values, axis, [(i, i ^ bit) for i in range(count)])  40.9 us
    unnamed x129, local copies, waits for them, and re-layouts  32 us
    concatenate x10, other arithmetic, arrive(): self.values = jnp.concatenate([self.values, arrived[:rows]], axis=0)  6.46 us
  transfers between devices with their start and end apart: 50, of which 24 were waited for; matrix products, arithmetic and copies ran while one was open for 9% of the time, Pallas kernels for 29%

profile of v2, /device:TPU:0, one launch (start us, length us, event | category | flops | bytes accessed | tf_op | source)
XLA Modules:
  0.0 304.9 jit_solution(12861920635258683928)
XLA Ops:
  13.0 4.0 %shard_map.254 = (bf16[480,1024]{1,0:T(8,128)(2,1)S(1)}, bf16[480,768]{1,0:T(8,128)(2,1)S(1)}) custom-call(s32[2]{0:T(128)S(1)} %pad_add_fusion.me, bf16[240,1024]{1,0:T(8,128)(2,1)S(1)} %copy-done.14, bf16[240,1024]{1,0:T(8,128)(2,1)S(1)} %copy-done.46, f32[1,1024]{1,0:T(1,128)S(1)} %bitcast.30, f32[1,1024]{1,0:T(1,128)S(1)} %bitcast.33, ...), custom_call_target="tpu_custom_call" | custom-call | flops 754974720 | bytes 4287488 | tf_op jit(solution)/shard_map/pallas_call | solution.py:69
  21.7 9.1 %shard_map.255 = (bf16[480,1024]{1,0:T(8,128)(2,1)S(1)}, bf16[960,768]{1,0:T(8,128)(2,1)S(1)}, bf16[12,160,320]{2,1,0:T(8,128)(2,1)S(1)}, bf16[480,256]{1,0:T(8,...) custom-call(s32[2]{0:T(128)S(1)} %pad_add_fusion.me, ...), custom_call_target="tpu_custom_call" | custom-call | flops 1321205760 | bytes 9239296 | tf_op jit(solution)/shard_map/pallas_call | solution.py:69
  34.7 6.2 %shard_map.256 = (bf16[12,160,320]{2,1,0:T(8,128)(2,1)S(1)}, bf16[480,256]{1,0:T(8,128)(2,1)S(1)}, bf16[240,1024]{1,0:T(8,128)(2,1)}, f32[240,1024]{1,0:T(8,128)S(1)}) custom-call(s32[2]{0:T(128)S(1)} %pad_add_fusion.me, bf16[960,768]{1,0:T(8,128)(2,1)S(1)} %get-tuple-element.157.qkv, s32[3,320]{1,0:T(4,128)S(1)} %copy-done.33, bf16[256,1024]{1,0:T(8,128)(2,1)S(1)} %copy-done.12), custom_call_target="tpu_custom_call" | custom-call | flops 566231040 | bytes 4951808 | tf_op jit(solution)/shard_map/pallas_call | solution.py:69
  49.1 3.9 %shard_map.257 = (bf16[480,1024]{1,0:T(8,128)(2,1)S(1)}, f32[480,1024]{1,0:T(8,128)S(1)}) custom-call(s32[2]{0:T(128)S(1)} %pad_add_fusion.me, bf16[240,1024]{1,0:T(8,128)(2,1)} %grad.1, bf16[240,1024]{1,0:T(8,128)(2,1)} %collective-permute-done.5.grad_b, f32[480,1]{1,0:T(8,128)S(1)} %copy-done.31, bf16[1024,1024]{1,0:T(8,128)(2,1)S(1)} %copy-done.40), custom_call_target="tpu_custom_call" | custom-call | flops 1006632960 | bytes 6031232 | tf_op jit(solution)/shard_map/pallas_call | solution.py:69
  57.7 3.7 %shard_map.258 = (f32[240,1024]{1,0:T(8,128)S(1)}, bf16[240,1024]{1,0:T(8,128)(2,1)}) custom-call(s32[2]{0:T(128)S(1)} %pad_add_fusion.me, bf16[240,1024]{1,0:T(8,128)(2,1)S(1)} %copy-done.15, f32[240,1024]{1,0:T(8,128)S(1)} %copy-done.24, bf16[240,1024]{1,0:T(8,128)(2,1)} %collective-permute-done.6.near, bf16[240,1024]{1,0:T(8,128)(2,1)} %collective-permute-done.7.far, ...), custom_call_target="tpu_custom_call" | custom-call | bytes 3944448 | tf_op jit(solution)/shard_map/pallas_call | solution.py:69
  69.3 8.2 %shard_map.259 = (bf16[480,1024]{1,0:T(8,128)(2,1)S(1)}, bf16[480,1024]{1,0:T(8,128)(2,1)S(1)}, f32[1,1024]{1,0:T(1,128)S(1)}, bf16[240,1024]{1,0:T(8,128)(2,1)S(1)}, f32[240,1024]{1,0:T(8,128)S(1)}) custom-call(s32[2]{0:T(128)S(1)} %pad_add_fusion.me, bf16[240,1024]{1,0:T(8,128)(2,1)} %get-tuple-element.128.norm_a, ...), custom_call_target="tpu_custom_call" | custom-call | flops 2013265920 | bytes 8495104 | tf_op jit(solution)/shard_map/pallas_call | solution.py:69
  79.4 4.0 %shard_map.260 = (bf16[480,1024]{1,0:T(8,128)(2,1)S(1)}, f32[480,1024]{1,0:T(8,128)S(1)}) custom-call(s32[2]{0:T(128)S(1)} %pad_add_fusion.me, bf16[240,1024]{1,0:T(8,128)(2,1)} %collective-permute-done.4.grad_a, bf16[240,1024]{1,0:T(8,128)(2,1)} %collective-permute-done.10.grad_b, f32[480,1]{1,0:T(8,128)S(1)} %copy-done.30, bf16[1024,1024]{1,0:T(8,128)(2,1)S(1)} %copy-done.41), custom_call_target="tpu_custom_call" | custom-call | flops 1006632960 | bytes 6031232 | tf_op jit(solution)/shard_map/pallas_call | solution.py:69
  91.3 8.2 %shard_map.261 = (bf16[480,1024]{1,0:T(8,128)(2,1)S(1)}, bf16[480,1024]{1,0:T(8,128)(2,1)S(1)}, f32[1,1024]{1,0:T(1,128)S(1)}, bf16[240,1024]{1,0:T(8,128)(2,1)S(1)}, f32[240,1024]{1,0:T(8,128)S(1)}) custom-call(s32[2]{0:T(128)S(1)} %pad_add_fusion.me, bf16[240,1024]{1,0:T(8,128)(2,1)} %collective-permute-done.9.norm_a, ...), custom_call_target="tpu_custom_call" | custom-call | flops 2013265920 | bytes 8495104 | tf_op jit(solution)/shard_map/pallas_call | solution.py:69
  105.7 2.8 shard_map.262
  110.1 3.0 shard_map.263
  118.4 3.4 %shard_map.265 = (f32[240,1024]{1,0:T(8,128)S(1)}, bf16[240,1024]{1,0:T(8,128)(2,1)S(1)}, f32[4,1024]{1,0:T(4,128)S(1)}) custom-call(s32[2]{0:T(128)S(1)} %pad_add_fusion.me, f32[240,1024]{1,0:T(8,128)S(1)} %copy-done.22, bf16[240,1024]{1,0:T(8,128)(2,1)S(1)} %collective-permute-done.13.near, bf16[240,1024]{1,0:T(8,128)(2,1)S(1)} %collective-permute-done.14.far, ...), custom_call_target="tpu_custom_call" | custom-call | bytes 4936640 | tf_op jit(solution)/shard_map/pallas_call | solution.py:69
  122.8 2.8 shard_map.266
  127.0 6.6 %shard_map.267 = (f32[480,256]{1,0:T(8,128)S(1)}, f32[960,512]{1,0:T(8,128)S(1)}) custom-call(s32[2]{0:T(128)S(1)} %pad_add_fusion.me, bf16[240,1024]{1,0:T(8,128)(2,1)S(1)} %get-tuple-element.150.mid_a, bf16[240,1024]{1,0:T(8,128)(2,1)S(1)} %collective-permute-done.16.mid_b, bf16[960,768]{1,0:T(8,128)(2,1)S(1)} %copy-done.1, ...), custom_call_target="tpu_custom_call" | custom-call | flops 1038090240 | bytes 6668288 | tf_op jit(solution)/shard_map/pallas_call | solution.py:69
  141.8 8.7 %shard_map.269 = (bf16[480,768]{1,0:T(8,128)(2,1)S(1)}, bf16[480,768]{1,0:T(8,128)(2,1)}, bf16[480,768]{1,0:T(8,128)(2,1)S(1)}, bf16[480,768]{1,0:T(8,128)(2,1)S...) custom-call(s32[2]{0:T(128)S(1)} %pad_add_fusion.me, ...), custom_call_target="tpu_custom_call" | custom-call | flops 1793064960 | bytes 12666880 | tf_op jit(solution)/shard_map/pallas_call | solution.py:69
  162.3 2.9 shard_map.271
  169.6 2.8 shard_map.274
  173.4 5.5 %collective-permute-done.28 = bf16[128,1024]{1,0:T(8,128)(2,1)S(1)} collective-permute-done((bf16[128,1024]{1,0:T(8,128)(2,1)S(1)}, bf16[128,1024]{1,0:T(8,128)(2,1)S(1)}, u32[]{:S(2)}, u32[]{:S(2)}) %collective-permute-start.28) | collective-permute-done | bytes 262176 | tf_op jit(solution)/shard_map/ppermute | solution.py:30
  179.2 4.5 %collective-permute-done.27 = bf16[512,512]{1,0:T(8,128)(2,1)S(1)} collective-permute-done((bf16[512,512]{1,0:T(8,128)(2,1)S(1)}, bf16[512,512]{1,0:T(8,128)(2,1)S(1)}, u32[]{:S(2)}, u32[]{:S(2)}) %collective-permute-start.27) | collective-permute-done | bytes 524320 | tf_op jit(solution)/shard_map/ppermute | solution.py:30
  184.0 3.2 %shard_map.275 = (f32[240,1024]{1,0:T(8,128)}, f32[2,1024]{1,0:T(2,128)S(1)}) custom-call(s32[2]{0:T(128)S(1)} %pad_add_fusion.me, f32[240,1024]{1,0:T(8,128)S(1)} %get-tuple-element.189.hold, bf16[240,1024]{1,0:T(8,128)(2,1)S(1)} %collective-permute-done.29.near, bf16[240,1024]{1,0:T(8,128)(2,1)S(1)} %collective-permute-done.30.far, ...), custom_call_target="tpu_custom_call" | custom-call | bytes 4435968 | tf_op jit(solution)/shard_map/pallas_call | solution.py:69
  199.4 8.6 %collective-permute-done.32 = bf16[256,512]{1,0:T(8,128)(2,1)S(1)} collective-permute-done((bf16[256,512]{1,0:T(8,128)(2,1)S(1)}, bf16[256,512]{1,0:T(8,128)(2,1)S(1)}, u32[]{:S(2)}, u32[]{:S(2)}) %collective-permute-start.32) | collective-permute-done | bytes 262176 | tf_op jit(solution)/shard_map/ppermute | solution.py:30
  209.3 6.1 %collective-permute-done.38 = bf16[256,512]{1,0:T(8,128)(2,1)S(1)} collective-permute-done((bf16[256,512]{1,0:T(8,128)(2,1)S(1)}, bf16[256,512]{1,0:T(8,128)(2,1)S(1)}, u32[]{:S(2)}, u32[]{:S(2)}) %collective-permute-start.38) | collective-permute-done | bytes 262176 | tf_op jit(solution)/shard_map/ppermute | solution.py:30
  215.7 6.6 %collective-permute-done.33 = bf16[128,512]{1,0:T(8,128)(2,1)S(1)} collective-permute-done((bf16[128,512]{1,0:T(8,128)(2,1)S(1)}, bf16[128,512]{1,0:T(8,128)(2,1)S(1)}, u32[]{:S(2)}, u32[]{:S(2)}) %collective-permute-start.33) | collective-permute-done | bytes 131104 | tf_op jit(solution)/shard_map/ppermute | solution.py:30
  225.5 8.6 %collective-permute-done.37 = bf16[160,512]{1,0:T(8,128)(2,1)S(1)} collective-permute-done((bf16[160,512]{1,0:T(8,128)(2,1)S(1)}, bf16[160,512]{1,0:T(8,128)(2,1)S(1)}, u32[]{:S(2)}, u32[]{:S(2)}) %collective-permute-start.37) | collective-permute-done | bytes 163872 | tf_op jit(solution)/shard_map/ppermute | solution.py:30
  234.1 4.1 %collective-permute-done.43 = bf16[128,512]{1,0:T(8,128)(2,1)S(1)} collective-permute-done((bf16[128,512]{1,0:T(8,128)(2,1)S(1)}, bf16[128,512]{1,0:T(8,128)(2,1)S(1)}, u32[]{:S(2)}, u32[]{:S(2)}) %collective-permute-start.43) | collective-permute-done | bytes 131104 | tf_op jit(solution)/shard_map/ppermute | solution.py:30
  242.1 5.3 %collective-permute-done.44 = bf16[256,512]{1,0:T(8,128)(2,1)S(1)} collective-permute-done((bf16[256,512]{1,0:T(8,128)(2,1)S(1)}, bf16[256,512]{1,0:T(8,128)(2,1)S(1)}, u32[]{:S(2)}, u32[]{:S(2)}) %collective-permute-start.44) | collective-permute-done | bytes 262176 | tf_op jit(solution)/shard_map/ppermute | solution.py:30
  249.3 4.5 %collective-permute-done.41 = bf16[288,512]{1,0:T(8,128)(2,1)S(1)} collective-permute-done((bf16[288,512]{1,0:T(8,128)(2,1)S(1)}, bf16[288,512]{1,0:T(8,128)(2,1)S(1)}, u32[]{:S(2)}, u32[]{:S(2)}) %collective-permute-start.41) | collective-permute-done | bytes 294944 | tf_op jit(solution)/shard_map/ppermute | solution.py:30
  257.5 7.5 %collective-permute-done.48 = bf16[256,1024]{1,0:T(8,128)(2,1)S(1)} collective-permute-done((bf16[256,1024]{1,0:T(8,128)(2,1)S(1)}, bf16[256,1024]{1,0:T(8,128)(2,1)S(1)}, u32[]{:S(2)}, u32[]{:S(2)}) %collective-permute-start.48) | collective-permute-done | bytes 524320 | tf_op jit(solution)/shard_map/ppermute | solution.py:30
  267.9 10.5 %collective-permute-done.42 = bf16[544,512]{1,0:T(8,128)(2,1)S(1)} collective-permute-done((bf16[544,512]{1,0:T(8,128)(2,1)S(1)}, bf16[544,512]{1,0:T(8,128)(2,1)S(1)}, u32[]{:S(2)}, u32[]{:S(2)}) %collective-permute-start.42) | collective-permute-done | bytes 557088 | tf_op jit(solution)/shard_map/ppermute | solution.py:30
  280.2 4.0 %shard_map.277 = (f32[1024,768]{1,0:T(8,128)}, f32[256,1024]{1,0:T(8,128)}) custom-call(s32[2]{0:T(128)S(1)} %pad_add_fusion.me, bf16[1024,512]{1,0:T(8,128)(2,1)S(1)} %pad_maximum_fusion.2.first, bf16[1024,512]{1,0:T(8,128)(2,1)S(1)} %pad_maximum_fusion.3.second), custom_call_target="tpu_custom_call" | custom-call | bytes 6291456 | tf_op jit(solution)/shard_map/pallas_call | solution.py:69
  288.1 4.1 %shard_map.278 = f32[1024,1024]{1,0:T(8,128)} custom-call(s32[2]{0:T(128)S(1)} %pad_add_fusion.me, bf16[1024,1024]{1,0:T(8,128)(2,1)S(1)} %pad_maximum_fusion.gathered), custom_call_target="tpu_custom_call" | custom-call | bytes 6291456 | tf_op jit(solution)/shard_map/pallas_call | solution.py:69
  292.2 7.1 %collective-permute-done.49 = bf16[512,1024]{1,0:T(8,128)(2,1)} collective-permute-done((bf16[512,1024]{1,0:T(8,128)(2,1)}, bf16[512,1024]{1,0:T(8,128)(2,1)}, u32[]{:S(2)}, u32[]{:S(2)}) %collective-permute-start.49) | collective-permute-done | bytes 1048608 | tf_op jit(solution)/shard_map/ppermute | solution.py:30
  300.8 4.1 %shard_map.279 = f32[1024,1024]{1,0:T(8,128)} custom-call(s32[2]{0:T(128)S(1)} %pad_add_fusion.me, bf16[1024,1024]{1,0:T(8,128)(2,1)S(1)} %pad_maximum_fusion.1.gathered), custom_call_target="tpu_custom_call" | custom-call | bytes 6291456 | tf_op jit(solution)/shard_map/pallas_call | solution.py:69
  (304 shorter events, 128.9 us)
Async XLA Ops:
  1.2 15.8 %collective-permute-start.1 = (bf16[240,1024]{1,0:T(8,128)(2,1)}, bf16[240,1024]{1,0:T(8,128)(2,1)S(1)}, u32[]{:S(2)}, u32[]{:S(2)}) collective-permute-start(bf16[240,1024]{1,0:T(8,128)(2,1)} %tok.3), channel_id=1, source_target_pairs={{0,2},{1,3},{2,0},{3,1},{4,6},{5,7},{6,4},{7,5},{8,10},{9,11},{10,... | collective-permute-start | bytes 1474568 | tf_op jit(solution)/shard_map/ppermute | solution.py:30
  18.0 14.4 %collective-permute-start.4 = (bf16[240,1024]{1,0:T(8,128)(2,1)}, bf16[240,1024]{1,0:T(8,128)(2,1)}, u32[]{:S(2)}, u32[]{:S(2)}) collective-permute-start(bf16[240,1024]{1,0:T(8,128)(2,1)} %grad.1), channel_id=1, source_target_pairs={{0,2},{1,3},{2,0},{3,1},{4,6},{5,7},{6,4},{7,5},{8,10},{9,11},{10,... | collective-permute-start | bytes 1474568 | tf_op jit(solution)/shard_map/ppermute | solution.py:30
  32.0 14.4 %collective-permute-start.5 = (bf16[240,1024]{1,0:T(8,128)(2,1)}, bf16[240,1024]{1,0:T(8,128)(2,1)}, u32[]{:S(2)}, u32[]{:S(2)}) collective-permute-start(bf16[240,1024]{1,0:T(8,128)(2,1)} %grad.1), channel_id=1, source_target_pairs={{0,1},{1,0},{2,3},{3,2},{4,5},{5,4},{6,7},{7,6},{8,9},{9,8},{10,11... | collective-permute-start | bytes 1474568 | tf_op jit(solution)/shard_map/ppermute | solution.py:30
  43.8 13.8 %collective-permute-start.7 = (bf16[240,1024]{1,0:T(8,128)(2,1)}, bf16[240,1024]{1,0:T(8,128)(2,1)}, u32[]{:S(2)}, u32[]{:S(2)}) collective-permute-start(bf16[240,1024]{1,0:T(8,128)(2,1)} %add_convert_fusion.3), channel_id=1, source_target_pairs={{0,2},{1,3},{2,0},{3,1},{4,6},{5,7},{6,4},{7,5},{8,10},{9,11},{10,... | collective-permute-start | bytes 1474568 | tf_op jit(solution)/shard_map/ppermute | solution.py:30
  62.3 17.1 %collective-permute-start.10 = (bf16[240,1024]{1,0:T(8,128)(2,1)}, bf16[240,1024]{1,0:T(8,128)(2,1)}, u32[]{:S(2)}, u32[]{:S(2)}) collective-permute-start(bf16[240,1024]{1,0:T(8,128)(2,1)} %collective-permute-done.4.grad_a), channel_id=1, source_target_pairs={{0,1},{1,0},{2,3},{3,2},{4,5},{5,4},{6,7},{7,6},{8,9},{9,8},{10,11... | collective-permute-start | bytes 1474568 | tf_op jit(solution)/shard_map/ppermute | solution.py:30
  62.8 22.9 %collective-permute-start.9 = (bf16[240,1024]{1,0:T(8,128)(2,1)}, bf16[240,1024]{1,0:T(8,128)(2,1)}, u32[]{:S(2)}, u32[]{:S(2)}) collective-permute-start(bf16[240,1024]{1,0:T(8,128)(2,1)} %get-tuple-element.128.norm_a), channel_id=1, source_target_pairs={{0,2},{1,3},{2,0},{3,1},{4,6},{5,7},{6,4},{7,5},{8,10},{9,11},{10,... | collective-permute-start | bytes 1474568 | tf_op jit(solution)/shard_map/ppermute | solution.py:30
  101.0 15.6 %collective-permute-start.13 = (bf16[240,1024]{1,0:T(8,128)(2,1)S(1)}, bf16[240,1024]{1,0:T(8,128)(2,1)S(1)}, u32[]{:S(2)}, u32[]{:S(2)}) collective-permute-start(bf16[240,1024]{1,0:T(8,128)(2,1)S(1)} %copy-done.48), channel_id=1, source_target_pairs={{0,1},{1,0},{2,3},{3,2},{4,5},{5,4},{6,7},{7,6},{8,9},{9,8},{10,11... | collective-permute-start | bytes 1474568 | tf_op jit(solution)/shard_map/ppermute | solution.py:30
  104.7 13.7 %collective-permute-start.14 = (bf16[240,1024]{1,0:T(8,128)(2,1)S(1)}, bf16[240,1024]{1,0:T(8,128)(2,1)S(1)}, u32[]{:S(2)}, u32[]{:S(2)}) collective-permute-start(bf16[240,1024]{1,0:T(8,128)(2,1)S(1)} %add_convert_fusion.2), channel_id=1, source_target_pairs={{0,2},{1,3},{2,0},{3,1},{4,6},{5,7},{6,4},{7,5},{8,10},{9,11},{10,... | collective-permute-start | bytes 1474568 | tf_op jit(solution)/shard_map/ppermute | solution.py:30
  108.5 29.3 %collective-permute-start.18 = (bf16[512,1024]{1,0:T(8,128)(2,1)S(1)}, bf16[512,1024]{1,0:T(8,128)(2,1)S(1)}, u32[]{:S(2)}, u32[]{:S(2)}) collective-permute-start(bf16[512,1024]{1,0:T(8,128)(2,1)S(1)} %shard_map.262), channel_id=1, source_target_pairs={{0,4},{4,0},{8,12},{12,8},{16,20},{20,16},{24,28},{28,24},{1,5},{5... | collective-permute-start | bytes 3145736 | tf_op jit(solution)/shard_map/ppermute | solution.py:30
  113.1 25.1 %collective-permute-start.19 = (bf16[512,1024]{1,0:T(8,128)(2,1)S(1)}, bf16[512,1024]{1,0:T(8,128)(2,1)S(1)}, u32[]{:S(2)}, u32[]{:S(2)}) collective-permute-start(bf16[512,1024]{1,0:T(8,128)(2,1)S(1)} %shard_map.263), channel_id=1, source_target_pairs={{0,8},{4,12},{8,0},{12,4},{16,24},{20,28},{24,16},{28,20},{1,9},{5... | collective-permute-start | bytes 3145736 | tf_op jit(solution)/shard_map/ppermute | solution.py:30
  121.8 14.6 %collective-permute-start.15 = (bf16[240,1024]{1,0:T(8,128)(2,1)S(1)}, bf16[240,1024]{1,0:T(8,128)(2,1)S(1)}, u32[]{:S(2)}, u32[]{:S(2)}) collective-permute-start(bf16[240,1024]{1,0:T(8,128)(2,1)S(1)} %get-tuple-element.150.mid_a), channel_id=1, source_target_pairs={{0,2},{1,3},{2,0},{3,1},{4,6},{5,7},{6,4},{7,5},{8,10},{9,11},{10,... | collective-permute-start | bytes 1474568 | tf_op jit(solution)/shard_map/ppermute | solution.py:30
  136.7 17.3 %collective-permute-start.23 = (bf16[240,1024]{1,0:T(8,128)(2,1)S(1)}, bf16[240,1024]{1,0:T(8,128)(2,1)S(1)}, u32[]{:S(2)}, u32[]{:S(2)}) collective-permute-start(bf16[240,1024]{1,0:T(8,128)(2,1)S(1)} %add_convert_fusion.1), channel_id=1, source_target_pairs={{0,2},{1,3},{2,0},{3,1},{4,6},{5,7},{6,4},{7,5},{8,10},{9,11},{10,... | collective-permute-start | bytes 1474568 | tf_op jit(solution)/shard_map/ppermute | solution.py:30
  138.6 13.6 %collective-permute-start.20 = (bf16[256,1024]{1,0:T(8,128)(2,1)S(1)}, bf16[256,1024]{1,0:T(8,128)(2,1)S(1)}, u32[]{:S(2)}, u32[]{:S(2)}) collective-permute-start(bf16[256,1024]{1,0:T(8,128)(2,1)S(1)} %get-tuple-element.225), channel_id=1, source_target_pairs={{0,8},{4,12},{8,0},{12,4},{16,24},{20,28},{24,16},{28,20},{1,9},{5... | collective-permute-start | bytes 1572872 | tf_op jit(solution)/shard_map/ppermute | solution.py:30
  140.6 13.4 %collective-permute-start.24 = (bf16[256,1024]{1,0:T(8,128)(2,1)S(1)}, bf16[256,1024]{1,0:T(8,128)(2,1)S(1)}, u32[]{:S(2)}, u32[]{:S(2)}) collective-permute-start(bf16[256,1024]{1,0:T(8,128)(2,1)S(1)} %get-tuple-element.223), channel_id=1, source_target_pairs={{0,4},{4,0},{8,12},{12,8},{16,20},{20,16},{24,28},{28,24},{1,5},{5... | collective-permute-start | bytes 1572872 | tf_op jit(solution)/shard_map/ppermute | solution.py:30
  154.2 19.2 %collective-permute-start.26 = (bf16[128,1024]{1,0:T(8,128)(2,1)S(1)}, bf16[128,1024]{1,0:T(8,128)(2,1)S(1)}, u32[]{:S(2)}, u32[]{:S(2)}) collective-permute-start(bf16[128,1024]{1,0:T(8,128)(2,1)S(1)} %fusion.9), channel_id=1, source_target_pairs={{0,16},{4,20},{8,24},{12,28},{16,0},{20,4},{24,8},{28,12},{1,17},{... | collective-permute-start | bytes 786440 | tf_op jit(solution)/shard_map/ppermute | solution.py:30
  157.0 21.9 %collective-permute-start.28 = (bf16[128,1024]{1,0:T(8,128)(2,1)S(1)}, bf16[128,1024]{1,0:T(8,128)(2,1)S(1)}, u32[]{:S(2)}, u32[]{:S(2)}) collective-permute-start(bf16[128,1024]{1,0:T(8,128)(2,1)S(1)} %fusion.8), channel_id=1, source_target_pairs={{0,16},{4,20},{8,24},{12,28},{16,0},{20,4},{24,8},{28,12},{1,17},{... | collective-permute-start | bytes 786440 | tf_op jit(solution)/shard_map/ppermute | solution.py:30
  157.5 26.5 %collective-permute-start.30 = (bf16[240,1024]{1,0:T(8,128)(2,1)S(1)}, bf16[240,1024]{1,0:T(8,128)(2,1)S(1)}, u32[]{:S(2)}, u32[]{:S(2)}) collective-permute-start(bf16[240,1024]{1,0:T(8,128)(2,1)S(1)} %add_convert_fusion), channel_id=1, source_target_pairs={{0,2},{1,3},{2,0},{3,1},{4,6},{5,7},{6,4},{7,5},{8,10},{9,11},{10,... | collective-permute-start | bytes 1474568 | tf_op jit(solution)/shard_map/ppermute | solution.py:30
  160.7 18.4 %collective-permute-start.25 = (bf16[512,512]{1,0:T(8,128)(2,1)S(1)}, bf16[512,512]{1,0:T(8,128)(2,1)S(1)}, u32[]{:S(2)}, u32[]{:S(2)}) collective-permute-start(bf16[512,512]{1,0:T(8,128)(2,1)S(1)} %shard_map.270), channel_id=1, source_target_pairs={{0,4},{4,0},{8,12},{12,8},{16,20},{20,16},{24,28},{28,24},{1,5},{5... | collective-permute-start | bytes 1572872 | tf_op jit(solution)/shard_map/ppermute | solution.py:30
  165.2 18.5 %collective-permute-start.27 = (bf16[512,512]{1,0:T(8,128)(2,1)S(1)}, bf16[512,512]{1,0:T(8,128)(2,1)S(1)}, u32[]{:S(2)}, u32[]{:S(2)}) collective-permute-start(bf16[512,512]{1,0:T(8,128)(2,1)S(1)} %shard_map.271), channel_id=1, source_target_pairs={{0,4},{4,0},{8,12},{12,8},{16,20},{20,16},{24,28},{28,24},{1,5},{5... | collective-permute-start | bytes 1572872 | tf_op jit(solution)/shard_map/ppermute | solution.py:30
  187.4 21.9 %collective-permute-start.34 = (bf16[128,1024]{1,0:T(8,128)(2,1)S(1)}, bf16[128,1024]{1,0:T(8,128)(2,1)S(1)}, u32[]{:S(2)}, u32[]{:S(2)}) collective-permute-start(bf16[128,1024]{1,0:T(8,128)(2,1)S(1)} %fusion.6), channel_id=1, source_target_pairs={{0,16},{4,20},{8,24},{12,28},{16,0},{20,4},{24,8},{28,12},{1,17},{... | collective-permute-start | bytes 786440 | tf_op jit(solution)/shard_map/ppermute | solution.py:30
  190.1 25.6 %collective-permute-start.40 = (bf16[128,1024]{1,0:T(8,128)(2,1)S(1)}, bf16[128,1024]{1,0:T(8,128)(2,1)S(1)}, u32[]{:S(2)}, u32[]{:S(2)}) collective-permute-start(bf16[128,1024]{1,0:T(8,128)(2,1)S(1)} %fusion.3), channel_id=1, source_target_pairs={{0,16},{4,20},{8,24},{12,28},{16,0},{20,4},{24,8},{28,12},{1,17},{... | collective-permute-start | bytes 786440 | tf_op jit(solution)/shard_map/ppermute | solution.py:30
  190.4 17.6 %collective-permute-start.32 = (bf16[256,512]{1,0:T(8,128)(2,1)S(1)}, bf16[256,512]{1,0:T(8,128)(2,1)S(1)}, u32[]{:S(2)}, u32[]{:S(2)}) collective-permute-start(bf16[256,512]{1,0:T(8,128)(2,1)S(1)} %get-tuple-element.229), channel_id=1, source_target_pairs={{0,8},{4,12},{8,0},{12,4},{16,24},{20,28},{24,16},{28,20},{1,9},{5... | collective-permute-start | bytes 786440 | tf_op jit(solution)/shard_map/ppermute | solution.py:30
  190.8 24.6 %collective-permute-start.38 = (bf16[256,512]{1,0:T(8,128)(2,1)S(1)}, bf16[256,512]{1,0:T(8,128)(2,1)S(1)}, u32[]{:S(2)}, u32[]{:S(2)}) collective-permute-start(bf16[256,512]{1,0:T(8,128)(2,1)S(1)} %get-tuple-element.227), channel_id=1, source_target_pairs={{0,8},{4,12},{8,0},{12,4},{16,24},{20,28},{24,16},{28,20},{1,9},{5... | collective-permute-start | bytes 786440 | tf_op jit(solution)/shard_map/ppermute | solution.py:30
  208.0 14.3 %collective-permute-start.33 = (bf16[128,512]{1,0:T(8,128)(2,1)S(1)}, bf16[128,512]{1,0:T(8,128)(2,1)S(1)}, u32[]{:S(2)}, u32[]{:S(2)}) collective-permute-start(bf16[128,512]{1,0:T(8,128)(2,1)S(1)} %fusion.13), channel_id=1, source_target_pairs={{0,16},{4,20},{8,24},{12,28},{16,0},{20,4},{24,8},{28,12},{1,17},{... | collective-permute-start | bytes 393224 | tf_op jit(solution)/shard_map/ppermute | solution.py:30
  225.1 13.1 %collective-permute-start.43 = (bf16[128,512]{1,0:T(8,128)(2,1)S(1)}, bf16[128,512]{1,0:T(8,128)(2,1)S(1)}, u32[]{:S(2)}, u32[]{:S(2)}) collective-permute-start(bf16[128,512]{1,0:T(8,128)(2,1)S(1)} %fusion.12), channel_id=1, source_target_pairs={{0,16},{4,20},{8,24},{12,28},{16,0},{20,4},{24,8},{28,12},{1,17},{... | collective-permute-start | bytes 393224 | tf_op jit(solution)/shard_map/ppermute | solution.py:30
  238.3 15.5 %collective-permute-start.41 = (bf16[288,512]{1,0:T(8,128)(2,1)S(1)}, bf16[288,512]{1,0:T(8,128)(2,1)S(1)}, u32[]{:S(2)}, u32[]{:S(2)}) collective-permute-start(bf16[288,512]{1,0:T(8,128)(2,1)S(1)} %pad_maximum_fusion.9), channel_id=1, source_target_pairs={{0,8},{4,12},{8,0},{12,4},{16,24},{20,28},{24,16},{28,20},{1,9},{5... | collective-permute-start | bytes 884744 | tf_op jit(solution)/shard_map/ppermute | solution.py:30
  240.3 16.0 %collective-permute-start.46 = (bf16[256,1024]{1,0:T(8,128)(2,1)S(1)}, bf16[256,1024]{1,0:T(8,128)(2,1)S(1)}, u32[]{:S(2)}, u32[]{:S(2)}) collective-permute-start(bf16[256,1024]{1,0:T(8,128)(2,1)S(1)} %pad_maximum_fusion.7), channel_id=1, source_target_pairs={{0,4},{4,0},{8,12},{12,8},{16,20},{20,16},{24,28},{28,24},{1,5},{5... | collective-permute-start | bytes 1572872 | tf_op jit(solution)/shard_map/ppermute | solution.py:30
  242.0 23.0 %collective-permute-start.48 = (bf16[256,1024]{1,0:T(8,128)(2,1)S(1)}, bf16[256,1024]{1,0:T(8,128)(2,1)S(1)}, u32[]{:S(2)}, u32[]{:S(2)}) collective-permute-start(bf16[256,1024]{1,0:T(8,128)(2,1)S(1)} %pad_maximum_fusion.6), channel_id=1, source_target_pairs={{0,8},{4,12},{8,0},{12,4},{16,24},{20,28},{24,16},{28,20},{1,9},{5... | collective-permute-start | bytes 1572872 | tf_op jit(solution)/shard_map/ppermute | solution.py:30
  247.5 20.3 %collective-permute-start.45 = (bf16[512,512]{1,0:T(8,128)(2,1)S(1)}, bf16[512,512]{1,0:T(8,128)(2,1)S(1)}, u32[]{:S(2)}, u32[]{:S(2)}) collective-permute-start(bf16[512,512]{1,0:T(8,128)(2,1)S(1)} %pad_maximum_fusion.8), channel_id=1, source_target_pairs={{0,4},{4,0},{8,12},{12,8},{16,20},{20,16},{24,28},{28,24},{1,5},{5... | collective-permute-start | bytes 1572872 | tf_op jit(solution)/shard_map/ppermute | solution.py:30
  254.5 23.8 %collective-permute-start.42 = (bf16[544,512]{1,0:T(8,128)(2,1)S(1)}, bf16[544,512]{1,0:T(8,128)(2,1)S(1)}, u32[]{:S(2)}, u32[]{:S(2)}) collective-permute-start(bf16[544,512]{1,0:T(8,128)(2,1)S(1)} %constant_dynamic-update-slice_fusion.8), channel_id=1, source_target_pairs={{0,4},{4,0},{8,12},{12,8},{16,20},{20,16},{24,28},{28,24},{1,5},{5... | collective-permute-start | bytes 1671176 | tf_op jit(solution)/shard_map/ppermute | solution.py:30
  257.5 29.2 %collective-permute-start.47 = (bf16[512,1024]{1,0:T(8,128)(2,1)}, bf16[512,1024]{1,0:T(8,128)(2,1)}, u32[]{:S(2)}, u32[]{:S(2)}) collective-permute-start(bf16[512,1024]{1,0:T(8,128)(2,1)} %pad_maximum_fusion.4), channel_id=1, source_target_pairs={{0,8},{4,12},{8,0},{12,4},{16,24},{20,28},{24,16},{28,20},{1,9},{5... | collective-permute-start | bytes 3145736 | tf_op jit(solution)/shard_map/ppermute | solution.py:30
  266.0 33.3 %collective-permute-start.49 = (bf16[512,1024]{1,0:T(8,128)(2,1)}, bf16[512,1024]{1,0:T(8,128)(2,1)}, u32[]{:S(2)}, u32[]{:S(2)}) collective-permute-start(bf16[512,1024]{1,0:T(8,128)(2,1)} %pad_maximum_fusion.5), channel_id=1, source_target_pairs={{0,4},{4,0},{8,12},{12,8},{16,20},{20,16},{24,28},{28,24},{1,5},{5... | collective-permute-start | bytes 3145736 | tf_op jit(solution)/shard_map/ppermute | solution.py:30
  (80 other events, 375.9 us)

commit v3 on v2

v3 whole, which is shorter than its diff:
```python
import functools

import jax
import jax.numpy as jnp
from jax import lax
from jax.experimental import pallas as pl
from jax.experimental.pallas import tpu as pltpu
from jax.sharding import PartitionSpec as P

HD = 64
SLOTS = 320
HALF = SLOTS // 2
PIECES = 8
EPSILON = 1e-06
BF = jnp.bfloat16
F32 = jnp.float32
MIB = 1 << 20


def mm(left, right, dims=((1,), (0,))):
    return lax.dot_general(left, right, (dims, ((), ())), preferred_element_type=F32)


NT = ((1,), (1,))
TN = ((0,), (0,))


def swap(values, axis, bit):
    count = lax.axis_size(axis)
    return lax.ppermute(values, axis, [(i, i ^ bit) for i in range(count)])


def after(values, *earlier):
    return lax.optimization_barrier((values, *earlier))[0]


def shape(dims, kind=F32):
    return jax.ShapeDtypeStruct(dims, kind)


STAY = []


def stay(*arrays):
    STAY.extend(arrays)


def leave(*arrays):
    for array in arrays:
        STAY[:] = [x for x in STAY if x is not array]


def run(body, operands, outs, scratch=(), flops=0, room=12):
    used = list(operands[1:])
    waiting = [x for x in STAY if all(x is not y for y in used)]
    ins = [pltpu.with_memory_space_constraint(x, pltpu.VMEM) for x in [*used, *waiting]]
    moved = sum(x.size * x.dtype.itemsize for x in [*used, *outs])

    def kernel(*refs):
        own = 1 + len(used)
        body(*refs[:own], *refs[own + len(waiting) :])

    return pl.pallas_call(
        kernel,
        out_shape=[pltpu.VMEM(x.shape, x.dtype) for x in outs],
        in_specs=[pl.BlockSpec(memory_space=pltpu.SMEM)]
        + [pl.BlockSpec(memory_space=pltpu.VMEM)] * len(ins),
        out_specs=[pl.BlockSpec(memory_space=pltpu.VMEM)] * len(outs),
        scratch_shapes=scratch,
        compiler_params=pltpu.CompilerParams(vmem_limit_bytes=room * MIB),
        cost_estimate=pl.CostEstimate(
            flops=int(flops * WEIGHT), bytes_accessed=0, transcendentals=0
        ),
    )(operands[0], *ins)


WEIGHT = 20


def add_low(me, left, right, out):
    out[...] = (left[...] + right[...].astype(F32)).astype(BF)


def add_round(left, right):
    return run(add_low, (jnp.zeros((1,), jnp.int32), left, right), [shape(left.shape, BF)])[0]


def add_halves(me, left, right, send, hold):
    middle = send.shape[0]
    send[...] = (left[middle:, :] + right[middle:, :].astype(F32)).astype(BF)
    hold[...] = left[:middle, :] + right[:middle, :].astype(F32)


def run_out(body, operands, outs, scratch=(), room=16):
    ins = [pltpu.with_memory_space_constraint(x, pltpu.VMEM) for x in operands[1:]]
    return pl.pallas_call(
        body,
        out_shape=[pltpu.HBM(x.shape, x.dtype) for x in outs],
        in_specs=[pl.BlockSpec(memory_space=pltpu.SMEM)]
        + [pl.BlockSpec(memory_space=pltpu.VMEM)] * len(ins),
        out_specs=[pl.BlockSpec(memory_space=pltpu.HBM)] * len(outs),
        scratch_shapes=scratch,
        compiler_params=pltpu.CompilerParams(vmem_limit_bytes=room * MIB),
        cost_estimate=pl.CostEstimate(
            flops=0, bytes_accessed=0, transcendentals=0
        ),
    )(operands[0], *ins)


def blocks(count, size, step):
    def one(i, carry):
        step(pl.ds(pl.multiple_of(i * size, size), size), i)
        return carry

    lax.fori_loop(0, count, one, 0)


def row_tiles(rows, size, step):
    def one(i, carry):
        step(pl.ds(pl.multiple_of(i * size, size), size))
        return carry

    lax.fori_loop(0, rows // size, one, 0)


def normalise(values):
    average = jnp.mean(values, axis=-1, keepdims=True)
    centred = values - average
    factor = lax.rsqrt(jnp.mean(centred * centred, axis=-1, keepdims=True) + EPSILON)
    return centred * factor, factor


def norm_back(grad, gain, z, factor):
    s = grad * gain
    return factor * (
        s - jnp.mean(s, axis=-1, keepdims=True) - z * jnp.mean(s * z, axis=-1, keepdims=True)
    )


def fold(values):
    return functools.reduce(
        lambda a, b: a + b, [values[i : i + 8] for i in range(0, values.shape[0], 8)]
    )


GAIN_ONE, SHIFT_ONE, OUT_BIAS, GAIN_TWO, SHIFT_TWO, UP_BIAS, DOWN_BIAS = range(7)


def row(vectors, number):
    return vectors[number : number + 1, :]


def project_side(blocks, vectors, weight, bias, normed, put):
    rows = blocks[0].shape[0]
    for i, block in enumerate(blocks):

        def step(at, block=block, i=i):
            z, _ = normalise(block[at, :].astype(F32))
            tile = pl.ds(pl.multiple_of(at.start + i * rows, 16), at.size)
            normed[tile, :] = (z * row(vectors, GAIN_ONE) + row(vectors, SHIFT_ONE)).astype(BF)

        row_tiles(rows, 48, step)
        put(i, (mm(normed[i * rows : (i + 1) * rows, :], weight[...]) + bias[...]).astype(BF))


def project_local(me, tok_a, tok_b, vectors, weight, bias, normed, proj):
    rows = tok_a.shape[0]

    def put(i, values):
        proj[i * rows : (i + 1) * rows, :] = values

    project_side((tok_a, tok_b), vectors, weight, bias, normed, put)


def attend(side, qkv, keep, probs, heads_out):
    half_lane = lax.broadcasted_iota(jnp.int32, (1, 2 * HD), 1) // HD
    width = qkv.shape[1] // 3

    def one(j, carry):
        place = 3 * side + j
        image = place // 2
        queries = pl.ds(pl.multiple_of(place * HALF, 16), HALF)
        keys = pl.ds(pl.multiple_of(image * SLOTS, 16), SLOTS)
        live = keep[pl.ds(image, 1), :] > 0
        for pair in range(width // (2 * HD)):
            lanes = pl.ds(pair * 2 * HD, 2 * HD)
            q = qkv[queries, lanes] * 0.125
            k = qkv[keys, pl.ds(width + pair * 2 * HD, 2 * HD)]
            v = qkv[keys, pl.ds(2 * width + pair * 2 * HD, 2 * HD)]
            outs = []
            for e in range(2):
                scores = mm(jnp.where(half_lane == e, q, jnp.zeros_like(q)), k, NT)
                scores = jnp.where(live, scores, -1000000000.0)
                power = jnp.exp(scores - jnp.max(scores, axis=-1, keepdims=True))
                p = (power / jnp.sum(power, axis=-1, keepdims=True)).astype(BF)
                probs[j * 4 + pair * 2 + e] = p
                outs.append(mm(p, v))
            heads_out[pl.ds(pl.multiple_of(j * HALF, 16), HALF), lanes] = jnp.where(
                half_lane == 0, outs[0], outs[1]
            ).astype(BF)
        return carry

    lax.fori_loop(0, 3, one, 0)


def out_project(core, heads_out, weight, send, hold):
    rows = send.shape[0]
    send[...] = mm(
        heads_out[pl.ds(pl.multiple_of((1 - core) * rows, 16), rows), :], weight[...]
    ).astype(BF)
    hold[...] = mm(heads_out[pl.ds(pl.multiple_of(core * rows, 16), rows), :], weight[...])


def attend_far(
    me, near, tok_a, tok_b, vectors, weight, bias, keep, out_w,
    normed, qkv, probs, heads_out, send, hold,
):
    rows = tok_a.shape[0]
    core, far = me[0] & 1, me[0] >> 1
    for i in range(2):
        at = pl.multiple_of((2 * far + (core ^ i)) * rows, 16)
        qkv[pl.ds(at, rows), :] = near[i * rows : (i + 1) * rows, :]

    def put(i, values):
        at = pl.multiple_of((2 * (1 - far) + (core ^ i)) * rows, 16)
        qkv[pl.ds(at, rows), :] = values

    project_side((tok_a, tok_b), vectors, weight, bias, normed, put)
    attend(1 - far, qkv, keep, probs, heads_out)
    out_project(core, heads_out, out_w, send, hold)


def attend_near(me, qkv, keep, out_w, probs, heads_out, send, hold):
    core, far = me[0] & 1, me[0] >> 1
    attend(far, qkv, keep, probs, heads_out)
    out_project(core, heads_out, out_w, send, hold)


def second_norm(me, tok, hold, near, far, vectors, middle, second):
    def step(at):
        total = hold[at, :] + near[at, :].astype(F32) + far[at, :].astype(F32)
        values = tok[at, :].astype(F32) + total + row(vectors, OUT_BIAS)
        middle[at, :] = values
        z, _ = normalise(values)
        second[at, :] = (z * row(vectors, GAIN_TWO) + row(vectors, SHIFT_TWO)).astype(BF)

    row_tiles(tok.shape[0], 48, step)


def act_back(me, cot_a, cot_b, down, act_grad):
    rows = cot_a.shape[0]

    def step(at, i):
        act_grad[:rows, at] = mm(cot_a[...], down[at, :], NT)
        act_grad[rows:, at] = mm(cot_b[...], down[at, :], NT)

    blocks(down.shape[0] // 256, 256, step)


def feed_forward(
    me, norm_a, norm_b, up, vectors, act_grad, act, pre_low, bias_grad, send, hold, total, pre
):
    rows = norm_a.shape[0]

    def step(at, number):
        for i, block in enumerate((norm_a, norm_b)):
            pre[pl.ds(i * rows, rows), :] = mm(block[...], up[:, at])
        own_bias = vectors[UP_BIAS : UP_BIAS + 1, at]

        def one(i, sums):
            tile = pl.ds(pl.multiple_of(i * 32, 32), 32)
            x = pre[tile, :] + own_bias
            share = 0.5 + 0.5 * lax.erf(x * 0.7071067811865476)
            slope = share + x * (0.3989422804014327 * jnp.exp(-0.5 * x * x))
            act[tile, at] = (x * share).astype(BF)
            grad = act_grad[tile, at] * slope
            pre_low[tile, at] = grad.astype(BF)
            return sums + fold(grad)

        sums = lax.fori_loop(0, 2 * rows // 32, one, jnp.zeros((8, pre.shape[1]), F32))
        bias_grad[:, at] = jnp.sum(sums, axis=0, keepdims=True)
        part = mm(pre_low[:, at], up[:, at], NT)

        @pl.when(number == 0)
        def _():
            total[...] = part

        @pl.when(number > 0)
        def _():
            total[...] += part

    blocks(up.shape[1] // 256, 256, step)
    hold[...] = total[:rows, :]
    send[...] = total[rows:, :].astype(BF)


def feed_out(me, act, down, send, hold):
    rows = send.shape[0]
    send[...] = mm(act[rows:, :], down[...]).astype(BF)
    hold[...] = mm(act[:rows, :], down[...])


def gather_pieces(me, lefts, order, base, turned):
    piece = lefts[0].shape[1] // PIECES
    for i in range(PIECES // 2):
        at = pl.ds(pl.multiple_of(piece_of(base + i, order, me[1]) * piece, piece), piece)
        for left, to in zip(lefts, turned, strict=True):
            to[i * piece : (i + 1) * piece, :] = left[:, at].T


def weight_pieces(order, base, low, count, me, *refs):
    lefts, rights = refs[: count[0]], refs[count[0] : sum(count)]
    out, turned = refs[sum(count)], refs[sum(count) + 1 :]
    gather_pieces(me, lefts, order, base, turned)
    rows = min(lefts[0].shape[0], rights[0].shape[0])
    left_each, right_each = lefts[0].shape[0] // rows, rights[0].shape[0] // rows

    def step(at, i):
        found = None
        from_ = pl.ds(pl.multiple_of(at.start + low, 128), at.size)
        for k in range(max(count)):
            left, right = turned[k // left_each], rights[k // right_each]
            inner = (k % left_each) * rows
            part = mm(
                left[:, inner : inner + rows], right[pl.ds((k % right_each) * rows, rows), from_]
            )
            found = part if found is None else found + part
        out[:, at] = found.astype(out.dtype)

    blocks(out.shape[1] // 256, 256, step)


def mixed_pieces(order, base, low, me, *refs):
    lefts, rights, heads, mids, out = refs[:2], refs[2:4], refs[4:6], refs[6:10], refs[10]
    turned = refs[11:13]
    gather_pieces(me, lefts, order, base, turned)
    width = rights[0].shape[1] - low
    for at in range(0, width, 256):
        found = mm(turned[0][...], rights[0][:, low + at : low + at + 256])
        found = found + mm(turned[1][...], rights[1][:, low + at : low + at + 256])
        out[:, at : at + 256] = found.astype(out.dtype)
    core = me[0] & 1
    rows = mids[0].shape[0]
    piece = mids[0].shape[1] // PIECES
    half = heads[0].shape[1] // 2
    for i in range(PIECES // 2):
        at = pl.ds(pl.multiple_of(piece_of(base + i, order, me[1]) * piece, piece), piece)
        both = None
        for k in range(4):
            inside = pl.ds(pl.multiple_of((core ^ (k % 2)) * rows, 16), rows)
            part = mm(heads[k // 2][inside, :], mids[k][:, at], TN)
            both = part if both is None else both + part
        to = pl.ds(i * piece, piece)
        out[to, width : width + half] = both[:half].astype(out.dtype)
        out[to, width + half :] = both[half:].astype(out.dtype)


def middle_back(me, hold, near, far, middle, cot_low, vectors, middle_grad, middle_low, sums, parts):
    parts[...] = jnp.zeros_like(parts)

    def step(at):
        second = hold[at, :] + near[at, :].astype(F32) + far[at, :].astype(F32)
        z, factor = normalise(middle[at, :])
        cot = cot_low[at, :].astype(F32)
        total = cot + norm_back(second, row(vectors, GAIN_TWO), z, factor)
        middle_grad[at, :] = total
        middle_low[at, :] = total.astype(BF)
        parts[0] += fold(total)
        parts[1] += fold(cot)
        parts[2] += fold(second * z)
        parts[3] += fold(second)

    row_tiles(hold.shape[0], 48, step)
    for i in range(4):
        sums[i : i + 1, :] = jnp.sum(parts[i], axis=0, keepdims=True)


def attend_back(side, mid_blocks, core, qkv, probs, out_w, grads, pg_q, keys_grad):
    rows = mid_blocks[0].shape[0]
    half_lane = lax.broadcasted_iota(jnp.int32, (1, 2 * HD), 1) // HD
    width = qkv.shape[1] // 3
    for i, block in enumerate(mid_blocks):
        at = pl.multiple_of((core ^ i) * rows, 16)
        grads[pl.ds(at, rows), :] = mm(block[...], out_w[...], NT).astype(BF)

    def one(j, carry):
        place = 3 * side + j
        image = place // 2
        inside = pl.ds(pl.multiple_of(j * HALF, 16), HALF)
        queries = pl.ds(pl.multiple_of(place * HALF, 16), HALF)
        keys = pl.ds(pl.multiple_of(image * SLOTS, 16), SLOTS)
        for pair in range(width // (2 * HD)):
            lanes = pl.ds(pair * 2 * HD, 2 * HD)
            q = qkv[queries, lanes]
            k = qkv[keys, pl.ds(width + pair * 2 * HD, 2 * HD)]
            v = qkv[keys, pl.ds(2 * width + pair * 2 * HD, 2 * HD)]
            g = grads[inside, lanes]
            found = []
            for e in range(2):
                p = probs[j * 4 + pair * 2 + e]
                wide = p.astype(F32)
                prob_grad = mm(jnp.where(half_lane == e, g, jnp.zeros_like(g)), v, NT)
                delta = jnp.sum(wide * prob_grad, axis=-1, keepdims=True)
                score_grad = (wide * (prob_grad - delta) * 0.125).astype(BF)
                found.append(
                    (mm(score_grad, k), mm(score_grad, q, TN), mm(p, g, TN))
                )
            q_grad, k_grad, v_grad = (
                jnp.where(half_lane == 0, a, b) for a, b in zip(*found, strict=True)
            )
            pg_q[inside, lanes] = q_grad
            keys_grad[keys, lanes] += k_grad
            keys_grad[keys, pl.ds(width + pair * 2 * HD, 2 * HD)] += v_grad
        return carry

    lax.fori_loop(0, 3, one, 0)


def back_near(me, mid_a, mid_b, qkv, probs, out_w, pg_q, keys_grad, grads):
    core, far = me[0] & 1, me[0] >> 1
    keys_grad[...] = jnp.zeros_like(keys_grad)
    attend_back(far, (mid_a, mid_b), core, qkv, probs, out_w, grads, pg_q, keys_grad)


def back_far(
    me, mid_a, mid_b, qkv, probs, out_w, near_q, near_keys, in_w,
    proj_near, proj_far, flat_near, flat_far, bias_grad, send, hold, grads, far_q, keys_grad,
):
    core, far = me[0] & 1, me[0] >> 1
    rows = mid_a.shape[0]
    width = far_q.shape[1]
    keys_grad[...] = near_keys[...]
    attend_back(1 - far, (mid_a, mid_b), core, qkv, probs, out_w, grads, far_q, keys_grad)
    bias_grad[...] = jnp.concatenate(
        [
            jnp.sum(far_q[...], axis=0, keepdims=True) + jnp.sum(near_q[...], axis=0, keepdims=True),
            jnp.sum(keys_grad[:, width:], axis=0, keepdims=True),
        ],
        axis=1,
    )
    sides = ((proj_near, flat_near, near_q), (proj_far, flat_far, far_q))
    for side, (out, flat, q_part) in enumerate(sides):
        for i in range(2):
            inside = pl.multiple_of((core ^ i) * rows, 16)
            place = pl.multiple_of((2 * (far ^ side) + (core ^ i)) * rows, 16)
            to = pl.ds(i * rows, rows)
            out[to, :width] = q_part[pl.ds(inside, rows), :].astype(BF)
            out[to, width:] = keys_grad[pl.ds(place, rows), :].astype(BF)
        for head in range(width // HD):
            for kind in range(3):
                at = (head * 3 + kind) * HD
                flat[:, at : at + HD] = out[:, kind * width + head * HD :][:, :HD]
    send[...] = mm(proj_far[rows:, :], in_w[...], NT).astype(BF)
    hold[...] = mm(proj_far[:rows, :], in_w[...], NT)


def first_back(me, proj, in_w, send, hold):
    rows = send.shape[0]
    send[...] = mm(proj[rows:, :], in_w[...], NT).astype(BF)
    hold[...] = mm(proj[:rows, :], in_w[...], NT)


def mixed_piece(me, norm_a, norm_b, proj_a, proj_b, heads_a, heads_b, mid_a, mid_b, out):
    width = proj_a.shape[1]
    out[:, :width] = (
        mm(norm_a[...], proj_a[...], TN) + mm(norm_b[...], proj_b[...], TN)
    ).astype(out.dtype)
    both = mm(heads_a[...], mid_a[...], TN) + mm(heads_b[...], mid_b[...], TN)
    half = both.shape[0] // 2
    out[:, width : width + half] = both[:half].astype(out.dtype)
    out[:, width + half :] = both[half:].astype(out.dtype)


def token_back(me, hold, near, far, tok, middle_grad, vectors, tokens_grad, sums, parts):
    parts[...] = jnp.zeros_like(parts)

    def step(at):
        first = hold[at, :] + near[at, :].astype(F32) + far[at, :].astype(F32)
        z, factor = normalise(tok[at, :].astype(F32))
        tokens_grad[at, :] = middle_grad[at, :] + norm_back(
            first, row(vectors, GAIN_ONE), z, factor
        )
        parts[0] += fold(first * z)
        parts[1] += fold(first)

    row_tiles(hold.shape[0], 48, step)
    for i in range(2):
        sums[i : i + 1, :] = jnp.sum(parts[i], axis=0, keepdims=True)


def place_pieces(order, me, *refs):
    parts, out, wide, sems = refs[:-3], refs[-3], refs[-2], refs[-1]
    piece = out.shape[0] // PIECES
    copies = []
    for i in range(PIECES):
        part, row = locate(parts, i * piece)
        wide[i] = part[row : row + piece, :].astype(F32)
        to = pl.ds(pl.multiple_of(piece_of(i, order, me[1]) * piece, piece), piece)
        copies.append(pltpu.make_async_copy(wide.at[i], out.at[to, :], sems.at[i]))
        copies[-1].start()
    for copy in copies:
        copy.wait()


def locate(parts, row):
    for part in parts:
        if row < part.shape[0]:
            return part, row
        row -= part.shape[0]


def place_mixed(order, other, me, *refs):
    count = (len(refs) - 5) // 2
    first, second = refs[:count], refs[count : 2 * count]
    in_out, out_out, wide, flat, sems = refs[2 * count :]
    piece = in_out.shape[0] // PIECES
    half = out_out.shape[0] // 2
    split = first[0].shape[1]
    rest = in_out.shape[1] - split
    copies = []
    for i in range(PIECES):
        place = piece_of(i, order, me[1])
        to = pl.ds(pl.multiple_of(place * piece, piece), piece)
        part, row = locate(first, i * piece)
        wide[i, :, :split] = part[row : row + piece, :].astype(F32)
        copies.append(
            pltpu.make_async_copy(wide.at[i, :, :split], in_out.at[to, :split], sems.at[i])
        )
        copies[-1].start()
        place = piece_of(i, other, me[1])
        to = pl.ds(pl.multiple_of(place * piece, piece), piece)
        part, row = locate(second, i * piece)
        wide[i, :, split:] = part[row : row + piece, :rest].astype(F32)
        flat[i, :half, :] = part[row : row + piece, rest : rest + half].astype(F32)
        flat[i, half:, :] = part[row : row + piece, rest + half :].astype(F32)
        copies.append(
            pltpu.make_async_copy(wide.at[i, :, split:], in_out.at[to, split:], sems.at[PIECES + i])
        )
        copies[-1].start()
        copies.append(
            pltpu.make_async_copy(flat.at[i], out_out.at[:, to], sems.at[2 * PIECES + i])
        )
        copies[-1].start()
    for copy in copies:
        copy.wait()


def piece_of(position, order, me):
    relative = 0
    for step, bit in enumerate(order):
        relative = relative | (((position >> (len(order) - 1 - step)) & 1) << bit)
    return relative ^ (me & (PIECES - 1))


def pack(values):
    high = values.astype(BF)
    return jnp.concatenate([high, (values - high.astype(F32)).astype(BF)], axis=0)


def add_small(own, other):
    return pack(unpack(own) + unpack(other))


def unpack(packed):
    half = packed.shape[0] // 2
    return packed[:half].astype(F32) + packed[half:].astype(F32)


class Reduction:
    def __init__(self, send, order):
        self.send, self.order = send, order
        self.count = lax.axis_size("dp").bit_length() - 1
        self.bits = [*order, *range(len(order), self.count), *reversed(order)]
        self.values, self.small, self.came, self.at = None, None, None, 0

    def take(self, *earlier):
        self.came = swap(self.send, "dp", 1 << self.bits[self.at])
        if earlier:
            self.came = after(self.came, *earlier)
        return self.came

    def arrive(self, *earlier):
        if self.came is None:
            self.take()
        arrived = after(self.came, *earlier)
        self.came = None
        self.at += 1
        halving = len(self.order)
        if self.at < halving:
            dims = (self.values.shape[0] // 2, self.values.shape[1])
            leave(self.values)
            self.send, self.values = run(
                add_halves,
                (jnp.zeros((1,), jnp.int32), self.values, arrived),
                [shape(dims, BF), shape(dims)],
            )
            stay(self.values)
        elif self.at == halving:
            leave(self.values)
            self.values = add_round(self.values, arrived)
            self.send = self.values
        elif self.at <= self.count:
            self.values = (self.values.astype(F32) + arrived.astype(F32)).astype(BF)
            self.send = self.values
        else:
            rows = self.values.shape[0]
            if self.small is not None:
                self.small = pack(unpack(self.small) + unpack(arrived[rows:]))
            if self.at == len(self.bits):
                self.parts = (self.values, arrived)
                return arrived
            self.values = jnp.concatenate([self.values, arrived[:rows]], axis=0)
            self.send = self.values
            if self.small is not None:
                self.send = jnp.concatenate([self.values, self.small], axis=0)
        return self.send

    def join(self, small):
        for bit in range(len(self.order), self.count):
            small = pack(unpack(small) + unpack(swap(small, "dp", 1 << bit)))
        self.small = small
        self.send = jnp.concatenate([self.values, small], axis=0)


ORDER_A = (0, 1, 2)
ORDER_B = (1, 0, 2)


def weight_grad(me, lefts, rights, order, kept, low=0, wide=None):
    rows, columns = lefts[0].shape
    wide = wide or rights[0].shape[1]
    half = columns // 2
    return run(
        functools.partial(
            weight_pieces, order, 0 if kept else PIECES // 2, low, (len(lefts), len(rights))
        ),
        (me, *lefts, *rights),
        [shape((half, wide), F32 if kept else BF)],
        scratch=[pltpu.VMEM((half, rows), BF)] * len(lefts),
        flops=2 * len(lefts) * rows * half * wide,
    )[0]


def mixed_grad(me, normed, proj, heads, mids, order, kept, low):
    rows, columns = normed[0].shape
    half = columns // 2
    wide = proj[0].shape[1] - low + heads[0].shape[1]
    return run(
        functools.partial(mixed_pieces, order, 0 if kept else PIECES // 2, low),
        (me, *normed, *proj, *heads, *mids),
        [shape((half, wide), F32 if kept else BF)],
        scratch=[pltpu.VMEM((half, rows), BF)] * 2,
        flops=2 * 2 * rows * half * wide,
    )[0]


def place(me, parts, order):
    rows, wide = 2 * parts[0].shape[0], parts[0].shape[1]
    return run_out(
        functools.partial(place_pieces, order),
        (me, *parts),
        [shape((rows, wide))],
        scratch=[
            pltpu.VMEM((PIECES, rows // PIECES, wide), F32),
            pltpu.SemaphoreType.DMA((PIECES,)),
        ],
    )[0]


def on_device(
    tokens,
    keep_mask,
    grad_out,
    in_weight,
    in_bias,
    out_weight,
    out_bias,
    up_weight,
    up_bias,
    down_weight,
    down_bias,
    gain_one,
    shift_one,
    gain_two,
    shift_two,
):
    rows, model = tokens.shape
    leave(*STAY)
    me = jnp.stack([lax.axis_index("tensor"), lax.axis_index("dp")]).astype(jnp.int32)
    images = keep_mask.shape[0]
    heads = in_weight.shape[1] // (3 * HD)
    width = heads * HD
    hidden = up_weight.shape[1]

    def line(values):
        return values.reshape(1, -1)

    side = 2 * rows
    block = 256
    project_flops = 2 * side * model * 3 * width
    attend_flops = 3 * heads * 4 * HALF * SLOTS * 128 + 2 * side * width * model
    back_flops = 3 * heads * 10 * HALF * SLOTS * 128 + 2 * side * width * model

    def act_grad_of(one, other):
        return run(
            act_back,
            (me, one, other, down_weight),
            [shape((side, hidden))],
            flops=2 * side * model * hidden,
        )[0]

    def feed(one, other, act_grad):
        return run(
            feed_forward,
            (me, one, other, up_weight, vectors, act_grad),
            [
                shape((side, hidden), BF),
                shape((side, hidden), BF),
                shape((1, hidden)),
                shape((rows, model), BF),
                shape((rows, model)),
            ],
            scratch=[pltpu.VMEM((side, model), F32), pltpu.VMEM((side, block), F32)],
            flops=4 * side * model * hidden,
        )

    def feed_back(me, act):
        return run(
            feed_out,
            (me, act, down_weight),
            [shape((rows, model), BF), shape((rows, model))],
            flops=2 * side * model * hidden,
        )

    tok_far = swap(tokens, "tensor", 2)
    tok_core = swap(tokens, "tensor", 1)
    keep_flat = keep_mask.reshape(-1).astype(F32)
    keep_own = lax.dynamic_slice_in_dim(keep_flat, me[0] * rows, rows)[:, None]
    cot = (grad_out.astype(F32) * keep_own).astype(BF)
    cot_core = swap(cot, "tensor", 1)
    in_grouped = in_weight.reshape(model, heads, 3, HD).transpose(0, 2, 1, 3)
    in_grouped = in_grouped.reshape(model, 3 * width)
    pair = in_bias.reshape(heads, 2, HD).transpose(1, 0, 2).reshape(2, width)
    bias_full = jnp.concatenate([pair[:1], jnp.zeros((1, width), F32), pair[1:]], axis=1)
    vectors = jnp.stack(
        [gain_one, shift_one, out_bias, gain_two, shift_two, up_bias, down_bias, down_bias]
    )
    stay(in_grouped, bias_full, vectors, out_weight, down_weight, up_weight, tokens, cot)
    norm_near, proj_near = run(
        project_local,
        (me, tokens, tok_core, vectors, in_grouped, bias_full),
        [shape((side, model), BF), shape((side, 3 * width), BF)],
        flops=project_flops,
    )
    stay(norm_near)
    tok_far = after(tok_far, proj_near)

    tok_both = swap(tok_far, "tensor", 1)
    cot_far = swap(after(cot, tok_far), "tensor", 2)
    attend_outs = [
        shape((3 * heads, HALF, SLOTS), BF),
        shape((side, width), BF),
        shape((rows, model), BF),
        shape((rows, model), F32),
    ]
    norm_far, qkv, probs_far, heads_far, send, far_hold = run(
        attend_far,
        (
            me, proj_near, tok_far, tok_both, vectors, in_grouped, bias_full, keep_mask, out_weight,
        ),
        [shape((side, model), BF), shape((2 * side, 3 * width), BF), *attend_outs],
        flops=project_flops + attend_flops,
    )
    stay(norm_far, qkv, probs_far, heads_far)
    leave(bias_full)
    arrived = after(swap(send, "tensor", 1), cot_far)
    far_sum = add_round(far_hold, arrived)
    cot_far = after(cot_far, far_sum)
    cot_both = swap(cot_far, "tensor", 1)
    arrived_far = swap(far_sum, "tensor", 2)
    probs_near, heads_near, send, hold = run(
        attend_near,
        (after(me, far_sum), qkv, keep_mask, out_weight),
        attend_outs,
        flops=attend_flops,
    )
    stay(probs_near, heads_near, hold)
    act_grad_near = act_grad_of(cot, cot_core)
    stay(act_grad_near, cot_core)
    arrived_near = after(swap(send, "tensor", 1), arrived_far)
    middle, second = run(
        second_norm,
        (
            after(me, act_grad_near), tokens, hold, arrived_near, arrived_far, vectors,
        ),
        [shape((rows, model)), shape((rows, model), BF)],
    )

    leave(hold)
    stay(middle, second)

    second_far = swap(second, "tensor", 2)
    second_core = swap(second, "tensor", 1)
    act_near, pre_near, up_bias_near, near_send, near_hold = feed(
        second, second_core, act_grad_near
    )
    leave(act_grad_near)
    stay(act_near, pre_near, near_hold, second_core)
    act_grad_far = act_grad_of(cot_far, cot_both)
    stay(cot_far, cot_both, act_grad_far)
    second_far = after(second_far, act_grad_far)
    second_both = swap(second_far, "tensor", 1)
    act_far, pre_far, up_bias_far, far_send, far_hold = feed(
        second_far, second_both, act_grad_far
    )
    far_sum = add_round(far_hold, swap(far_send, "tensor", 1))
    arrived_far = swap(far_sum, "tensor", 2)
    leave(act_grad_far, up_weight)
    stay(act_far, pre_far, second_far, second_both)
    acts, cots = (act_near, act_far), (cot, cot_core, cot_far, cot_both)
    down_send = weight_grad(after(me, far_sum), acts, cots, ORDER_A, False)
    down = Reduction(down_send, ORDER_A)
    seconds = (second, second_core, second_far, second_both)
    pres = (pre_near, pre_far)
    up_send = weight_grad(after(me, down_send), seconds, pres, ORDER_B, False)
    up = Reduction(up_send, ORDER_B)
    arrived_near = swap(near_send, "tensor", 1)
    feed_send, feed_hold = feed_back(after(me, up_send), act_far)
    feed_far = add_round(feed_hold, swap(feed_send, "tensor", 1))
    middle_grad, middle_low, middle_sums = run(
        middle_back,
        (
            after(me, feed_hold), near_hold, arrived_near, arrived_far, middle, cot, vectors,
        ),
        [shape((rows, model)), shape((rows, model), BF), shape((4, model))],
        scratch=[pltpu.VMEM((4, 8, model), F32)],
    )

    mid_far = swap(middle_low, "tensor", 2)
    mid_core = swap(middle_low, "tensor", 1)
    grads = pltpu.VMEM((side, width), BF)
    leave(near_hold)
    stay(middle_grad, middle_low)
    down.values = weight_grad(after(me, middle_low), acts, cots, ORDER_A, True)
    leave(act_far, cot_core, cot_far, cot_both)
    stay(down.values)
    near_q, near_keys = run(
        back_near,
        (after(me, down.values), middle_low, mid_core, qkv, probs_near, out_weight),
        [shape((side, width)), shape((2 * side, 2 * width))],
        scratch=[grads],
        flops=back_flops,
    )
    leave(probs_near)
    stay(near_q, near_keys, mid_core)
    up.values = weight_grad(after(me, near_q), seconds, pres, ORDER_B, True)
    leave(second, second_core, second_far, second_both, pre_near, pre_far)
    stay(up.values)
    mid_far = after(mid_far, up.values)
    mid_both = swap(mid_far, "tensor", 1)
    feed_far = swap(after(feed_far, mid_far), "tensor", 2)
    down.arrive(mid_far)
    up.arrive(mid_far)
    proj_near, proj_far, flat_near, flat_far, bias_grad, far_send, far_hold = run(
        back_far,
        (
            after(me, down.send, up.send), mid_far, mid_both, qkv, probs_far,
            out_weight, near_q, near_keys, in_grouped,
        ),
        [
            shape((side, 3 * width), BF),
            shape((side, 3 * width), BF),
            shape((side, 3 * width), BF),
            shape((side, 3 * width), BF),
            shape((1, 2 * width)),
            shape((rows, model), BF),
            shape((rows, model)),
        ],
        scratch=[
            grads,
            pltpu.VMEM((side, width), F32),
            pltpu.VMEM((2 * side, 2 * width), F32),
        ],
        flops=back_flops + project_flops,
    )
    leave(qkv, probs_far, near_q, near_keys, out_weight)
    stay(proj_near, flat_near, flat_far, mid_far, mid_both)
    down.take(bias_grad)
    up.take(bias_grad)
    arrived = after(swap(far_send, "tensor", 1), feed_far, down.came, up.came)
    far_sum = add_round(far_hold, arrived)
    arrived_far = swap(far_sum, "tensor", 2)

    down.arrive(far_sum)
    up.arrive(far_sum)
    near_send, hold = run(
        first_back,
        (after(me, down.send, up.send), proj_near, in_grouped),
        [shape((rows, model), BF), shape((rows, model))],
        flops=project_flops,
    )
    leave(in_grouped, proj_near)
    stay(hold)
    normed = (norm_near, norm_far)
    split = (3 * width + width) // 2
    flat = (flat_near, flat_far)
    head_rows = (heads_near, heads_far)
    mids = (middle_low, mid_core, mid_far, mid_both)
    arrived_near = swap(near_send, "tensor", 1)
    first_send = weight_grad(after(me, hold), normed, flat, ORDER_A, False, 0, split)
    first = Reduction(first_send, ORDER_A)
    mixed_send = mixed_grad(
        after(me, first_send), normed, flat, head_rows, mids, ORDER_B, False, split
    )
    mixed = Reduction(mixed_send, ORDER_B)
    first.values = weight_grad(after(me, mixed_send), normed, flat, ORDER_A, True, 0, split)
    stay(first.values)
    mixed.values = mixed_grad(
        after(me, first.values), normed, flat, head_rows, mids, ORDER_B, True, split
    )
    leave(norm_near, norm_far, flat_near, flat_far, heads_near, heads_far)
    leave(middle_low, mid_core, mid_far, mid_both)
    stay(mixed.values)
    tokens_grad, token_sums = run(
        token_back,
        (
            after(me, mixed.values), hold, arrived_near, arrived_far, tokens, middle_grad, vectors,
        ),
        [shape((rows, model)), shape((2, model))],
        scratch=[pltpu.VMEM((2, 8, model), F32)],
    )
    leave(hold, tokens, middle_grad, vectors)
    feed_send, feed_hold = feed_back(after(me, token_sums), act_near)
    feed_rows = feed_hold + swap(feed_send, "tensor", 1).astype(F32) + feed_far.astype(F32)
    output = (keep_own * (middle + feed_rows + down_bias)).astype(BF)
    leave(*STAY)
    stay(down.values, up.values, first.values, mixed.values)

    now = down.arrive(feed_hold)
    now = first.arrive(now)
    shared = pack(jnp.concatenate([middle_sums, token_sums], axis=0))
    shared = add_small(shared, swap(shared, "tensor", 1))
    shared = unpack(add_small(shared, swap(shared, "tensor", 2)))
    own = jnp.concatenate(
        [up_bias_near + up_bias_far, jnp.pad(bias_grad, ((0, 0), (0, hidden - 2 * width)))], axis=0
    )
    small = jnp.concatenate([shared, own], axis=0)
    small = pack(jnp.concatenate([small[:, :split], small[:, split:]], axis=0))
    now = mixed.arrive(now)
    now = up.arrive(now)
    now = down.arrive(now)
    now = mixed.arrive(now)
    now = first.arrive(now)
    now = up.arrive(now)
    now = down.arrive(now)
    now = mixed.arrive(now)
    now = first.arrive(now)
    while first.at < first.count:
        now = first.arrive(now)
    first.join(small)
    now = mixed.arrive(now)
    now = first.arrive(now)
    now = up.arrive(now)
    last = [mixed, first, down, up]
    while any(x.at < len(x.bits) for x in last):
        for x in last:
            if x.at < len(x.bits):
                now = x.arrive(now)
    small = unpack(first.small)
    small = jnp.concatenate([small[:8], small[8:]], axis=1)
    piece = model // PIECES
    down_sum = place(me, down.parts, ORDER_A)
    up_sum = place(me, up.parts, ORDER_B)
    in_sum, out_sum = run_out(
        functools.partial(place_mixed, ORDER_A, ORDER_B),
        (me, *first.parts, *mixed.parts),
        [shape((model, 3 * width)), shape((width, model))],
        scratch=[
            pltpu.VMEM((PIECES, piece, 3 * width), F32),
            pltpu.VMEM((PIECES, width, piece), F32),
            pltpu.SemaphoreType.DMA((3 * PIECES,)),
        ],
    )
    in_bias_sum = small[7, : 2 * width].reshape(2, heads, HD).transpose(1, 0, 2).reshape(-1)
    return (
        output,
        tokens_grad,
        in_sum,
        in_bias_sum,
        out_sum,
        small[0],
        up_sum,
        small[6],
        down_sum,
        small[1],
        small[4],
        small[5],
        small[2],
        small[3],
    )


def solution(mesh):
    rows = P(("dp", "tensor"), None)
    placed = (
        rows,
        P("dp", None),
        rows,
        P(None, "tensor"),
        P("tensor"),
        P("tensor", None),
        P(),
        P(None, "tensor"),
        P("tensor"),
        P("tensor", None),
        P(),
        P(),
        P(),
        P(),
        P(),
    )
    given = (
        rows,
        rows,
        P(None, "tensor"),
        P("tensor"),
        P("tensor", None),
        P(),
        P(None, "tensor"),
        P("tensor"),
        P("tensor", None),
        P(),
        P(),
        P(),
        P(),
        P(),
    )
    return jax.shard_map(on_device, mesh=mesh, in_specs=placed, out_specs=given, check_vma=False)
```

time: 306 us -> 250 us (0.82)
  local copies, waits for them, and re-layouts: 45.7 us -> 11.8 us
  Pallas kernels: 108 us -> 92 us
  waiting for transfers between devices: 96.5 us -> 105 us
  other arithmetic: 12.1 us -> 4.21 us
  starting transfers between devices: 40.9 us -> 35.3 us
    unnamed x129 -> x41, local copies, waits for them, and re-layouts: 32 us -> 5.79 us
    pallas_call x26 -> x42, Pallas kernels: 108 us -> 92 us  [the longest x39 83.9 us: run(): pl.pallas_call(kernel, out_shape=[pltpu.VMEM(x.shape, x.dtype) for x in o...]
    ppermute x50, waiting for transfers between devices: 96.5 us -> 105 us  [swap(): return lax.ppermute(values, axis, [(i, i ^ bit) for i in range(count)])]
    concatenate x10 -> x7, other arithmetic: 6.46 us -> 0.3 us  [arrive(): self.values = jnp.concatenate([self.values, arrived[:rows]], axis=0)]
    ppermute x50, starting transfers between devices: 40.9 us -> 35.3 us  [swap(): return lax.ppermute(values, axis, [(i, i ^ bit) for i in range(count)])]
    slice x10 -> x0, local copies, waits for them, and re-layouts: 3.35 us -> none  [the longest x1 1.46 us: on_device(): output = (keep_near[:rows] * (middle + feed_rows + down_bias)).astype(BF)]
  transfers between devices with their start and end apart: 50 -> 50, of which waited for: 24 -> 29; matrix products, arithmetic and copies ran while one was open for 9% -> 5% of each run, Pallas kernels for 29% -> 31%
where the time goes in v3:
time: 250 us
  waiting for transfers between devices  105 us (42%)
  Pallas kernels  92 us (37%)
  starting transfers between devices  35.3 us (14%)
  local copies, waits for them, and re-layouts  11.8 us (5%)
  other arithmetic  4.21 us (2%)
    ppermute x50, waiting for transfers between devices, swap(): return lax.ppermute(values, axis, [(i, i ^ bit) for i in range(count)])  105 us
    pallas_call x39, Pallas kernels, run(): pl.pallas_call(kernel, out_shape=[pltpu.VMEM(x.shape, x.dtype) for x in o...  83.9 us
    ppermute x50, starting transfers between devices, swap(): return lax.ppermute(values, axis, [(i, i ^ bit) for i in range(count)])  35.3 us
    pallas_call x3, Pallas kernels, run_out(): pl.pallas_call(body, out_shape=[pltpu.HBM(x.shape, x.dtype) for x in outs...  8.04 us
    unnamed x41, local copies, waits for them, and re-layouts  5.79 us
  transfers between devices with their start and end apart: 50, of which 29 were waited for; matrix products, arithmetic and copies ran while one was open for 5% of the time, Pallas kernels for 31%

profile of v3, /device:TPU:0, one launch (start us, length us, event | category | flops | bytes accessed | tf_op | source)
XLA Modules:
  0.0 250.1 jit_solution(8268699109270427647)
XLA Ops:
  0.6 3.0 %collective-permute-start.2 = (bf16[240,1024]{1,0:T(8,128)(2,1)}, bf16[240,1024]{1,0:T(8,128)(2,1)}, u32[]{:S(2)}, u32[]{:S(2)}) collective-permute-start(bf16[240,1024]{1,0:T(8,128)(2,1)} %refs_4_.3), channel_id=1, source_target_pairs={{0,2},{1,3},{2,0},{3,1},{4,6},{5,7},{6,4},{7,5},{8,10},{9,11},{10,... | collective-permute-start | bytes 1474568 | tf_op jit(solution)/shard_map/ppermute | solution.py:30
  8.6 2.7 %copy.36.refs_4_.refs_5_.refs_3_.refs_6_.refs_7_.refs_8_.refs_2_ = bf16[1024,768]{1,0:T(8,128)(2,1)} copy(bf16[1024,768]{0,1:T(8,128)(2,1)} %bitcast.24) | data formatting | bytes 3145728 | tf_op jit(solution)/shard_map/reshape | solution.py:742
  15.8 4.6 %shard_map.254 = (bf16[480,1024]{1,0:T(8,128)(2,1)S(1)}, bf16[480,768]{1,0:T(8,128)(2,1)S(1)}) custom-call(s32[2]{0:T(128)S(1)} %pad_add_fusion.refs_0_.me, bf16[240,1024]{1,0:T(8,128)(2,1)S(1)} %copy-done.3, bf16[240,1024]{1,0:T(8,128)(2,1)} %collective-permute-done.1.refs_2_, ...), custom_call_target="tpu_custom_call" | custom-call | flops 15099494400 | tf_op jit(solution)/shard_map/pallas_call | solution.py:63
  22.8 9.6 %shard_map.255 = (bf16[480,1024]{1,0:T(8,128)(2,1)S(1)}, bf16[960,768]{1,0:T(8,128)(2,1)S(1)}, bf16[12,160,320]{2,1,0:T(8,128)(2,1)S(1)}, bf16[480,256]{1,0:T(8,...) custom-call(s32[2]{0:T(128)S(1)} %pad_add_fusion.refs_0_.me, ...), custom_call_target="tpu_custom_call" | custom-call | flops 26424115200 | tf_op jit(solution)/shard_map/pallas_call | solution.py:63
  34.9 5.6 %shard_map.257 = (bf16[12,160,320]{2,1,0:T(8,128)(2,1)S(1)}, bf16[480,256]{1,0:T(8,128)(2,1)S(1)}, bf16[240,1024]{1,0:T(8,128)(2,1)S(1)}, f32[240,1024]{1,0:T(8,128)S(1)}) custom-call(s32[2]{0:T(128)S(1)} %pad_add_fusion.refs_0_.me, bf16[960,768]{1,0:T(8,128)(2,1)S(1)} %get-tuple-element.131.refs_12_.refs_1_.refs_11_.refs_13_.refs_14_.refs_15_.refs_10_.refs_3_, ...), custom_call_target="tpu_custom_call" | custom-call | flops 11324620800 | tf_op jit(solution)/shard_map/pallas_call | solution.py:63
  40.6 2.5 shard_map.258.refs_18_.refs_5_
  43.1 5.0 %collective-permute-done.7.refs_4_ = bf16[240,1024]{1,0:T(8,128)(2,1)S(1)} collective-permute-done((bf16[240,1024]{1,0:T(8,128)(2,1)S(1)}, bf16[240,1024]{1,0:T(8,128)(2,1)S(1)}, u32[]{:S(2)}, u32[]{:S(2)}) %collective-permute-start.7) | collective-permute-done | bytes 491552 | tf_op jit(solution)/shard_map/ppermute | solution.py:30
  51.7 6.5 %shard_map.260 = (bf16[480,1024]{1,0:T(8,128)(2,1)S(1)}, bf16[480,1024]{1,0:T(8,128)(2,1)S(1)}, f32[1,1024]{1,0:T(1,128)S(1)}, bf16[240,1024]{1,0:T(8,128)(2,1)S(1)}, f32[240,1024]{1,0:T(8,128)S(1)}) custom-call(s32[2]{0:T(128)S(1)} %pad_add_fusion.refs_0_.me, bf16[240,1024]{1,0:T(8,128)(2,1)S(1)} %get-tuple-element.146.refs_1_.refs_19_.refs_20_.refs_17_.refs_18_, ...), custom_call_target="tpu_custom_call" | custom-call | flops 40265318400 | tf_op jit(solution)/shard_map/pallas_call | solution.py:63
  60.6 2.9 %collective-permute-done.8.refs_1_.refs_25_.refs_3_.refs_27_.refs_24_.refs_22_ = bf16[240,1024]{1,0:T(8,128)(2,1)S(1)} collective-permute-done((bf16[240,1024]{1,0:T(8,128)(2,1)S(1)}, bf16[240,1024]{1,0:T(8,128)(2,1)S(1)}, u32[]{:S(2)}, u32[]{:S(2)}) %collective-permute-start.8) | collective-permute-done | bytes 491552 | tf_op jit(solution)/shard_map/ppermute | solution.py:30
  65.4 6.5 %shard_map.262 = (bf16[480,1024]{1,0:T(8,128)(2,1)S(1)}, bf16[480,1024]{1,0:T(8,128)(2,1)S(1)}, f32[1,1024]{1,0:T(1,128)S(1)}, bf16[240,1024]{1,0:T(8,128)(2,1)S(1)}, f32[240,1024]{1,0:T(8,128)S(1)}) custom-call(s32[2]{0:T(128)S(1)} %pad_add_fusion.refs_0_.me, ...), custom_call_target="tpu_custom_call" | custom-call | flops 40265318400 | tf_op jit(solution)/shard_map/pallas_call | solution.py:63
  74.3 2.8 %shard_map.264 = bf16[512,1024]{1,0:T(8,128)(2,1)S(1)} custom-call(s32[2]{0:T(128)S(1)} %pad_add_fusion.refs_0_.me, bf16[480,1024]{1,0:T(8,128)(2,1)S(1)} %get-tuple-element.148.refs_20_.refs_21_.refs_1_.refs_22_.refs_18_.refs_16_.refs_19_.refs_13_.refs_12_.refs_10_, bf16[480,1024]{1,0:T(8,128)(2,1)S(1)} %get-tuple-element.155.refs_2_.refs_26_.refs_1_.refs_25_, ...), custom_call_target="tpu_custom_call" | custom-call | flops 20132659200 | tf_op jit(solution)/shard_map/pallas_call | solution.py:63
  77.1 2.9 %shard_map.265 = bf16[512,1024]{1,0:T(8,128)(2,1)S(1)} custom-call(s32[2]{0:T(128)S(1)} %pad_add_fusion.refs_0_.me, bf16[240,1024]{1,0:T(8,128)(2,1)S(1)} %get-tuple-element.146.refs_1_.refs_19_.refs_20_.refs_17_.refs_18_, bf16[240,1024]{1,0:T(8,128)(2,1)S(1)} %collective-permute-done.10.refs_2_.refs_23_.refs_24_.refs_21_.refs_22_.refs_20_, ...), custom_call_target="tpu_custom_call" | custom-call | flops 20132659200 | tf_op jit(solution)/shard_map/pallas_call | solution.py:63
  89.8 2.8 %shard_map.268.refs_25_.refs_23_.refs_1_ = f32[512,1024]{1,0:T(8,128)S(1)} custom-call(s32[2]{0:T(128)S(1)} %pad_add_fusion.refs_0_.me, bf16[480,1024]{1,0:T(8,128)(2,1)S(1)} %get-tuple-element.148.refs_20_.refs_21_.refs_1_.refs_22_.refs_18_.refs_16_.refs_19_.refs_13_.refs_12_.refs_10_, ...), custom_call_target="tpu_custom_call" | custom-call | flops 20132659200 | tf_op jit(solution)/shard_map/pallas_call | solution.py:63
  92.7 6.6 %shard_map.269 = (f32[480,256]{1,0:T(8,128)S(1)}, f32[960,512]{1,0:T(8,128)S(1)}) custom-call(s32[2]{0:T(128)S(1)} %pad_add_fusion.refs_0_.me, bf16[240,1024]{1,0:T(8,128)(2,1)S(1)} %get-tuple-element.162.refs_27_.refs_1_.refs_22_.refs_18_.refs_20_.refs_15_.refs_14_.refs_7_, ...), custom_call_target="tpu_custom_call" | custom-call | flops 20761804800 | tf_op jit(solution)/shard_map/pallas_call | solution.py:63
  99.3 2.7 %shard_map.270.refs_22_.refs_1_ = f32[512,1024]{1,0:T(8,128)S(1)} custom-call(s32[2]{0:T(128)S(1)} %pad_add_fusion.refs_0_.me, bf16[240,1024]{1,0:T(8,128)(2,1)S(1)} %get-tuple-element.146.refs_1_.refs_19_.refs_20_.refs_17_.refs_18_, bf16[240,1024]{1,0:T(8,128)(2,1)S(1)} %collective-permute-done.10.refs_2_.refs_23_.refs_24_.refs_21_.refs_22_.refs_20_, ...), custom_call_target="tpu_custom_call" | custom-call | flops 20132659200 | tf_op jit(solution)/shard_map/pallas_call | solution.py:63
  108.9 8.8 %shard_map.273 = (bf16[480,768]{1,0:T(8,128)(2,1)S(1)}, bf16[480,768]{1,0:T(8,128)(2,1)}, bf16[480,768]{1,0:T(8,128)(2,1)S(1)}, bf16[480,768]{1,0:T(8,128)(2,1)S...) custom-call(s32[2]{0:T(128)S(1)} %pad_add_fusion.refs_0_.me, ...), custom_call_target="tpu_custom_call" | custom-call | flops 35861299200 | tf_op jit(solution)/shard_map/pallas_call | solution.py:63
  121.0 2.7 %collective-permute-start.34 = (bf16[128,1024]{1,0:T(8,128)(2,1)S(1)}, bf16[128,1024]{1,0:T(8,128)(2,1)S(1)}, u32[]{:S(2)}, u32[]{:S(2)}) collective-permute-start(bf16[128,1024]{1,0:T(8,128)(2,1)S(1)} %get-tuple-element.192), channel_id=1, source_target_pairs={{0,16},{4,20},{8,24},{12,28},{16,0},{20,4},{24,8},{28,12},{1,17},{... | collective-permute-start | bytes 786440 | tf_op jit(solution)/shard_map/ppermute | solution.py:30
  139.7 6.5 %collective-permute-done.29.refs_2_ = bf16[128,1024]{1,0:T(8,128)(2,1)S(1)} collective-permute-done((bf16[128,1024]{1,0:T(8,128)(2,1)S(1)}, bf16[128,1024]{1,0:T(8,128)(2,1)S(1)}, u32[]{:S(2)}, u32[]{:S(2)}) %collective-permute-start.29) | collective-permute-done | bytes 262176 | tf_op jit(solution)/shard_map/ppermute | solution.py:30
  149.4 2.7 %collective-permute-start.30 = (bf16[256,512]{1,0:T(8,128)(2,1)S(1)}, bf16[256,512]{1,0:T(8,128)(2,1)S(1)}, u32[]{:S(2)}, u32[]{:S(2)}) collective-permute-start(bf16[256,512]{1,0:T(8,128)(2,1)S(1)} %get-tuple-element.210), channel_id=1, source_target_pairs={{0,8},{4,12},{8,0},{12,4},{16,24},{20,28},{24,16},{28,20},{1,9},{5... | collective-permute-start | bytes 786440 | tf_op jit(solution)/shard_map/ppermute | solution.py:30
  152.2 10.6 %collective-permute-done.31.refs_2_ = bf16[512,512]{1,0:T(8,128)(2,1)S(1)} collective-permute-done((bf16[512,512]{1,0:T(8,128)(2,1)S(1)}, bf16[512,512]{1,0:T(8,128)(2,1)S(1)}, u32[]{:S(2)}, u32[]{:S(2)}) %collective-permute-start.31) | collective-permute-done | bytes 524320 | tf_op jit(solution)/shard_map/ppermute | solution.py:30
  166.3 3.0 %collective-permute-done.32.refs_2_ = bf16[256,512]{1,0:T(8,128)(2,1)S(1)} collective-permute-done((bf16[256,512]{1,0:T(8,128)(2,1)S(1)}, bf16[256,512]{1,0:T(8,128)(2,1)S(1)}, u32[]{:S(2)}, u32[]{:S(2)}) %collective-permute-start.32) | collective-permute-done | bytes 262176 | tf_op jit(solution)/shard_map/ppermute | solution.py:30
  169.6 2.6 %collective-permute-done.30.refs_2_ = bf16[256,512]{1,0:T(8,128)(2,1)S(1)} collective-permute-done((bf16[256,512]{1,0:T(8,128)(2,1)S(1)}, bf16[256,512]{1,0:T(8,128)(2,1)S(1)}, u32[]{:S(2)}, u32[]{:S(2)}) %collective-permute-start.30) | collective-permute-done | bytes 262176 | tf_op jit(solution)/shard_map/ppermute | solution.py:30
  173.2 4.1 %collective-permute-done.38 = bf16[128,1024]{1,0:T(8,128)(2,1)S(1)} collective-permute-done((bf16[128,1024]{1,0:T(8,128)(2,1)S(1)}, bf16[128,1024]{1,0:T(8,128)(2,1)S(1)}, u32[]{:S(2)}, u32[]{:S(2)}) %collective-permute-start.38) | collective-permute-done | bytes 262176 | tf_op jit(solution)/shard_map/ppermute | solution.py:30
  177.4 9.0 %collective-permute-done.37 = bf16[256,1024]{1,0:T(8,128)(2,1)S(1)} collective-permute-done((bf16[256,1024]{1,0:T(8,128)(2,1)S(1)}, bf16[256,1024]{1,0:T(8,128)(2,1)S(1)}, u32[]{:S(2)}, u32[]{:S(2)}) %collective-permute-start.37) | collective-permute-done | bytes 524320 | tf_op jit(solution)/shard_map/ppermute | solution.py:30
  186.6 2.8 %collective-permute-start.42 = (bf16[128,512]{1,0:T(8,128)(2,1)S(1)}, bf16[128,512]{1,0:T(8,128)(2,1)S(1)}, u32[]{:S(2)}, u32[]{:S(2)}) collective-permute-start(bf16[128,512]{1,0:T(8,128)(2,1)S(1)} %shard_map.291), channel_id=1, source_target_pairs={{0,16},{4,20},{8,24},{12,28},{16,0},{20,4},{24,8},{28,12},{1,17},{... | collective-permute-start | bytes 393224 | tf_op jit(solution)/shard_map/ppermute | solution.py:30
  189.7 9.9 %collective-permute-done.42 = bf16[128,512]{1,0:T(8,128)(2,1)S(1)} collective-permute-done((bf16[128,512]{1,0:T(8,128)(2,1)S(1)}, bf16[128,512]{1,0:T(8,128)(2,1)S(1)}, u32[]{:S(2)}, u32[]{:S(2)}) %collective-permute-start.42) | collective-permute-done | bytes 131104 | tf_op jit(solution)/shard_map/ppermute | solution.py:30
  207.0 4.9 %collective-permute-done.43 = bf16[288,512]{1,0:T(8,128)(2,1)S(1)} collective-permute-done((bf16[288,512]{1,0:T(8,128)(2,1)S(1)}, bf16[288,512]{1,0:T(8,128)(2,1)S(1)}, u32[]{:S(2)}, u32[]{:S(2)}) %collective-permute-start.43) | collective-permute-done | bytes 294944 | tf_op jit(solution)/shard_map/ppermute | solution.py:30
  214.7 14.7 %collective-permute-done.49.refs_1_ = bf16[512,1024]{1,0:T(8,128)(2,1)S(1)} collective-permute-done((bf16[512,1024]{1,0:T(8,128)(2,1)S(1)}, bf16[512,1024]{1,0:T(8,128)(2,1)S(1)}, u32[]{:S(2)}, u32[]{:S(2)}) %collective-permute-start.49) | collective-permute-done | bytes 1048608 | tf_op jit(solution)/shard_map/ppermute | solution.py:30
  229.4 2.6 %shard_map.295 = f32[1024,1024]{1,0:T(8,128)} custom-call(s32[2]{0:T(128)S(1)} %pad_add_fusion.refs_0_.me, bf16[512,1024]{1,0:T(8,128)(2,1)S(1)} %pad_maximum_fusion.refs_0_, bf16[512,1024]{1,0:T(8,128)(2,1)S(1)} %collective-permute-done.49.refs_1_), custom_call_target="tpu_custom_call" | custom-call | tf_op jit(solution)/shard_map/pallas_call | solution.py:96
  234.3 8.9 %collective-permute-done.47.refs_3_ = bf16[512,512]{1,0:T(8,128)(2,1)S(1)} collective-permute-done((bf16[512,512]{1,0:T(8,128)(2,1)S(1)}, bf16[512,512]{1,0:T(8,128)(2,1)S(1)}, u32[]{:S(2)}, u32[]{:S(2)}) %collective-permute-start.47) | collective-permute-done | bytes 524320 | tf_op jit(solution)/shard_map/ppermute | solution.py:30
  243.3 2.6 %shard_map.294 = f32[1024,1024]{1,0:T(8,128)} custom-call(s32[2]{0:T(128)S(1)} %pad_add_fusion.refs_0_.me, bf16[512,1024]{1,0:T(8,128)(2,1)S(1)} %pad_maximum_fusion.1.refs_0_, bf16[512,1024]{1,0:T(8,128)(2,1)S(1)} %collective-permute-done.48.refs_1_), custom_call_target="tpu_custom_call" | custom-call | tf_op jit(solution)/shard_map/pallas_call | solution.py:96
  246.7 2.8 %shard_map.293 = (f32[1024,768]{1,0:T(8,128)}, f32[256,1024]{1,0:T(8,128)}) custom-call(s32[2]{0:T(128)S(1)} %pad_add_fusion.refs_0_.me, bf16[512,512]{1,0:T(8,128)(2,1)S(1)} %pad_maximum_fusion.5.refs_0_, bf16[544,512]{1,0:T(8,128)(2,1)S(1)} %collective-permute-done.46.refs_1_, bf16[512,512]{1,0:T(8,128)(2,1)S(1)} %pad_maximum_fusion.4.refs_2_, ...), custom_call_target="tpu_custom_call" | custom-call | tf_op jit(solution)/shard_map/pallas_call | solution.py:96
  (196 shorter events, 82.8 us)
Async XLA Ops:
  0.6 19.8 %collective-permute-start.2 = (bf16[240,1024]{1,0:T(8,128)(2,1)}, bf16[240,1024]{1,0:T(8,128)(2,1)}, u32[]{:S(2)}, u32[]{:S(2)}) collective-permute-start(bf16[240,1024]{1,0:T(8,128)(2,1)} %refs_4_.3), channel_id=1, source_target_pairs={{0,2},{1,3},{2,0},{3,1},{4,6},{5,7},{6,4},{7,5},{8,10},{9,11},{10,... | collective-permute-start | bytes 1474568 | tf_op jit(solution)/shard_map/ppermute | solution.py:30
  21.1 13.2 %collective-permute-start.5 = (bf16[240,1024]{1,0:T(8,128)(2,1)S(1)}, bf16[240,1024]{1,0:T(8,128)(2,1)S(1)}, u32[]{:S(2)}, u32[]{:S(2)}) collective-permute-start(bf16[240,1024]{1,0:T(8,128)(2,1)S(1)} %multiply_convert_fusion.1.refs_9_.refs_12_.refs_1_.refs_10_.refs_3_.refs_7_.refs_5_.refs_8_.refs_6_.refs_14_), channel_id=1, source_target_pairs={{0,2},{1,3},{2,0},{3,1},{4,6},{5,7},{6,4},{7,5},{8,10},{9,11},{10,... | collective-permute-start | bytes 1474568 | tf_op jit(solution)/shard_map/ppermute | solution.py:30
  34.5 13.6 %collective-permute-start.7 = (bf16[240,1024]{1,0:T(8,128)(2,1)S(1)}, bf16[240,1024]{1,0:T(8,128)(2,1)S(1)}, u32[]{:S(2)}, u32[]{:S(2)}) collective-permute-start(bf16[240,1024]{1,0:T(8,128)(2,1)S(1)} %shard_map.256), channel_id=1, source_target_pairs={{0,2},{1,3},{2,0},{3,1},{4,6},{5,7},{6,4},{7,5},{8,10},{9,11},{10,... | collective-permute-start | bytes 1474568 | tf_op jit(solution)/shard_map/ppermute | solution.py:30
  50.3 13.2 %collective-permute-start.8 = (bf16[240,1024]{1,0:T(8,128)(2,1)S(1)}, bf16[240,1024]{1,0:T(8,128)(2,1)S(1)}, u32[]{:S(2)}, u32[]{:S(2)}) collective-permute-start(bf16[240,1024]{1,0:T(8,128)(2,1)S(1)} %get-tuple-element.146.refs_1_.refs_19_.refs_20_.refs_17_.refs_18_), channel_id=1, source_target_pairs={{0,2},{1,3},{2,0},{3,1},{4,6},{5,7},{6,4},{7,5},{8,10},{9,11},{10,... | collective-permute-start | bytes 1474568 | tf_op jit(solution)/shard_map/ppermute | solution.py:30
  72.1 13.1 %collective-permute-start.13 = (bf16[240,1024]{1,0:T(8,128)(2,1)S(1)}, bf16[240,1024]{1,0:T(8,128)(2,1)S(1)}, u32[]{:S(2)}, u32[]{:S(2)}) collective-permute-start(bf16[240,1024]{1,0:T(8,128)(2,1)S(1)} %get-tuple-element.161), channel_id=1, source_target_pairs={{0,1},{1,0},{2,3},{3,2},{4,5},{5,4},{6,7},{7,6},{8,9},{9,8},{10,11... | collective-permute-start | bytes 1474568 | tf_op jit(solution)/shard_map/ppermute | solution.py:30
  73.9 13.3 %collective-permute-start.14 = (bf16[240,1024]{1,0:T(8,128)(2,1)S(1)}, bf16[240,1024]{1,0:T(8,128)(2,1)S(1)}, u32[]{:S(2)}, u32[]{:S(2)}) collective-permute-start(bf16[240,1024]{1,0:T(8,128)(2,1)S(1)} %shard_map.263), channel_id=1, source_target_pairs={{0,2},{1,3},{2,0},{3,1},{4,6},{5,7},{6,4},{7,5},{8,10},{9,11},{10,... | collective-permute-start | bytes 1474568 | tf_op jit(solution)/shard_map/ppermute | solution.py:30
  80.0 25.0 %collective-permute-start.19 = (bf16[512,1024]{1,0:T(8,128)(2,1)S(1)}, bf16[512,1024]{1,0:T(8,128)(2,1)S(1)}, u32[]{:S(2)}, u32[]{:S(2)}) collective-permute-start(bf16[512,1024]{1,0:T(8,128)(2,1)S(1)} %shard_map.265), channel_id=1, source_target_pairs={{0,8},{4,12},{8,0},{12,4},{16,24},{20,28},{24,16},{28,20},{1,9},{5... | collective-permute-start | bytes 3145736 | tf_op jit(solution)/shard_map/ppermute | solution.py:30
  81.9 24.6 %collective-permute-start.15 = (bf16[512,1024]{1,0:T(8,128)(2,1)S(1)}, bf16[512,1024]{1,0:T(8,128)(2,1)S(1)}, u32[]{:S(2)}, u32[]{:S(2)}) collective-permute-start(bf16[512,1024]{1,0:T(8,128)(2,1)S(1)} %shard_map.264), channel_id=1, source_target_pairs={{0,4},{4,0},{8,12},{12,8},{16,20},{20,16},{24,28},{28,24},{1,5},{5... | collective-permute-start | bytes 3145736 | tf_op jit(solution)/shard_map/ppermute | solution.py:30
  85.1 18.1 %collective-permute-start.22 = (bf16[240,1024]{1,0:T(8,128)(2,1)S(1)}, bf16[240,1024]{1,0:T(8,128)(2,1)S(1)}, u32[]{:S(2)}, u32[]{:S(2)}) collective-permute-start(bf16[240,1024]{1,0:T(8,128)(2,1)S(1)} %get-tuple-element.181), channel_id=1, source_target_pairs={{0,1},{1,0},{2,3},{3,2},{4,5},{5,4},{6,7},{7,6},{8,9},{9,8},{10,11... | collective-permute-start | bytes 1474568 | tf_op jit(solution)/shard_map/ppermute | solution.py:30
  89.5 13.6 %collective-permute-start.16 = (bf16[240,1024]{1,0:T(8,128)(2,1)S(1)}, bf16[240,1024]{1,0:T(8,128)(2,1)S(1)}, u32[]{:S(2)}, u32[]{:S(2)}) collective-permute-start(bf16[240,1024]{1,0:T(8,128)(2,1)S(1)} %get-tuple-element.162.refs_27_.refs_1_.refs_22_.refs_18_.refs_20_.refs_15_.refs_14_.refs_7_), channel_id=1, source_target_pairs={{0,2},{1,3},{2,0},{3,1},{4,6},{5,7},{6,4},{7,5},{8,10},{9,11},{10,... | collective-permute-start | bytes 1474568 | tf_op jit(solution)/shard_map/ppermute | solution.py:30
  103.2 17.4 %collective-permute-start.23 = (bf16[240,1024]{1,0:T(8,128)(2,1)S(1)}, bf16[240,1024]{1,0:T(8,128)(2,1)S(1)}, u32[]{:S(2)}, u32[]{:S(2)}) collective-permute-start(bf16[240,1024]{1,0:T(8,128)(2,1)S(1)} %shard_map.274), channel_id=1, source_target_pairs={{0,2},{1,3},{2,0},{3,1},{4,6},{5,7},{6,4},{7,5},{8,10},{9,11},{10,... | collective-permute-start | bytes 1474568 | tf_op jit(solution)/shard_map/ppermute | solution.py:30
  106.9 12.6 %collective-permute-start.24 = (bf16[256,1024]{1,0:T(8,128)(2,1)S(1)}, bf16[256,1024]{1,0:T(8,128)(2,1)S(1)}, u32[]{:S(2)}, u32[]{:S(2)}) collective-permute-start(bf16[256,1024]{1,0:T(8,128)(2,1)S(1)} %get-tuple-element.174), channel_id=1, source_target_pairs={{0,4},{4,0},{8,12},{12,8},{16,20},{20,16},{24,28},{28,24},{1,5},{5... | collective-permute-start | bytes 1572872 | tf_op jit(solution)/shard_map/ppermute | solution.py:30
  108.4 12.2 %collective-permute-start.18 = (bf16[256,1024]{1,0:T(8,128)(2,1)S(1)}, bf16[256,1024]{1,0:T(8,128)(2,1)S(1)}, u32[]{:S(2)}, u32[]{:S(2)}) collective-permute-start(bf16[256,1024]{1,0:T(8,128)(2,1)S(1)} %get-tuple-element.172), channel_id=1, source_target_pairs={{0,8},{4,12},{8,0},{12,4},{16,24},{20,28},{24,16},{28,20},{1,9},{5... | collective-permute-start | bytes 1572872 | tf_op jit(solution)/shard_map/ppermute | solution.py:30
  121.0 43.2 %collective-permute-start.34 = (bf16[128,1024]{1,0:T(8,128)(2,1)S(1)}, bf16[128,1024]{1,0:T(8,128)(2,1)S(1)}, u32[]{:S(2)}, u32[]{:S(2)}) collective-permute-start(bf16[128,1024]{1,0:T(8,128)(2,1)S(1)} %get-tuple-element.192), channel_id=1, source_target_pairs={{0,16},{4,20},{8,24},{12,28},{16,0},{20,4},{24,8},{28,12},{1,17},{... | collective-permute-start | bytes 786440 | tf_op jit(solution)/shard_map/ppermute | solution.py:30
  123.6 22.5 %collective-permute-start.29 = (bf16[128,1024]{1,0:T(8,128)(2,1)S(1)}, bf16[128,1024]{1,0:T(8,128)(2,1)S(1)}, u32[]{:S(2)}, u32[]{:S(2)}) collective-permute-start(bf16[128,1024]{1,0:T(8,128)(2,1)S(1)} %get-tuple-element.189), channel_id=1, source_target_pairs={{0,16},{4,20},{8,24},{12,28},{16,0},{20,4},{24,8},{28,12},{1,17},{... | collective-permute-start | bytes 786440 | tf_op jit(solution)/shard_map/ppermute | solution.py:30
  124.0 11.6 %collective-permute-start.26 = (bf16[240,1024]{1,0:T(8,128)(2,1)S(1)}, bf16[240,1024]{1,0:T(8,128)(2,1)S(1)}, u32[]{:S(2)}, u32[]{:S(2)}) collective-permute-start(bf16[240,1024]{1,0:T(8,128)(2,1)S(1)} %shard_map.275), channel_id=1, source_target_pairs={{0,2},{1,3},{2,0},{3,1},{4,6},{5,7},{6,4},{7,5},{8,10},{9,11},{10,... | collective-permute-start | bytes 1474568 | tf_op jit(solution)/shard_map/ppermute | solution.py:30
  130.5 32.2 %collective-permute-start.31 = (bf16[512,512]{1,0:T(8,128)(2,1)S(1)}, bf16[512,512]{1,0:T(8,128)(2,1)S(1)}, u32[]{:S(2)}, u32[]{:S(2)}) collective-permute-start(bf16[512,512]{1,0:T(8,128)(2,1)S(1)} %shard_map.280), channel_id=1, source_target_pairs={{0,8},{4,12},{8,0},{12,4},{16,24},{20,28},{24,16},{28,20},{1,9},{5... | collective-permute-start | bytes 1572872 | tf_op jit(solution)/shard_map/ppermute | solution.py:30
  134.9 14.4 %collective-permute-start.28 = (bf16[512,512]{1,0:T(8,128)(2,1)S(1)}, bf16[512,512]{1,0:T(8,128)(2,1)S(1)}, u32[]{:S(2)}, u32[]{:S(2)}) collective-permute-start(bf16[512,512]{1,0:T(8,128)(2,1)S(1)} %shard_map.279), channel_id=1, source_target_pairs={{0,4},{4,0},{8,12},{12,8},{16,20},{20,16},{24,28},{28,24},{1,5},{5... | collective-permute-start | bytes 1572872 | tf_op jit(solution)/shard_map/ppermute | solution.py:30
  146.2 18.1 %collective-permute-start.33 = (bf16[128,1024]{1,0:T(8,128)(2,1)S(1)}, bf16[128,1024]{1,0:T(8,128)(2,1)S(1)}, u32[]{:S(2)}, u32[]{:S(2)}) collective-permute-start(bf16[128,1024]{1,0:T(8,128)(2,1)S(1)} %shard_map.285), channel_id=1, source_target_pairs={{0,16},{4,20},{8,24},{12,28},{16,0},{20,4},{24,8},{28,12},{1,17},{... | collective-permute-start | bytes 786440 | tf_op jit(solution)/shard_map/ppermute | solution.py:30
  146.4 18.0 %collective-permute-start.40 = (bf16[12,1024]{1,0:T(8,128)(2,1)S(1)}, bf16[12,1024]{1,0:T(8,128)(2,1)S(1)}, u32[]{:S(2)}, u32[]{:S(2)}) collective-permute-start(bf16[12,1024]{1,0:T(8,128)(2,1)S(1)} %pad_maximum_fusion.11), channel_id=1, source_target_pairs={{0,2},{1,3},{2,0},{3,1},{4,6},{5,7},{6,4},{7,5},{8,10},{9,11},{10,... | collective-permute-start | bytes 73736 | tf_op jit(solution)/shard_map/ppermute | solution.py:30
  149.4 22.8 %collective-permute-start.30 = (bf16[256,512]{1,0:T(8,128)(2,1)S(1)}, bf16[256,512]{1,0:T(8,128)(2,1)S(1)}, u32[]{:S(2)}, u32[]{:S(2)}) collective-permute-start(bf16[256,512]{1,0:T(8,128)(2,1)S(1)} %get-tuple-element.210), channel_id=1, source_target_pairs={{0,8},{4,12},{8,0},{12,4},{16,24},{20,28},{24,16},{28,20},{1,9},{5... | collective-permute-start | bytes 786440 | tf_op jit(solution)/shard_map/ppermute | solution.py:30
  164.2 13.1 %collective-permute-start.38 = (bf16[128,1024]{1,0:T(8,128)(2,1)S(1)}, bf16[128,1024]{1,0:T(8,128)(2,1)S(1)}, u32[]{:S(2)}, u32[]{:S(2)}) collective-permute-start(bf16[128,1024]{1,0:T(8,128)(2,1)S(1)} %shard_map.288), channel_id=1, source_target_pairs={{0,16},{4,20},{8,24},{12,28},{16,0},{20,4},{24,8},{28,12},{1,17},{... | collective-permute-start | bytes 786440 | tf_op jit(solution)/shard_map/ppermute | solution.py:30
  164.4 22.1 %collective-permute-start.37 = (bf16[256,1024]{1,0:T(8,128)(2,1)S(1)}, bf16[256,1024]{1,0:T(8,128)(2,1)S(1)}, u32[]{:S(2)}, u32[]{:S(2)}) collective-permute-start(bf16[256,1024]{1,0:T(8,128)(2,1)S(1)} %pad_maximum_fusion.2), channel_id=1, source_target_pairs={{0,8},{4,12},{8,0},{12,4},{16,24},{20,28},{24,16},{28,20},{1,9},{5... | collective-permute-start | bytes 1572872 | tf_op jit(solution)/shard_map/ppermute | solution.py:30
  169.3 17.2 %collective-permute-start.36 = (bf16[128,512]{1,0:T(8,128)(2,1)S(1)}, bf16[128,512]{1,0:T(8,128)(2,1)S(1)}, u32[]{:S(2)}, u32[]{:S(2)}) collective-permute-start(bf16[128,512]{1,0:T(8,128)(2,1)S(1)} %get-tuple-element.217), channel_id=1, source_target_pairs={{0,16},{4,20},{8,24},{12,28},{16,0},{20,4},{24,8},{28,12},{1,17},{... | collective-permute-start | bytes 393224 | tf_op jit(solution)/shard_map/ppermute | solution.py:30
  172.2 17.1 %collective-permute-start.35 = (bf16[128,512]{1,0:T(8,128)(2,1)S(1)}, bf16[128,512]{1,0:T(8,128)(2,1)S(1)}, u32[]{:S(2)}, u32[]{:S(2)}) collective-permute-start(bf16[128,512]{1,0:T(8,128)(2,1)S(1)} %get-tuple-element.221), channel_id=1, source_target_pairs={{0,16},{4,20},{8,24},{12,28},{16,0},{20,4},{24,8},{28,12},{1,17},{... | collective-permute-start | bytes 393224 | tf_op jit(solution)/shard_map/ppermute | solution.py:30
  177.4 25.3 %collective-permute-start.45 = (bf16[256,1024]{1,0:T(8,128)(2,1)S(1)}, bf16[256,1024]{1,0:T(8,128)(2,1)S(1)}, u32[]{:S(2)}, u32[]{:S(2)}) collective-permute-start(bf16[256,1024]{1,0:T(8,128)(2,1)S(1)} %pad_maximum_fusion.3), channel_id=1, source_target_pairs={{0,4},{4,0},{8,12},{12,8},{16,20},{20,16},{24,28},{28,24},{1,5},{5... | collective-permute-start | bytes 1572872 | tf_op jit(solution)/shard_map/ppermute | solution.py:30
  186.6 13.1 %collective-permute-start.42 = (bf16[128,512]{1,0:T(8,128)(2,1)S(1)}, bf16[128,512]{1,0:T(8,128)(2,1)S(1)}, u32[]{:S(2)}, u32[]{:S(2)}) collective-permute-start(bf16[128,512]{1,0:T(8,128)(2,1)S(1)} %shard_map.291), channel_id=1, source_target_pairs={{0,16},{4,20},{8,24},{12,28},{16,0},{20,4},{24,8},{28,12},{1,17},{... | collective-permute-start | bytes 393224 | tf_op jit(solution)/shard_map/ppermute | solution.py:30
  189.4 12.4 %collective-permute-start.41 = (bf16[160,512]{1,0:T(8,128)(2,1)S(1)}, bf16[160,512]{1,0:T(8,128)(2,1)S(1)}, u32[]{:S(2)}, u32[]{:S(2)}) collective-permute-start(bf16[160,512]{1,0:T(8,128)(2,1)S(1)} %pad_maximum_fusion.8), channel_id=1, source_target_pairs={{0,16},{4,20},{8,24},{12,28},{16,0},{20,4},{24,8},{28,12},{1,17},{... | collective-permute-start | bytes 491528 | tf_op jit(solution)/shard_map/ppermute | solution.py:30
  202.1 27.3 %collective-permute-start.49 = (bf16[512,1024]{1,0:T(8,128)(2,1)S(1)}, bf16[512,1024]{1,0:T(8,128)(2,1)S(1)}, u32[]{:S(2)}, u32[]{:S(2)}) collective-permute-start(bf16[512,1024]{1,0:T(8,128)(2,1)S(1)} %pad_maximum_fusion.refs_0_), channel_id=1, source_target_pairs={{0,4},{4,0},{8,12},{12,8},{16,20},{20,16},{24,28},{28,24},{1,5},{5... | collective-permute-start | bytes 3145736 | tf_op jit(solution)/shard_map/ppermute | solution.py:30
  202.7 31.6 %collective-permute-start.48 = (bf16[512,1024]{1,0:T(8,128)(2,1)S(1)}, bf16[512,1024]{1,0:T(8,128)(2,1)S(1)}, u32[]{:S(2)}, u32[]{:S(2)}) collective-permute-start(bf16[512,1024]{1,0:T(8,128)(2,1)S(1)} %pad_maximum_fusion.1.refs_0_), channel_id=1, source_target_pairs={{0,8},{4,12},{8,0},{12,4},{16,24},{20,28},{24,16},{28,20},{1,9},{5... | collective-permute-start | bytes 3145736 | tf_op jit(solution)/shard_map/ppermute | solution.py:30
  211.9 31.3 %collective-permute-start.46 = (bf16[544,512]{1,0:T(8,128)(2,1)S(1)}, bf16[544,512]{1,0:T(8,128)(2,1)S(1)}, u32[]{:S(2)}, u32[]{:S(2)}) collective-permute-start(bf16[544,512]{1,0:T(8,128)(2,1)S(1)} %fusion.14), channel_id=1, source_target_pairs={{0,4},{4,0},{8,12},{12,8},{16,20},{20,16},{24,28},{28,24},{1,5},{5... | collective-permute-start | bytes 1671176 | tf_op jit(solution)/shard_map/ppermute | solution.py:30
  212.5 30.7 %collective-permute-start.47 = (bf16[512,512]{1,0:T(8,128)(2,1)S(1)}, bf16[512,512]{1,0:T(8,128)(2,1)S(1)}, u32[]{:S(2)}, u32[]{:S(2)}) collective-permute-start(bf16[512,512]{1,0:T(8,128)(2,1)S(1)} %pad_maximum_fusion.4.refs_2_), channel_id=1, source_target_pairs={{0,8},{4,12},{8,0},{12,4},{16,24},{20,28},{24,16},{28,20},{1,9},{5... | collective-permute-start | bytes 1572872 | tf_op jit(solution)/shard_map/ppermute | solution.py:30
  (36 other events, 190.0 us)

commit v4 on v3

--- a/solution.py
+++ b/solution.py
@@ -152,6 +152,7 @@
 
 def project_side(blocks, vectors, weight, bias, normed, put):
     rows = blocks[0].shape[0]
+    width = weight.shape[1] // 3
     for i, block in enumerate(blocks):
 
         def step(at, block=block, i=i):
@@ -160,7 +161,12 @@
             normed[tile, :] = (z * row(vectors, GAIN_ONE) + row(vectors, SHIFT_ONE)).astype(BF)
 
         row_tiles(rows, 48, step)
-        put(i, (mm(normed[i * rows : (i + 1) * rows, :], weight[...]) + bias[...]).astype(BF))
+        found = (mm(normed[i * rows : (i + 1) * rows, :], weight[...]) + bias[...]).astype(BF)
+        kinds = [
+            [found[:, (3 * head + kind) * HD :][:, :HD] for head in range(width // HD)]
+            for kind in range(3)
+        ]
+        put(i, jnp.concatenate(sum(kinds, []), axis=1))
 
 
 def project_local(me, tok_a, tok_b, vectors, weight, bias, normed, proj):
@@ -211,21 +217,30 @@
     hold[...] = mm(heads_out[pl.ds(pl.multiple_of(core * rows, 16), rows), :], weight[...])
 
 
+def project_one(me, tok, vectors, weight, bias, normed, proj):
+    def put(i, values):
+        proj[...] = values
+
+    project_side((tok,), vectors, weight, bias, normed, put)
+
+
 def attend_far(
-    me, near, tok_a, tok_b, vectors, weight, bias, keep, out_w,
+    me, near, first, tok, vectors, weight, bias, keep, out_w,
     normed, qkv, probs, heads_out, send, hold,
 ):
-    rows = tok_a.shape[0]
+    rows = tok.shape[0]
     core, far = me[0] & 1, me[0] >> 1
     for i in range(2):
         at = pl.multiple_of((2 * far + (core ^ i)) * rows, 16)
         qkv[pl.ds(at, rows), :] = near[i * rows : (i + 1) * rows, :]
+    at = pl.multiple_of((2 * (1 - far) + core) * rows, 16)
+    qkv[pl.ds(at, rows), :] = first[...]
 
     def put(i, values):
-        at = pl.multiple_of((2 * (1 - far) + (core ^ i)) * rows, 16)
+        at = pl.multiple_of((2 * (1 - far) + (1 - core)) * rows, 16)
         qkv[pl.ds(at, rows), :] = values
 
-    project_side((tok_a, tok_b), vectors, weight, bias, normed, put)
+    project_side((tok,), vectors, weight, bias, normed, put)
     attend(1 - far, qkv, keep, probs, heads_out)
     out_project(core, heads_out, out_w, send, hold)
 
@@ -257,47 +272,61 @@
     blocks(down.shape[0] // 256, 256, step)
 
 
-def feed_forward(
-    me, norm_a, norm_b, up, vectors, act_grad, act, pre_low, bias_grad, send, hold, total, pre
-):
-    rows = norm_a.shape[0]
-
-    def step(at, number):
-        for i, block in enumerate((norm_a, norm_b)):
-            pre[pl.ds(i * rows, rows), :] = mm(block[...], up[:, at])
+def feed_forward(low, count, me, *refs):
+    norms = refs[:count]
+    up, vectors, act_grad, act, pre_low, bias_grad = refs[count : count + 6]
+    outs, total, pre = refs[count + 6 : 2 * count + 6], refs[-2], refs[-1]
+    rows = norms[0].shape[0]
+    wide = pre.shape[2]
+    number = up.shape[1] // wide
+    bias_grad[...] = jnp.zeros_like(bias_grad)
+    total[...] = jnp.zeros_like(total)
+
+    def columns(i):
+        return pl.ds(pl.multiple_of(i * wide, wide), wide)
+
+    def elements(slot, at, block):
         own_bias = vectors[UP_BIAS : UP_BIAS + 1, at]
-
-        def one(i, sums):
-            tile = pl.ds(pl.multiple_of(i * 32, 32), 32)
-            x = pre[tile, :] + own_bias
+        sums = None
+        for i in range(0, rows, 16):
+            to = pl.ds(block * rows + i, 16)
+            x = pre[slot, i : i + 16, :] + own_bias
             share = 0.5 + 0.5 * lax.erf(x * 0.7071067811865476)
             slope = share + x * (0.3989422804014327 * jnp.exp(-0.5 * x * x))
-            act[tile, at] = (x * share).astype(BF)
-            grad = act_grad[tile, at] * slope
-            pre_low[tile, at] = grad.astype(BF)
-            return sums + fold(grad)
-
-        sums = lax.fori_loop(0, 2 * rows // 32, one, jnp.zeros((8, pre.shape[1]), F32))
-        bias_grad[:, at] = jnp.sum(sums, axis=0, keepdims=True)
-        part = mm(pre_low[:, at], up[:, at], NT)
-
-        @pl.when(number == 0)
-        def _():
-            total[...] = part
-
-        @pl.when(number > 0)
-        def _():
-            total[...] += part
-
-    blocks(up.shape[1] // 256, 256, step)
-    hold[...] = total[:rows, :]
-    send[...] = total[rows:, :].astype(BF)
-
-
-def feed_out(me, act, down, send, hold):
+            act[to, at] = (x * share).astype(BF)
+            grad = act_grad[pl.ds(low + block * rows + i, 16), at] * slope
+            pre_low[to, at] = grad.astype(BF)
+            part = grad[:8] + grad[8:]
+            sums = part if sums is None else sums + part
+        bias_grad[:, at] += jnp.sum(sums, axis=0, keepdims=True)
+
+    pre[0] = mm(norms[0][...], up[:, :wide])
+
+    def one(i, carry):
+        if count == 2:
+            steps = ((i, 0), (i, 1), (jnp.minimum(i + 1, number - 1), 0))
+        else:
+            steps = ((2 * i, 0), (2 * i + 1, 0), (jnp.minimum(2 * i + 2, number - 1), 0))
+        for slot in range(2):
+            column, block = steps[slot]
+            later, other = steps[slot + 1]
+            pre[1 - slot] = mm(norms[other][...], up[:, columns(later)])
+            elements(slot, columns(column), block)
+            inside = pl.ds(block * rows, rows)
+            total[inside, :] += mm(pre_low[inside, columns(column)], up[:, columns(column)], NT)
+        return carry
+
+    lax.fori_loop(0, number * count // 2, one, 0)
+    for i, out in enumerate(outs):
+        out[...] = total[i * rows : (i + 1) * rows, :].astype(out.dtype)
+
+
+def feed_out(count, me, *refs):
+    acts, (down, send, hold) = refs[:count], refs[count:]
     rows = send.shape[0]
-    send[...] = mm(act[rows:, :], down[...]).astype(BF)
-    hold[...] = mm(act[:rows, :], down[...])
+    one = acts[-1][rows:, :] if count == 1 else acts[1][...]
+    send[...] = mm(one, down[...]).astype(BF)
+    hold[...] = mm(acts[0][:rows, :], down[...])
 
 
 def gather_pieces(me, lefts, order, base, turned):
@@ -308,22 +337,29 @@
             to[i * piece : (i + 1) * piece, :] = left[:, at].T
 
 
+def segments(lefts, rights):
+    found, left, right, a, b = [], 0, 0, 0, 0
+    while left < len(lefts):
+        rows = min(lefts[left].shape[0] - a, rights[right].shape[0] - b)
+        found.append((left, a, right, b, rows))
+        a, b = a + rows, b + rows
+        if a == lefts[left].shape[0]:
+            left, a = left + 1, 0
+        if b == rights[right].shape[0]:
+            right, b = right + 1, 0
+    return found
+
+
 def weight_pieces(order, base, low, count, me, *refs):
     lefts, rights = refs[: count[0]], refs[count[0] : sum(count)]
     out, turned = refs[sum(count)], refs[sum(count) + 1 :]
     gather_pieces(me, lefts, order, base, turned)
-    rows = min(lefts[0].shape[0], rights[0].shape[0])
-    left_each, right_each = lefts[0].shape[0] // rows, rights[0].shape[0] // rows
 
     def step(at, i):
         found = None
         from_ = pl.ds(pl.multiple_of(at.start + low, 128), at.size)
-        for k in range(max(count)):
-            left, right = turned[k // left_each], rights[k // right_each]
-            inner = (k % left_each) * rows
-            part = mm(
-                left[:, inner : inner + rows], right[pl.ds((k % right_each) * rows, rows), from_]
-            )
+        for left, a, right, b, rows in segments(lefts, rights):
+            part = mm(turned[left][:, a : a + rows], rights[right][b : b + rows, from_])
             found = part if found is None else found + part
         out[:, at] = found.astype(out.dtype)
 
@@ -331,13 +367,18 @@
 
 
 def mixed_pieces(order, base, low, me, *refs):
-    lefts, rights, heads, mids, out = refs[:2], refs[2:4], refs[4:6], refs[6:10], refs[10]
-    turned = refs[11:13]
+    lefts, rights, heads, mids, out = refs[:3], refs[3:5], refs[5:7], refs[7:11], refs[11]
+    turned = refs[12:]
     gather_pieces(me, lefts, order, base, turned)
     width = rights[0].shape[1] - low
     for at in range(0, width, 256):
-        found = mm(turned[0][...], rights[0][:, low + at : low + at + 256])
-        found = found + mm(turned[1][...], rights[1][:, low + at : low + at + 256])
+        found = None
+        for left, a, right, b, rows in segments(lefts, rights):
+            part = mm(
+                turned[left][:, a : a + rows],
+                rights[right][b : b + rows, low + at : low + at + 256],
+            )
+            found = part if found is None else found + part
         out[:, at : at + 256] = found.astype(out.dtype)
     core = me[0] & 1
     rows = mids[0].shape[0]
@@ -424,7 +465,7 @@
 
 def back_far(
     me, mid_a, mid_b, qkv, probs, out_w, near_q, near_keys, in_w,
-    proj_near, proj_far, flat_near, flat_far, bias_grad, send, hold, grads, far_q, keys_grad,
+    flat_near, flat_far, bias_grad, send, hold, grads, far_q, keys_grad, group,
 ):
     core, far = me[0] & 1, me[0] >> 1
     rows = mid_a.shape[0]
@@ -438,20 +479,19 @@
         ],
         axis=1,
     )
-    sides = ((proj_near, flat_near, near_q), (proj_far, flat_far, far_q))
-    for side, (out, flat, q_part) in enumerate(sides):
+    for side, (flat, q_part) in enumerate(((flat_near, near_q), (flat_far, far_q))):
         for i in range(2):
             inside = pl.multiple_of((core ^ i) * rows, 16)
             place = pl.multiple_of((2 * (far ^ side) + (core ^ i)) * rows, 16)
             to = pl.ds(i * rows, rows)
-            out[to, :width] = q_part[pl.ds(inside, rows), :].astype(BF)
-            out[to, width:] = keys_grad[pl.ds(place, rows), :].astype(BF)
+            group[to, :width] = q_part[pl.ds(inside, rows), :].astype(BF)
+            group[to, width:] = keys_grad[pl.ds(place, rows), :].astype(BF)
         for head in range(width // HD):
             for kind in range(3):
                 at = (head * 3 + kind) * HD
-                flat[:, at : at + HD] = out[:, kind * width + head * HD :][:, :HD]
-    send[...] = mm(proj_far[rows:, :], in_w[...], NT).astype(BF)
-    hold[...] = mm(proj_far[:rows, :], in_w[...], NT)
+                flat[:, at : at + HD] = group[:, kind * width + head * HD :][:, :HD]
+    send[...] = mm(flat_far[rows:, :], in_w[...], NT).astype(BF)
+    hold[...] = mm(flat_far[:rows, :], in_w[...], NT)
 
 
 def first_back(me, proj, in_w, send, hold):
@@ -627,30 +667,27 @@
 
 
 def weight_grad(me, lefts, rights, order, kept, low=0, wide=None):
-    rows, columns = lefts[0].shape
+    half = lefts[0].shape[1] // 2
     wide = wide or rights[0].shape[1]
-    half = columns // 2
+    count = (len(lefts), len(rights))
     return run(
-        functools.partial(
-            weight_pieces, order, 0 if kept else PIECES // 2, low, (len(lefts), len(rights))
-        ),
+        functools.partial(weight_pieces, order, 0 if kept else PIECES // 2, low, count),
         (me, *lefts, *rights),
         [shape((half, wide), F32 if kept else BF)],
-        scratch=[pltpu.VMEM((half, rows), BF)] * len(lefts),
-        flops=2 * len(lefts) * rows * half * wide,
+        scratch=[pltpu.VMEM((half, x.shape[0]), BF) for x in lefts],
+        flops=2 * 960 * half * wide,
     )[0]
 
 
 def mixed_grad(me, normed, proj, heads, mids, order, kept, low):
-    rows, columns = normed[0].shape
-    half = columns // 2
+    half = normed[0].shape[1] // 2
     wide = proj[0].shape[1] - low + heads[0].shape[1]
     return run(
         functools.partial(mixed_pieces, order, 0 if kept else PIECES // 2, low),
         (me, *normed, *proj, *heads, *mids),
         [shape((half, wide), F32 if kept else BF)],
-        scratch=[pltpu.VMEM((half, rows), BF)] * 2,
-        flops=2 * 2 * rows * half * wide,
+        scratch=[pltpu.VMEM((half, x.shape[0]), BF) for x in normed],
+        flops=2 * 960 * half * wide,
     )[0]
 
 
@@ -709,25 +746,25 @@
             flops=2 * side * model * hidden,
         )[0]
 
-    def feed(one, other, act_grad):
+    def feed(norms, act_grad, low, kinds):
+        tall = rows * len(norms)
         return run(
-            feed_forward,
-            (me, one, other, up_weight, vectors, act_grad),
+            functools.partial(feed_forward, low, len(norms)),
+            (me, *norms, up_weight, vectors, act_grad),
             [
-                shape((side, hidden), BF),
-                shape((side, hidden), BF),
+                shape((tall, hidden), BF),
+                shape((tall, hidden), BF),
                 shape((1, hidden)),
-                shape((rows, model), BF),
-                shape((rows, model)),
+                *[shape((rows, model), kind) for kind in kinds],
             ],
-            scratch=[pltpu.VMEM((side, model), F32), pltpu.VMEM((side, block), F32)],
-            flops=4 * side * model * hidden,
+            scratch=[pltpu.VMEM((tall, model), F32), pltpu.VMEM((2, rows, block), F32)],
+            flops=4 * tall * model * hidden,
         )
 
-    def feed_back(me, act):
+    def feed_back(me, *acts):
         return run(
-            feed_out,
-            (me, act, down_weight),
+            functools.partial(feed_out, len(acts)),
+            (me, *acts, down_weight),
             [shape((rows, model), BF), shape((rows, model))],
             flops=2 * side * model * hidden,
         )
@@ -738,21 +775,20 @@
     keep_own = lax.dynamic_slice_in_dim(keep_flat, me[0] * rows, rows)[:, None]
     cot = (grad_out.astype(F32) * keep_own).astype(BF)
     cot_core = swap(cot, "tensor", 1)
-    in_grouped = in_weight.reshape(model, heads, 3, HD).transpose(0, 2, 1, 3)
-    in_grouped = in_grouped.reshape(model, 3 * width)
-    pair = in_bias.reshape(heads, 2, HD).transpose(1, 0, 2).reshape(2, width)
-    bias_full = jnp.concatenate([pair[:1], jnp.zeros((1, width), F32), pair[1:]], axis=1)
+    pair = in_bias.reshape(heads, 2, HD)
+    bias_full = jnp.concatenate([pair[:, :1], jnp.zeros((heads, 1, HD), F32), pair[:, 1:]], axis=1)
+    bias_full = bias_full.reshape(1, 3 * width)
     vectors = jnp.stack(
         [gain_one, shift_one, out_bias, gain_two, shift_two, up_bias, down_bias, down_bias]
     )
-    stay(in_grouped, bias_full, vectors, out_weight, down_weight, up_weight, tokens, cot)
+    stay(in_weight, bias_full, vectors, tokens, cot)
     norm_near, proj_near = run(
         project_local,
-        (me, tokens, tok_core, vectors, in_grouped, bias_full),
+        (me, tokens, tok_core, vectors, in_weight, bias_full),
         [shape((side, model), BF), shape((side, 3 * width), BF)],
         flops=project_flops,
     )
-    stay(norm_near)
+    stay(norm_near, out_weight)
     tok_far = after(tok_far, proj_near)
 
     tok_both = swap(tok_far, "tensor", 1)
@@ -763,15 +799,22 @@
         shape((rows, model), BF),
         shape((rows, model), F32),
     ]
-    norm_far, qkv, probs_far, heads_far, send, far_hold = run(
+    norm_y, proj_y = run(
+        project_one,
+        (me, tok_far, vectors, in_weight, bias_full),
+        [shape((rows, model), BF), shape((rows, 3 * width), BF)],
+        flops=project_flops // 2,
+    )
+    stay(norm_y)
+    norm_both, qkv, probs_far, heads_far, send, far_hold = run(
         attend_far,
         (
-            me, proj_near, tok_far, tok_both, vectors, in_grouped, bias_full, keep_mask, out_weight,
+            me, proj_near, proj_y, tok_both, vectors, in_weight, bias_full, keep_mask, out_weight,
         ),
-        [shape((side, model), BF), shape((2 * side, 3 * width), BF), *attend_outs],
+        [shape((rows, model), BF), shape((2 * side, 3 * width), BF), *attend_outs],
         flops=project_flops + attend_flops,
     )
-    stay(norm_far, qkv, probs_far, heads_far)
+    stay(norm_both, qkv, probs_far, heads_far, down_weight, up_weight)
     leave(bias_full)
     arrived = after(swap(send, "tensor", 1), cot_far)
     far_sum = add_round(far_hold, arrived)
@@ -801,8 +844,8 @@
 
     second_far = swap(second, "tensor", 2)
     second_core = swap(second, "tensor", 1)
-    act_near, pre_near, up_bias_near, near_send, near_hold = feed(
-        second, second_core, act_grad_near
+    act_near, pre_near, up_bias_near, near_hold, near_send = feed(
+        (second, second_core), act_grad_near, 0, (F32, BF)
     )
     leave(act_grad_near)
     stay(act_near, pre_near, near_hold, second_core)
@@ -810,22 +853,23 @@
     stay(cot_far, cot_both, act_grad_far)
     second_far = after(second_far, act_grad_far)
     second_both = swap(second_far, "tensor", 1)
-    act_far, pre_far, up_bias_far, far_send, far_hold = feed(
-        second_far, second_both, act_grad_far
-    )
+    act_y, pre_y, up_bias_y, far_hold = feed((second_far,), act_grad_far, 0, (F32,))
+    stay(act_y, pre_y, second_far, far_hold)
+    act_both, pre_both, up_bias_both, far_send = feed((second_both,), act_grad_far, rows, (BF,))
+    leave(far_hold)
     far_sum = add_round(far_hold, swap(far_send, "tensor", 1))
     arrived_far = swap(far_sum, "tensor", 2)
     leave(act_grad_far, up_weight)
-    stay(act_far, pre_far, second_far, second_both)
-    acts, cots = (act_near, act_far), (cot, cot_core, cot_far, cot_both)
+    stay(act_both, pre_both, second_both)
+    acts, cots = (act_near, act_y, act_both), (cot, cot_core, cot_far, cot_both)
     down_send = weight_grad(after(me, far_sum), acts, cots, ORDER_A, False)
     down = Reduction(down_send, ORDER_A)
     seconds = (second, second_core, second_far, second_both)
-    pres = (pre_near, pre_far)
+    pres = (pre_near, pre_y, pre_both)
     up_send = weight_grad(after(me, down_send), seconds, pres, ORDER_B, False)
     up = Reduction(up_send, ORDER_B)
     arrived_near = swap(near_send, "tensor", 1)
-    feed_send, feed_hold = feed_back(after(me, up_send), act_far)
+    feed_send, feed_hold = feed_back(after(me, up_send), act_y, act_both)
     feed_far = add_round(feed_hold, swap(feed_send, "tensor", 1))
     middle_grad, middle_low, middle_sums = run(
         middle_back,
@@ -842,7 +886,7 @@
     leave(near_hold)
     stay(middle_grad, middle_low)
     down.values = weight_grad(after(me, middle_low), acts, cots, ORDER_A, True)
-    leave(act_far, cot_core, cot_far, cot_both)
+    leave(act_y, act_both, cot_core, cot_far, cot_both)
     stay(down.values)
     near_q, near_keys = run(
         back_near,
@@ -854,22 +898,20 @@
     leave(probs_near)
     stay(near_q, near_keys, mid_core)
     up.values = weight_grad(after(me, near_q), seconds, pres, ORDER_B, True)
-    leave(second, second_core, second_far, second_both, pre_near, pre_far)
+    leave(second, second_core, second_far, second_both, pre_near, pre_y, pre_both)
     stay(up.values)
     mid_far = after(mid_far, up.values)
     mid_both = swap(mid_far, "tensor", 1)
     feed_far = swap(after(feed_far, mid_far), "tensor", 2)
     down.arrive(mid_far)
     up.arrive(mid_far)
-    proj_near, proj_far, flat_near, flat_far, bias_grad, far_send, far_hold = run(
+    flat_near, flat_far, bias_grad, far_send, far_hold = run(
         back_far,
         (
             after(me, down.send, up.send), mid_far, mid_both, qkv, probs_far,
-            out_weight, near_q, near_keys, in_grouped,
+            out_weight, near_q, near_keys, in_weight,
         ),
         [
-            shape((side, 3 * width), BF),
-            shape((side, 3 * width), BF),
             shape((side, 3 * width), BF),
             shape((side, 3 * width), BF),
             shape((1, 2 * width)),
@@ -880,11 +922,12 @@
             grads,
             pltpu.VMEM((side, width), F32),
             pltpu.VMEM((2 * side, 2 * width), F32),
+            pltpu.VMEM((side, 3 * width), BF),
         ],
         flops=back_flops + project_flops,
     )
     leave(qkv, probs_far, near_q, near_keys, out_weight)
-    stay(proj_near, flat_near, flat_far, mid_far, mid_both)
+    stay(flat_near, flat_far, mid_far, mid_both)
     down.take(bias_grad)
     up.take(bias_grad)
     arrived = after(swap(far_send, "tensor", 1), feed_far, down.came, up.came)
@@ -895,13 +938,13 @@
     up.arrive(far_sum)
     near_send, hold = run(
         first_back,
-        (after(me, down.send, up.send), proj_near, in_grouped),
+        (after(me, down.send, up.send), flat_near, in_weight),
         [shape((rows, model), BF), shape((rows, model))],
         flops=project_flops,
     )
-    leave(in_grouped, proj_near)
+    leave(in_weight)
     stay(hold)
-    normed = (norm_near, norm_far)
+    normed = (norm_near, norm_y, norm_both)
     split = (3 * width + width) // 2
     flat = (flat_near, flat_far)
     head_rows = (heads_near, heads_far)
@@ -918,7 +961,7 @@
     mixed.values = mixed_grad(
         after(me, first.values), normed, flat, head_rows, mids, ORDER_B, True, split
     )
-    leave(norm_near, norm_far, flat_near, flat_far, heads_near, heads_far)
+    leave(norm_near, norm_y, norm_both, flat_near, flat_far, heads_near, heads_far)
     leave(middle_low, mid_core, mid_far, mid_both)
     stay(mixed.values)
     tokens_grad, token_sums = run(
@@ -942,7 +985,7 @@
     shared = add_small(shared, swap(shared, "tensor", 1))
     shared = unpack(add_small(shared, swap(shared, "tensor", 2)))
     own = jnp.concatenate(
-        [up_bias_near + up_bias_far, jnp.pad(bias_grad, ((0, 0), (0, hidden - 2 * width)))], axis=0
+        [up_bias_near + up_bias_y + up_bias_both, jnp.pad(bias_grad, ((0, 0), (0, hidden - 2 * width)))], axis=0
     )
     small = jnp.concatenate([shared, own], axis=0)
     small = pack(jnp.concatenate([small[:, :split], small[:, split:]], axis=0))

time: 250 us -> 241 us (0.964)
  starting transfers between devices: 35.3 us -> 45.8 us
  waiting for transfers between devices: 105 us -> 94.9 us
  local copies, waits for them, and re-layouts: 11.8 us -> 6.21 us
  Pallas kernels: 92 us -> 88 us
    ppermute x50, starting transfers between devices: 35.3 us -> 45.8 us  [swap(): return lax.ppermute(values, axis, [(i, i ^ bit) for i in range(count)])]
    ppermute x50, waiting for transfers between devices: 105 us -> 94.9 us  [swap(): return lax.ppermute(values, axis, [(i, i ^ bit) for i in range(count)])]
    pallas_call x39 -> x41, Pallas kernels: 83.9 us -> 80 us  [run(): pl.pallas_call(kernel, out_shape=[pltpu.VMEM(x.shape, x.dtype) for x in o...]
    reshape x2, local copies, waits for them, and re-layouts: 3.49 us -> 0.85 us  [the longest x1 0.76 us: on_device(): pair = in_bias.reshape(heads, 2, HD)]
    unnamed x41 -> x26, local copies, waits for them, and re-layouts: 5.79 us -> 3.49 us
  transfers between devices with their start and end apart: 50 -> 50, of which waited for: 29 -> 25; matrix products, arithmetic and copies ran while one was open for 5% -> 3% of each run, Pallas kernels for 31% -> 32%
where the time goes in v4:
time: 241 us
  waiting for transfers between devices  94.9 us (39%)
  Pallas kernels  88 us (37%)
  starting transfers between devices  45.8 us (19%)
  local copies, waits for them, and re-layouts  6.21 us (3%)
  other arithmetic  4.25 us (2%)
    ppermute x50, waiting for transfers between devices, swap(): return lax.ppermute(values, axis, [(i, i ^ bit) for i in range(count)])  94.9 us
    pallas_call x41, Pallas kernels, run(): pl.pallas_call(kernel, out_shape=[pltpu.VMEM(x.shape, x.dtype) for x in o...  80 us
    ppermute x50, starting transfers between devices, swap(): return lax.ppermute(values, axis, [(i, i ^ bit) for i in range(count)])  45.8 us
    pallas_call x3, Pallas kernels, run_out(): pl.pallas_call(body, out_shape=[pltpu.HBM(x.shape, x.dtype) for x in outs...  8.04 us
  transfers between devices with their start and end apart: 50, of which 25 were waited for; matrix products, arithmetic and copies ran while one was open for 3% of the time, Pallas kernels for 32%

profile of v4, /device:TPU:0, one launch (start us, length us, event | category | flops | bytes accessed | tf_op | source)
XLA Modules:
  0.0 240.5 jit_solution(678388425928686974)
XLA Ops:
  0.6 3.0 %collective-permute-start.2 = (bf16[240,1024]{1,0:T(8,128)(2,1)}, bf16[240,1024]{1,0:T(8,128)(2,1)S(1)}, u32[]{:S(2)}, u32[]{:S(2)}) collective-permute-start(bf16[240,1024]{1,0:T(8,128)(2,1)} %refs_4_.13), channel_id=1, source_target_pairs={{0,2},{1,3},{2,0},{3,1},{4,6},{5,7},{6,4},{7,5},{8,10},{9,11},{10,... | collective-permute-start | bytes 1474568 | tf_op jit(solution)/shard_map/ppermute | solution.py:30
  10.1 4.1 %shard_map.254 = (bf16[480,1024]{1,0:T(8,128)(2,1)S(1)}, bf16[480,768]{1,0:T(8,128)(2,1)S(1)}) custom-call(s32[2]{0:T(128)S(1)} %pad_add_fusion.refs_0_.me, bf16[240,1024]{1,0:T(8,128)(2,1)S(1)} %copy-done.3, bf16[240,1024]{1,0:T(8,128)(2,1)S(1)} %collective-permute-done.1.refs_2_, ...), custom_call_target="tpu_custom_call" | custom-call | flops 15099494400 | tf_op jit(solution)/shard_map/pallas_call | solution.py:63
  19.1 7.4 %shard_map.256 = (bf16[240,1024]{1,0:T(8,128)(2,1)S(1)}, bf16[960,768]{1,0:T(8,128)(2,1)S(1)}, bf16[12,160,320]{2,1,0:T(8,128)(2,1)S(1)}, bf16[480,256]{1,0:T(8,...) custom-call(s32[2]{0:T(128)S(1)} %pad_add_fusion.refs_0_.me, ...), custom_call_target="tpu_custom_call" | custom-call | flops 26424115200 | tf_op jit(solution)/shard_map/pallas_call | solution.py:63
  30.7 5.6 %shard_map.258 = (bf16[12,160,320]{2,1,0:T(8,128)(2,1)S(1)}, bf16[480,256]{1,0:T(8,128)(2,1)S(1)}, bf16[240,1024]{1,0:T(8,128)(2,1)S(1)}, f32[240,1024]{1,0:T(8,128)S(1)}) custom-call(s32[2]{0:T(128)S(1)} %pad_add_fusion.refs_0_.me, bf16[960,768]{1,0:T(8,128)(2,1)S(1)} %get-tuple-element.137.refs_11_.refs_1_.refs_12_.refs_13_.refs_15_.refs_16_.refs_3_, ...), custom_call_target="tpu_custom_call" | custom-call | flops 11324620800 | tf_op jit(solution)/shard_map/pallas_call | solution.py:63
  38.9 3.1 %collective-permute-done.7.refs_4_ = bf16[240,1024]{1,0:T(8,128)(2,1)S(1)} collective-permute-done((bf16[240,1024]{1,0:T(8,128)(2,1)S(1)}, bf16[240,1024]{1,0:T(8,128)(2,1)S(1)}, u32[]{:S(2)}, u32[]{:S(2)}) %collective-permute-start.7) | collective-permute-done | bytes 491552 | tf_op jit(solution)/shard_map/ppermute | solution.py:30
  45.8 4.6 %shard_map.261 = (bf16[480,1024]{1,0:T(8,128)(2,1)S(1)}, bf16[480,1024]{1,0:T(8,128)(2,1)S(1)}, f32[1,1024]{1,0:T(1,128)S(1)}, f32[240,1024]{1,0:T(8,128)S(1)}, bf16[240,1024]{1,0:T(8,128)(2,1)S(1)}) custom-call(s32[2]{0:T(128)S(1)} %pad_add_fusion.refs_0_.me, bf16[240,1024]{1,0:T(8,128)(2,1)S(1)} %get-tuple-element.152.refs_1_.refs_20_.refs_22_.refs_19_.refs_18_, ...), custom_call_target="tpu_custom_call" | custom-call | flops 40265318400 | tf_op jit(solution)/shard_map/pallas_call | solution.py:63
  53.0 4.5 %collective-permute-done.8.refs_1_.refs_29_.refs_30_.refs_27_.refs_3_.refs_28_.refs_26_.refs_23_ = bf16[240,1024]{1,0:T(8,128)(2,1)S(1)} collective-permute-done((bf16[240,1024]{1,0:T(8,128)(2,1)S(1)}, bf16[240,1024]{1,0:T(8,128)(2,1)S(1)}, u32[]{:S(2)}, u32[]{:S(2)}) %collective-permute-start.8) | collective-permute-done | bytes 491552 | tf_op jit(solution)/shard_map/ppermute | solution.py:30
  57.5 2.8 %shard_map.263 = (bf16[240,1024]{1,0:T(8,128)(2,1)S(1)}, bf16[240,1024]{1,0:T(8,128)(2,1)S(1)}, f32[1,1024]{1,0:T(1,128)S(1)}, f32[240,1024]{1,0:T(8,128)S(1)}) custom-call(s32[2]{0:T(128)S(1)} %pad_add_fusion.refs_0_.me, bf16[240,1024]{1,0:T(8,128)(2,1)S(1)} %collective-permute-done.8.refs_1_.refs_29_.refs_30_.refs_27_.refs_3_.refs_28_.refs_26_.refs_23_, ...), custom_call_target="tpu_custom_call" | custom-call | flops 20132659200 | tf_op jit(solution)/shard_map/pallas_call | solution.py:63
  60.2 2.8 %shard_map.264 = (bf16[240,1024]{1,0:T(8,128)(2,1)S(1)}, bf16[240,1024]{1,0:T(8,128)(2,1)S(1)}, f32[1,1024]{1,0:T(1,128)S(1)}, bf16[240,1024]{1,0:T(8,128)(2,1)S(1)}) custom-call(s32[2]{0:T(128)S(1)} %pad_add_fusion.refs_0_.me, bf16[240,1024]{1,0:T(8,128)(2,1)S(1)} %collective-permute-done.11.refs_1_.refs_29_.refs_4_.refs_31_.refs_28_.refs_25_, ...), custom_call_target="tpu_custom_call" | custom-call | flops 20132659200 | tf_op jit(solution)/shard_map/pallas_call | solution.py:63
  66.8 2.8 %shard_map.266 = bf16[512,1024]{1,0:T(8,128)(2,1)S(1)} custom-call(s32[2]{0:T(128)S(1)} %pad_add_fusion.refs_0_.me, bf16[480,1024]{1,0:T(8,128)(2,1)S(1)} %get-tuple-element.154.refs_21_.refs_1_.refs_24_.refs_20_.refs_19_.refs_22_.refs_17_.refs_14_.refs_13_.refs_10_, bf16[240,1024]{1,0:T(8,128)(2,1)S(1)} %get-tuple-element.159.refs_27_.refs_28_.refs_2_.refs_1_.refs_26_, ...), custom_call_target="tpu_custom_call" | custom-call | flops 20132659200 | tf_op jit(solution)/shard_map/pallas_call | solution.py:63
  69.6 2.9 %shard_map.267 = bf16[512,1024]{1,0:T(8,128)(2,1)S(1)} custom-call(s32[2]{0:T(128)S(1)} %pad_add_fusion.refs_0_.me, bf16[240,1024]{1,0:T(8,128)(2,1)S(1)} %get-tuple-element.152.refs_1_.refs_20_.refs_22_.refs_19_.refs_18_, bf16[240,1024]{1,0:T(8,128)(2,1)S(1)} %collective-permute-done.10.refs_2_.refs_24_.refs_25_.refs_23_.refs_21_, ...), custom_call_target="tpu_custom_call" | custom-call | flops 20132659200 | tf_op jit(solution)/shard_map/pallas_call | solution.py:63
  82.6 2.8 %shard_map.270.refs_27_.refs_25_.refs_1_ = f32[512,1024]{1,0:T(8,128)S(1)} custom-call(s32[2]{0:T(128)S(1)} %pad_add_fusion.refs_0_.me, bf16[480,1024]{1,0:T(8,128)(2,1)S(1)} %get-tuple-element.154.refs_21_.refs_1_.refs_24_.refs_20_.refs_19_.refs_22_.refs_17_.refs_14_.refs_13_.refs_10_, ...), custom_call_target="tpu_custom_call" | custom-call | flops 20132659200 | tf_op jit(solution)/shard_map/pallas_call | solution.py:63
  85.4 6.6 %shard_map.271 = (f32[480,256]{1,0:T(8,128)S(1)}, f32[960,512]{1,0:T(8,128)S(1)}) custom-call(s32[2]{0:T(128)S(1)} %pad_add_fusion.refs_0_.me, bf16[240,1024]{1,0:T(8,128)(2,1)S(1)} %get-tuple-element.170.refs_30_.refs_1_.refs_24_.refs_19_.refs_21_.refs_16_.refs_15_.refs_8_, ...), custom_call_target="tpu_custom_call" | custom-call | flops 20761804800 | tf_op jit(solution)/shard_map/pallas_call | solution.py:63
  92.1 2.7 %shard_map.272.refs_23_.refs_1_ = f32[512,1024]{1,0:T(8,128)S(1)} custom-call(s32[2]{0:T(128)S(1)} %pad_add_fusion.refs_0_.me, bf16[240,1024]{1,0:T(8,128)(2,1)S(1)} %get-tuple-element.152.refs_1_.refs_20_.refs_22_.refs_19_.refs_18_, bf16[240,1024]{1,0:T(8,128)(2,1)S(1)} %collective-permute-done.10.refs_2_.refs_24_.refs_25_.refs_23_.refs_21_, ...), custom_call_target="tpu_custom_call" | custom-call | flops 20132659200 | tf_op jit(solution)/shard_map/pallas_call | solution.py:63
  101.5 8.1 %shard_map.275 = (bf16[480,768]{1,0:T(8,128)(2,1)S(1)}, bf16[480,768]{1,0:T(8,128)(2,1)S(1)}, f32[1,512]{1,0:T(1,128)S(1)}, bf16[240,1024]{1,0:T(8,128)(2,1)S(1)}, f32[240,1024]{1,0:T(8,128)S(1)}) custom-call(s32[2]{0:T(128)S(1)} %pad_add_fusion.refs_0_.me, ...), custom_call_target="tpu_custom_call" | custom-call | flops 35861299200 | tf_op jit(solution)/shard_map/pallas_call | solution.py:63
  113.8 2.7 %collective-permute-start.34 = (bf16[128,1024]{1,0:T(8,128)(2,1)S(1)}, bf16[128,1024]{1,0:T(8,128)(2,1)S(1)}, u32[]{:S(2)}, u32[]{:S(2)}) collective-permute-start(bf16[128,1024]{1,0:T(8,128)(2,1)S(1)} %get-tuple-element.199), channel_id=1, source_target_pairs={{0,16},{4,20},{8,24},{12,28},{16,0},{20,4},{24,8},{28,12},{1,17},{... | collective-permute-start | bytes 786440 | tf_op jit(solution)/shard_map/ppermute | solution.py:30
  132.1 6.0 %collective-permute-done.29.refs_2_ = bf16[128,1024]{1,0:T(8,128)(2,1)S(1)} collective-permute-done((bf16[128,1024]{1,0:T(8,128)(2,1)S(1)}, bf16[128,1024]{1,0:T(8,128)(2,1)S(1)}, u32[]{:S(2)}, u32[]{:S(2)}) %collective-permute-start.29) | collective-permute-done | bytes 262176 | tf_op jit(solution)/shard_map/ppermute | solution.py:30
  143.1 5.3 %collective-permute-done.31.refs_2_ = bf16[512,512]{1,0:T(8,128)(2,1)S(1)} collective-permute-done((bf16[512,512]{1,0:T(8,128)(2,1)S(1)}, bf16[512,512]{1,0:T(8,128)(2,1)S(1)}, u32[]{:S(2)}, u32[]{:S(2)}) %collective-permute-start.31) | collective-permute-done | bytes 524320 | tf_op jit(solution)/shard_map/ppermute | solution.py:30
  149.2 5.9 %collective-permute-start.38 = (bf16[128,1024]{1,0:T(8,128)(2,1)S(1)}, bf16[128,1024]{1,0:T(8,128)(2,1)S(1)}, u32[]{:S(2)}, u32[]{:S(2)}) collective-permute-start(bf16[128,1024]{1,0:T(8,128)(2,1)S(1)} %shard_map.290), channel_id=1, source_target_pairs={{0,16},{4,20},{8,24},{12,28},{16,0},{20,4},{24,8},{28,12},{1,17},{... | collective-permute-start | bytes 786440 | tf_op jit(solution)/shard_map/ppermute | solution.py:30
  156.9 5.0 %collective-permute-start.37 = (bf16[256,1024]{1,0:T(8,128)(2,1)S(1)}, bf16[256,1024]{1,0:T(8,128)(2,1)S(1)}, u32[]{:S(2)}, u32[]{:S(2)}) collective-permute-start(bf16[256,1024]{1,0:T(8,128)(2,1)S(1)} %pad_maximum_fusion.2), channel_id=1, source_target_pairs={{0,8},{4,12},{8,0},{12,4},{16,24},{20,28},{24,16},{28,20},{1,9},{5... | collective-permute-start | bytes 1572872 | tf_op jit(solution)/shard_map/ppermute | solution.py:30
  162.1 2.8 %collective-permute-done.30.refs_2_ = bf16[256,512]{1,0:T(8,128)(2,1)S(1)} collective-permute-done((bf16[256,512]{1,0:T(8,128)(2,1)S(1)}, bf16[256,512]{1,0:T(8,128)(2,1)S(1)}, u32[]{:S(2)}, u32[]{:S(2)}) %collective-permute-start.30) | collective-permute-done | bytes 262176 | tf_op jit(solution)/shard_map/ppermute | solution.py:30
  165.1 3.0 %collective-permute-done.38 = bf16[128,1024]{1,0:T(8,128)(2,1)S(1)} collective-permute-done((bf16[128,1024]{1,0:T(8,128)(2,1)S(1)}, bf16[128,1024]{1,0:T(8,128)(2,1)S(1)}, u32[]{:S(2)}, u32[]{:S(2)}) %collective-permute-start.38) | collective-permute-done | bytes 262176 | tf_op jit(solution)/shard_map/ppermute | solution.py:30
  169.1 8.4 %collective-permute-done.37 = bf16[256,1024]{1,0:T(8,128)(2,1)S(1)} collective-permute-done((bf16[256,1024]{1,0:T(8,128)(2,1)S(1)}, bf16[256,1024]{1,0:T(8,128)(2,1)S(1)}, u32[]{:S(2)}, u32[]{:S(2)}) %collective-permute-start.37) | collective-permute-done | bytes 524320 | tf_op jit(solution)/shard_map/ppermute | solution.py:30
  177.6 2.7 %collective-permute-start.42 = (bf16[128,512]{1,0:T(8,128)(2,1)S(1)}, bf16[128,512]{1,0:T(8,128)(2,1)S(1)}, u32[]{:S(2)}, u32[]{:S(2)}) collective-permute-start(bf16[128,512]{1,0:T(8,128)(2,1)S(1)} %shard_map.293), channel_id=1, source_target_pairs={{0,16},{4,20},{8,24},{12,28},{16,0},{20,4},{24,8},{28,12},{1,17},{... | collective-permute-start | bytes 393224 | tf_op jit(solution)/shard_map/ppermute | solution.py:30
  180.7 9.5 %collective-permute-done.42 = bf16[128,512]{1,0:T(8,128)(2,1)S(1)} collective-permute-done((bf16[128,512]{1,0:T(8,128)(2,1)S(1)}, bf16[128,512]{1,0:T(8,128)(2,1)S(1)}, u32[]{:S(2)}, u32[]{:S(2)}) %collective-permute-start.42) | collective-permute-done | bytes 131104 | tf_op jit(solution)/shard_map/ppermute | solution.py:30
  194.6 2.9 %collective-permute-done.44 = bf16[256,512]{1,0:T(8,128)(2,1)S(1)} collective-permute-done((bf16[256,512]{1,0:T(8,128)(2,1)S(1)}, bf16[256,512]{1,0:T(8,128)(2,1)S(1)}, u32[]{:S(2)}, u32[]{:S(2)}) %collective-permute-start.44) | collective-permute-done | bytes 262176 | tf_op jit(solution)/shard_map/ppermute | solution.py:30
  197.5 4.8 %collective-permute-done.43 = bf16[288,512]{1,0:T(8,128)(2,1)S(1)} collective-permute-done((bf16[288,512]{1,0:T(8,128)(2,1)S(1)}, bf16[288,512]{1,0:T(8,128)(2,1)S(1)}, u32[]{:S(2)}, u32[]{:S(2)}) %collective-permute-start.43) | collective-permute-done | bytes 294944 | tf_op jit(solution)/shard_map/ppermute | solution.py:30
  204.7 15.2 %collective-permute-done.49.refs_1_ = bf16[512,1024]{1,0:T(8,128)(2,1)S(1)} collective-permute-done((bf16[512,1024]{1,0:T(8,128)(2,1)S(1)}, bf16[512,1024]{1,0:T(8,128)(2,1)S(1)}, u32[]{:S(2)}, u32[]{:S(2)}) %collective-permute-start.49) | collective-permute-done | bytes 1048608 | tf_op jit(solution)/shard_map/ppermute | solution.py:30
  220.0 2.6 %shard_map.297 = f32[1024,1024]{1,0:T(8,128)} custom-call(s32[2]{0:T(128)S(1)} %pad_add_fusion.refs_0_.me, bf16[512,1024]{1,0:T(8,128)(2,1)S(1)} %pad_maximum_fusion.refs_0_, bf16[512,1024]{1,0:T(8,128)(2,1)S(1)} %collective-permute-done.49.refs_1_), custom_call_target="tpu_custom_call" | custom-call | tf_op jit(solution)/shard_map/pallas_call | solution.py:96
  224.8 8.9 %collective-permute-done.47.refs_3_ = bf16[512,512]{1,0:T(8,128)(2,1)S(1)} collective-permute-done((bf16[512,512]{1,0:T(8,128)(2,1)S(1)}, bf16[512,512]{1,0:T(8,128)(2,1)S(1)}, u32[]{:S(2)}, u32[]{:S(2)}) %collective-permute-start.47) | collective-permute-done | bytes 524320 | tf_op jit(solution)/shard_map/ppermute | solution.py:30
  233.7 2.6 %shard_map.296 = f32[1024,1024]{1,0:T(8,128)} custom-call(s32[2]{0:T(128)S(1)} %pad_add_fusion.refs_0_.me, bf16[512,1024]{1,0:T(8,128)(2,1)S(1)} %pad_maximum_fusion.1.refs_0_, bf16[512,1024]{1,0:T(8,128)(2,1)S(1)} %collective-permute-done.48.refs_1_), custom_call_target="tpu_custom_call" | custom-call | tf_op jit(solution)/shard_map/pallas_call | solution.py:96
  237.1 2.8 %shard_map.295 = (f32[1024,768]{1,0:T(8,128)}, f32[256,1024]{1,0:T(8,128)}) custom-call(s32[2]{0:T(128)S(1)} %pad_add_fusion.refs_0_.me, bf16[512,512]{1,0:T(8,128)(2,1)S(1)} %pad_maximum_fusion.5.refs_0_, bf16[544,512]{1,0:T(8,128)(2,1)S(1)} %collective-permute-done.46.refs_1_, bf16[512,512]{1,0:T(8,128)(2,1)S(1)} %pad_maximum_fusion.4.refs_2_, ...), custom_call_target="tpu_custom_call" | custom-call | tf_op jit(solution)/shard_map/pallas_call | solution.py:96
  (179 shorter events, 84.4 us)
Async XLA Ops:
  0.6 14.5 %collective-permute-start.2 = (bf16[240,1024]{1,0:T(8,128)(2,1)}, bf16[240,1024]{1,0:T(8,128)(2,1)S(1)}, u32[]{:S(2)}, u32[]{:S(2)}) collective-permute-start(bf16[240,1024]{1,0:T(8,128)(2,1)} %refs_4_.13), channel_id=1, source_target_pairs={{0,2},{1,3},{2,0},{3,1},{4,6},{5,7},{6,4},{7,5},{8,10},{9,11},{10,... | collective-permute-start | bytes 1474568 | tf_op jit(solution)/shard_map/ppermute | solution.py:30
  15.1 13.6 %collective-permute-start.5 = (bf16[240,1024]{1,0:T(8,128)(2,1)S(1)}, bf16[240,1024]{1,0:T(8,128)(2,1)S(1)}, u32[]{:S(2)}, u32[]{:S(2)}) collective-permute-start(bf16[240,1024]{1,0:T(8,128)(2,1)S(1)} %multiply_convert_fusion.1.refs_6_.refs_10_.refs_7_.refs_1_.refs_8_.refs_4_.refs_11_.refs_5_.refs_9_.refs_14_, ...), channel_id=1, source_target_pairs={{0,2},{1,3},{2,0},{3,1},{4,6},{5,7},{6,4},{7,5},{8,10},{9,11},{10,... | collective-permute-start | bytes 1474568 | tf_op jit(solution)/shard_map/ppermute | solution.py:30
  28.9 13.1 %collective-permute-start.7 = (bf16[240,1024]{1,0:T(8,128)(2,1)S(1)}, bf16[240,1024]{1,0:T(8,128)(2,1)S(1)}, u32[]{:S(2)}, u32[]{:S(2)}) collective-permute-start(bf16[240,1024]{1,0:T(8,128)(2,1)S(1)} %shard_map.257), channel_id=1, source_target_pairs={{0,2},{1,3},{2,0},{3,1},{4,6},{5,7},{6,4},{7,5},{8,10},{9,11},{10,... | collective-permute-start | bytes 1474568 | tf_op jit(solution)/shard_map/ppermute | solution.py:30
  44.3 13.2 %collective-permute-start.8 = (bf16[240,1024]{1,0:T(8,128)(2,1)S(1)}, bf16[240,1024]{1,0:T(8,128)(2,1)S(1)}, u32[]{:S(2)}, u32[]{:S(2)}) collective-permute-start(bf16[240,1024]{1,0:T(8,128)(2,1)S(1)} %get-tuple-element.152.refs_1_.refs_20_.refs_22_.refs_19_.refs_18_), channel_id=1, source_target_pairs={{0,2},{1,3},{2,0},{3,1},{4,6},{5,7},{6,4},{7,5},{8,10},{9,11},{10,... | collective-permute-start | bytes 1474568 | tf_op jit(solution)/shard_map/ppermute | solution.py:30
  63.6 13.9 %collective-permute-start.13 = (bf16[240,1024]{1,0:T(8,128)(2,1)S(1)}, bf16[240,1024]{1,0:T(8,128)(2,1)S(1)}, u32[]{:S(2)}, u32[]{:S(2)}) collective-permute-start(bf16[240,1024]{1,0:T(8,128)(2,1)S(1)} %get-tuple-element.169), channel_id=1, source_target_pairs={{0,1},{1,0},{2,3},{3,2},{4,5},{5,4},{6,7},{7,6},{8,9},{9,8},{10,11... | collective-permute-start | bytes 1474568 | tf_op jit(solution)/shard_map/ppermute | solution.py:30
  65.2 13.6 %collective-permute-start.14 = (bf16[240,1024]{1,0:T(8,128)(2,1)S(1)}, bf16[240,1024]{1,0:T(8,128)(2,1)S(1)}, u32[]{:S(2)}, u32[]{:S(2)}) collective-permute-start(bf16[240,1024]{1,0:T(8,128)(2,1)S(1)} %shard_map.265), channel_id=1, source_target_pairs={{0,2},{1,3},{2,0},{3,1},{4,6},{5,7},{6,4},{7,5},{8,10},{9,11},{10,... | collective-permute-start | bytes 1474568 | tf_op jit(solution)/shard_map/ppermute | solution.py:30
  72.5 25.2 %collective-permute-start.19 = (bf16[512,1024]{1,0:T(8,128)(2,1)S(1)}, bf16[512,1024]{1,0:T(8,128)(2,1)S(1)}, u32[]{:S(2)}, u32[]{:S(2)}) collective-permute-start(bf16[512,1024]{1,0:T(8,128)(2,1)S(1)} %shard_map.267), channel_id=1, source_target_pairs={{0,8},{4,12},{8,0},{12,4},{16,24},{20,28},{24,16},{28,20},{1,9},{5... | collective-permute-start | bytes 3145736 | tf_op jit(solution)/shard_map/ppermute | solution.py:30
  74.2 24.9 %collective-permute-start.15 = (bf16[512,1024]{1,0:T(8,128)(2,1)S(1)}, bf16[512,1024]{1,0:T(8,128)(2,1)S(1)}, u32[]{:S(2)}, u32[]{:S(2)}) collective-permute-start(bf16[512,1024]{1,0:T(8,128)(2,1)S(1)} %shard_map.266), channel_id=1, source_target_pairs={{0,4},{4,0},{8,12},{12,8},{16,20},{20,16},{24,28},{28,24},{1,5},{5... | collective-permute-start | bytes 3145736 | tf_op jit(solution)/shard_map/ppermute | solution.py:30
  77.4 17.6 %collective-permute-start.22 = (bf16[240,1024]{1,0:T(8,128)(2,1)S(1)}, bf16[240,1024]{1,0:T(8,128)(2,1)S(1)}, u32[]{:S(2)}, u32[]{:S(2)}) collective-permute-start(bf16[240,1024]{1,0:T(8,128)(2,1)S(1)} %get-tuple-element.189), channel_id=1, source_target_pairs={{0,1},{1,0},{2,3},{3,2},{4,5},{5,4},{6,7},{7,6},{8,9},{9,8},{10,11... | collective-permute-start | bytes 1474568 | tf_op jit(solution)/shard_map/ppermute | solution.py:30
  81.0 13.8 %collective-permute-start.16 = (bf16[240,1024]{1,0:T(8,128)(2,1)S(1)}, bf16[240,1024]{1,0:T(8,128)(2,1)S(1)}, u32[]{:S(2)}, u32[]{:S(2)}) collective-permute-start(bf16[240,1024]{1,0:T(8,128)(2,1)S(1)} %get-tuple-element.170.refs_30_.refs_1_.refs_24_.refs_19_.refs_21_.refs_16_.refs_15_.refs_8_), channel_id=1, source_target_pairs={{0,2},{1,3},{2,0},{3,1},{4,6},{5,7},{6,4},{7,5},{8,10},{9,11},{10,... | collective-permute-start | bytes 1474568 | tf_op jit(solution)/shard_map/ppermute | solution.py:30
  95.1 18.3 %collective-permute-start.23 = (bf16[240,1024]{1,0:T(8,128)(2,1)S(1)}, bf16[240,1024]{1,0:T(8,128)(2,1)S(1)}, u32[]{:S(2)}, u32[]{:S(2)}) collective-permute-start(bf16[240,1024]{1,0:T(8,128)(2,1)S(1)} %shard_map.276), channel_id=1, source_target_pairs={{0,2},{1,3},{2,0},{3,1},{4,6},{5,7},{6,4},{7,5},{8,10},{9,11},{10,... | collective-permute-start | bytes 1474568 | tf_op jit(solution)/shard_map/ppermute | solution.py:30
  99.4 12.8 %collective-permute-start.24 = (bf16[256,1024]{1,0:T(8,128)(2,1)S(1)}, bf16[256,1024]{1,0:T(8,128)(2,1)S(1)}, u32[]{:S(2)}, u32[]{:S(2)}) collective-permute-start(bf16[256,1024]{1,0:T(8,128)(2,1)S(1)} %get-tuple-element.182), channel_id=1, source_target_pairs={{0,4},{4,0},{8,12},{12,8},{16,20},{20,16},{24,28},{28,24},{1,5},{5... | collective-permute-start | bytes 1572872 | tf_op jit(solution)/shard_map/ppermute | solution.py:30
  101.0 12.5 %collective-permute-start.18 = (bf16[256,1024]{1,0:T(8,128)(2,1)S(1)}, bf16[256,1024]{1,0:T(8,128)(2,1)S(1)}, u32[]{:S(2)}, u32[]{:S(2)}) collective-permute-start(bf16[256,1024]{1,0:T(8,128)(2,1)S(1)} %get-tuple-element.180), channel_id=1, source_target_pairs={{0,8},{4,12},{8,0},{12,4},{16,24},{20,28},{24,16},{28,20},{1,9},{5... | collective-permute-start | bytes 1572872 | tf_op jit(solution)/shard_map/ppermute | solution.py:30
  113.8 35.3 %collective-permute-start.34 = (bf16[128,1024]{1,0:T(8,128)(2,1)S(1)}, bf16[128,1024]{1,0:T(8,128)(2,1)S(1)}, u32[]{:S(2)}, u32[]{:S(2)}) collective-permute-start(bf16[128,1024]{1,0:T(8,128)(2,1)S(1)} %get-tuple-element.199), channel_id=1, source_target_pairs={{0,16},{4,20},{8,24},{12,28},{16,0},{20,4},{24,8},{28,12},{1,17},{... | collective-permute-start | bytes 786440 | tf_op jit(solution)/shard_map/ppermute | solution.py:30
  116.5 21.6 %collective-permute-start.29 = (bf16[128,1024]{1,0:T(8,128)(2,1)S(1)}, bf16[128,1024]{1,0:T(8,128)(2,1)S(1)}, u32[]{:S(2)}, u32[]{:S(2)}) collective-permute-start(bf16[128,1024]{1,0:T(8,128)(2,1)S(1)} %get-tuple-element.196), channel_id=1, source_target_pairs={{0,16},{4,20},{8,24},{12,28},{16,0},{20,4},{24,8},{28,12},{1,17},{... | collective-permute-start | bytes 786440 | tf_op jit(solution)/shard_map/ppermute | solution.py:30
  122.4 26.0 %collective-permute-start.31 = (bf16[512,512]{1,0:T(8,128)(2,1)S(1)}, bf16[512,512]{1,0:T(8,128)(2,1)S(1)}, u32[]{:S(2)}, u32[]{:S(2)}) collective-permute-start(bf16[512,512]{1,0:T(8,128)(2,1)S(1)} %shard_map.282), channel_id=1, source_target_pairs={{0,8},{4,12},{8,0},{12,4},{16,24},{20,28},{24,16},{28,20},{1,9},{5... | collective-permute-start | bytes 1572872 | tf_op jit(solution)/shard_map/ppermute | solution.py:30
  127.5 13.7 %collective-permute-start.28 = (bf16[512,512]{1,0:T(8,128)(2,1)S(1)}, bf16[512,512]{1,0:T(8,128)(2,1)S(1)}, u32[]{:S(2)}, u32[]{:S(2)}) collective-permute-start(bf16[512,512]{1,0:T(8,128)(2,1)S(1)} %shard_map.281), channel_id=1, source_target_pairs={{0,4},{4,0},{8,12},{12,8},{16,20},{20,16},{24,28},{28,24},{1,5},{5... | collective-permute-start | bytes 1572872 | tf_op jit(solution)/shard_map/ppermute | solution.py:30
  138.2 18.7 %collective-permute-start.33 = (bf16[128,1024]{1,0:T(8,128)(2,1)S(1)}, bf16[128,1024]{1,0:T(8,128)(2,1)S(1)}, u32[]{:S(2)}, u32[]{:S(2)}) collective-permute-start(bf16[128,1024]{1,0:T(8,128)(2,1)S(1)} %shard_map.287), channel_id=1, source_target_pairs={{0,16},{4,20},{8,24},{12,28},{16,0},{20,4},{24,8},{28,12},{1,17},{... | collective-permute-start | bytes 786440 | tf_op jit(solution)/shard_map/ppermute | solution.py:30
  138.3 16.7 %collective-permute-start.40 = (bf16[12,1024]{1,0:T(8,128)(2,1)S(1)}, bf16[12,1024]{1,0:T(8,128)(2,1)S(1)}, u32[]{:S(2)}, u32[]{:S(2)}) collective-permute-start(bf16[12,1024]{1,0:T(8,128)(2,1)S(1)} %pad_maximum_fusion.11), channel_id=1, source_target_pairs={{0,2},{1,3},{2,0},{3,1},{4,6},{5,7},{6,4},{7,5},{8,10},{9,11},{10,... | collective-permute-start | bytes 73736 | tf_op jit(solution)/shard_map/ppermute | solution.py:30
  141.3 23.6 %collective-permute-start.30 = (bf16[256,512]{1,0:T(8,128)(2,1)S(1)}, bf16[256,512]{1,0:T(8,128)(2,1)S(1)}, u32[]{:S(2)}, u32[]{:S(2)}) collective-permute-start(bf16[256,512]{1,0:T(8,128)(2,1)S(1)} %get-tuple-element.217), channel_id=1, source_target_pairs={{0,8},{4,12},{8,0},{12,4},{16,24},{20,28},{24,16},{28,20},{1,9},{5... | collective-permute-start | bytes 786440 | tf_op jit(solution)/shard_map/ppermute | solution.py:30
  148.5 13.4 %collective-permute-start.32 = (bf16[256,512]{1,0:T(8,128)(2,1)S(1)}, bf16[256,512]{1,0:T(8,128)(2,1)S(1)}, u32[]{:S(2)}, u32[]{:S(2)}) collective-permute-start(bf16[256,512]{1,0:T(8,128)(2,1)S(1)} %get-tuple-element.220), channel_id=1, source_target_pairs={{0,4},{4,0},{8,12},{12,8},{16,20},{20,16},{24,28},{28,24},{1,5},{5... | collective-permute-start | bytes 786440 | tf_op jit(solution)/shard_map/ppermute | solution.py:30
  149.2 19.0 %collective-permute-start.38 = (bf16[128,1024]{1,0:T(8,128)(2,1)S(1)}, bf16[128,1024]{1,0:T(8,128)(2,1)S(1)}, u32[]{:S(2)}, u32[]{:S(2)}) collective-permute-start(bf16[128,1024]{1,0:T(8,128)(2,1)S(1)} %shard_map.290), channel_id=1, source_target_pairs={{0,16},{4,20},{8,24},{12,28},{16,0},{20,4},{24,8},{28,12},{1,17},{... | collective-permute-start | bytes 786440 | tf_op jit(solution)/shard_map/ppermute | solution.py:30
  156.9 20.6 %collective-permute-start.37 = (bf16[256,1024]{1,0:T(8,128)(2,1)S(1)}, bf16[256,1024]{1,0:T(8,128)(2,1)S(1)}, u32[]{:S(2)}, u32[]{:S(2)}) collective-permute-start(bf16[256,1024]{1,0:T(8,128)(2,1)S(1)} %pad_maximum_fusion.2), channel_id=1, source_target_pairs={{0,8},{4,12},{8,0},{12,4},{16,24},{20,28},{24,16},{28,20},{1,9},{5... | collective-permute-start | bytes 1572872 | tf_op jit(solution)/shard_map/ppermute | solution.py:30
  162.0 15.5 %collective-permute-start.36 = (bf16[128,512]{1,0:T(8,128)(2,1)S(1)}, bf16[128,512]{1,0:T(8,128)(2,1)S(1)}, u32[]{:S(2)}, u32[]{:S(2)}) collective-permute-start(bf16[128,512]{1,0:T(8,128)(2,1)S(1)} %get-tuple-element.224), channel_id=1, source_target_pairs={{0,16},{4,20},{8,24},{12,28},{16,0},{20,4},{24,8},{28,12},{1,17},{... | collective-permute-start | bytes 393224 | tf_op jit(solution)/shard_map/ppermute | solution.py:30
  164.9 15.4 %collective-permute-start.35 = (bf16[128,512]{1,0:T(8,128)(2,1)S(1)}, bf16[128,512]{1,0:T(8,128)(2,1)S(1)}, u32[]{:S(2)}, u32[]{:S(2)}) collective-permute-start(bf16[128,512]{1,0:T(8,128)(2,1)S(1)} %get-tuple-element.228), channel_id=1, source_target_pairs={{0,16},{4,20},{8,24},{12,28},{16,0},{20,4},{24,8},{28,12},{1,17},{... | collective-permute-start | bytes 393224 | tf_op jit(solution)/shard_map/ppermute | solution.py:30
  168.2 24.4 %collective-permute-start.45 = (bf16[256,1024]{1,0:T(8,128)(2,1)S(1)}, bf16[256,1024]{1,0:T(8,128)(2,1)S(1)}, u32[]{:S(2)}, u32[]{:S(2)}) collective-permute-start(bf16[256,1024]{1,0:T(8,128)(2,1)S(1)} %pad_maximum_fusion.3), channel_id=1, source_target_pairs={{0,4},{4,0},{8,12},{12,8},{16,20},{20,16},{24,28},{28,24},{1,5},{5... | collective-permute-start | bytes 1572872 | tf_op jit(solution)/shard_map/ppermute | solution.py:30
  177.6 12.6 %collective-permute-start.42 = (bf16[128,512]{1,0:T(8,128)(2,1)S(1)}, bf16[128,512]{1,0:T(8,128)(2,1)S(1)}, u32[]{:S(2)}, u32[]{:S(2)}) collective-permute-start(bf16[128,512]{1,0:T(8,128)(2,1)S(1)} %shard_map.293), channel_id=1, source_target_pairs={{0,16},{4,20},{8,24},{12,28},{16,0},{20,4},{24,8},{28,12},{1,17},{... | collective-permute-start | bytes 393224 | tf_op jit(solution)/shard_map/ppermute | solution.py:30
  180.4 11.9 %collective-permute-start.41 = (bf16[160,512]{1,0:T(8,128)(2,1)S(1)}, bf16[160,512]{1,0:T(8,128)(2,1)S(1)}, u32[]{:S(2)}, u32[]{:S(2)}) collective-permute-start(bf16[160,512]{1,0:T(8,128)(2,1)S(1)} %pad_maximum_fusion.8), channel_id=1, source_target_pairs={{0,16},{4,20},{8,24},{12,28},{16,0},{20,4},{24,8},{28,12},{1,17},{... | collective-permute-start | bytes 491528 | tf_op jit(solution)/shard_map/ppermute | solution.py:30
  192.6 27.4 %collective-permute-start.49 = (bf16[512,1024]{1,0:T(8,128)(2,1)S(1)}, bf16[512,1024]{1,0:T(8,128)(2,1)S(1)}, u32[]{:S(2)}, u32[]{:S(2)}) collective-permute-start(bf16[512,1024]{1,0:T(8,128)(2,1)S(1)} %pad_maximum_fusion.refs_0_), channel_id=1, source_target_pairs={{0,4},{4,0},{8,12},{12,8},{16,20},{20,16},{24,28},{28,24},{1,5},{5... | collective-permute-start | bytes 3145736 | tf_op jit(solution)/shard_map/ppermute | solution.py:30
  192.7 32.1 %collective-permute-start.48 = (bf16[512,1024]{1,0:T(8,128)(2,1)S(1)}, bf16[512,1024]{1,0:T(8,128)(2,1)S(1)}, u32[]{:S(2)}, u32[]{:S(2)}) collective-permute-start(bf16[512,1024]{1,0:T(8,128)(2,1)S(1)} %pad_maximum_fusion.1.refs_0_), channel_id=1, source_target_pairs={{0,8},{4,12},{8,0},{12,4},{16,24},{20,28},{24,16},{28,20},{1,9},{5... | collective-permute-start | bytes 3145736 | tf_op jit(solution)/shard_map/ppermute | solution.py:30
  202.4 31.3 %collective-permute-start.46 = (bf16[544,512]{1,0:T(8,128)(2,1)S(1)}, bf16[544,512]{1,0:T(8,128)(2,1)S(1)}, u32[]{:S(2)}, u32[]{:S(2)}) collective-permute-start(bf16[544,512]{1,0:T(8,128)(2,1)S(1)} %fusion.14), channel_id=1, source_target_pairs={{0,4},{4,0},{8,12},{12,8},{16,20},{20,16},{24,28},{28,24},{1,5},{5... | collective-permute-start | bytes 1671176 | tf_op jit(solution)/shard_map/ppermute | solution.py:30
  202.5 31.2 %collective-permute-start.47 = (bf16[512,512]{1,0:T(8,128)(2,1)S(1)}, bf16[512,512]{1,0:T(8,128)(2,1)S(1)}, u32[]{:S(2)}, u32[]{:S(2)}) collective-permute-start(bf16[512,512]{1,0:T(8,128)(2,1)S(1)} %pad_maximum_fusion.4.refs_2_), channel_id=1, source_target_pairs={{0,8},{4,12},{8,0},{12,4},{16,24},{20,28},{24,16},{28,20},{1,9},{5... | collective-permute-start | bytes 1572872 | tf_op jit(solution)/shard_map/ppermute | solution.py:30
  (29 other events, 184.1 us)

commit v5 on v4

--- a/solution.py
+++ b/solution.py
@@ -102,7 +102,7 @@
         scratch_shapes=scratch,
         compiler_params=pltpu.CompilerParams(vmem_limit_bytes=room * MIB),
         cost_estimate=pl.CostEstimate(
-            flops=0, bytes_accessed=0, transcendentals=0
+            flops=int(1e9 * WEIGHT), bytes_accessed=0, transcendentals=0
         ),
     )(operands[0], *ins)
 
@@ -620,6 +620,12 @@
         return self.came
 
     def arrive(self, *earlier):
+        found = self.step(*earlier)
+        while len(self.order) <= self.at < self.count:
+            found = self.step(found)
+        return found
+
+    def step(self, *earlier):
         if self.came is None:
             self.take()
         arrived = after(self.came, *earlier)
@@ -959,7 +965,7 @@
     first.values = weight_grad(after(me, mixed_send), normed, flat, ORDER_A, True, 0, split)
     stay(first.values)
     mixed.values = mixed_grad(
-        after(me, first.values), normed, flat, head_rows, mids, ORDER_B, True, split
+        after(me, first.values, arrived_near), normed, flat, head_rows, mids, ORDER_B, True, split
     )
     leave(norm_near, norm_y, norm_both, flat_near, flat_far, heads_near, heads_far)
     leave(middle_low, mid_core, mid_far, mid_both)
@@ -980,40 +986,41 @@
     stay(down.values, up.values, first.values, mixed.values)
 
     now = down.arrive(feed_hold)
+    shared = pack(jnp.concatenate([middle_sums, token_sums], axis=0))
+    shared = add_small(shared, after(swap(shared, "tensor", 1), now))
     now = first.arrive(now)
-    shared = pack(jnp.concatenate([middle_sums, token_sums], axis=0))
-    shared = add_small(shared, swap(shared, "tensor", 1))
-    shared = unpack(add_small(shared, swap(shared, "tensor", 2)))
+    now = mixed.arrive(now)
+    shared = unpack(add_small(shared, after(swap(shared, "tensor", 2), now)))
     own = jnp.concatenate(
         [up_bias_near + up_bias_y + up_bias_both, jnp.pad(bias_grad, ((0, 0), (0, hidden - 2 * width)))], axis=0
     )
     small = jnp.concatenate([shared, own], axis=0)
     small = pack(jnp.concatenate([small[:, :split], small[:, split:]], axis=0))
-    now = mixed.arrive(now)
     now = up.arrive(now)
     now = down.arrive(now)
     now = mixed.arrive(now)
     now = first.arrive(now)
     now = up.arrive(now)
-    now = down.arrive(now)
     now = mixed.arrive(now)
     now = first.arrive(now)
     while first.at < first.count:
         now = first.arrive(now)
     first.join(small)
+    now = down.arrive(now)
+    now = up.arrive(now)
     now = mixed.arrive(now)
     now = first.arrive(now)
-    now = up.arrive(now)
-    last = [mixed, first, down, up]
-    while any(x.at < len(x.bits) for x in last):
-        for x in last:
-            if x.at < len(x.bits):
-                now = x.arrive(now)
+    now = mixed.arrive(now)
+    now = first.arrive(now)
+    now = down.arrive(now)
+    down_sum = place(after(me, now), down.parts, ORDER_A)
+    up.arrive(down_sum)
+    up_sum = place(me, up.parts, ORDER_B)
+    now = mixed.arrive(up_sum)
+    first.arrive(now)
     small = unpack(first.small)
     small = jnp.concatenate([small[:8], small[8:]], axis=1)
     piece = model // PIECES
-    down_sum = place(me, down.parts, ORDER_A)
-    up_sum = place(me, up.parts, ORDER_B)
     in_sum, out_sum = run_out(
         functools.partial(place_mixed, ORDER_A, ORDER_B),
         (me, *first.parts, *mixed.parts),

time: 241 us -> 229 us (0.950)
  waiting for transfers between devices: 94.9 us -> 72.5 us
  starting transfers between devices: 45.8 us -> 56.4 us
    ppermute x50, waiting for transfers between devices: 94.9 us -> 72.5 us  [swap(): return lax.ppermute(values, axis, [(i, i ^ bit) for i in range(count)])]
    ppermute x50, starting transfers between devices: 45.8 us -> 56.4 us  [swap(): return lax.ppermute(values, axis, [(i, i ^ bit) for i in range(count)])]
  transfers between devices with their start and end apart: 50 -> 50, of which waited for: 25 -> 22; matrix products, arithmetic and copies ran while one was open for 3% -> 3% of each run, Pallas kernels for 32% -> 35%
where the time goes in v5:
time: 229 us
  Pallas kernels  88 us (38%)
  waiting for transfers between devices  72.5 us (32%)
  starting transfers between devices  56.4 us (25%)
  local copies, waits for them, and re-layouts  6.21 us (3%)
  other arithmetic  4.26 us (2%)
    pallas_call x41, Pallas kernels, run(): pl.pallas_call(kernel, out_shape=[pltpu.VMEM(x.shape, x.dtype) for x in o...  79.9 us
    ppermute x50, waiting for transfers between devices, swap(): return lax.ppermute(values, axis, [(i, i ^ bit) for i in range(count)])  72.5 us
    ppermute x50, starting transfers between devices, swap(): return lax.ppermute(values, axis, [(i, i ^ bit) for i in range(count)])  56.4 us
    pallas_call x3, Pallas kernels, run_out(): pl.pallas_call(body, out_shape=[pltpu.HBM(x.shape, x.dtype) for x in outs...  8.04 us
  transfers between devices with their start and end apart: 50, of which 22 were waited for; matrix products, arithmetic and copies ran while one was open for 3% of the time, Pallas kernels for 35%

profile of v5, /device:TPU:0, one launch (start us, length us, event | category | flops | bytes accessed | tf_op | source)
XLA Modules:
  0.0 228.6 jit_solution(18358911287425566229)
XLA Ops:
  0.6 3.0 %collective-permute-start.2 = (bf16[240,1024]{1,0:T(8,128)(2,1)}, bf16[240,1024]{1,0:T(8,128)(2,1)S(1)}, u32[]{:S(2)}, u32[]{:S(2)}) collective-permute-start(bf16[240,1024]{1,0:T(8,128)(2,1)} %refs_4_.13), channel_id=1, source_target_pairs={{0,2},{1,3},{2,0},{3,1},{4,6},{5,7},{6,4},{7,5},{8,10},{9,11},{10,... | collective-permute-start | bytes 1474568 | tf_op jit(solution)/shard_map/ppermute | solution.py:30
  10.1 4.1 %shard_map.254 = (bf16[480,1024]{1,0:T(8,128)(2,1)S(1)}, bf16[480,768]{1,0:T(8,128)(2,1)S(1)}) custom-call(s32[2]{0:T(128)S(1)} %pad_add_fusion.refs_0_.me, bf16[240,1024]{1,0:T(8,128)(2,1)S(1)} %copy-done.3, bf16[240,1024]{1,0:T(8,128)(2,1)S(1)} %collective-permute-done.1.refs_2_, ...), custom_call_target="tpu_custom_call" | custom-call | flops 15099494400 | tf_op jit(solution)/shard_map/pallas_call | solution.py:63
  19.1 7.4 %shard_map.256 = (bf16[240,1024]{1,0:T(8,128)(2,1)S(1)}, bf16[960,768]{1,0:T(8,128)(2,1)S(1)}, bf16[12,160,320]{2,1,0:T(8,128)(2,1)S(1)}, bf16[480,256]{1,0:T(8,...) custom-call(s32[2]{0:T(128)S(1)} %pad_add_fusion.refs_0_.me, ...), custom_call_target="tpu_custom_call" | custom-call | flops 26424115200 | tf_op jit(solution)/shard_map/pallas_call | solution.py:63
  30.7 5.6 %shard_map.258 = (bf16[12,160,320]{2,1,0:T(8,128)(2,1)S(1)}, bf16[480,256]{1,0:T(8,128)(2,1)S(1)}, bf16[240,1024]{1,0:T(8,128)(2,1)S(1)}, f32[240,1024]{1,0:T(8,128)S(1)}) custom-call(s32[2]{0:T(128)S(1)} %pad_add_fusion.refs_0_.me, bf16[960,768]{1,0:T(8,128)(2,1)S(1)} %get-tuple-element.140.refs_11_.refs_1_.refs_12_.refs_13_.refs_15_.refs_16_.refs_3_, ...), custom_call_target="tpu_custom_call" | custom-call | flops 11324620800 | tf_op jit(solution)/shard_map/pallas_call | solution.py:63
  36.4 2.5 %shard_map.259.refs_19_.refs_5_ = f32[480,1024]{1,0:T(8,128)S(1)} custom-call(s32[2]{0:T(128)S(1)} %pad_add_fusion.refs_0_.me, bf16[240,1024]{1,0:T(8,128)(2,1)S(1)} %multiply_convert_fusion.1.refs_6_.refs_10_.refs_7_.refs_1_.refs_8_.refs_4_.refs_11_.refs_5_.refs_9_.refs_14_.refs_3_, ...), custom_call_target="tpu_custom_call" | custom-call | flops 20132659200 | tf_op jit(solution)/shard_map/pallas_call | solution.py:63
  38.9 3.1 %collective-permute-done.7.refs_4_ = bf16[240,1024]{1,0:T(8,128)(2,1)S(1)} collective-permute-done((bf16[240,1024]{1,0:T(8,128)(2,1)S(1)}, bf16[240,1024]{1,0:T(8,128)(2,1)S(1)}, u32[]{:S(2)}, u32[]{:S(2)}) %collective-permute-start.7) | collective-permute-done | bytes 491552 | tf_op jit(solution)/shard_map/ppermute | solution.py:30
  45.8 4.6 %shard_map.261 = (bf16[480,1024]{1,0:T(8,128)(2,1)S(1)}, bf16[480,1024]{1,0:T(8,128)(2,1)S(1)}, f32[1,1024]{1,0:T(1,128)S(1)}, f32[240,1024]{1,0:T(8,128)S(1)}, bf16[240,1024]{1,0:T(8,128)(2,1)S(1)}) custom-call(s32[2]{0:T(128)S(1)} %pad_add_fusion.refs_0_.me, bf16[240,1024]{1,0:T(8,128)(2,1)S(1)} %get-tuple-element.155.refs_1_.refs_20_.refs_22_.refs_19_.refs_18_, ...), custom_call_target="tpu_custom_call" | custom-call | flops 40265318400 | tf_op jit(solution)/shard_map/pallas_call | solution.py:63
  50.5 2.5 %shard_map.262.refs_4_.refs_27_ = f32[480,1024]{1,0:T(8,128)S(1)} custom-call(s32[2]{0:T(128)S(1)} %pad_add_fusion.refs_0_.me, bf16[240,1024]{1,0:T(8,128)(2,1)S(1)} %collective-permute-done.5.refs_1_.refs_25_.refs_6_.refs_26_.refs_24_, bf16[240,1024]{1,0:T(8,128)(2,1)S(1)} %collective-permute-done.9.refs_2_.refs_26_.refs_7_.refs_27_.refs_25_, ...), custom_call_target="tpu_custom_call" | custom-call | flops 20132659200 | tf_op jit(solution)/shard_map/pallas_call | solution.py:63
  53.0 4.5 %collective-permute-done.8.refs_1_.refs_29_.refs_30_.refs_27_.refs_3_.refs_28_.refs_26_.refs_23_ = bf16[240,1024]{1,0:T(8,128)(2,1)S(1)} collective-permute-done((bf16[240,1024]{1,0:T(8,128)(2,1)S(1)}, bf16[240,1024]{1,0:T(8,128)(2,1)S(1)}, u32[]{:S(2)}, u32[]{:S(2)}) %collective-permute-start.8) | collective-permute-done | bytes 491552 | tf_op jit(solution)/shard_map/ppermute | solution.py:30
  57.5 2.8 %shard_map.263 = (bf16[240,1024]{1,0:T(8,128)(2,1)S(1)}, bf16[240,1024]{1,0:T(8,128)(2,1)S(1)}, f32[1,1024]{1,0:T(1,128)S(1)}, f32[240,1024]{1,0:T(8,128)S(1)}) custom-call(s32[2]{0:T(128)S(1)} %pad_add_fusion.refs_0_.me, bf16[240,1024]{1,0:T(8,128)(2,1)S(1)} %collective-permute-done.8.refs_1_.refs_29_.refs_30_.refs_27_.refs_3_.refs_28_.refs_26_.refs_23_, ...), custom_call_target="tpu_custom_call" | custom-call | flops 20132659200 | tf_op jit(solution)/shard_map/pallas_call | solution.py:63
  60.2 2.8 %shard_map.264 = (bf16[240,1024]{1,0:T(8,128)(2,1)S(1)}, bf16[240,1024]{1,0:T(8,128)(2,1)S(1)}, f32[1,1024]{1,0:T(1,128)S(1)}, bf16[240,1024]{1,0:T(8,128)(2,1)S(1)}) custom-call(s32[2]{0:T(128)S(1)} %pad_add_fusion.refs_0_.me, bf16[240,1024]{1,0:T(8,128)(2,1)S(1)} %collective-permute-done.11.refs_1_.refs_29_.refs_4_.refs_31_.refs_28_.refs_25_, ...), custom_call_target="tpu_custom_call" | custom-call | flops 20132659200 | tf_op jit(solution)/shard_map/pallas_call | solution.py:63
  66.8 2.8 %shard_map.266 = bf16[512,1024]{1,0:T(8,128)(2,1)S(1)} custom-call(s32[2]{0:T(128)S(1)} %pad_add_fusion.refs_0_.me, bf16[480,1024]{1,0:T(8,128)(2,1)S(1)} %get-tuple-element.157.refs_21_.refs_1_.refs_24_.refs_20_.refs_19_.refs_22_.refs_17_.refs_14_.refs_13_.refs_10_, bf16[240,1024]{1,0:T(8,128)(2,1)S(1)} %get-tuple-element.162.refs_27_.refs_28_.refs_2_.refs_1_.refs_26_, ...), custom_call_target="tpu_custom_call" | custom-call | flops 20132659200 | tf_op jit(solution)/shard_map/pallas_call | solution.py:63
  69.6 2.9 %shard_map.267 = bf16[512,1024]{1,0:T(8,128)(2,1)S(1)} custom-call(s32[2]{0:T(128)S(1)} %pad_add_fusion.refs_0_.me, bf16[240,1024]{1,0:T(8,128)(2,1)S(1)} %get-tuple-element.155.refs_1_.refs_20_.refs_22_.refs_19_.refs_18_, bf16[240,1024]{1,0:T(8,128)(2,1)S(1)} %collective-permute-done.10.refs_2_.refs_24_.refs_25_.refs_23_.refs_21_, ...), custom_call_target="tpu_custom_call" | custom-call | flops 20132659200 | tf_op jit(solution)/shard_map/pallas_call | solution.py:63
  82.6 2.8 %shard_map.270.refs_27_.refs_25_.refs_1_ = f32[512,1024]{1,0:T(8,128)S(1)} custom-call(s32[2]{0:T(128)S(1)} %pad_add_fusion.refs_0_.me, bf16[480,1024]{1,0:T(8,128)(2,1)S(1)} %get-tuple-element.157.refs_21_.refs_1_.refs_24_.refs_20_.refs_19_.refs_22_.refs_17_.refs_14_.refs_13_.refs_10_, ...), custom_call_target="tpu_custom_call" | custom-call | flops 20132659200 | tf_op jit(solution)/shard_map/pallas_call | solution.py:63
  85.4 6.6 %shard_map.271 = (f32[480,256]{1,0:T(8,128)S(1)}, f32[960,512]{1,0:T(8,128)S(1)}) custom-call(s32[2]{0:T(128)S(1)} %pad_add_fusion.refs_0_.me, bf16[240,1024]{1,0:T(8,128)(2,1)S(1)} %get-tuple-element.173.refs_30_.refs_1_.refs_24_.refs_19_.refs_21_.refs_16_.refs_15_.refs_8_, ...), custom_call_target="tpu_custom_call" | custom-call | flops 20761804800 | tf_op jit(solution)/shard_map/pallas_call | solution.py:63
  92.1 2.7 %shard_map.272.refs_23_.refs_1_ = f32[512,1024]{1,0:T(8,128)S(1)} custom-call(s32[2]{0:T(128)S(1)} %pad_add_fusion.refs_0_.me, bf16[240,1024]{1,0:T(8,128)(2,1)S(1)} %get-tuple-element.155.refs_1_.refs_20_.refs_22_.refs_19_.refs_18_, bf16[240,1024]{1,0:T(8,128)(2,1)S(1)} %collective-permute-done.10.refs_2_.refs_24_.refs_25_.refs_23_.refs_21_, ...), custom_call_target="tpu_custom_call" | custom-call | flops 20132659200 | tf_op jit(solution)/shard_map/pallas_call | solution.py:63
  101.5 8.1 %shard_map.275 = (bf16[480,768]{1,0:T(8,128)(2,1)S(1)}, bf16[480,768]{1,0:T(8,128)(2,1)S(1)}, f32[1,512]{1,0:T(1,128)S(1)}, bf16[240,1024]{1,0:T(8,128)(2,1)S(1)}, f32[240,1024]{1,0:T(8,128)S(1)}) custom-call(s32[2]{0:T(128)S(1)} %pad_add_fusion.refs_0_.me, ...), custom_call_target="tpu_custom_call" | custom-call | flops 35861299200 | tf_op jit(solution)/shard_map/pallas_call | solution.py:63
  109.6 2.6 %collective-permute-done.24.refs_2_ = bf16[256,1024]{1,0:T(8,128)(2,1)S(1)} collective-permute-done((bf16[256,1024]{1,0:T(8,128)(2,1)S(1)}, bf16[256,1024]{1,0:T(8,128)(2,1)S(1)}, u32[]{:S(2)}, u32[]{:S(2)}) %collective-permute-start.24) | collective-permute-done | bytes 524320 | tf_op jit(solution)/shard_map/ppermute | solution.py:30
  113.8 2.7 %collective-permute-start.34 = (bf16[128,1024]{1,0:T(8,128)(2,1)S(1)}, bf16[128,1024]{1,0:T(8,128)(2,1)S(1)}, u32[]{:S(2)}, u32[]{:S(2)}) collective-permute-start(bf16[128,1024]{1,0:T(8,128)(2,1)S(1)} %get-tuple-element.202), channel_id=1, source_target_pairs={{0,16},{4,20},{8,24},{12,28},{16,0},{20,4},{24,8},{28,12},{1,17},{... | collective-permute-start | bytes 786440 | tf_op jit(solution)/shard_map/ppermute | solution.py:30
  131.6 6.5 %collective-permute-done.29.refs_2_ = bf16[128,1024]{1,0:T(8,128)(2,1)S(1)} collective-permute-done((bf16[128,1024]{1,0:T(8,128)(2,1)S(1)}, bf16[128,1024]{1,0:T(8,128)(2,1)S(1)}, u32[]{:S(2)}, u32[]{:S(2)}) %collective-permute-start.29) | collective-permute-done | bytes 262176 | tf_op jit(solution)/shard_map/ppermute | solution.py:30
  139.9 6.1 %collective-permute-done.31.refs_2_ = bf16[512,512]{1,0:T(8,128)(2,1)S(1)} collective-permute-done((bf16[512,512]{1,0:T(8,128)(2,1)S(1)}, bf16[512,512]{1,0:T(8,128)(2,1)S(1)}, u32[]{:S(2)}, u32[]{:S(2)}) %collective-permute-start.31) | collective-permute-done | bytes 524320 | tf_op jit(solution)/shard_map/ppermute | solution.py:30
  146.9 9.3 %collective-permute-start.37 = (bf16[128,1024]{1,0:T(8,128)(2,1)S(1)}, bf16[128,1024]{1,0:T(8,128)(2,1)S(1)}, u32[]{:S(2)}, u32[]{:S(2)}) collective-permute-start(bf16[128,1024]{1,0:T(8,128)(2,1)S(1)} %shard_map.290), channel_id=1, source_target_pairs={{0,16},{4,20},{8,24},{12,28},{16,0},{20,4},{24,8},{28,12},{1,17},{... | collective-permute-start | bytes 786440 | tf_op jit(solution)/shard_map/ppermute | solution.py:30
  157.4 3.8 %collective-permute-start.36 = (bf16[128,512]{1,0:T(8,128)(2,1)S(1)}, bf16[128,512]{1,0:T(8,128)(2,1)S(1)}, u32[]{:S(2)}, u32[]{:S(2)}) collective-permute-start(bf16[128,512]{1,0:T(8,128)(2,1)S(1)} %get-tuple-element.227), channel_id=1, source_target_pairs={{0,16},{4,20},{8,24},{12,28},{16,0},{20,4},{24,8},{28,12},{1,17},{... | collective-permute-start | bytes 393224 | tf_op jit(solution)/shard_map/ppermute | solution.py:30
  163.3 4.5 %collective-permute-start.35 = (bf16[128,512]{1,0:T(8,128)(2,1)S(1)}, bf16[128,512]{1,0:T(8,128)(2,1)S(1)}, u32[]{:S(2)}, u32[]{:S(2)}) collective-permute-start(bf16[128,512]{1,0:T(8,128)(2,1)S(1)} %get-tuple-element.231), channel_id=1, source_target_pairs={{0,16},{4,20},{8,24},{12,28},{16,0},{20,4},{24,8},{28,12},{1,17},{... | collective-permute-start | bytes 393224 | tf_op jit(solution)/shard_map/ppermute | solution.py:30
  168.5 6.1 %collective-permute-done.36.refs_2_ = bf16[128,512]{1,0:T(8,128)(2,1)S(1)} collective-permute-done((bf16[128,512]{1,0:T(8,128)(2,1)S(1)}, bf16[128,512]{1,0:T(8,128)(2,1)S(1)}, u32[]{:S(2)}, u32[]{:S(2)}) %collective-permute-start.36) | collective-permute-done | bytes 131104 | tf_op jit(solution)/shard_map/ppermute | solution.py:30
  174.6 3.4 %collective-permute-start.41 = (bf16[128,512]{1,0:T(8,128)(2,1)S(1)}, bf16[128,512]{1,0:T(8,128)(2,1)S(1)}, u32[]{:S(2)}, u32[]{:S(2)}) collective-permute-start(bf16[128,512]{1,0:T(8,128)(2,1)S(1)} %shard_map.293), channel_id=1, source_target_pairs={{0,16},{4,20},{8,24},{12,28},{16,0},{20,4},{24,8},{28,12},{1,17},{... | collective-permute-start | bytes 393224 | tf_op jit(solution)/shard_map/ppermute | solution.py:30
  184.5 5.5 %collective-permute-start.44 = (bf16[288,512]{1,0:T(8,128)(2,1)S(1)}, bf16[288,512]{1,0:T(8,128)(2,1)S(1)}, u32[]{:S(2)}, u32[]{:S(2)}) collective-permute-start(bf16[288,512]{1,0:T(8,128)(2,1)S(1)} %pad_maximum_fusion.6), channel_id=1, source_target_pairs={{0,8},{4,12},{8,0},{12,4},{16,24},{20,28},{24,16},{28,20},{1,9},{5... | collective-permute-start | bytes 884744 | tf_op jit(solution)/shard_map/ppermute | solution.py:30
  191.1 19.3 %collective-permute-done.45 = bf16[256,512]{1,0:T(8,128)(2,1)S(1)} collective-permute-done((bf16[256,512]{1,0:T(8,128)(2,1)S(1)}, bf16[256,512]{1,0:T(8,128)(2,1)S(1)}, u32[]{:S(2)}, u32[]{:S(2)}) %collective-permute-start.45) | collective-permute-done | bytes 262176 | tf_op jit(solution)/shard_map/ppermute | solution.py:30
  211.0 2.6 %shard_map.295 = f32[1024,1024]{1,0:T(8,128)} custom-call(s32[2]{0:T(128)S(1)} %pad_add_fusion.refs_0_.me, bf16[512,1024]{1,0:T(8,128)(2,1)S(1)} %pad_maximum_fusion.refs_0_, bf16[512,1024]{1,0:T(8,128)(2,1)S(1)} %collective-permute-done.49.refs_1_), custom_call_target="tpu_custom_call" | custom-call | flops 20000000000 | tf_op jit(solution)/shard_map/pallas_call | solution.py:96
  215.3 2.6 %shard_map.296 = f32[1024,1024]{1,0:T(8,128)} custom-call(s32[2]{0:T(128)S(1)} %pad_add_fusion.refs_0_.me, bf16[512,1024]{1,0:T(8,128)(2,1)S(1)} %pad_maximum_fusion.1.refs_0_, bf16[512,1024]{1,0:T(8,128)(2,1)S(1)} %collective-permute-done.48.refs_1_), custom_call_target="tpu_custom_call" | custom-call | flops 20000000000 | tf_op jit(solution)/shard_map/pallas_call | solution.py:96
  217.9 6.5 %collective-permute-done.47.refs_3_ = bf16[512,512]{1,0:T(8,128)(2,1)S(1)} collective-permute-done((bf16[512,512]{1,0:T(8,128)(2,1)S(1)}, bf16[512,512]{1,0:T(8,128)(2,1)S(1)}, u32[]{:S(2)}, u32[]{:S(2)}) %collective-permute-start.47) | collective-permute-done | bytes 524320 | tf_op jit(solution)/shard_map/ppermute | solution.py:30
  225.2 2.8 %shard_map.297 = (f32[1024,768]{1,0:T(8,128)}, f32[256,1024]{1,0:T(8,128)}) custom-call(s32[2]{0:T(128)S(1)} %pad_add_fusion.refs_0_.me, bf16[512,512]{1,0:T(8,128)(2,1)S(1)} %pad_maximum_fusion.5.refs_0_, bf16[544,512]{1,0:T(8,128)(2,1)S(1)} %collective-permute-done.46.refs_1_, bf16[512,512]{1,0:T(8,128)(2,1)S(1)} %pad_maximum_fusion.4.refs_2_, ...), custom_call_target="tpu_custom_call" | custom-call | flops 20000000000 | tf_op jit(solution)/shard_map/pallas_call | solution.py:96
  (179 shorter events, 74.3 us)
Async XLA Ops:
  0.6 14.5 %collective-permute-start.2 = (bf16[240,1024]{1,0:T(8,128)(2,1)}, bf16[240,1024]{1,0:T(8,128)(2,1)S(1)}, u32[]{:S(2)}, u32[]{:S(2)}) collective-permute-start(bf16[240,1024]{1,0:T(8,128)(2,1)} %refs_4_.13), channel_id=1, source_target_pairs={{0,2},{1,3},{2,0},{3,1},{4,6},{5,7},{6,4},{7,5},{8,10},{9,11},{10,... | collective-permute-start | bytes 1474568 | tf_op jit(solution)/shard_map/ppermute | solution.py:30
  15.1 13.6 %collective-permute-start.5 = (bf16[240,1024]{1,0:T(8,128)(2,1)S(1)}, bf16[240,1024]{1,0:T(8,128)(2,1)S(1)}, u32[]{:S(2)}, u32[]{:S(2)}) collective-permute-start(bf16[240,1024]{1,0:T(8,128)(2,1)S(1)} %multiply_convert_fusion.1.refs_6_.refs_10_.refs_7_.refs_1_.refs_8_.refs_4_.refs_11_.refs_5_.refs_9_.refs_14_, ...), channel_id=1, source_target_pairs={{0,2},{1,3},{2,0},{3,1},{4,6},{5,7},{6,4},{7,5},{8,10},{9,11},{10,... | collective-permute-start | bytes 1474568 | tf_op jit(solution)/shard_map/ppermute | solution.py:30
  28.9 13.1 %collective-permute-start.7 = (bf16[240,1024]{1,0:T(8,128)(2,1)S(1)}, bf16[240,1024]{1,0:T(8,128)(2,1)S(1)}, u32[]{:S(2)}, u32[]{:S(2)}) collective-permute-start(bf16[240,1024]{1,0:T(8,128)(2,1)S(1)} %shard_map.257), channel_id=1, source_target_pairs={{0,2},{1,3},{2,0},{3,1},{4,6},{5,7},{6,4},{7,5},{8,10},{9,11},{10,... | collective-permute-start | bytes 1474568 | tf_op jit(solution)/shard_map/ppermute | solution.py:30
  44.3 13.2 %collective-permute-start.8 = (bf16[240,1024]{1,0:T(8,128)(2,1)S(1)}, bf16[240,1024]{1,0:T(8,128)(2,1)S(1)}, u32[]{:S(2)}, u32[]{:S(2)}) collective-permute-start(bf16[240,1024]{1,0:T(8,128)(2,1)S(1)} %get-tuple-element.155.refs_1_.refs_20_.refs_22_.refs_19_.refs_18_), channel_id=1, source_target_pairs={{0,2},{1,3},{2,0},{3,1},{4,6},{5,7},{6,4},{7,5},{8,10},{9,11},{10,... | collective-permute-start | bytes 1474568 | tf_op jit(solution)/shard_map/ppermute | solution.py:30
  63.6 13.9 %collective-permute-start.13 = (bf16[240,1024]{1,0:T(8,128)(2,1)S(1)}, bf16[240,1024]{1,0:T(8,128)(2,1)S(1)}, u32[]{:S(2)}, u32[]{:S(2)}) collective-permute-start(bf16[240,1024]{1,0:T(8,128)(2,1)S(1)} %get-tuple-element.172), channel_id=1, source_target_pairs={{0,1},{1,0},{2,3},{3,2},{4,5},{5,4},{6,7},{7,6},{8,9},{9,8},{10,11... | collective-permute-start | bytes 1474568 | tf_op jit(solution)/shard_map/ppermute | solution.py:30
  65.2 13.6 %collective-permute-start.14 = (bf16[240,1024]{1,0:T(8,128)(2,1)S(1)}, bf16[240,1024]{1,0:T(8,128)(2,1)S(1)}, u32[]{:S(2)}, u32[]{:S(2)}) collective-permute-start(bf16[240,1024]{1,0:T(8,128)(2,1)S(1)} %shard_map.265), channel_id=1, source_target_pairs={{0,2},{1,3},{2,0},{3,1},{4,6},{5,7},{6,4},{7,5},{8,10},{9,11},{10,... | collective-permute-start | bytes 1474568 | tf_op jit(solution)/shard_map/ppermute | solution.py:30
  72.5 25.2 %collective-permute-start.19 = (bf16[512,1024]{1,0:T(8,128)(2,1)S(1)}, bf16[512,1024]{1,0:T(8,128)(2,1)S(1)}, u32[]{:S(2)}, u32[]{:S(2)}) collective-permute-start(bf16[512,1024]{1,0:T(8,128)(2,1)S(1)} %shard_map.267), channel_id=1, source_target_pairs={{0,8},{4,12},{8,0},{12,4},{16,24},{20,28},{24,16},{28,20},{1,9},{5... | collective-permute-start | bytes 3145736 | tf_op jit(solution)/shard_map/ppermute | solution.py:30
  74.2 24.9 %collective-permute-start.15 = (bf16[512,1024]{1,0:T(8,128)(2,1)S(1)}, bf16[512,1024]{1,0:T(8,128)(2,1)S(1)}, u32[]{:S(2)}, u32[]{:S(2)}) collective-permute-start(bf16[512,1024]{1,0:T(8,128)(2,1)S(1)} %shard_map.266), channel_id=1, source_target_pairs={{0,4},{4,0},{8,12},{12,8},{16,20},{20,16},{24,28},{28,24},{1,5},{5... | collective-permute-start | bytes 3145736 | tf_op jit(solution)/shard_map/ppermute | solution.py:30
  77.4 17.6 %collective-permute-start.22 = (bf16[240,1024]{1,0:T(8,128)(2,1)S(1)}, bf16[240,1024]{1,0:T(8,128)(2,1)S(1)}, u32[]{:S(2)}, u32[]{:S(2)}) collective-permute-start(bf16[240,1024]{1,0:T(8,128)(2,1)S(1)} %get-tuple-element.192), channel_id=1, source_target_pairs={{0,1},{1,0},{2,3},{3,2},{4,5},{5,4},{6,7},{7,6},{8,9},{9,8},{10,11... | collective-permute-start | bytes 1474568 | tf_op jit(solution)/shard_map/ppermute | solution.py:30
  81.0 13.8 %collective-permute-start.16 = (bf16[240,1024]{1,0:T(8,128)(2,1)S(1)}, bf16[240,1024]{1,0:T(8,128)(2,1)S(1)}, u32[]{:S(2)}, u32[]{:S(2)}) collective-permute-start(bf16[240,1024]{1,0:T(8,128)(2,1)S(1)} %get-tuple-element.173.refs_30_.refs_1_.refs_24_.refs_19_.refs_21_.refs_16_.refs_15_.refs_8_), channel_id=1, source_target_pairs={{0,2},{1,3},{2,0},{3,1},{4,6},{5,7},{6,4},{7,5},{8,10},{9,11},{10,... | collective-permute-start | bytes 1474568 | tf_op jit(solution)/shard_map/ppermute | solution.py:30
  95.1 18.4 %collective-permute-start.23 = (bf16[240,1024]{1,0:T(8,128)(2,1)S(1)}, bf16[240,1024]{1,0:T(8,128)(2,1)S(1)}, u32[]{:S(2)}, u32[]{:S(2)}) collective-permute-start(bf16[240,1024]{1,0:T(8,128)(2,1)S(1)} %shard_map.276), channel_id=1, source_target_pairs={{0,2},{1,3},{2,0},{3,1},{4,6},{5,7},{6,4},{7,5},{8,10},{9,11},{10,... | collective-permute-start | bytes 1474568 | tf_op jit(solution)/shard_map/ppermute | solution.py:30
  99.4 12.8 %collective-permute-start.24 = (bf16[256,1024]{1,0:T(8,128)(2,1)S(1)}, bf16[256,1024]{1,0:T(8,128)(2,1)S(1)}, u32[]{:S(2)}, u32[]{:S(2)}) collective-permute-start(bf16[256,1024]{1,0:T(8,128)(2,1)S(1)} %get-tuple-element.185), channel_id=1, source_target_pairs={{0,4},{4,0},{8,12},{12,8},{16,20},{20,16},{24,28},{28,24},{1,5},{5... | collective-permute-start | bytes 1572872 | tf_op jit(solution)/shard_map/ppermute | solution.py:30
  101.0 12.5 %collective-permute-start.18 = (bf16[256,1024]{1,0:T(8,128)(2,1)S(1)}, bf16[256,1024]{1,0:T(8,128)(2,1)S(1)}, u32[]{:S(2)}, u32[]{:S(2)}) collective-permute-start(bf16[256,1024]{1,0:T(8,128)(2,1)S(1)} %get-tuple-element.183), channel_id=1, source_target_pairs={{0,8},{4,12},{8,0},{12,4},{16,24},{20,28},{24,16},{28,20},{1,9},{5... | collective-permute-start | bytes 1572872 | tf_op jit(solution)/shard_map/ppermute | solution.py:30
  113.8 32.3 %collective-permute-start.34 = (bf16[128,1024]{1,0:T(8,128)(2,1)S(1)}, bf16[128,1024]{1,0:T(8,128)(2,1)S(1)}, u32[]{:S(2)}, u32[]{:S(2)}) collective-permute-start(bf16[128,1024]{1,0:T(8,128)(2,1)S(1)} %get-tuple-element.202), channel_id=1, source_target_pairs={{0,16},{4,20},{8,24},{12,28},{16,0},{20,4},{24,8},{28,12},{1,17},{... | collective-permute-start | bytes 786440 | tf_op jit(solution)/shard_map/ppermute | solution.py:30
  116.5 21.6 %collective-permute-start.29 = (bf16[128,1024]{1,0:T(8,128)(2,1)S(1)}, bf16[128,1024]{1,0:T(8,128)(2,1)S(1)}, u32[]{:S(2)}, u32[]{:S(2)}) collective-permute-start(bf16[128,1024]{1,0:T(8,128)(2,1)S(1)} %get-tuple-element.199), channel_id=1, source_target_pairs={{0,16},{4,20},{8,24},{12,28},{16,0},{20,4},{24,8},{28,12},{1,17},{... | collective-permute-start | bytes 786440 | tf_op jit(solution)/shard_map/ppermute | solution.py:30
  122.4 23.6 %collective-permute-start.31 = (bf16[512,512]{1,0:T(8,128)(2,1)S(1)}, bf16[512,512]{1,0:T(8,128)(2,1)S(1)}, u32[]{:S(2)}, u32[]{:S(2)}) collective-permute-start(bf16[512,512]{1,0:T(8,128)(2,1)S(1)} %shard_map.282), channel_id=1, source_target_pairs={{0,8},{4,12},{8,0},{12,4},{16,24},{20,28},{24,16},{28,20},{1,9},{5... | collective-permute-start | bytes 1572872 | tf_op jit(solution)/shard_map/ppermute | solution.py:30
  125.1 14.8 %collective-permute-start.28 = (bf16[512,512]{1,0:T(8,128)(2,1)S(1)}, bf16[512,512]{1,0:T(8,128)(2,1)S(1)}, u32[]{:S(2)}, u32[]{:S(2)}) collective-permute-start(bf16[512,512]{1,0:T(8,128)(2,1)S(1)} %shard_map.281), channel_id=1, source_target_pairs={{0,4},{4,0},{8,12},{12,8},{16,20},{20,16},{24,28},{28,24},{1,5},{5... | collective-permute-start | bytes 1572872 | tf_op jit(solution)/shard_map/ppermute | solution.py:30
  138.8 18.4 %collective-permute-start.33 = (bf16[128,1024]{1,0:T(8,128)(2,1)S(1)}, bf16[128,1024]{1,0:T(8,128)(2,1)S(1)}, u32[]{:S(2)}, u32[]{:S(2)}) collective-permute-start(bf16[128,1024]{1,0:T(8,128)(2,1)S(1)} %shard_map.287), channel_id=1, source_target_pairs={{0,16},{4,20},{8,24},{12,28},{16,0},{20,4},{24,8},{28,12},{1,17},{... | collective-permute-start | bytes 786440 | tf_op jit(solution)/shard_map/ppermute | solution.py:30
  139.8 50.2 %collective-permute-start.27 = (bf16[240,1024]{1,0:T(8,128)(2,1)S(1)}, bf16[240,1024]{1,0:T(8,128)(2,1)S(1)}, u32[]{:S(2)}, u32[]{:S(2)}) collective-permute-start(bf16[240,1024]{1,0:T(8,128)(2,1)S(1)} %get-tuple-element.215), channel_id=1, source_target_pairs={{0,1},{1,0},{2,3},{3,2},{4,5},{5,4},{6,7},{7,6},{8,9},{9,8},{10,11... | collective-permute-start | bytes 1474568 | tf_op jit(solution)/shard_map/ppermute | solution.py:30
  146.0 17.3 %collective-permute-start.30 = (bf16[256,512]{1,0:T(8,128)(2,1)S(1)}, bf16[256,512]{1,0:T(8,128)(2,1)S(1)}, u32[]{:S(2)}, u32[]{:S(2)}) collective-permute-start(bf16[256,512]{1,0:T(8,128)(2,1)S(1)} %get-tuple-element.220), channel_id=1, source_target_pairs={{0,8},{4,12},{8,0},{12,4},{16,24},{20,28},{24,16},{28,20},{1,9},{5... | collective-permute-start | bytes 786440 | tf_op jit(solution)/shard_map/ppermute | solution.py:30
  146.1 11.2 %collective-permute-start.32 = (bf16[256,512]{1,0:T(8,128)(2,1)S(1)}, bf16[256,512]{1,0:T(8,128)(2,1)S(1)}, u32[]{:S(2)}, u32[]{:S(2)}) collective-permute-start(bf16[256,512]{1,0:T(8,128)(2,1)S(1)} %get-tuple-element.223), channel_id=1, source_target_pairs={{0,4},{4,0},{8,12},{12,8},{16,20},{20,16},{24,28},{28,24},{1,5},{5... | collective-permute-start | bytes 786440 | tf_op jit(solution)/shard_map/ppermute | solution.py:30
  146.9 20.9 %collective-permute-start.37 = (bf16[128,1024]{1,0:T(8,128)(2,1)S(1)}, bf16[128,1024]{1,0:T(8,128)(2,1)S(1)}, u32[]{:S(2)}, u32[]{:S(2)}) collective-permute-start(bf16[128,1024]{1,0:T(8,128)(2,1)S(1)} %shard_map.290), channel_id=1, source_target_pairs={{0,16},{4,20},{8,24},{12,28},{16,0},{20,4},{24,8},{28,12},{1,17},{... | collective-permute-start | bytes 786440 | tf_op jit(solution)/shard_map/ppermute | solution.py:30
  157.3 23.5 %collective-permute-start.43 = (bf16[256,1024]{1,0:T(8,128)(2,1)S(1)}, bf16[256,1024]{1,0:T(8,128)(2,1)S(1)}, u32[]{:S(2)}, u32[]{:S(2)}) collective-permute-start(bf16[256,1024]{1,0:T(8,128)(2,1)S(1)} %pad_maximum_fusion.2), channel_id=1, source_target_pairs={{0,8},{4,12},{8,0},{12,4},{16,24},{20,28},{24,16},{28,20},{1,9},{5... | collective-permute-start | bytes 1572872 | tf_op jit(solution)/shard_map/ppermute | solution.py:30
  157.4 17.1 %collective-permute-start.36 = (bf16[128,512]{1,0:T(8,128)(2,1)S(1)}, bf16[128,512]{1,0:T(8,128)(2,1)S(1)}, u32[]{:S(2)}, u32[]{:S(2)}) collective-permute-start(bf16[128,512]{1,0:T(8,128)(2,1)S(1)} %get-tuple-element.227), channel_id=1, source_target_pairs={{0,16},{4,20},{8,24},{12,28},{16,0},{20,4},{24,8},{28,12},{1,17},{... | collective-permute-start | bytes 393224 | tf_op jit(solution)/shard_map/ppermute | solution.py:30
  163.3 14.7 %collective-permute-start.35 = (bf16[128,512]{1,0:T(8,128)(2,1)S(1)}, bf16[128,512]{1,0:T(8,128)(2,1)S(1)}, u32[]{:S(2)}, u32[]{:S(2)}) collective-permute-start(bf16[128,512]{1,0:T(8,128)(2,1)S(1)} %get-tuple-element.231), channel_id=1, source_target_pairs={{0,16},{4,20},{8,24},{12,28},{16,0},{20,4},{24,8},{28,12},{1,17},{... | collective-permute-start | bytes 393224 | tf_op jit(solution)/shard_map/ppermute | solution.py:30
  167.9 13.1 %collective-permute-start.42 = (bf16[256,1024]{1,0:T(8,128)(2,1)S(1)}, bf16[256,1024]{1,0:T(8,128)(2,1)S(1)}, u32[]{:S(2)}, u32[]{:S(2)}) collective-permute-start(bf16[256,1024]{1,0:T(8,128)(2,1)S(1)} %pad_maximum_fusion.3), channel_id=1, source_target_pairs={{0,4},{4,0},{8,12},{12,8},{16,20},{20,16},{24,28},{28,24},{1,5},{5... | collective-permute-start | bytes 1572872 | tf_op jit(solution)/shard_map/ppermute | solution.py:30
  180.9 30.1 %collective-permute-start.49 = (bf16[512,1024]{1,0:T(8,128)(2,1)S(1)}, bf16[512,1024]{1,0:T(8,128)(2,1)S(1)}, u32[]{:S(2)}, u32[]{:S(2)}) collective-permute-start(bf16[512,1024]{1,0:T(8,128)(2,1)S(1)} %pad_maximum_fusion.refs_0_), channel_id=1, source_target_pairs={{0,4},{4,0},{8,12},{12,8},{16,20},{20,16},{24,28},{28,24},{1,5},{5... | collective-permute-start | bytes 3145736 | tf_op jit(solution)/shard_map/ppermute | solution.py:30
  182.6 27.8 %collective-permute-start.45 = (bf16[256,512]{1,0:T(8,128)(2,1)S(1)}, bf16[256,512]{1,0:T(8,128)(2,1)S(1)}, u32[]{:S(2)}, u32[]{:S(2)}) collective-permute-start(bf16[256,512]{1,0:T(8,128)(2,1)S(1)} %pad_maximum_fusion.7), channel_id=1, source_target_pairs={{0,4},{4,0},{8,12},{12,8},{16,20},{20,16},{24,28},{28,24},{1,5},{5... | collective-permute-start | bytes 786440 | tf_op jit(solution)/shard_map/ppermute | solution.py:30
  184.5 26.0 %collective-permute-start.44 = (bf16[288,512]{1,0:T(8,128)(2,1)S(1)}, bf16[288,512]{1,0:T(8,128)(2,1)S(1)}, u32[]{:S(2)}, u32[]{:S(2)}) collective-permute-start(bf16[288,512]{1,0:T(8,128)(2,1)S(1)} %pad_maximum_fusion.6), channel_id=1, source_target_pairs={{0,8},{4,12},{8,0},{12,4},{16,24},{20,28},{24,16},{28,20},{1,9},{5... | collective-permute-start | bytes 884744 | tf_op jit(solution)/shard_map/ppermute | solution.py:30
  191.1 24.2 %collective-permute-start.48 = (bf16[512,1024]{1,0:T(8,128)(2,1)S(1)}, bf16[512,1024]{1,0:T(8,128)(2,1)S(1)}, u32[]{:S(2)}, u32[]{:S(2)}) collective-permute-start(bf16[512,1024]{1,0:T(8,128)(2,1)S(1)} %pad_maximum_fusion.1.refs_0_), channel_id=1, source_target_pairs={{0,8},{4,12},{8,0},{12,4},{16,24},{20,28},{24,16},{28,20},{1,9},{5... | collective-permute-start | bytes 3145736 | tf_op jit(solution)/shard_map/ppermute | solution.py:30
  210.4 14.0 %collective-permute-start.47 = (bf16[512,512]{1,0:T(8,128)(2,1)S(1)}, bf16[512,512]{1,0:T(8,128)(2,1)S(1)}, u32[]{:S(2)}, u32[]{:S(2)}) collective-permute-start(bf16[512,512]{1,0:T(8,128)(2,1)S(1)} %pad_maximum_fusion.4.refs_2_), channel_id=1, source_target_pairs={{0,8},{4,12},{8,0},{12,4},{16,24},{20,28},{24,16},{28,20},{1,9},{5... | collective-permute-start | bytes 1572872 | tf_op jit(solution)/shard_map/ppermute | solution.py:30
  210.6 13.8 %collective-permute-start.46 = (bf16[544,512]{1,0:T(8,128)(2,1)S(1)}, bf16[544,512]{1,0:T(8,128)(2,1)S(1)}, u32[]{:S(2)}, u32[]{:S(2)}) collective-permute-start(bf16[544,512]{1,0:T(8,128)(2,1)S(1)} %fusion.14), channel_id=1, source_target_pairs={{0,4},{4,0},{8,12},{12,8},{16,20},{20,16},{24,28},{28,24},{1,5},{5... | collective-permute-start | bytes 1671176 | tf_op jit(solution)/shard_map/ppermute | solution.py:30
  (29 other events, 172.6 us)

commit v6 on v5

--- a/solution.py
+++ b/solution.py
@@ -549,40 +549,61 @@
         row -= part.shape[0]
 
 
-def place_mixed(order, other, me, *refs):
-    count = (len(refs) - 5) // 2
-    first, second = refs[:count], refs[count : 2 * count]
-    in_out, out_out, wide, flat, sems = refs[2 * count :]
+def place_half(half, count, order, other, me, first, second, *refs):
+    in_out, out_out, wide, flat, sems = refs[count:]
     piece = in_out.shape[0] // PIECES
-    half = out_out.shape[0] // 2
-    split = first[0].shape[1]
+    middle = out_out.shape[0] // 2
+    split = first.shape[1]
     rest = in_out.shape[1] - split
     copies = []
-    for i in range(PIECES):
-        place = piece_of(i, order, me[1])
+    for i in range(PIECES // 2):
+        part = pl.ds(i * piece, piece)
+        place = piece_of(half * PIECES // 2 + i, order, me[1])
         to = pl.ds(pl.multiple_of(place * piece, piece), piece)
-        part, row = locate(first, i * piece)
-        wide[i, :, :split] = part[row : row + piece, :].astype(F32)
+        wide[i, :, :split] = first[part, :].astype(F32)
         copies.append(
-            pltpu.make_async_copy(wide.at[i, :, :split], in_out.at[to, :split], sems.at[i])
+            pltpu.make_async_copy(wide.at[i, :, :split], in_out.at[to, :split], sems.at[3 * i])
         )
         copies[-1].start()
-        place = piece_of(i, other, me[1])
+        place = piece_of(half * PIECES // 2 + i, other, me[1])
         to = pl.ds(pl.multiple_of(place * piece, piece), piece)
-        part, row = locate(second, i * piece)
-        wide[i, :, split:] = part[row : row + piece, :rest].astype(F32)
-        flat[i, :half, :] = part[row : row + piece, rest : rest + half].astype(F32)
-        flat[i, half:, :] = part[row : row + piece, rest + half :].astype(F32)
+        wide[i, :, split:] = second[part, :rest].astype(F32)
+        flat[i, :middle, :] = second[part, rest : rest + middle].astype(F32)
+        flat[i, middle:, :] = second[part, rest + middle :].astype(F32)
         copies.append(
-            pltpu.make_async_copy(wide.at[i, :, split:], in_out.at[to, split:], sems.at[PIECES + i])
+            pltpu.make_async_copy(wide.at[i, :, split:], in_out.at[to, split:], sems.at[3 * i + 1])
         )
         copies[-1].start()
         copies.append(
-            pltpu.make_async_copy(flat.at[i], out_out.at[:, to], sems.at[2 * PIECES + i])
+            pltpu.make_async_copy(flat.at[i], out_out.at[:, to], sems.at[3 * i + 2])
         )
         copies[-1].start()
     for copy in copies:
         copy.wait()
+
+
+def place_mixed(me, half, first, second, outs, into=()):
+    ins = [pltpu.with_memory_space_constraint(x, pltpu.VMEM) for x in (first, second)]
+    half_pieces = PIECES // 2
+    tall, wide = outs[0].shape
+    return pl.pallas_call(
+        functools.partial(place_half, half, len(into), ORDER_A, ORDER_B),
+        out_shape=[pltpu.HBM(x.shape, x.dtype) for x in outs],
+        in_specs=[pl.BlockSpec(memory_space=pltpu.SMEM)]
+        + [pl.BlockSpec(memory_space=pltpu.VMEM)] * 2
+        + [pl.BlockSpec(memory_space=pltpu.HBM)] * len(into),
+        out_specs=[pl.BlockSpec(memory_space=pltpu.HBM)] * 2,
+        scratch_shapes=[
+            pltpu.VMEM((half_pieces, tall // PIECES, wide), F32),
+            pltpu.VMEM((half_pieces, outs[1].shape[0], tall // PIECES), F32),
+            pltpu.SemaphoreType.DMA((3 * half_pieces,)),
+        ],
+        input_output_aliases={3: 0, 4: 1} if into else {},
+        compiler_params=pltpu.CompilerParams(vmem_limit_bytes=16 * MIB),
+        cost_estimate=pl.CostEstimate(
+            flops=int(1e9 * WEIGHT), bytes_accessed=0, transcendentals=0
+        ),
+    )(me, *ins, *into)
 
 
 def piece_of(position, order, me):
@@ -1010,27 +1031,20 @@
     now = up.arrive(now)
     now = mixed.arrive(now)
     now = first.arrive(now)
+    now = first.arrive(now)
     now = mixed.arrive(now)
-    now = first.arrive(now)
     now = down.arrive(now)
     down_sum = place(after(me, now), down.parts, ORDER_A)
     up.arrive(down_sum)
     up_sum = place(me, up.parts, ORDER_B)
-    now = mixed.arrive(up_sum)
+    outs = [shape((model, 3 * width)), shape((width, model))]
+    into = place_mixed(after(me, up_sum), 0, first.values, mixed.values, outs)
+    now = mixed.arrive(into[1])
     first.arrive(now)
     small = unpack(first.small)
     small = jnp.concatenate([small[:8], small[8:]], axis=1)
     piece = model // PIECES
-    in_sum, out_sum = run_out(
-        functools.partial(place_mixed, ORDER_A, ORDER_B),
-        (me, *first.parts, *mixed.parts),
-        [shape((model, 3 * width)), shape((width, model))],
-        scratch=[
-            pltpu.VMEM((PIECES, piece, 3 * width), F32),
-            pltpu.VMEM((PIECES, width, piece), F32),
-            pltpu.SemaphoreType.DMA((3 * PIECES,)),
-        ],
-    )
+    in_sum, out_sum = place_mixed(me, 1, first.parts[1], mixed.parts[1], outs, into)
     in_bias_sum = small[7, : 2 * width].reshape(2, heads, HD).transpose(1, 0, 2).reshape(-1)
     return (
         output,

time: 229 us -> 228 us (level)
  waiting for transfers between devices: 72.5 us -> 67.7 us
  starting transfers between devices: 56.4 us -> 59.2 us
    ppermute x50, waiting for transfers between devices: 72.5 us -> 67.7 us  [swap(): return lax.ppermute(values, axis, [(i, i ^ bit) for i in range(count)])]
    pallas_call x0 -> x2, Pallas kernels: none -> 3.93 us  [place_mixed(): pl.pallas_call(functools.partial(place_half, half, len(into), ORDER_A, OR...]
    ppermute x50, starting transfers between devices: 56.4 us -> 59.2 us  [swap(): return lax.ppermute(values, axis, [(i, i ^ bit) for i in range(count)])]
    pallas_call x3 -> x2, Pallas kernels: 8.04 us -> 5.29 us  [run_out(): pl.pallas_call(body, out_shape=[pltpu.HBM(x.shape, x.dtype) for x in outs...]
  transfers between devices with their start and end apart: 50 -> 50, of which waited for: 22 -> 22; matrix products, arithmetic and copies ran while one was open for 3% -> 3% of each run, Pallas kernels for 35% -> 36%
where the time goes in v6:
time: 228 us
  Pallas kernels  89.1 us (39%)
  waiting for transfers between devices  67.7 us (30%)
  starting transfers between devices  59.2 us (26%)
  local copies, waits for them, and re-layouts  6.21 us (3%)
  other arithmetic  4.24 us (2%)
    pallas_call x41, Pallas kernels, run(): pl.pallas_call(kernel, out_shape=[pltpu.VMEM(x.shape, x.dtype) for x in o...  79.9 us
    ppermute x50, waiting for transfers between devices, swap(): return lax.ppermute(values, axis, [(i, i ^ bit) for i in range(count)])  67.7 us
    ppermute x50, starting transfers between devices, swap(): return lax.ppermute(values, axis, [(i, i ^ bit) for i in range(count)])  59.2 us
    pallas_call x2, Pallas kernels, run_out(): pl.pallas_call(body, out_shape=[pltpu.HBM(x.shape, x.dtype) for x in outs...  5.29 us
  transfers between devices with their start and end apart: 50, of which 22 were waited for; matrix products, arithmetic and copies ran while one was open for 3% of the time, Pallas kernels for 36%

profile of v6, /device:TPU:0, one launch (start us, length us, event | category | flops | bytes accessed | tf_op | source)
XLA Modules:
  0.0 227.8 jit_solution(4048582610483084899)
XLA Ops:
  0.6 3.0 %collective-permute-start.2 = (bf16[240,1024]{1,0:T(8,128)(2,1)}, bf16[240,1024]{1,0:T(8,128)(2,1)S(1)}, u32[]{:S(2)}, u32[]{:S(2)}) collective-permute-start(bf16[240,1024]{1,0:T(8,128)(2,1)} %refs_4_.13), channel_id=1, source_target_pairs={{0,2},{1,3},{2,0},{3,1},{4,6},{5,7},{6,4},{7,5},{8,10},{9,11},{10,... | collective-permute-start | bytes 1474568 | tf_op jit(solution)/shard_map/ppermute | solution.py:30
  10.1 4.1 %shard_map.254 = (bf16[480,1024]{1,0:T(8,128)(2,1)S(1)}, bf16[480,768]{1,0:T(8,128)(2,1)S(1)}) custom-call(s32[2]{0:T(128)S(1)} %pad_add_fusion.refs_0_.me, bf16[240,1024]{1,0:T(8,128)(2,1)S(1)} %copy-done.3, bf16[240,1024]{1,0:T(8,128)(2,1)S(1)} %collective-permute-done.1.refs_2_, ...), custom_call_target="tpu_custom_call" | custom-call | flops 15099494400 | tf_op jit(solution)/shard_map/pallas_call | solution.py:63
  19.1 7.4 %shard_map.256 = (bf16[240,1024]{1,0:T(8,128)(2,1)S(1)}, bf16[960,768]{1,0:T(8,128)(2,1)S(1)}, bf16[12,160,320]{2,1,0:T(8,128)(2,1)S(1)}, bf16[480,256]{1,0:T(8,...) custom-call(s32[2]{0:T(128)S(1)} %pad_add_fusion.refs_0_.me, ...), custom_call_target="tpu_custom_call" | custom-call | flops 26424115200 | tf_op jit(solution)/shard_map/pallas_call | solution.py:63
  30.7 5.6 %shard_map.258 = (bf16[12,160,320]{2,1,0:T(8,128)(2,1)S(1)}, bf16[480,256]{1,0:T(8,128)(2,1)S(1)}, bf16[240,1024]{1,0:T(8,128)(2,1)S(1)}, f32[240,1024]{1,0:T(8,128)S(1)}) custom-call(s32[2]{0:T(128)S(1)} %pad_add_fusion.refs_0_.me, bf16[960,768]{1,0:T(8,128)(2,1)S(1)} %get-tuple-element.143.refs_11_.refs_1_.refs_12_.refs_13_.refs_15_.refs_16_.refs_3_, ...), custom_call_target="tpu_custom_call" | custom-call | flops 11324620800 | tf_op jit(solution)/shard_map/pallas_call | solution.py:63
  36.4 2.5 %shard_map.259.refs_19_.refs_5_ = f32[480,1024]{1,0:T(8,128)S(1)} custom-call(s32[2]{0:T(128)S(1)} %pad_add_fusion.refs_0_.me, bf16[240,1024]{1,0:T(8,128)(2,1)S(1)} %multiply_convert_fusion.1.refs_6_.refs_10_.refs_7_.refs_1_.refs_8_.refs_4_.refs_11_.refs_5_.refs_9_.refs_14_.refs_3_, ...), custom_call_target="tpu_custom_call" | custom-call | flops 20132659200 | tf_op jit(solution)/shard_map/pallas_call | solution.py:63
  38.9 3.1 %collective-permute-done.7.refs_4_ = bf16[240,1024]{1,0:T(8,128)(2,1)S(1)} collective-permute-done((bf16[240,1024]{1,0:T(8,128)(2,1)S(1)}, bf16[240,1024]{1,0:T(8,128)(2,1)S(1)}, u32[]{:S(2)}, u32[]{:S(2)}) %collective-permute-start.7) | collective-permute-done | bytes 491552 | tf_op jit(solution)/shard_map/ppermute | solution.py:30
  45.8 4.6 %shard_map.261 = (bf16[480,1024]{1,0:T(8,128)(2,1)S(1)}, bf16[480,1024]{1,0:T(8,128)(2,1)S(1)}, f32[1,1024]{1,0:T(1,128)S(1)}, f32[240,1024]{1,0:T(8,128)S(1)}, bf16[240,1024]{1,0:T(8,128)(2,1)S(1)}) custom-call(s32[2]{0:T(128)S(1)} %pad_add_fusion.refs_0_.me, bf16[240,1024]{1,0:T(8,128)(2,1)S(1)} %get-tuple-element.158.refs_1_.refs_20_.refs_22_.refs_19_.refs_18_, ...), custom_call_target="tpu_custom_call" | custom-call | flops 40265318400 | tf_op jit(solution)/shard_map/pallas_call | solution.py:63
  50.5 2.5 %shard_map.262.refs_4_.refs_27_ = f32[480,1024]{1,0:T(8,128)S(1)} custom-call(s32[2]{0:T(128)S(1)} %pad_add_fusion.refs_0_.me, bf16[240,1024]{1,0:T(8,128)(2,1)S(1)} %collective-permute-done.5.refs_1_.refs_25_.refs_6_.refs_26_.refs_24_, bf16[240,1024]{1,0:T(8,128)(2,1)S(1)} %collective-permute-done.9.refs_2_.refs_26_.refs_7_.refs_27_.refs_25_, ...), custom_call_target="tpu_custom_call" | custom-call | flops 20132659200 | tf_op jit(solution)/shard_map/pallas_call | solution.py:63
  53.0 4.5 %collective-permute-done.8.refs_1_.refs_29_.refs_30_.refs_27_.refs_3_.refs_28_.refs_26_.refs_23_ = bf16[240,1024]{1,0:T(8,128)(2,1)S(1)} collective-permute-done((bf16[240,1024]{1,0:T(8,128)(2,1)S(1)}, bf16[240,1024]{1,0:T(8,128)(2,1)S(1)}, u32[]{:S(2)}, u32[]{:S(2)}) %collective-permute-start.8) | collective-permute-done | bytes 491552 | tf_op jit(solution)/shard_map/ppermute | solution.py:30
  57.5 2.8 %shard_map.263 = (bf16[240,1024]{1,0:T(8,128)(2,1)S(1)}, bf16[240,1024]{1,0:T(8,128)(2,1)S(1)}, f32[1,1024]{1,0:T(1,128)S(1)}, f32[240,1024]{1,0:T(8,128)S(1)}) custom-call(s32[2]{0:T(128)S(1)} %pad_add_fusion.refs_0_.me, bf16[240,1024]{1,0:T(8,128)(2,1)S(1)} %collective-permute-done.8.refs_1_.refs_29_.refs_30_.refs_27_.refs_3_.refs_28_.refs_26_.refs_23_, ...), custom_call_target="tpu_custom_call" | custom-call | flops 20132659200 | tf_op jit(solution)/shard_map/pallas_call | solution.py:63
  60.2 2.8 %shard_map.264 = (bf16[240,1024]{1,0:T(8,128)(2,1)S(1)}, bf16[240,1024]{1,0:T(8,128)(2,1)S(1)}, f32[1,1024]{1,0:T(1,128)S(1)}, bf16[240,1024]{1,0:T(8,128)(2,1)S(1)}) custom-call(s32[2]{0:T(128)S(1)} %pad_add_fusion.refs_0_.me, bf16[240,1024]{1,0:T(8,128)(2,1)S(1)} %collective-permute-done.11.refs_1_.refs_29_.refs_4_.refs_31_.refs_28_.refs_25_, ...), custom_call_target="tpu_custom_call" | custom-call | flops 20132659200 | tf_op jit(solution)/shard_map/pallas_call | solution.py:63
  66.8 2.8 %shard_map.266 = bf16[512,1024]{1,0:T(8,128)(2,1)S(1)} custom-call(s32[2]{0:T(128)S(1)} %pad_add_fusion.refs_0_.me, bf16[480,1024]{1,0:T(8,128)(2,1)S(1)} %get-tuple-element.160.refs_21_.refs_1_.refs_24_.refs_20_.refs_19_.refs_22_.refs_17_.refs_14_.refs_13_.refs_10_, bf16[240,1024]{1,0:T(8,128)(2,1)S(1)} %get-tuple-element.165.refs_27_.refs_28_.refs_2_.refs_1_.refs_26_, ...), custom_call_target="tpu_custom_call" | custom-call | flops 20132659200 | tf_op jit(solution)/shard_map/pallas_call | solution.py:63
  69.6 2.9 %shard_map.267 = bf16[512,1024]{1,0:T(8,128)(2,1)S(1)} custom-call(s32[2]{0:T(128)S(1)} %pad_add_fusion.refs_0_.me, bf16[240,1024]{1,0:T(8,128)(2,1)S(1)} %get-tuple-element.158.refs_1_.refs_20_.refs_22_.refs_19_.refs_18_, bf16[240,1024]{1,0:T(8,128)(2,1)S(1)} %collective-permute-done.10.refs_2_.refs_24_.refs_25_.refs_23_.refs_21_, ...), custom_call_target="tpu_custom_call" | custom-call | flops 20132659200 | tf_op jit(solution)/shard_map/pallas_call | solution.py:63
  82.6 2.8 %shard_map.270.refs_27_.refs_25_.refs_1_ = f32[512,1024]{1,0:T(8,128)S(1)} custom-call(s32[2]{0:T(128)S(1)} %pad_add_fusion.refs_0_.me, bf16[480,1024]{1,0:T(8,128)(2,1)S(1)} %get-tuple-element.160.refs_21_.refs_1_.refs_24_.refs_20_.refs_19_.refs_22_.refs_17_.refs_14_.refs_13_.refs_10_, ...), custom_call_target="tpu_custom_call" | custom-call | flops 20132659200 | tf_op jit(solution)/shard_map/pallas_call | solution.py:63
  85.4 6.6 %shard_map.271 = (f32[480,256]{1,0:T(8,128)S(1)}, f32[960,512]{1,0:T(8,128)S(1)}) custom-call(s32[2]{0:T(128)S(1)} %pad_add_fusion.refs_0_.me, bf16[240,1024]{1,0:T(8,128)(2,1)S(1)} %get-tuple-element.176.refs_30_.refs_1_.refs_24_.refs_19_.refs_21_.refs_16_.refs_15_.refs_8_, ...), custom_call_target="tpu_custom_call" | custom-call | flops 20761804800 | tf_op jit(solution)/shard_map/pallas_call | solution.py:63
  92.1 2.7 %shard_map.272.refs_23_.refs_1_ = f32[512,1024]{1,0:T(8,128)S(1)} custom-call(s32[2]{0:T(128)S(1)} %pad_add_fusion.refs_0_.me, bf16[240,1024]{1,0:T(8,128)(2,1)S(1)} %get-tuple-element.158.refs_1_.refs_20_.refs_22_.refs_19_.refs_18_, bf16[240,1024]{1,0:T(8,128)(2,1)S(1)} %collective-permute-done.10.refs_2_.refs_24_.refs_25_.refs_23_.refs_21_, ...), custom_call_target="tpu_custom_call" | custom-call | flops 20132659200 | tf_op jit(solution)/shard_map/pallas_call | solution.py:63
  101.5 8.1 %shard_map.275 = (bf16[480,768]{1,0:T(8,128)(2,1)S(1)}, bf16[480,768]{1,0:T(8,128)(2,1)S(1)}, f32[1,512]{1,0:T(1,128)S(1)}, bf16[240,1024]{1,0:T(8,128)(2,1)S(1)}, f32[240,1024]{1,0:T(8,128)S(1)}) custom-call(s32[2]{0:T(128)S(1)} %pad_add_fusion.refs_0_.me, ...), custom_call_target="tpu_custom_call" | custom-call | flops 35861299200 | tf_op jit(solution)/shard_map/pallas_call | solution.py:63
  109.6 2.6 %collective-permute-done.24.refs_2_ = bf16[256,1024]{1,0:T(8,128)(2,1)S(1)} collective-permute-done((bf16[256,1024]{1,0:T(8,128)(2,1)S(1)}, bf16[256,1024]{1,0:T(8,128)(2,1)S(1)}, u32[]{:S(2)}, u32[]{:S(2)}) %collective-permute-start.24) | collective-permute-done | bytes 524320 | tf_op jit(solution)/shard_map/ppermute | solution.py:30
  113.8 2.7 %collective-permute-start.34 = (bf16[128,1024]{1,0:T(8,128)(2,1)S(1)}, bf16[128,1024]{1,0:T(8,128)(2,1)S(1)}, u32[]{:S(2)}, u32[]{:S(2)}) collective-permute-start(bf16[128,1024]{1,0:T(8,128)(2,1)S(1)} %get-tuple-element.205), channel_id=1, source_target_pairs={{0,16},{4,20},{8,24},{12,28},{16,0},{20,4},{24,8},{28,12},{1,17},{... | collective-permute-start | bytes 786440 | tf_op jit(solution)/shard_map/ppermute | solution.py:30
  131.6 6.5 %collective-permute-done.29.refs_2_ = bf16[128,1024]{1,0:T(8,128)(2,1)S(1)} collective-permute-done((bf16[128,1024]{1,0:T(8,128)(2,1)S(1)}, bf16[128,1024]{1,0:T(8,128)(2,1)S(1)}, u32[]{:S(2)}, u32[]{:S(2)}) %collective-permute-start.29) | collective-permute-done | bytes 262176 | tf_op jit(solution)/shard_map/ppermute | solution.py:30
  139.9 6.1 %collective-permute-done.31.refs_2_ = bf16[512,512]{1,0:T(8,128)(2,1)S(1)} collective-permute-done((bf16[512,512]{1,0:T(8,128)(2,1)S(1)}, bf16[512,512]{1,0:T(8,128)(2,1)S(1)}, u32[]{:S(2)}, u32[]{:S(2)}) %collective-permute-start.31) | collective-permute-done | bytes 524320 | tf_op jit(solution)/shard_map/ppermute | solution.py:30
  147.0 9.3 %collective-permute-start.37 = (bf16[128,1024]{1,0:T(8,128)(2,1)S(1)}, bf16[128,1024]{1,0:T(8,128)(2,1)S(1)}, u32[]{:S(2)}, u32[]{:S(2)}) collective-permute-start(bf16[128,1024]{1,0:T(8,128)(2,1)S(1)} %shard_map.290), channel_id=1, source_target_pairs={{0,16},{4,20},{8,24},{12,28},{16,0},{20,4},{24,8},{28,12},{1,17},{... | collective-permute-start | bytes 786440 | tf_op jit(solution)/shard_map/ppermute | solution.py:30
  157.4 3.8 %collective-permute-start.36 = (bf16[128,512]{1,0:T(8,128)(2,1)S(1)}, bf16[128,512]{1,0:T(8,128)(2,1)S(1)}, u32[]{:S(2)}, u32[]{:S(2)}) collective-permute-start(bf16[128,512]{1,0:T(8,128)(2,1)S(1)} %get-tuple-element.230), channel_id=1, source_target_pairs={{0,16},{4,20},{8,24},{12,28},{16,0},{20,4},{24,8},{28,12},{1,17},{... | collective-permute-start | bytes 393224 | tf_op jit(solution)/shard_map/ppermute | solution.py:30
  163.3 4.5 %collective-permute-start.35 = (bf16[128,512]{1,0:T(8,128)(2,1)S(1)}, bf16[128,512]{1,0:T(8,128)(2,1)S(1)}, u32[]{:S(2)}, u32[]{:S(2)}) collective-permute-start(bf16[128,512]{1,0:T(8,128)(2,1)S(1)} %get-tuple-element.234), channel_id=1, source_target_pairs={{0,16},{4,20},{8,24},{12,28},{16,0},{20,4},{24,8},{28,12},{1,17},{... | collective-permute-start | bytes 393224 | tf_op jit(solution)/shard_map/ppermute | solution.py:30
  168.5 6.1 %collective-permute-done.36.refs_2_ = bf16[128,512]{1,0:T(8,128)(2,1)S(1)} collective-permute-done((bf16[128,512]{1,0:T(8,128)(2,1)S(1)}, bf16[128,512]{1,0:T(8,128)(2,1)S(1)}, u32[]{:S(2)}, u32[]{:S(2)}) %collective-permute-start.36) | collective-permute-done | bytes 131104 | tf_op jit(solution)/shard_map/ppermute | solution.py:30
  174.6 3.4 %collective-permute-start.41 = (bf16[128,512]{1,0:T(8,128)(2,1)S(1)}, bf16[128,512]{1,0:T(8,128)(2,1)S(1)}, u32[]{:S(2)}, u32[]{:S(2)}) collective-permute-start(bf16[128,512]{1,0:T(8,128)(2,1)S(1)} %shard_map.293), channel_id=1, source_target_pairs={{0,16},{4,20},{8,24},{12,28},{16,0},{20,4},{24,8},{28,12},{1,17},{... | collective-permute-start | bytes 393224 | tf_op jit(solution)/shard_map/ppermute | solution.py:30
  184.6 6.7 %collective-permute-start.44 = (bf16[288,512]{1,0:T(8,128)(2,1)S(1)}, bf16[288,512]{1,0:T(8,128)(2,1)S(1)}, u32[]{:S(2)}, u32[]{:S(2)}) collective-permute-start(bf16[288,512]{1,0:T(8,128)(2,1)S(1)} %pad_maximum_fusion.6), channel_id=1, source_target_pairs={{0,8},{4,12},{8,0},{12,4},{16,24},{20,28},{24,16},{28,20},{1,9},{5... | collective-permute-start | bytes 884744 | tf_op jit(solution)/shard_map/ppermute | solution.py:30
  192.4 6.8 %collective-permute-done.44 = bf16[288,512]{1,0:T(8,128)(2,1)S(1)} collective-permute-done((bf16[288,512]{1,0:T(8,128)(2,1)S(1)}, bf16[288,512]{1,0:T(8,128)(2,1)S(1)}, u32[]{:S(2)}, u32[]{:S(2)}) %collective-permute-start.44) | collective-permute-done | bytes 294944 | tf_op jit(solution)/shard_map/ppermute | solution.py:30
  199.4 13.2 %collective-permute-done.46 = bf16[256,512]{1,0:T(8,128)(2,1)S(1)} collective-permute-done((bf16[256,512]{1,0:T(8,128)(2,1)S(1)}, bf16[256,512]{1,0:T(8,128)(2,1)S(1)}, u32[]{:S(2)}, u32[]{:S(2)}) %collective-permute-start.46) | collective-permute-done | bytes 262176 | tf_op jit(solution)/shard_map/ppermute | solution.py:30
  212.7 2.8 %collective-permute-start.47 = (bf16[512,512]{1,0:T(8,128)(2,1)S(1)}, bf16[512,512]{1,0:T(8,128)(2,1)S(1)}, u32[]{:S(2)}, u32[]{:S(2)}) collective-permute-start(bf16[512,512]{1,0:T(8,128)(2,1)S(1)} %pad_maximum_fusion.4.second), channel_id=1, source_target_pairs={{0,8},{4,12},{8,0},{12,4},{16,24},{20,28},{24,16},{28,20},{1,9},{5... | collective-permute-start | bytes 1572872 | tf_op jit(solution)/shard_map/ppermute | solution.py:30
  215.5 2.6 %shard_map.295 = f32[1024,1024]{1,0:T(8,128)} custom-call(s32[2]{0:T(128)S(1)} %pad_add_fusion.refs_0_.me, bf16[512,1024]{1,0:T(8,128)(2,1)S(1)} %pad_maximum_fusion.refs_0_, bf16[512,1024]{1,0:T(8,128)(2,1)S(1)} %collective-permute-done.49.refs_1_), custom_call_target="tpu_custom_call" | custom-call | flops 20000000000 | tf_op jit(solution)/shard_map/pallas_call | solution.py:96
  218.2 2.6 %shard_map.296 = f32[1024,1024]{1,0:T(8,128)} custom-call(s32[2]{0:T(128)S(1)} %pad_add_fusion.refs_0_.me, bf16[512,1024]{1,0:T(8,128)(2,1)S(1)} %pad_maximum_fusion.1.refs_0_, bf16[512,1024]{1,0:T(8,128)(2,1)S(1)} %collective-permute-done.48.refs_1_), custom_call_target="tpu_custom_call" | custom-call | flops 20000000000 | tf_op jit(solution)/shard_map/pallas_call | solution.py:96
  (180 shorter events, 77.9 us)
Async XLA Ops:
  0.6 14.5 %collective-permute-start.2 = (bf16[240,1024]{1,0:T(8,128)(2,1)}, bf16[240,1024]{1,0:T(8,128)(2,1)S(1)}, u32[]{:S(2)}, u32[]{:S(2)}) collective-permute-start(bf16[240,1024]{1,0:T(8,128)(2,1)} %refs_4_.13), channel_id=1, source_target_pairs={{0,2},{1,3},{2,0},{3,1},{4,6},{5,7},{6,4},{7,5},{8,10},{9,11},{10,... | collective-permute-start | bytes 1474568 | tf_op jit(solution)/shard_map/ppermute | solution.py:30
  15.1 13.6 %collective-permute-start.5 = (bf16[240,1024]{1,0:T(8,128)(2,1)S(1)}, bf16[240,1024]{1,0:T(8,128)(2,1)S(1)}, u32[]{:S(2)}, u32[]{:S(2)}) collective-permute-start(bf16[240,1024]{1,0:T(8,128)(2,1)S(1)} %multiply_convert_fusion.1.refs_6_.refs_10_.refs_7_.refs_1_.refs_8_.refs_4_.refs_11_.refs_5_.refs_9_.refs_14_, ...), channel_id=1, source_target_pairs={{0,2},{1,3},{2,0},{3,1},{4,6},{5,7},{6,4},{7,5},{8,10},{9,11},{10,... | collective-permute-start | bytes 1474568 | tf_op jit(solution)/shard_map/ppermute | solution.py:30
  28.9 13.1 %collective-permute-start.7 = (bf16[240,1024]{1,0:T(8,128)(2,1)S(1)}, bf16[240,1024]{1,0:T(8,128)(2,1)S(1)}, u32[]{:S(2)}, u32[]{:S(2)}) collective-permute-start(bf16[240,1024]{1,0:T(8,128)(2,1)S(1)} %shard_map.257), channel_id=1, source_target_pairs={{0,2},{1,3},{2,0},{3,1},{4,6},{5,7},{6,4},{7,5},{8,10},{9,11},{10,... | collective-permute-start | bytes 1474568 | tf_op jit(solution)/shard_map/ppermute | solution.py:30
  44.3 13.2 %collective-permute-start.8 = (bf16[240,1024]{1,0:T(8,128)(2,1)S(1)}, bf16[240,1024]{1,0:T(8,128)(2,1)S(1)}, u32[]{:S(2)}, u32[]{:S(2)}) collective-permute-start(bf16[240,1024]{1,0:T(8,128)(2,1)S(1)} %get-tuple-element.158.refs_1_.refs_20_.refs_22_.refs_19_.refs_18_), channel_id=1, source_target_pairs={{0,2},{1,3},{2,0},{3,1},{4,6},{5,7},{6,4},{7,5},{8,10},{9,11},{10,... | collective-permute-start | bytes 1474568 | tf_op jit(solution)/shard_map/ppermute | solution.py:30
  63.6 13.9 %collective-permute-start.13 = (bf16[240,1024]{1,0:T(8,128)(2,1)S(1)}, bf16[240,1024]{1,0:T(8,128)(2,1)S(1)}, u32[]{:S(2)}, u32[]{:S(2)}) collective-permute-start(bf16[240,1024]{1,0:T(8,128)(2,1)S(1)} %get-tuple-element.175), channel_id=1, source_target_pairs={{0,1},{1,0},{2,3},{3,2},{4,5},{5,4},{6,7},{7,6},{8,9},{9,8},{10,11... | collective-permute-start | bytes 1474568 | tf_op jit(solution)/shard_map/ppermute | solution.py:30
  65.2 13.6 %collective-permute-start.14 = (bf16[240,1024]{1,0:T(8,128)(2,1)S(1)}, bf16[240,1024]{1,0:T(8,128)(2,1)S(1)}, u32[]{:S(2)}, u32[]{:S(2)}) collective-permute-start(bf16[240,1024]{1,0:T(8,128)(2,1)S(1)} %shard_map.265), channel_id=1, source_target_pairs={{0,2},{1,3},{2,0},{3,1},{4,6},{5,7},{6,4},{7,5},{8,10},{9,11},{10,... | collective-permute-start | bytes 1474568 | tf_op jit(solution)/shard_map/ppermute | solution.py:30
  72.5 25.2 %collective-permute-start.19 = (bf16[512,1024]{1,0:T(8,128)(2,1)S(1)}, bf16[512,1024]{1,0:T(8,128)(2,1)S(1)}, u32[]{:S(2)}, u32[]{:S(2)}) collective-permute-start(bf16[512,1024]{1,0:T(8,128)(2,1)S(1)} %shard_map.267), channel_id=1, source_target_pairs={{0,8},{4,12},{8,0},{12,4},{16,24},{20,28},{24,16},{28,20},{1,9},{5... | collective-permute-start | bytes 3145736 | tf_op jit(solution)/shard_map/ppermute | solution.py:30
  74.2 24.9 %collective-permute-start.15 = (bf16[512,1024]{1,0:T(8,128)(2,1)S(1)}, bf16[512,1024]{1,0:T(8,128)(2,1)S(1)}, u32[]{:S(2)}, u32[]{:S(2)}) collective-permute-start(bf16[512,1024]{1,0:T(8,128)(2,1)S(1)} %shard_map.266), channel_id=1, source_target_pairs={{0,4},{4,0},{8,12},{12,8},{16,20},{20,16},{24,28},{28,24},{1,5},{5... | collective-permute-start | bytes 3145736 | tf_op jit(solution)/shard_map/ppermute | solution.py:30
  77.4 17.6 %collective-permute-start.22 = (bf16[240,1024]{1,0:T(8,128)(2,1)S(1)}, bf16[240,1024]{1,0:T(8,128)(2,1)S(1)}, u32[]{:S(2)}, u32[]{:S(2)}) collective-permute-start(bf16[240,1024]{1,0:T(8,128)(2,1)S(1)} %get-tuple-element.195), channel_id=1, source_target_pairs={{0,1},{1,0},{2,3},{3,2},{4,5},{5,4},{6,7},{7,6},{8,9},{9,8},{10,11... | collective-permute-start | bytes 1474568 | tf_op jit(solution)/shard_map/ppermute | solution.py:30
  81.0 13.8 %collective-permute-start.16 = (bf16[240,1024]{1,0:T(8,128)(2,1)S(1)}, bf16[240,1024]{1,0:T(8,128)(2,1)S(1)}, u32[]{:S(2)}, u32[]{:S(2)}) collective-permute-start(bf16[240,1024]{1,0:T(8,128)(2,1)S(1)} %get-tuple-element.176.refs_30_.refs_1_.refs_24_.refs_19_.refs_21_.refs_16_.refs_15_.refs_8_), channel_id=1, source_target_pairs={{0,2},{1,3},{2,0},{3,1},{4,6},{5,7},{6,4},{7,5},{8,10},{9,11},{10,... | collective-permute-start | bytes 1474568 | tf_op jit(solution)/shard_map/ppermute | solution.py:30
  95.1 18.3 %collective-permute-start.23 = (bf16[240,1024]{1,0:T(8,128)(2,1)S(1)}, bf16[240,1024]{1,0:T(8,128)(2,1)S(1)}, u32[]{:S(2)}, u32[]{:S(2)}) collective-permute-start(bf16[240,1024]{1,0:T(8,128)(2,1)S(1)} %shard_map.276), channel_id=1, source_target_pairs={{0,2},{1,3},{2,0},{3,1},{4,6},{5,7},{6,4},{7,5},{8,10},{9,11},{10,... | collective-permute-start | bytes 1474568 | tf_op jit(solution)/shard_map/ppermute | solution.py:30
  99.4 12.8 %collective-permute-start.24 = (bf16[256,1024]{1,0:T(8,128)(2,1)S(1)}, bf16[256,1024]{1,0:T(8,128)(2,1)S(1)}, u32[]{:S(2)}, u32[]{:S(2)}) collective-permute-start(bf16[256,1024]{1,0:T(8,128)(2,1)S(1)} %get-tuple-element.188), channel_id=1, source_target_pairs={{0,4},{4,0},{8,12},{12,8},{16,20},{20,16},{24,28},{28,24},{1,5},{5... | collective-permute-start | bytes 1572872 | tf_op jit(solution)/shard_map/ppermute | solution.py:30
  101.0 12.5 %collective-permute-start.18 = (bf16[256,1024]{1,0:T(8,128)(2,1)S(1)}, bf16[256,1024]{1,0:T(8,128)(2,1)S(1)}, u32[]{:S(2)}, u32[]{:S(2)}) collective-permute-start(bf16[256,1024]{1,0:T(8,128)(2,1)S(1)} %get-tuple-element.186), channel_id=1, source_target_pairs={{0,8},{4,12},{8,0},{12,4},{16,24},{20,28},{24,16},{28,20},{1,9},{5... | collective-permute-start | bytes 1572872 | tf_op jit(solution)/shard_map/ppermute | solution.py:30
  113.8 32.3 %collective-permute-start.34 = (bf16[128,1024]{1,0:T(8,128)(2,1)S(1)}, bf16[128,1024]{1,0:T(8,128)(2,1)S(1)}, u32[]{:S(2)}, u32[]{:S(2)}) collective-permute-start(bf16[128,1024]{1,0:T(8,128)(2,1)S(1)} %get-tuple-element.205), channel_id=1, source_target_pairs={{0,16},{4,20},{8,24},{12,28},{16,0},{20,4},{24,8},{28,12},{1,17},{... | collective-permute-start | bytes 786440 | tf_op jit(solution)/shard_map/ppermute | solution.py:30
  116.5 21.6 %collective-permute-start.29 = (bf16[128,1024]{1,0:T(8,128)(2,1)S(1)}, bf16[128,1024]{1,0:T(8,128)(2,1)S(1)}, u32[]{:S(2)}, u32[]{:S(2)}) collective-permute-start(bf16[128,1024]{1,0:T(8,128)(2,1)S(1)} %get-tuple-element.202), channel_id=1, source_target_pairs={{0,16},{4,20},{8,24},{12,28},{16,0},{20,4},{24,8},{28,12},{1,17},{... | collective-permute-start | bytes 786440 | tf_op jit(solution)/shard_map/ppermute | solution.py:30
  122.4 23.7 %collective-permute-start.31 = (bf16[512,512]{1,0:T(8,128)(2,1)S(1)}, bf16[512,512]{1,0:T(8,128)(2,1)S(1)}, u32[]{:S(2)}, u32[]{:S(2)}) collective-permute-start(bf16[512,512]{1,0:T(8,128)(2,1)S(1)} %shard_map.282), channel_id=1, source_target_pairs={{0,8},{4,12},{8,0},{12,4},{16,24},{20,28},{24,16},{28,20},{1,9},{5... | collective-permute-start | bytes 1572872 | tf_op jit(solution)/shard_map/ppermute | solution.py:30
  125.1 14.8 %collective-permute-start.28 = (bf16[512,512]{1,0:T(8,128)(2,1)S(1)}, bf16[512,512]{1,0:T(8,128)(2,1)S(1)}, u32[]{:S(2)}, u32[]{:S(2)}) collective-permute-start(bf16[512,512]{1,0:T(8,128)(2,1)S(1)} %shard_map.281), channel_id=1, source_target_pairs={{0,4},{4,0},{8,12},{12,8},{16,20},{20,16},{24,28},{28,24},{1,5},{5... | collective-permute-start | bytes 1572872 | tf_op jit(solution)/shard_map/ppermute | solution.py:30
  138.8 18.4 %collective-permute-start.33 = (bf16[128,1024]{1,0:T(8,128)(2,1)S(1)}, bf16[128,1024]{1,0:T(8,128)(2,1)S(1)}, u32[]{:S(2)}, u32[]{:S(2)}) collective-permute-start(bf16[128,1024]{1,0:T(8,128)(2,1)S(1)} %shard_map.287), channel_id=1, source_target_pairs={{0,16},{4,20},{8,24},{12,28},{16,0},{20,4},{24,8},{28,12},{1,17},{... | collective-permute-start | bytes 786440 | tf_op jit(solution)/shard_map/ppermute | solution.py:30
  139.8 51.5 %collective-permute-start.27 = (bf16[240,1024]{1,0:T(8,128)(2,1)S(1)}, bf16[240,1024]{1,0:T(8,128)(2,1)S(1)}, u32[]{:S(2)}, u32[]{:S(2)}) collective-permute-start(bf16[240,1024]{1,0:T(8,128)(2,1)S(1)} %get-tuple-element.218), channel_id=1, source_target_pairs={{0,1},{1,0},{2,3},{3,2},{4,5},{5,4},{6,7},{7,6},{8,9},{9,8},{10,11... | collective-permute-start | bytes 1474568 | tf_op jit(solution)/shard_map/ppermute | solution.py:30
  146.0 17.2 %collective-permute-start.30 = (bf16[256,512]{1,0:T(8,128)(2,1)S(1)}, bf16[256,512]{1,0:T(8,128)(2,1)S(1)}, u32[]{:S(2)}, u32[]{:S(2)}) collective-permute-start(bf16[256,512]{1,0:T(8,128)(2,1)S(1)} %get-tuple-element.223), channel_id=1, source_target_pairs={{0,8},{4,12},{8,0},{12,4},{16,24},{20,28},{24,16},{28,20},{1,9},{5... | collective-permute-start | bytes 786440 | tf_op jit(solution)/shard_map/ppermute | solution.py:30
  146.1 11.2 %collective-permute-start.32 = (bf16[256,512]{1,0:T(8,128)(2,1)S(1)}, bf16[256,512]{1,0:T(8,128)(2,1)S(1)}, u32[]{:S(2)}, u32[]{:S(2)}) collective-permute-start(bf16[256,512]{1,0:T(8,128)(2,1)S(1)} %get-tuple-element.226), channel_id=1, source_target_pairs={{0,4},{4,0},{8,12},{12,8},{16,20},{20,16},{24,28},{28,24},{1,5},{5... | collective-permute-start | bytes 786440 | tf_op jit(solution)/shard_map/ppermute | solution.py:30
  147.0 20.9 %collective-permute-start.37 = (bf16[128,1024]{1,0:T(8,128)(2,1)S(1)}, bf16[128,1024]{1,0:T(8,128)(2,1)S(1)}, u32[]{:S(2)}, u32[]{:S(2)}) collective-permute-start(bf16[128,1024]{1,0:T(8,128)(2,1)S(1)} %shard_map.290), channel_id=1, source_target_pairs={{0,16},{4,20},{8,24},{12,28},{16,0},{20,4},{24,8},{28,12},{1,17},{... | collective-permute-start | bytes 786440 | tf_op jit(solution)/shard_map/ppermute | solution.py:30
  157.3 23.5 %collective-permute-start.43 = (bf16[256,1024]{1,0:T(8,128)(2,1)S(1)}, bf16[256,1024]{1,0:T(8,128)(2,1)S(1)}, u32[]{:S(2)}, u32[]{:S(2)}) collective-permute-start(bf16[256,1024]{1,0:T(8,128)(2,1)S(1)} %pad_maximum_fusion.2), channel_id=1, source_target_pairs={{0,8},{4,12},{8,0},{12,4},{16,24},{20,28},{24,16},{28,20},{1,9},{5... | collective-permute-start | bytes 1572872 | tf_op jit(solution)/shard_map/ppermute | solution.py:30
  157.4 17.1 %collective-permute-start.36 = (bf16[128,512]{1,0:T(8,128)(2,1)S(1)}, bf16[128,512]{1,0:T(8,128)(2,1)S(1)}, u32[]{:S(2)}, u32[]{:S(2)}) collective-permute-start(bf16[128,512]{1,0:T(8,128)(2,1)S(1)} %get-tuple-element.230), channel_id=1, source_target_pairs={{0,16},{4,20},{8,24},{12,28},{16,0},{20,4},{24,8},{28,12},{1,17},{... | collective-permute-start | bytes 393224 | tf_op jit(solution)/shard_map/ppermute | solution.py:30
  163.3 14.7 %collective-permute-start.35 = (bf16[128,512]{1,0:T(8,128)(2,1)S(1)}, bf16[128,512]{1,0:T(8,128)(2,1)S(1)}, u32[]{:S(2)}, u32[]{:S(2)}) collective-permute-start(bf16[128,512]{1,0:T(8,128)(2,1)S(1)} %get-tuple-element.234), channel_id=1, source_target_pairs={{0,16},{4,20},{8,24},{12,28},{16,0},{20,4},{24,8},{28,12},{1,17},{... | collective-permute-start | bytes 393224 | tf_op jit(solution)/shard_map/ppermute | solution.py:30
  167.9 13.1 %collective-permute-start.42 = (bf16[256,1024]{1,0:T(8,128)(2,1)S(1)}, bf16[256,1024]{1,0:T(8,128)(2,1)S(1)}, u32[]{:S(2)}, u32[]{:S(2)}) collective-permute-start(bf16[256,1024]{1,0:T(8,128)(2,1)S(1)} %pad_maximum_fusion.3), channel_id=1, source_target_pairs={{0,4},{4,0},{8,12},{12,8},{16,20},{20,16},{24,28},{28,24},{1,5},{5... | collective-permute-start | bytes 1572872 | tf_op jit(solution)/shard_map/ppermute | solution.py:30
  180.9 34.6 %collective-permute-start.49 = (bf16[512,1024]{1,0:T(8,128)(2,1)S(1)}, bf16[512,1024]{1,0:T(8,128)(2,1)S(1)}, u32[]{:S(2)}, u32[]{:S(2)}) collective-permute-start(bf16[512,1024]{1,0:T(8,128)(2,1)S(1)} %pad_maximum_fusion.refs_0_), channel_id=1, source_target_pairs={{0,4},{4,0},{8,12},{12,8},{16,20},{20,16},{24,28},{28,24},{1,5},{5... | collective-permute-start | bytes 3145736 | tf_op jit(solution)/shard_map/ppermute | solution.py:30
  184.6 14.6 %collective-permute-start.44 = (bf16[288,512]{1,0:T(8,128)(2,1)S(1)}, bf16[288,512]{1,0:T(8,128)(2,1)S(1)}, u32[]{:S(2)}, u32[]{:S(2)}) collective-permute-start(bf16[288,512]{1,0:T(8,128)(2,1)S(1)} %pad_maximum_fusion.6), channel_id=1, source_target_pairs={{0,8},{4,12},{8,0},{12,4},{16,24},{20,28},{24,16},{28,20},{1,9},{5... | collective-permute-start | bytes 884744 | tf_op jit(solution)/shard_map/ppermute | solution.py:30
  192.4 20.3 %collective-permute-start.46 = (bf16[256,512]{1,0:T(8,128)(2,1)S(1)}, bf16[256,512]{1,0:T(8,128)(2,1)S(1)}, u32[]{:S(2)}, u32[]{:S(2)}) collective-permute-start(bf16[256,512]{1,0:T(8,128)(2,1)S(1)} %pad_maximum_fusion.7), channel_id=1, source_target_pairs={{0,4},{4,0},{8,12},{12,8},{16,20},{20,16},{24,28},{28,24},{1,5},{5... | collective-permute-start | bytes 786440 | tf_op jit(solution)/shard_map/ppermute | solution.py:30
  192.4 25.8 %collective-permute-start.48 = (bf16[512,1024]{1,0:T(8,128)(2,1)S(1)}, bf16[512,1024]{1,0:T(8,128)(2,1)S(1)}, u32[]{:S(2)}, u32[]{:S(2)}) collective-permute-start(bf16[512,1024]{1,0:T(8,128)(2,1)S(1)} %pad_maximum_fusion.1.refs_0_), channel_id=1, source_target_pairs={{0,8},{4,12},{8,0},{12,4},{16,24},{20,28},{24,16},{28,20},{1,9},{5... | collective-permute-start | bytes 3145736 | tf_op jit(solution)/shard_map/ppermute | solution.py:30
  199.3 25.1 %collective-permute-start.45 = (bf16[544,512]{1,0:T(8,128)(2,1)S(1)}, bf16[544,512]{1,0:T(8,128)(2,1)S(1)}, u32[]{:S(2)}, u32[]{:S(2)}) collective-permute-start(bf16[544,512]{1,0:T(8,128)(2,1)S(1)} %fusion.14), channel_id=1, source_target_pairs={{0,4},{4,0},{8,12},{12,8},{16,20},{20,16},{24,28},{28,24},{1,5},{5... | collective-permute-start | bytes 1671176 | tf_op jit(solution)/shard_map/ppermute | solution.py:30
  212.7 11.7 %collective-permute-start.47 = (bf16[512,512]{1,0:T(8,128)(2,1)S(1)}, bf16[512,512]{1,0:T(8,128)(2,1)S(1)}, u32[]{:S(2)}, u32[]{:S(2)}) collective-permute-start(bf16[512,512]{1,0:T(8,128)(2,1)S(1)} %pad_maximum_fusion.4.second), channel_id=1, source_target_pairs={{0,8},{4,12},{8,0},{12,4},{16,24},{20,28},{24,16},{28,20},{1,9},{5... | collective-permute-start | bytes 1572872 | tf_op jit(solution)/shard_map/ppermute | solution.py:30
  (29 other events, 175.4 us)

commit v7 on v6

--- a/solution.py
+++ b/solution.py
@@ -614,8 +614,8 @@
 
 
 def pack(values):
-    high = values.astype(BF)
-    return jnp.concatenate([high, (values - high.astype(F32)).astype(BF)], axis=0)
+    high = lax.reduce_precision(values, exponent_bits=8, mantissa_bits=7)
+    return jnp.concatenate([high.astype(BF), (values - high).astype(BF)], axis=0)
 
 
 def add_small(own, other):
@@ -760,7 +760,7 @@
         return values.reshape(1, -1)
 
     side = 2 * rows
-    block = 256
+    block = 512
     project_flops = 2 * side * model * 3 * width
     attend_flops = 3 * heads * 4 * HALF * SLOTS * 128 + 2 * side * width * model
     back_flops = 3 * heads * 10 * HALF * SLOTS * 128 + 2 * side * width * model

time: 228 us -> 228 us (level)
  transfers between devices with their start and end apart: 50 -> 50, of which waited for: 22 -> 23; matrix products, arithmetic and copies ran while one was open for 3% -> 3% of each run, Pallas kernels for 36% -> 36%
where the time goes in v7:
time: 228 us; the launch traced here: 227 us
  Pallas kernels  88.5 us (39%)
  waiting for transfers between devices  68.5 us (30%)
  starting transfers between devices  58.6 us (26%)
  local copies, waits for them, and re-layouts  6.21 us (3%)
  other arithmetic  4.22 us (2%)
    pallas_call x41, Pallas kernels, run(): pl.pallas_call(kernel, out_shape=[pltpu.VMEM(x.shape, x.dtype) for x in o...  79.3 us
    ppermute x50, waiting for transfers between devices, swap(): return lax.ppermute(values, axis, [(i, i ^ bit) for i in range(count)])  68.5 us
    ppermute x50, starting transfers between devices, swap(): return lax.ppermute(values, axis, [(i, i ^ bit) for i in range(count)])  58.6 us
    pallas_call x2, Pallas kernels, run_out(): pl.pallas_call(body, out_shape=[pltpu.HBM(x.shape, x.dtype) for x in outs...  5.29 us
  transfers between devices with their start and end apart: 50, of which 23 were waited for; matrix products, arithmetic and copies ran while one was open for 3% of the time, Pallas kernels for 36%

profile of v7, /device:TPU:0, one launch (start us, length us, event | category | flops | bytes accessed | tf_op | source)
XLA Modules:
  0.0 227.4 jit_solution(12949416721918396808)
XLA Ops:
  0.6 3.0 %collective-permute-start.2 = (bf16[240,1024]{1,0:T(8,128)(2,1)}, bf16[240,1024]{1,0:T(8,128)(2,1)S(1)}, u32[]{:S(2)}, u32[]{:S(2)}) collective-permute-start(bf16[240,1024]{1,0:T(8,128)(2,1)} %refs_4_.13), channel_id=1, source_target_pairs={{0,2},{1,3},{2,0},{3,1},{4,6},{5,7},{6,4},{7,5},{8,10},{9,11},{10,... | collective-permute-start | bytes 1474568 | tf_op jit(solution)/shard_map/ppermute | solution.py:30
  10.1 4.1 %shard_map.254 = (bf16[480,1024]{1,0:T(8,128)(2,1)S(1)}, bf16[480,768]{1,0:T(8,128)(2,1)S(1)}) custom-call(s32[2]{0:T(128)S(1)} %pad_add_fusion.refs_0_.me, bf16[240,1024]{1,0:T(8,128)(2,1)S(1)} %copy-done.3, bf16[240,1024]{1,0:T(8,128)(2,1)S(1)} %collective-permute-done.1.refs_2_, ...), custom_call_target="tpu_custom_call" | custom-call | flops 15099494400 | tf_op jit(solution)/shard_map/pallas_call | solution.py:63
  19.1 7.4 %shard_map.256 = (bf16[240,1024]{1,0:T(8,128)(2,1)S(1)}, bf16[960,768]{1,0:T(8,128)(2,1)S(1)}, bf16[12,160,320]{2,1,0:T(8,128)(2,1)S(1)}, bf16[480,256]{1,0:T(8,...) custom-call(s32[2]{0:T(128)S(1)} %pad_add_fusion.refs_0_.me, ...), custom_call_target="tpu_custom_call" | custom-call | flops 26424115200 | tf_op jit(solution)/shard_map/pallas_call | solution.py:63
  30.7 5.6 %shard_map.258 = (bf16[12,160,320]{2,1,0:T(8,128)(2,1)S(1)}, bf16[480,256]{1,0:T(8,128)(2,1)S(1)}, bf16[240,1024]{1,0:T(8,128)(2,1)S(1)}, f32[240,1024]{1,0:T(8,128)S(1)}) custom-call(s32[2]{0:T(128)S(1)} %pad_add_fusion.refs_0_.me, bf16[960,768]{1,0:T(8,128)(2,1)S(1)} %get-tuple-element.143.refs_11_.refs_1_.refs_12_.refs_13_.refs_15_.refs_16_.refs_3_, ...), custom_call_target="tpu_custom_call" | custom-call | flops 11324620800 | tf_op jit(solution)/shard_map/pallas_call | solution.py:63
  36.4 2.5 %shard_map.259.refs_19_.refs_5_ = f32[480,1024]{1,0:T(8,128)S(1)} custom-call(s32[2]{0:T(128)S(1)} %pad_add_fusion.refs_0_.me, bf16[240,1024]{1,0:T(8,128)(2,1)S(1)} %multiply_convert_fusion.1.refs_6_.refs_10_.refs_7_.refs_1_.refs_8_.refs_4_.refs_11_.refs_5_.refs_9_.refs_14_.refs_3_, ...), custom_call_target="tpu_custom_call" | custom-call | flops 20132659200 | tf_op jit(solution)/shard_map/pallas_call | solution.py:63
  38.9 3.1 %collective-permute-done.7.refs_4_ = bf16[240,1024]{1,0:T(8,128)(2,1)S(1)} collective-permute-done((bf16[240,1024]{1,0:T(8,128)(2,1)S(1)}, bf16[240,1024]{1,0:T(8,128)(2,1)S(1)}, u32[]{:S(2)}, u32[]{:S(2)}) %collective-permute-start.7) | collective-permute-done | bytes 491552 | tf_op jit(solution)/shard_map/ppermute | solution.py:30
  45.8 4.2 %shard_map.261 = (bf16[480,1024]{1,0:T(8,128)(2,1)S(1)}, bf16[480,1024]{1,0:T(8,128)(2,1)S(1)}, f32[1,1024]{1,0:T(1,128)S(1)}, f32[240,1024]{1,0:T(8,128)S(1)}, bf16[240,1024]{1,0:T(8,128)(2,1)S(1)}) custom-call(s32[2]{0:T(128)S(1)} %pad_add_fusion.refs_0_.me, bf16[240,1024]{1,0:T(8,128)(2,1)S(1)} %get-tuple-element.158.refs_1_.refs_20_.refs_22_.refs_19_.refs_18_, ...), custom_call_target="tpu_custom_call" | custom-call | flops 40265318400 | tf_op jit(solution)/shard_map/pallas_call | solution.py:63
  50.1 2.7 %shard_map.262.refs_4_.refs_27_ = f32[480,1024]{1,0:T(8,128)S(1)} custom-call(s32[2]{0:T(128)S(1)} %pad_add_fusion.refs_0_.me, bf16[240,1024]{1,0:T(8,128)(2,1)S(1)} %collective-permute-done.5.refs_1_.refs_25_.refs_6_.refs_26_.refs_24_, bf16[240,1024]{1,0:T(8,128)(2,1)S(1)} %collective-permute-done.9.refs_2_.refs_26_.refs_7_.refs_27_.refs_25_, ...), custom_call_target="tpu_custom_call" | custom-call | flops 20132659200 | tf_op jit(solution)/shard_map/pallas_call | solution.py:63
  52.8 4.7 %collective-permute-done.8.refs_1_.refs_29_.refs_30_.refs_27_.refs_3_.refs_28_.refs_26_.refs_23_ = bf16[240,1024]{1,0:T(8,128)(2,1)S(1)} collective-permute-done((bf16[240,1024]{1,0:T(8,128)(2,1)S(1)}, bf16[240,1024]{1,0:T(8,128)(2,1)S(1)}, u32[]{:S(2)}, u32[]{:S(2)}) %collective-permute-start.8) | collective-permute-done | bytes 491552 | tf_op jit(solution)/shard_map/ppermute | solution.py:30
  57.5 2.5 %shard_map.263 = (bf16[240,1024]{1,0:T(8,128)(2,1)S(1)}, bf16[240,1024]{1,0:T(8,128)(2,1)S(1)}, f32[1,1024]{1,0:T(1,128)S(1)}, f32[240,1024]{1,0:T(8,128)S(1)}) custom-call(s32[2]{0:T(128)S(1)} %pad_add_fusion.refs_0_.me, bf16[240,1024]{1,0:T(8,128)(2,1)S(1)} %collective-permute-done.8.refs_1_.refs_29_.refs_30_.refs_27_.refs_3_.refs_28_.refs_26_.refs_23_, ...), custom_call_target="tpu_custom_call" | custom-call | flops 20132659200 | tf_op jit(solution)/shard_map/pallas_call | solution.py:63
  60.0 2.5 %shard_map.264 = (bf16[240,1024]{1,0:T(8,128)(2,1)S(1)}, bf16[240,1024]{1,0:T(8,128)(2,1)S(1)}, f32[1,1024]{1,0:T(1,128)S(1)}, bf16[240,1024]{1,0:T(8,128)(2,1)S(1)}) custom-call(s32[2]{0:T(128)S(1)} %pad_add_fusion.refs_0_.me, bf16[240,1024]{1,0:T(8,128)(2,1)S(1)} %collective-permute-done.11.refs_1_.refs_29_.refs_4_.refs_31_.refs_28_.refs_25_, ...), custom_call_target="tpu_custom_call" | custom-call | flops 20132659200 | tf_op jit(solution)/shard_map/pallas_call | solution.py:63
  66.3 2.8 %shard_map.266 = bf16[512,1024]{1,0:T(8,128)(2,1)S(1)} custom-call(s32[2]{0:T(128)S(1)} %pad_add_fusion.refs_0_.me, bf16[480,1024]{1,0:T(8,128)(2,1)S(1)} %get-tuple-element.160.refs_21_.refs_1_.refs_24_.refs_20_.refs_19_.refs_22_.refs_17_.refs_14_.refs_13_.refs_10_, bf16[240,1024]{1,0:T(8,128)(2,1)S(1)} %get-tuple-element.165.refs_27_.refs_28_.refs_2_.refs_1_.refs_26_, ...), custom_call_target="tpu_custom_call" | custom-call | flops 20132659200 | tf_op jit(solution)/shard_map/pallas_call | solution.py:63
  69.1 2.7 %shard_map.267 = bf16[512,1024]{1,0:T(8,128)(2,1)S(1)} custom-call(s32[2]{0:T(128)S(1)} %pad_add_fusion.refs_0_.me, bf16[240,1024]{1,0:T(8,128)(2,1)S(1)} %get-tuple-element.158.refs_1_.refs_20_.refs_22_.refs_19_.refs_18_, bf16[240,1024]{1,0:T(8,128)(2,1)S(1)} %collective-permute-done.10.refs_2_.refs_24_.refs_25_.refs_23_.refs_21_, ...), custom_call_target="tpu_custom_call" | custom-call | flops 20132659200 | tf_op jit(solution)/shard_map/pallas_call | solution.py:63
  82.1 2.8 %shard_map.270.refs_27_.refs_25_.refs_1_ = f32[512,1024]{1,0:T(8,128)S(1)} custom-call(s32[2]{0:T(128)S(1)} %pad_add_fusion.refs_0_.me, bf16[480,1024]{1,0:T(8,128)(2,1)S(1)} %get-tuple-element.160.refs_21_.refs_1_.refs_24_.refs_20_.refs_19_.refs_22_.refs_17_.refs_14_.refs_13_.refs_10_, ...), custom_call_target="tpu_custom_call" | custom-call | flops 20132659200 | tf_op jit(solution)/shard_map/pallas_call | solution.py:63
  84.9 6.6 %shard_map.271 = (f32[480,256]{1,0:T(8,128)S(1)}, f32[960,512]{1,0:T(8,128)S(1)}) custom-call(s32[2]{0:T(128)S(1)} %pad_add_fusion.refs_0_.me, bf16[240,1024]{1,0:T(8,128)(2,1)S(1)} %get-tuple-element.176.refs_30_.refs_1_.refs_24_.refs_19_.refs_21_.refs_16_.refs_15_.refs_8_, ...), custom_call_target="tpu_custom_call" | custom-call | flops 20761804800 | tf_op jit(solution)/shard_map/pallas_call | solution.py:63
  91.5 2.7 %shard_map.272.refs_23_.refs_1_ = f32[512,1024]{1,0:T(8,128)S(1)} custom-call(s32[2]{0:T(128)S(1)} %pad_add_fusion.refs_0_.me, bf16[240,1024]{1,0:T(8,128)(2,1)S(1)} %get-tuple-element.158.refs_1_.refs_20_.refs_22_.refs_19_.refs_18_, bf16[240,1024]{1,0:T(8,128)(2,1)S(1)} %collective-permute-done.10.refs_2_.refs_24_.refs_25_.refs_23_.refs_21_, ...), custom_call_target="tpu_custom_call" | custom-call | flops 20132659200 | tf_op jit(solution)/shard_map/pallas_call | solution.py:63
  100.8 8.3 %shard_map.275 = (bf16[480,768]{1,0:T(8,128)(2,1)S(1)}, bf16[480,768]{1,0:T(8,128)(2,1)S(1)}, f32[1,512]{1,0:T(1,128)S(1)}, bf16[240,1024]{1,0:T(8,128)(2,1)S(1)}, f32[240,1024]{1,0:T(8,128)S(1)}) custom-call(s32[2]{0:T(128)S(1)} %pad_add_fusion.refs_0_.me, ...), custom_call_target="tpu_custom_call" | custom-call | flops 35861299200 | tf_op jit(solution)/shard_map/pallas_call | solution.py:63
  113.1 2.7 %collective-permute-start.34 = (bf16[128,1024]{1,0:T(8,128)(2,1)S(1)}, bf16[128,1024]{1,0:T(8,128)(2,1)S(1)}, u32[]{:S(2)}, u32[]{:S(2)}) collective-permute-start(bf16[128,1024]{1,0:T(8,128)(2,1)S(1)} %get-tuple-element.205), channel_id=1, source_target_pairs={{0,16},{4,20},{8,24},{12,28},{16,0},{20,4},{24,8},{28,12},{1,17},{... | collective-permute-start | bytes 786440 | tf_op jit(solution)/shard_map/ppermute | solution.py:30
  131.3 6.3 %collective-permute-done.29.refs_2_ = bf16[128,1024]{1,0:T(8,128)(2,1)S(1)} collective-permute-done((bf16[128,1024]{1,0:T(8,128)(2,1)S(1)}, bf16[128,1024]{1,0:T(8,128)(2,1)S(1)}, u32[]{:S(2)}, u32[]{:S(2)}) %collective-permute-start.29) | collective-permute-done | bytes 262176 | tf_op jit(solution)/shard_map/ppermute | solution.py:30
  139.5 6.0 %collective-permute-done.31.refs_2_ = bf16[512,512]{1,0:T(8,128)(2,1)S(1)} collective-permute-done((bf16[512,512]{1,0:T(8,128)(2,1)S(1)}, bf16[512,512]{1,0:T(8,128)(2,1)S(1)}, u32[]{:S(2)}, u32[]{:S(2)}) %collective-permute-start.31) | collective-permute-done | bytes 524320 | tf_op jit(solution)/shard_map/ppermute | solution.py:30
  146.4 9.1 %collective-permute-start.37 = (bf16[128,1024]{1,0:T(8,128)(2,1)S(1)}, bf16[128,1024]{1,0:T(8,128)(2,1)S(1)}, u32[]{:S(2)}, u32[]{:S(2)}) collective-permute-start(bf16[128,1024]{1,0:T(8,128)(2,1)S(1)} %shard_map.290), channel_id=1, source_target_pairs={{0,16},{4,20},{8,24},{12,28},{16,0},{20,4},{24,8},{28,12},{1,17},{... | collective-permute-start | bytes 786440 | tf_op jit(solution)/shard_map/ppermute | solution.py:30
  156.9 3.8 %collective-permute-start.36 = (bf16[128,512]{1,0:T(8,128)(2,1)S(1)}, bf16[128,512]{1,0:T(8,128)(2,1)S(1)}, u32[]{:S(2)}, u32[]{:S(2)}) collective-permute-start(bf16[128,512]{1,0:T(8,128)(2,1)S(1)} %get-tuple-element.230), channel_id=1, source_target_pairs={{0,16},{4,20},{8,24},{12,28},{16,0},{20,4},{24,8},{28,12},{1,17},{... | collective-permute-start | bytes 393224 | tf_op jit(solution)/shard_map/ppermute | solution.py:30
  162.7 4.8 %collective-permute-start.35 = (bf16[128,512]{1,0:T(8,128)(2,1)S(1)}, bf16[128,512]{1,0:T(8,128)(2,1)S(1)}, u32[]{:S(2)}, u32[]{:S(2)}) collective-permute-start(bf16[128,512]{1,0:T(8,128)(2,1)S(1)} %get-tuple-element.234), channel_id=1, source_target_pairs={{0,16},{4,20},{8,24},{12,28},{16,0},{20,4},{24,8},{28,12},{1,17},{... | collective-permute-start | bytes 393224 | tf_op jit(solution)/shard_map/ppermute | solution.py:30
  168.1 6.1 %collective-permute-done.36.refs_2_ = bf16[128,512]{1,0:T(8,128)(2,1)S(1)} collective-permute-done((bf16[128,512]{1,0:T(8,128)(2,1)S(1)}, bf16[128,512]{1,0:T(8,128)(2,1)S(1)}, u32[]{:S(2)}, u32[]{:S(2)}) %collective-permute-start.36) | collective-permute-done | bytes 131104 | tf_op jit(solution)/shard_map/ppermute | solution.py:30
  174.1 3.5 %collective-permute-start.41 = (bf16[128,512]{1,0:T(8,128)(2,1)S(1)}, bf16[128,512]{1,0:T(8,128)(2,1)S(1)}, u32[]{:S(2)}, u32[]{:S(2)}) collective-permute-start(bf16[128,512]{1,0:T(8,128)(2,1)S(1)} %shard_map.293), channel_id=1, source_target_pairs={{0,16},{4,20},{8,24},{12,28},{16,0},{20,4},{24,8},{28,12},{1,17},{... | collective-permute-start | bytes 393224 | tf_op jit(solution)/shard_map/ppermute | solution.py:30
  182.1 2.4 %collective-permute-done.40 = bf16[160,512]{1,0:T(8,128)(2,1)S(1)} collective-permute-done((bf16[160,512]{1,0:T(8,128)(2,1)S(1)}, bf16[160,512]{1,0:T(8,128)(2,1)S(1)}, u32[]{:S(2)}, u32[]{:S(2)}) %collective-permute-start.40) | collective-permute-done | bytes 163872 | tf_op jit(solution)/shard_map/ppermute | solution.py:30
  184.6 6.0 %collective-permute-start.44 = (bf16[288,512]{1,0:T(8,128)(2,1)S(1)}, bf16[288,512]{1,0:T(8,128)(2,1)S(1)}, u32[]{:S(2)}, u32[]{:S(2)}) collective-permute-start(bf16[288,512]{1,0:T(8,128)(2,1)S(1)} %pad_maximum_fusion.6), channel_id=1, source_target_pairs={{0,8},{4,12},{8,0},{12,4},{16,24},{20,28},{24,16},{28,20},{1,9},{5... | collective-permute-start | bytes 884744 | tf_op jit(solution)/shard_map/ppermute | solution.py:30
  191.7 6.8 %collective-permute-done.44 = bf16[288,512]{1,0:T(8,128)(2,1)S(1)} collective-permute-done((bf16[288,512]{1,0:T(8,128)(2,1)S(1)}, bf16[288,512]{1,0:T(8,128)(2,1)S(1)}, u32[]{:S(2)}, u32[]{:S(2)}) %collective-permute-start.44) | collective-permute-done | bytes 294944 | tf_op jit(solution)/shard_map/ppermute | solution.py:30
  198.7 13.5 %collective-permute-done.46 = bf16[256,512]{1,0:T(8,128)(2,1)S(1)} collective-permute-done((bf16[256,512]{1,0:T(8,128)(2,1)S(1)}, bf16[256,512]{1,0:T(8,128)(2,1)S(1)}, u32[]{:S(2)}, u32[]{:S(2)}) %collective-permute-start.46) | collective-permute-done | bytes 262176 | tf_op jit(solution)/shard_map/ppermute | solution.py:30
  212.2 2.7 %collective-permute-start.47 = (bf16[512,512]{1,0:T(8,128)(2,1)S(1)}, bf16[512,512]{1,0:T(8,128)(2,1)S(1)}, u32[]{:S(2)}, u32[]{:S(2)}) collective-permute-start(bf16[512,512]{1,0:T(8,128)(2,1)S(1)} %pad_maximum_fusion.4.second), channel_id=1, source_target_pairs={{0,8},{4,12},{8,0},{12,4},{16,24},{20,28},{24,16},{28,20},{1,9},{5... | collective-permute-start | bytes 1572872 | tf_op jit(solution)/shard_map/ppermute | solution.py:30
  215.0 2.6 %shard_map.295 = f32[1024,1024]{1,0:T(8,128)} custom-call(s32[2]{0:T(128)S(1)} %pad_add_fusion.refs_0_.me, bf16[512,1024]{1,0:T(8,128)(2,1)S(1)} %pad_maximum_fusion.refs_0_, bf16[512,1024]{1,0:T(8,128)(2,1)S(1)} %collective-permute-done.49.refs_1_), custom_call_target="tpu_custom_call" | custom-call | flops 20000000000 | tf_op jit(solution)/shard_map/pallas_call | solution.py:96
  217.7 2.6 %shard_map.296 = f32[1024,1024]{1,0:T(8,128)} custom-call(s32[2]{0:T(128)S(1)} %pad_add_fusion.refs_0_.me, bf16[512,1024]{1,0:T(8,128)(2,1)S(1)} %pad_maximum_fusion.1.refs_0_, bf16[512,1024]{1,0:T(8,128)(2,1)S(1)} %collective-permute-done.48.refs_1_), custom_call_target="tpu_custom_call" | custom-call | flops 20000000000 | tf_op jit(solution)/shard_map/pallas_call | solution.py:96
  (179 shorter events, 78.7 us)
Async XLA Ops:
  0.6 14.5 %collective-permute-start.2 = (bf16[240,1024]{1,0:T(8,128)(2,1)}, bf16[240,1024]{1,0:T(8,128)(2,1)S(1)}, u32[]{:S(2)}, u32[]{:S(2)}) collective-permute-start(bf16[240,1024]{1,0:T(8,128)(2,1)} %refs_4_.13), channel_id=1, source_target_pairs={{0,2},{1,3},{2,0},{3,1},{4,6},{5,7},{6,4},{7,5},{8,10},{9,11},{10,... | collective-permute-start | bytes 1474568 | tf_op jit(solution)/shard_map/ppermute | solution.py:30
  15.1 13.6 %collective-permute-start.5 = (bf16[240,1024]{1,0:T(8,128)(2,1)S(1)}, bf16[240,1024]{1,0:T(8,128)(2,1)S(1)}, u32[]{:S(2)}, u32[]{:S(2)}) collective-permute-start(bf16[240,1024]{1,0:T(8,128)(2,1)S(1)} %multiply_convert_fusion.1.refs_6_.refs_10_.refs_7_.refs_1_.refs_8_.refs_4_.refs_11_.refs_5_.refs_9_.refs_14_, ...), channel_id=1, source_target_pairs={{0,2},{1,3},{2,0},{3,1},{4,6},{5,7},{6,4},{7,5},{8,10},{9,11},{10,... | collective-permute-start | bytes 1474568 | tf_op jit(solution)/shard_map/ppermute | solution.py:30
  28.9 13.1 %collective-permute-start.7 = (bf16[240,1024]{1,0:T(8,128)(2,1)S(1)}, bf16[240,1024]{1,0:T(8,128)(2,1)S(1)}, u32[]{:S(2)}, u32[]{:S(2)}) collective-permute-start(bf16[240,1024]{1,0:T(8,128)(2,1)S(1)} %shard_map.257), channel_id=1, source_target_pairs={{0,2},{1,3},{2,0},{3,1},{4,6},{5,7},{6,4},{7,5},{8,10},{9,11},{10,... | collective-permute-start | bytes 1474568 | tf_op jit(solution)/shard_map/ppermute | solution.py:30
  44.3 13.2 %collective-permute-start.8 = (bf16[240,1024]{1,0:T(8,128)(2,1)S(1)}, bf16[240,1024]{1,0:T(8,128)(2,1)S(1)}, u32[]{:S(2)}, u32[]{:S(2)}) collective-permute-start(bf16[240,1024]{1,0:T(8,128)(2,1)S(1)} %get-tuple-element.158.refs_1_.refs_20_.refs_22_.refs_19_.refs_18_), channel_id=1, source_target_pairs={{0,2},{1,3},{2,0},{3,1},{4,6},{5,7},{6,4},{7,5},{8,10},{9,11},{10,... | collective-permute-start | bytes 1474568 | tf_op jit(solution)/shard_map/ppermute | solution.py:30
  63.1 13.7 %collective-permute-start.13 = (bf16[240,1024]{1,0:T(8,128)(2,1)S(1)}, bf16[240,1024]{1,0:T(8,128)(2,1)S(1)}, u32[]{:S(2)}, u32[]{:S(2)}) collective-permute-start(bf16[240,1024]{1,0:T(8,128)(2,1)S(1)} %get-tuple-element.175), channel_id=1, source_target_pairs={{0,1},{1,0},{2,3},{3,2},{4,5},{5,4},{6,7},{7,6},{8,9},{9,8},{10,11... | collective-permute-start | bytes 1474568 | tf_op jit(solution)/shard_map/ppermute | solution.py:30
  64.6 13.6 %collective-permute-start.14 = (bf16[240,1024]{1,0:T(8,128)(2,1)S(1)}, bf16[240,1024]{1,0:T(8,128)(2,1)S(1)}, u32[]{:S(2)}, u32[]{:S(2)}) collective-permute-start(bf16[240,1024]{1,0:T(8,128)(2,1)S(1)} %shard_map.265), channel_id=1, source_target_pairs={{0,2},{1,3},{2,0},{3,1},{4,6},{5,7},{6,4},{7,5},{8,10},{9,11},{10,... | collective-permute-start | bytes 1474568 | tf_op jit(solution)/shard_map/ppermute | solution.py:30
  71.8 25.2 %collective-permute-start.19 = (bf16[512,1024]{1,0:T(8,128)(2,1)S(1)}, bf16[512,1024]{1,0:T(8,128)(2,1)S(1)}, u32[]{:S(2)}, u32[]{:S(2)}) collective-permute-start(bf16[512,1024]{1,0:T(8,128)(2,1)S(1)} %shard_map.267), channel_id=1, source_target_pairs={{0,8},{4,12},{8,0},{12,4},{16,24},{20,28},{24,16},{28,20},{1,9},{5... | collective-permute-start | bytes 3145736 | tf_op jit(solution)/shard_map/ppermute | solution.py:30
  73.5 24.9 %collective-permute-start.15 = (bf16[512,1024]{1,0:T(8,128)(2,1)S(1)}, bf16[512,1024]{1,0:T(8,128)(2,1)S(1)}, u32[]{:S(2)}, u32[]{:S(2)}) collective-permute-start(bf16[512,1024]{1,0:T(8,128)(2,1)S(1)} %shard_map.266), channel_id=1, source_target_pairs={{0,4},{4,0},{8,12},{12,8},{16,20},{20,16},{24,28},{28,24},{1,5},{5... | collective-permute-start | bytes 3145736 | tf_op jit(solution)/shard_map/ppermute | solution.py:30
  76.7 17.8 %collective-permute-start.22 = (bf16[240,1024]{1,0:T(8,128)(2,1)S(1)}, bf16[240,1024]{1,0:T(8,128)(2,1)S(1)}, u32[]{:S(2)}, u32[]{:S(2)}) collective-permute-start(bf16[240,1024]{1,0:T(8,128)(2,1)S(1)} %get-tuple-element.195), channel_id=1, source_target_pairs={{0,1},{1,0},{2,3},{3,2},{4,5},{5,4},{6,7},{7,6},{8,9},{9,8},{10,11... | collective-permute-start | bytes 1474568 | tf_op jit(solution)/shard_map/ppermute | solution.py:30
  80.5 13.8 %collective-permute-start.16 = (bf16[240,1024]{1,0:T(8,128)(2,1)S(1)}, bf16[240,1024]{1,0:T(8,128)(2,1)S(1)}, u32[]{:S(2)}, u32[]{:S(2)}) collective-permute-start(bf16[240,1024]{1,0:T(8,128)(2,1)S(1)} %get-tuple-element.176.refs_30_.refs_1_.refs_24_.refs_19_.refs_21_.refs_16_.refs_15_.refs_8_), channel_id=1, source_target_pairs={{0,2},{1,3},{2,0},{3,1},{4,6},{5,7},{6,4},{7,5},{8,10},{9,11},{10,... | collective-permute-start | bytes 1474568 | tf_op jit(solution)/shard_map/ppermute | solution.py:30
  94.6 18.2 %collective-permute-start.23 = (bf16[240,1024]{1,0:T(8,128)(2,1)S(1)}, bf16[240,1024]{1,0:T(8,128)(2,1)S(1)}, u32[]{:S(2)}, u32[]{:S(2)}) collective-permute-start(bf16[240,1024]{1,0:T(8,128)(2,1)S(1)} %shard_map.276), channel_id=1, source_target_pairs={{0,2},{1,3},{2,0},{3,1},{4,6},{5,7},{6,4},{7,5},{8,10},{9,11},{10,... | collective-permute-start | bytes 1474568 | tf_op jit(solution)/shard_map/ppermute | solution.py:30
  98.7 12.8 %collective-permute-start.24 = (bf16[256,1024]{1,0:T(8,128)(2,1)S(1)}, bf16[256,1024]{1,0:T(8,128)(2,1)S(1)}, u32[]{:S(2)}, u32[]{:S(2)}) collective-permute-start(bf16[256,1024]{1,0:T(8,128)(2,1)S(1)} %get-tuple-element.188), channel_id=1, source_target_pairs={{0,4},{4,0},{8,12},{12,8},{16,20},{20,16},{24,28},{28,24},{1,5},{5... | collective-permute-start | bytes 1572872 | tf_op jit(solution)/shard_map/ppermute | solution.py:30
  100.3 12.5 %collective-permute-start.18 = (bf16[256,1024]{1,0:T(8,128)(2,1)S(1)}, bf16[256,1024]{1,0:T(8,128)(2,1)S(1)}, u32[]{:S(2)}, u32[]{:S(2)}) collective-permute-start(bf16[256,1024]{1,0:T(8,128)(2,1)S(1)} %get-tuple-element.186), channel_id=1, source_target_pairs={{0,8},{4,12},{8,0},{12,4},{16,24},{20,28},{24,16},{28,20},{1,9},{5... | collective-permute-start | bytes 1572872 | tf_op jit(solution)/shard_map/ppermute | solution.py:30
  113.1 32.5 %collective-permute-start.34 = (bf16[128,1024]{1,0:T(8,128)(2,1)S(1)}, bf16[128,1024]{1,0:T(8,128)(2,1)S(1)}, u32[]{:S(2)}, u32[]{:S(2)}) collective-permute-start(bf16[128,1024]{1,0:T(8,128)(2,1)S(1)} %get-tuple-element.205), channel_id=1, source_target_pairs={{0,16},{4,20},{8,24},{12,28},{16,0},{20,4},{24,8},{28,12},{1,17},{... | collective-permute-start | bytes 786440 | tf_op jit(solution)/shard_map/ppermute | solution.py:30
  115.8 21.9 %collective-permute-start.29 = (bf16[128,1024]{1,0:T(8,128)(2,1)S(1)}, bf16[128,1024]{1,0:T(8,128)(2,1)S(1)}, u32[]{:S(2)}, u32[]{:S(2)}) collective-permute-start(bf16[128,1024]{1,0:T(8,128)(2,1)S(1)} %get-tuple-element.202), channel_id=1, source_target_pairs={{0,16},{4,20},{8,24},{12,28},{16,0},{20,4},{24,8},{28,12},{1,17},{... | collective-permute-start | bytes 786440 | tf_op jit(solution)/shard_map/ppermute | solution.py:30
  121.7 23.8 %collective-permute-start.31 = (bf16[512,512]{1,0:T(8,128)(2,1)S(1)}, bf16[512,512]{1,0:T(8,128)(2,1)S(1)}, u32[]{:S(2)}, u32[]{:S(2)}) collective-permute-start(bf16[512,512]{1,0:T(8,128)(2,1)S(1)} %shard_map.282), channel_id=1, source_target_pairs={{0,8},{4,12},{8,0},{12,4},{16,24},{20,28},{24,16},{28,20},{1,9},{5... | collective-permute-start | bytes 1572872 | tf_op jit(solution)/shard_map/ppermute | solution.py:30
  124.2 15.1 %collective-permute-start.28 = (bf16[512,512]{1,0:T(8,128)(2,1)S(1)}, bf16[512,512]{1,0:T(8,128)(2,1)S(1)}, u32[]{:S(2)}, u32[]{:S(2)}) collective-permute-start(bf16[512,512]{1,0:T(8,128)(2,1)S(1)} %shard_map.281), channel_id=1, source_target_pairs={{0,4},{4,0},{8,12},{12,8},{16,20},{20,16},{24,28},{28,24},{1,5},{5... | collective-permute-start | bytes 1572872 | tf_op jit(solution)/shard_map/ppermute | solution.py:30
  138.3 18.4 %collective-permute-start.33 = (bf16[128,1024]{1,0:T(8,128)(2,1)S(1)}, bf16[128,1024]{1,0:T(8,128)(2,1)S(1)}, u32[]{:S(2)}, u32[]{:S(2)}) collective-permute-start(bf16[128,1024]{1,0:T(8,128)(2,1)S(1)} %shard_map.287), channel_id=1, source_target_pairs={{0,16},{4,20},{8,24},{12,28},{16,0},{20,4},{24,8},{28,12},{1,17},{... | collective-permute-start | bytes 786440 | tf_op jit(solution)/shard_map/ppermute | solution.py:30
  139.4 51.2 %collective-permute-start.27 = (bf16[240,1024]{1,0:T(8,128)(2,1)S(1)}, bf16[240,1024]{1,0:T(8,128)(2,1)S(1)}, u32[]{:S(2)}, u32[]{:S(2)}) collective-permute-start(bf16[240,1024]{1,0:T(8,128)(2,1)S(1)} %get-tuple-element.218), channel_id=1, source_target_pairs={{0,1},{1,0},{2,3},{3,2},{4,5},{5,4},{6,7},{7,6},{8,9},{9,8},{10,11... | collective-permute-start | bytes 1474568 | tf_op jit(solution)/shard_map/ppermute | solution.py:30
  145.5 17.1 %collective-permute-start.30 = (bf16[256,512]{1,0:T(8,128)(2,1)S(1)}, bf16[256,512]{1,0:T(8,128)(2,1)S(1)}, u32[]{:S(2)}, u32[]{:S(2)}) collective-permute-start(bf16[256,512]{1,0:T(8,128)(2,1)S(1)} %get-tuple-element.223), channel_id=1, source_target_pairs={{0,8},{4,12},{8,0},{12,4},{16,24},{20,28},{24,16},{28,20},{1,9},{5... | collective-permute-start | bytes 786440 | tf_op jit(solution)/shard_map/ppermute | solution.py:30
  145.6 11.3 %collective-permute-start.32 = (bf16[256,512]{1,0:T(8,128)(2,1)S(1)}, bf16[256,512]{1,0:T(8,128)(2,1)S(1)}, u32[]{:S(2)}, u32[]{:S(2)}) collective-permute-start(bf16[256,512]{1,0:T(8,128)(2,1)S(1)} %get-tuple-element.226), channel_id=1, source_target_pairs={{0,4},{4,0},{8,12},{12,8},{16,20},{20,16},{24,28},{28,24},{1,5},{5... | collective-permute-start | bytes 786440 | tf_op jit(solution)/shard_map/ppermute | solution.py:30
  146.4 21.1 %collective-permute-start.37 = (bf16[128,1024]{1,0:T(8,128)(2,1)S(1)}, bf16[128,1024]{1,0:T(8,128)(2,1)S(1)}, u32[]{:S(2)}, u32[]{:S(2)}) collective-permute-start(bf16[128,1024]{1,0:T(8,128)(2,1)S(1)} %shard_map.290), channel_id=1, source_target_pairs={{0,16},{4,20},{8,24},{12,28},{16,0},{20,4},{24,8},{28,12},{1,17},{... | collective-permute-start | bytes 786440 | tf_op jit(solution)/shard_map/ppermute | solution.py:30
  156.8 23.5 %collective-permute-start.43 = (bf16[256,1024]{1,0:T(8,128)(2,1)S(1)}, bf16[256,1024]{1,0:T(8,128)(2,1)S(1)}, u32[]{:S(2)}, u32[]{:S(2)}) collective-permute-start(bf16[256,1024]{1,0:T(8,128)(2,1)S(1)} %pad_maximum_fusion.2), channel_id=1, source_target_pairs={{0,8},{4,12},{8,0},{12,4},{16,24},{20,28},{24,16},{28,20},{1,9},{5... | collective-permute-start | bytes 1572872 | tf_op jit(solution)/shard_map/ppermute | solution.py:30
  156.9 17.2 %collective-permute-start.36 = (bf16[128,512]{1,0:T(8,128)(2,1)S(1)}, bf16[128,512]{1,0:T(8,128)(2,1)S(1)}, u32[]{:S(2)}, u32[]{:S(2)}) collective-permute-start(bf16[128,512]{1,0:T(8,128)(2,1)S(1)} %get-tuple-element.230), channel_id=1, source_target_pairs={{0,16},{4,20},{8,24},{12,28},{16,0},{20,4},{24,8},{28,12},{1,17},{... | collective-permute-start | bytes 393224 | tf_op jit(solution)/shard_map/ppermute | solution.py:30
  162.7 15.0 %collective-permute-start.35 = (bf16[128,512]{1,0:T(8,128)(2,1)S(1)}, bf16[128,512]{1,0:T(8,128)(2,1)S(1)}, u32[]{:S(2)}, u32[]{:S(2)}) collective-permute-start(bf16[128,512]{1,0:T(8,128)(2,1)S(1)} %get-tuple-element.234), channel_id=1, source_target_pairs={{0,16},{4,20},{8,24},{12,28},{16,0},{20,4},{24,8},{28,12},{1,17},{... | collective-permute-start | bytes 393224 | tf_op jit(solution)/shard_map/ppermute | solution.py:30
  167.6 13.1 %collective-permute-start.42 = (bf16[256,1024]{1,0:T(8,128)(2,1)S(1)}, bf16[256,1024]{1,0:T(8,128)(2,1)S(1)}, u32[]{:S(2)}, u32[]{:S(2)}) collective-permute-start(bf16[256,1024]{1,0:T(8,128)(2,1)S(1)} %pad_maximum_fusion.3), channel_id=1, source_target_pairs={{0,4},{4,0},{8,12},{12,8},{16,20},{20,16},{24,28},{28,24},{1,5},{5... | collective-permute-start | bytes 1572872 | tf_op jit(solution)/shard_map/ppermute | solution.py:30
  180.4 34.6 %collective-permute-start.49 = (bf16[512,1024]{1,0:T(8,128)(2,1)S(1)}, bf16[512,1024]{1,0:T(8,128)(2,1)S(1)}, u32[]{:S(2)}, u32[]{:S(2)}) collective-permute-start(bf16[512,1024]{1,0:T(8,128)(2,1)S(1)} %pad_maximum_fusion.refs_0_), channel_id=1, source_target_pairs={{0,4},{4,0},{8,12},{12,8},{16,20},{20,16},{24,28},{28,24},{1,5},{5... | collective-permute-start | bytes 3145736 | tf_op jit(solution)/shard_map/ppermute | solution.py:30
  184.6 13.9 %collective-permute-start.44 = (bf16[288,512]{1,0:T(8,128)(2,1)S(1)}, bf16[288,512]{1,0:T(8,128)(2,1)S(1)}, u32[]{:S(2)}, u32[]{:S(2)}) collective-permute-start(bf16[288,512]{1,0:T(8,128)(2,1)S(1)} %pad_maximum_fusion.6), channel_id=1, source_target_pairs={{0,8},{4,12},{8,0},{12,4},{16,24},{20,28},{24,16},{28,20},{1,9},{5... | collective-permute-start | bytes 884744 | tf_op jit(solution)/shard_map/ppermute | solution.py:30
  191.7 20.5 %collective-permute-start.46 = (bf16[256,512]{1,0:T(8,128)(2,1)S(1)}, bf16[256,512]{1,0:T(8,128)(2,1)S(1)}, u32[]{:S(2)}, u32[]{:S(2)}) collective-permute-start(bf16[256,512]{1,0:T(8,128)(2,1)S(1)} %pad_maximum_fusion.7), channel_id=1, source_target_pairs={{0,4},{4,0},{8,12},{12,8},{16,20},{20,16},{24,28},{28,24},{1,5},{5... | collective-permute-start | bytes 786440 | tf_op jit(solution)/shard_map/ppermute | solution.py:30
  191.7 26.0 %collective-permute-start.48 = (bf16[512,1024]{1,0:T(8,128)(2,1)S(1)}, bf16[512,1024]{1,0:T(8,128)(2,1)S(1)}, u32[]{:S(2)}, u32[]{:S(2)}) collective-permute-start(bf16[512,1024]{1,0:T(8,128)(2,1)S(1)} %pad_maximum_fusion.1.refs_0_), channel_id=1, source_target_pairs={{0,8},{4,12},{8,0},{12,4},{16,24},{20,28},{24,16},{28,20},{1,9},{5... | collective-permute-start | bytes 3145736 | tf_op jit(solution)/shard_map/ppermute | solution.py:30
  198.6 25.4 %collective-permute-start.45 = (bf16[544,512]{1,0:T(8,128)(2,1)S(1)}, bf16[544,512]{1,0:T(8,128)(2,1)S(1)}, u32[]{:S(2)}, u32[]{:S(2)}) collective-permute-start(bf16[544,512]{1,0:T(8,128)(2,1)S(1)} %get-tuple-element.260), channel_id=1, source_target_pairs={{0,4},{4,0},{8,12},{12,8},{16,20},{20,16},{24,28},{28,24},{1,5},{5... | collective-permute-start | bytes 1671176 | tf_op jit(solution)/shard_map/ppermute | solution.py:30
  212.2 11.8 %collective-permute-start.47 = (bf16[512,512]{1,0:T(8,128)(2,1)S(1)}, bf16[512,512]{1,0:T(8,128)(2,1)S(1)}, u32[]{:S(2)}, u32[]{:S(2)}) collective-permute-start(bf16[512,512]{1,0:T(8,128)(2,1)S(1)} %pad_maximum_fusion.4.second), channel_id=1, source_target_pairs={{0,8},{4,12},{8,0},{12,4},{16,24},{20,28},{24,16},{28,20},{1,9},{5... | collective-permute-start | bytes 1572872 | tf_op jit(solution)/shard_map/ppermute | solution.py:30
  (29 other events, 173.9 us)

commit v8 on v7

--- a/solution.py
+++ b/solution.py
@@ -760,7 +760,7 @@
         return values.reshape(1, -1)
 
     side = 2 * rows
-    block = 512
+    block = 256
     project_flops = 2 * side * model * 3 * width
     attend_flops = 3 * heads * 4 * HALF * SLOTS * 128 + 2 * side * width * model
     back_flops = 3 * heads * 10 * HALF * SLOTS * 128 + 2 * side * width * model

time: 228 us -> 228 us (level)
  transfers between devices with their start and end apart: 50 -> 50, of which waited for: 23 -> 22; matrix products, arithmetic and copies ran while one was open for 3% -> 3% of each run, Pallas kernels for 36% -> 36%
where the time goes in v8:
time: 228 us
  Pallas kernels  89.1 us (39%)
  waiting for transfers between devices  67.6 us (30%)
  starting transfers between devices  59.3 us (26%)
  local copies, waits for them, and re-layouts  6.21 us (3%)
  other arithmetic  4.22 us (2%)
    pallas_call x41, Pallas kernels, run(): pl.pallas_call(kernel, out_shape=[pltpu.VMEM(x.shape, x.dtype) for x in o...  79.9 us
    ppermute x50, waiting for transfers between devices, swap(): return lax.ppermute(values, axis, [(i, i ^ bit) for i in range(count)])  67.6 us
    ppermute x50, starting transfers between devices, swap(): return lax.ppermute(values, axis, [(i, i ^ bit) for i in range(count)])  59.3 us
    pallas_call x2, Pallas kernels, run_out(): pl.pallas_call(body, out_shape=[pltpu.HBM(x.shape, x.dtype) for x in outs...  5.29 us
  transfers between devices with their start and end apart: 50, of which 22 were waited for; matrix products, arithmetic and copies ran while one was open for 3% of the time, Pallas kernels for 36%

profile of v8, /device:TPU:0, one launch (start us, length us, event | category | flops | bytes accessed | tf_op | source)
XLA Modules:
  0.0 227.8 jit_solution(8408060697206285730)
XLA Ops:
  0.6 3.0 %collective-permute-start.2 = (bf16[240,1024]{1,0:T(8,128)(2,1)}, bf16[240,1024]{1,0:T(8,128)(2,1)S(1)}, u32[]{:S(2)}, u32[]{:S(2)}) collective-permute-start(bf16[240,1024]{1,0:T(8,128)(2,1)} %refs_4_.13), channel_id=1, source_target_pairs={{0,2},{1,3},{2,0},{3,1},{4,6},{5,7},{6,4},{7,5},{8,10},{9,11},{10,... | collective-permute-start | bytes 1474568 | tf_op jit(solution)/shard_map/ppermute | solution.py:30
  10.1 4.1 %shard_map.254 = (bf16[480,1024]{1,0:T(8,128)(2,1)S(1)}, bf16[480,768]{1,0:T(8,128)(2,1)S(1)}) custom-call(s32[2]{0:T(128)S(1)} %pad_add_fusion.refs_0_.me, bf16[240,1024]{1,0:T(8,128)(2,1)S(1)} %copy-done.3, bf16[240,1024]{1,0:T(8,128)(2,1)S(1)} %collective-permute-done.1.refs_2_, ...), custom_call_target="tpu_custom_call" | custom-call | flops 15099494400 | tf_op jit(solution)/shard_map/pallas_call | solution.py:63
  19.1 7.4 %shard_map.256 = (bf16[240,1024]{1,0:T(8,128)(2,1)S(1)}, bf16[960,768]{1,0:T(8,128)(2,1)S(1)}, bf16[12,160,320]{2,1,0:T(8,128)(2,1)S(1)}, bf16[480,256]{1,0:T(8,...) custom-call(s32[2]{0:T(128)S(1)} %pad_add_fusion.refs_0_.me, ...), custom_call_target="tpu_custom_call" | custom-call | flops 26424115200 | tf_op jit(solution)/shard_map/pallas_call | solution.py:63
  30.7 5.6 %shard_map.258 = (bf16[12,160,320]{2,1,0:T(8,128)(2,1)S(1)}, bf16[480,256]{1,0:T(8,128)(2,1)S(1)}, bf16[240,1024]{1,0:T(8,128)(2,1)S(1)}, f32[240,1024]{1,0:T(8,128)S(1)}) custom-call(s32[2]{0:T(128)S(1)} %pad_add_fusion.refs_0_.me, bf16[960,768]{1,0:T(8,128)(2,1)S(1)} %get-tuple-element.143.refs_11_.refs_1_.refs_12_.refs_13_.refs_15_.refs_16_.refs_3_, ...), custom_call_target="tpu_custom_call" | custom-call | flops 11324620800 | tf_op jit(solution)/shard_map/pallas_call | solution.py:63
  36.4 2.5 %shard_map.259.refs_19_.refs_5_ = f32[480,1024]{1,0:T(8,128)S(1)} custom-call(s32[2]{0:T(128)S(1)} %pad_add_fusion.refs_0_.me, bf16[240,1024]{1,0:T(8,128)(2,1)S(1)} %multiply_convert_fusion.1.refs_6_.refs_10_.refs_7_.refs_1_.refs_8_.refs_4_.refs_11_.refs_5_.refs_9_.refs_14_.refs_3_, ...), custom_call_target="tpu_custom_call" | custom-call | flops 20132659200 | tf_op jit(solution)/shard_map/pallas_call | solution.py:63
  38.9 3.1 %collective-permute-done.7.refs_4_ = bf16[240,1024]{1,0:T(8,128)(2,1)S(1)} collective-permute-done((bf16[240,1024]{1,0:T(8,128)(2,1)S(1)}, bf16[240,1024]{1,0:T(8,128)(2,1)S(1)}, u32[]{:S(2)}, u32[]{:S(2)}) %collective-permute-start.7) | collective-permute-done | bytes 491552 | tf_op jit(solution)/shard_map/ppermute | solution.py:30
  45.8 4.6 %shard_map.261 = (bf16[480,1024]{1,0:T(8,128)(2,1)S(1)}, bf16[480,1024]{1,0:T(8,128)(2,1)S(1)}, f32[1,1024]{1,0:T(1,128)S(1)}, f32[240,1024]{1,0:T(8,128)S(1)}, bf16[240,1024]{1,0:T(8,128)(2,1)S(1)}) custom-call(s32[2]{0:T(128)S(1)} %pad_add_fusion.refs_0_.me, bf16[240,1024]{1,0:T(8,128)(2,1)S(1)} %get-tuple-element.158.refs_1_.refs_20_.refs_22_.refs_19_.refs_18_, ...), custom_call_target="tpu_custom_call" | custom-call | flops 40265318400 | tf_op jit(solution)/shard_map/pallas_call | solution.py:63
  50.5 2.5 %shard_map.262.refs_4_.refs_27_ = f32[480,1024]{1,0:T(8,128)S(1)} custom-call(s32[2]{0:T(128)S(1)} %pad_add_fusion.refs_0_.me, bf16[240,1024]{1,0:T(8,128)(2,1)S(1)} %collective-permute-done.5.refs_1_.refs_25_.refs_6_.refs_26_.refs_24_, bf16[240,1024]{1,0:T(8,128)(2,1)S(1)} %collective-permute-done.9.refs_2_.refs_26_.refs_7_.refs_27_.refs_25_, ...), custom_call_target="tpu_custom_call" | custom-call | flops 20132659200 | tf_op jit(solution)/shard_map/pallas_call | solution.py:63
  53.0 4.5 %collective-permute-done.8.refs_1_.refs_29_.refs_30_.refs_27_.refs_3_.refs_28_.refs_26_.refs_23_ = bf16[240,1024]{1,0:T(8,128)(2,1)S(1)} collective-permute-done((bf16[240,1024]{1,0:T(8,128)(2,1)S(1)}, bf16[240,1024]{1,0:T(8,128)(2,1)S(1)}, u32[]{:S(2)}, u32[]{:S(2)}) %collective-permute-start.8) | collective-permute-done | bytes 491552 | tf_op jit(solution)/shard_map/ppermute | solution.py:30
  57.5 2.8 %shard_map.263 = (bf16[240,1024]{1,0:T(8,128)(2,1)S(1)}, bf16[240,1024]{1,0:T(8,128)(2,1)S(1)}, f32[1,1024]{1,0:T(1,128)S(1)}, f32[240,1024]{1,0:T(8,128)S(1)}) custom-call(s32[2]{0:T(128)S(1)} %pad_add_fusion.refs_0_.me, bf16[240,1024]{1,0:T(8,128)(2,1)S(1)} %collective-permute-done.8.refs_1_.refs_29_.refs_30_.refs_27_.refs_3_.refs_28_.refs_26_.refs_23_, ...), custom_call_target="tpu_custom_call" | custom-call | flops 20132659200 | tf_op jit(solution)/shard_map/pallas_call | solution.py:63
  60.2 2.8 %shard_map.264 = (bf16[240,1024]{1,0:T(8,128)(2,1)S(1)}, bf16[240,1024]{1,0:T(8,128)(2,1)S(1)}, f32[1,1024]{1,0:T(1,128)S(1)}, bf16[240,1024]{1,0:T(8,128)(2,1)S(1)}) custom-call(s32[2]{0:T(128)S(1)} %pad_add_fusion.refs_0_.me, bf16[240,1024]{1,0:T(8,128)(2,1)S(1)} %collective-permute-done.11.refs_1_.refs_29_.refs_4_.refs_31_.refs_28_.refs_25_, ...), custom_call_target="tpu_custom_call" | custom-call | flops 20132659200 | tf_op jit(solution)/shard_map/pallas_call | solution.py:63
  66.8 2.8 %shard_map.266 = bf16[512,1024]{1,0:T(8,128)(2,1)S(1)} custom-call(s32[2]{0:T(128)S(1)} %pad_add_fusion.refs_0_.me, bf16[480,1024]{1,0:T(8,128)(2,1)S(1)} %get-tuple-element.160.refs_21_.refs_1_.refs_24_.refs_20_.refs_19_.refs_22_.refs_17_.refs_14_.refs_13_.refs_10_, bf16[240,1024]{1,0:T(8,128)(2,1)S(1)} %get-tuple-element.165.refs_27_.refs_28_.refs_2_.refs_1_.refs_26_, ...), custom_call_target="tpu_custom_call" | custom-call | flops 20132659200 | tf_op jit(solution)/shard_map/pallas_call | solution.py:63
  69.6 2.9 %shard_map.267 = bf16[512,1024]{1,0:T(8,128)(2,1)S(1)} custom-call(s32[2]{0:T(128)S(1)} %pad_add_fusion.refs_0_.me, bf16[240,1024]{1,0:T(8,128)(2,1)S(1)} %get-tuple-element.158.refs_1_.refs_20_.refs_22_.refs_19_.refs_18_, bf16[240,1024]{1,0:T(8,128)(2,1)S(1)} %collective-permute-done.10.refs_2_.refs_24_.refs_25_.refs_23_.refs_21_, ...), custom_call_target="tpu_custom_call" | custom-call | flops 20132659200 | tf_op jit(solution)/shard_map/pallas_call | solution.py:63
  82.6 2.8 %shard_map.270.refs_27_.refs_25_.refs_1_ = f32[512,1024]{1,0:T(8,128)S(1)} custom-call(s32[2]{0:T(128)S(1)} %pad_add_fusion.refs_0_.me, bf16[480,1024]{1,0:T(8,128)(2,1)S(1)} %get-tuple-element.160.refs_21_.refs_1_.refs_24_.refs_20_.refs_19_.refs_22_.refs_17_.refs_14_.refs_13_.refs_10_, ...), custom_call_target="tpu_custom_call" | custom-call | flops 20132659200 | tf_op jit(solution)/shard_map/pallas_call | solution.py:63
  85.4 6.6 %shard_map.271 = (f32[480,256]{1,0:T(8,128)S(1)}, f32[960,512]{1,0:T(8,128)S(1)}) custom-call(s32[2]{0:T(128)S(1)} %pad_add_fusion.refs_0_.me, bf16[240,1024]{1,0:T(8,128)(2,1)S(1)} %get-tuple-element.176.refs_30_.refs_1_.refs_24_.refs_19_.refs_21_.refs_16_.refs_15_.refs_8_, ...), custom_call_target="tpu_custom_call" | custom-call | flops 20761804800 | tf_op jit(solution)/shard_map/pallas_call | solution.py:63
  92.1 2.7 %shard_map.272.refs_23_.refs_1_ = f32[512,1024]{1,0:T(8,128)S(1)} custom-call(s32[2]{0:T(128)S(1)} %pad_add_fusion.refs_0_.me, bf16[240,1024]{1,0:T(8,128)(2,1)S(1)} %get-tuple-element.158.refs_1_.refs_20_.refs_22_.refs_19_.refs_18_, bf16[240,1024]{1,0:T(8,128)(2,1)S(1)} %collective-permute-done.10.refs_2_.refs_24_.refs_25_.refs_23_.refs_21_, ...), custom_call_target="tpu_custom_call" | custom-call | flops 20132659200 | tf_op jit(solution)/shard_map/pallas_call | solution.py:63
  101.5 8.1 %shard_map.275 = (bf16[480,768]{1,0:T(8,128)(2,1)S(1)}, bf16[480,768]{1,0:T(8,128)(2,1)S(1)}, f32[1,512]{1,0:T(1,128)S(1)}, bf16[240,1024]{1,0:T(8,128)(2,1)S(1)}, f32[240,1024]{1,0:T(8,128)S(1)}) custom-call(s32[2]{0:T(128)S(1)} %pad_add_fusion.refs_0_.me, ...), custom_call_target="tpu_custom_call" | custom-call | flops 35861299200 | tf_op jit(solution)/shard_map/pallas_call | solution.py:63
  109.6 2.6 %collective-permute-done.24.refs_2_ = bf16[256,1024]{1,0:T(8,128)(2,1)S(1)} collective-permute-done((bf16[256,1024]{1,0:T(8,128)(2,1)S(1)}, bf16[256,1024]{1,0:T(8,128)(2,1)S(1)}, u32[]{:S(2)}, u32[]{:S(2)}) %collective-permute-start.24) | collective-permute-done | bytes 524320 | tf_op jit(solution)/shard_map/ppermute | solution.py:30
  113.8 2.7 %collective-permute-start.34 = (bf16[128,1024]{1,0:T(8,128)(2,1)S(1)}, bf16[128,1024]{1,0:T(8,128)(2,1)S(1)}, u32[]{:S(2)}, u32[]{:S(2)}) collective-permute-start(bf16[128,1024]{1,0:T(8,128)(2,1)S(1)} %get-tuple-element.205), channel_id=1, source_target_pairs={{0,16},{4,20},{8,24},{12,28},{16,0},{20,4},{24,8},{28,12},{1,17},{... | collective-permute-start | bytes 786440 | tf_op jit(solution)/shard_map/ppermute | solution.py:30
  131.6 6.5 %collective-permute-done.29.refs_2_ = bf16[128,1024]{1,0:T(8,128)(2,1)S(1)} collective-permute-done((bf16[128,1024]{1,0:T(8,128)(2,1)S(1)}, bf16[128,1024]{1,0:T(8,128)(2,1)S(1)}, u32[]{:S(2)}, u32[]{:S(2)}) %collective-permute-start.29) | collective-permute-done | bytes 262176 | tf_op jit(solution)/shard_map/ppermute | solution.py:30
  139.9 6.1 %collective-permute-done.31.refs_2_ = bf16[512,512]{1,0:T(8,128)(2,1)S(1)} collective-permute-done((bf16[512,512]{1,0:T(8,128)(2,1)S(1)}, bf16[512,512]{1,0:T(8,128)(2,1)S(1)}, u32[]{:S(2)}, u32[]{:S(2)}) %collective-permute-start.31) | collective-permute-done | bytes 524320 | tf_op jit(solution)/shard_map/ppermute | solution.py:30
  147.0 9.3 %collective-permute-start.37 = (bf16[128,1024]{1,0:T(8,128)(2,1)S(1)}, bf16[128,1024]{1,0:T(8,128)(2,1)S(1)}, u32[]{:S(2)}, u32[]{:S(2)}) collective-permute-start(bf16[128,1024]{1,0:T(8,128)(2,1)S(1)} %shard_map.290), channel_id=1, source_target_pairs={{0,16},{4,20},{8,24},{12,28},{16,0},{20,4},{24,8},{28,12},{1,17},{... | collective-permute-start | bytes 786440 | tf_op jit(solution)/shard_map/ppermute | solution.py:30
  157.4 3.8 %collective-permute-start.36 = (bf16[128,512]{1,0:T(8,128)(2,1)S(1)}, bf16[128,512]{1,0:T(8,128)(2,1)S(1)}, u32[]{:S(2)}, u32[]{:S(2)}) collective-permute-start(bf16[128,512]{1,0:T(8,128)(2,1)S(1)} %get-tuple-element.230), channel_id=1, source_target_pairs={{0,16},{4,20},{8,24},{12,28},{16,0},{20,4},{24,8},{28,12},{1,17},{... | collective-permute-start | bytes 393224 | tf_op jit(solution)/shard_map/ppermute | solution.py:30
  163.3 4.5 %collective-permute-start.35 = (bf16[128,512]{1,0:T(8,128)(2,1)S(1)}, bf16[128,512]{1,0:T(8,128)(2,1)S(1)}, u32[]{:S(2)}, u32[]{:S(2)}) collective-permute-start(bf16[128,512]{1,0:T(8,128)(2,1)S(1)} %get-tuple-element.234), channel_id=1, source_target_pairs={{0,16},{4,20},{8,24},{12,28},{16,0},{20,4},{24,8},{28,12},{1,17},{... | collective-permute-start | bytes 393224 | tf_op jit(solution)/shard_map/ppermute | solution.py:30
  168.4 6.1 %collective-permute-done.36.refs_2_ = bf16[128,512]{1,0:T(8,128)(2,1)S(1)} collective-permute-done((bf16[128,512]{1,0:T(8,128)(2,1)S(1)}, bf16[128,512]{1,0:T(8,128)(2,1)S(1)}, u32[]{:S(2)}, u32[]{:S(2)}) %collective-permute-start.36) | collective-permute-done | bytes 131104 | tf_op jit(solution)/shard_map/ppermute | solution.py:30
  174.6 3.4 %collective-permute-start.41 = (bf16[128,512]{1,0:T(8,128)(2,1)S(1)}, bf16[128,512]{1,0:T(8,128)(2,1)S(1)}, u32[]{:S(2)}, u32[]{:S(2)}) collective-permute-start(bf16[128,512]{1,0:T(8,128)(2,1)S(1)} %shard_map.293), channel_id=1, source_target_pairs={{0,16},{4,20},{8,24},{12,28},{16,0},{20,4},{24,8},{28,12},{1,17},{... | collective-permute-start | bytes 393224 | tf_op jit(solution)/shard_map/ppermute | solution.py:30
  184.6 6.8 %collective-permute-start.44 = (bf16[288,512]{1,0:T(8,128)(2,1)S(1)}, bf16[288,512]{1,0:T(8,128)(2,1)S(1)}, u32[]{:S(2)}, u32[]{:S(2)}) collective-permute-start(bf16[288,512]{1,0:T(8,128)(2,1)S(1)} %pad_maximum_fusion.6), channel_id=1, source_target_pairs={{0,8},{4,12},{8,0},{12,4},{16,24},{20,28},{24,16},{28,20},{1,9},{5... | collective-permute-start | bytes 884744 | tf_op jit(solution)/shard_map/ppermute | solution.py:30
  192.5 6.8 %collective-permute-done.44 = bf16[288,512]{1,0:T(8,128)(2,1)S(1)} collective-permute-done((bf16[288,512]{1,0:T(8,128)(2,1)S(1)}, bf16[288,512]{1,0:T(8,128)(2,1)S(1)}, u32[]{:S(2)}, u32[]{:S(2)}) %collective-permute-start.44) | collective-permute-done | bytes 294944 | tf_op jit(solution)/shard_map/ppermute | solution.py:30
  199.5 13.2 %collective-permute-done.46 = bf16[256,512]{1,0:T(8,128)(2,1)S(1)} collective-permute-done((bf16[256,512]{1,0:T(8,128)(2,1)S(1)}, bf16[256,512]{1,0:T(8,128)(2,1)S(1)}, u32[]{:S(2)}, u32[]{:S(2)}) %collective-permute-start.46) | collective-permute-done | bytes 262176 | tf_op jit(solution)/shard_map/ppermute | solution.py:30
  212.7 2.8 %collective-permute-start.47 = (bf16[512,512]{1,0:T(8,128)(2,1)S(1)}, bf16[512,512]{1,0:T(8,128)(2,1)S(1)}, u32[]{:S(2)}, u32[]{:S(2)}) collective-permute-start(bf16[512,512]{1,0:T(8,128)(2,1)S(1)} %pad_maximum_fusion.4.second), channel_id=1, source_target_pairs={{0,8},{4,12},{8,0},{12,4},{16,24},{20,28},{24,16},{28,20},{1,9},{5... | collective-permute-start | bytes 1572872 | tf_op jit(solution)/shard_map/ppermute | solution.py:30
  215.5 2.6 %shard_map.295 = f32[1024,1024]{1,0:T(8,128)} custom-call(s32[2]{0:T(128)S(1)} %pad_add_fusion.refs_0_.me, bf16[512,1024]{1,0:T(8,128)(2,1)S(1)} %pad_maximum_fusion.refs_0_, bf16[512,1024]{1,0:T(8,128)(2,1)S(1)} %collective-permute-done.49.refs_1_), custom_call_target="tpu_custom_call" | custom-call | flops 20000000000 | tf_op jit(solution)/shard_map/pallas_call | solution.py:96
  218.2 2.6 %shard_map.296 = f32[1024,1024]{1,0:T(8,128)} custom-call(s32[2]{0:T(128)S(1)} %pad_add_fusion.refs_0_.me, bf16[512,1024]{1,0:T(8,128)(2,1)S(1)} %pad_maximum_fusion.1.refs_0_, bf16[512,1024]{1,0:T(8,128)(2,1)S(1)} %collective-permute-done.48.refs_1_), custom_call_target="tpu_custom_call" | custom-call | flops 20000000000 | tf_op jit(solution)/shard_map/pallas_call | solution.py:96
  (179 shorter events, 77.8 us)
Async XLA Ops:
  0.6 14.5 %collective-permute-start.2 = (bf16[240,1024]{1,0:T(8,128)(2,1)}, bf16[240,1024]{1,0:T(8,128)(2,1)S(1)}, u32[]{:S(2)}, u32[]{:S(2)}) collective-permute-start(bf16[240,1024]{1,0:T(8,128)(2,1)} %refs_4_.13), channel_id=1, source_target_pairs={{0,2},{1,3},{2,0},{3,1},{4,6},{5,7},{6,4},{7,5},{8,10},{9,11},{10,... | collective-permute-start | bytes 1474568 | tf_op jit(solution)/shard_map/ppermute | solution.py:30
  15.1 13.6 %collective-permute-start.5 = (bf16[240,1024]{1,0:T(8,128)(2,1)S(1)}, bf16[240,1024]{1,0:T(8,128)(2,1)S(1)}, u32[]{:S(2)}, u32[]{:S(2)}) collective-permute-start(bf16[240,1024]{1,0:T(8,128)(2,1)S(1)} %multiply_convert_fusion.1.refs_6_.refs_10_.refs_7_.refs_1_.refs_8_.refs_4_.refs_11_.refs_5_.refs_9_.refs_14_, ...), channel_id=1, source_target_pairs={{0,2},{1,3},{2,0},{3,1},{4,6},{5,7},{6,4},{7,5},{8,10},{9,11},{10,... | collective-permute-start | bytes 1474568 | tf_op jit(solution)/shard_map/ppermute | solution.py:30
  28.9 13.1 %collective-permute-start.7 = (bf16[240,1024]{1,0:T(8,128)(2,1)S(1)}, bf16[240,1024]{1,0:T(8,128)(2,1)S(1)}, u32[]{:S(2)}, u32[]{:S(2)}) collective-permute-start(bf16[240,1024]{1,0:T(8,128)(2,1)S(1)} %shard_map.257), channel_id=1, source_target_pairs={{0,2},{1,3},{2,0},{3,1},{4,6},{5,7},{6,4},{7,5},{8,10},{9,11},{10,... | collective-permute-start | bytes 1474568 | tf_op jit(solution)/shard_map/ppermute | solution.py:30
  44.3 13.2 %collective-permute-start.8 = (bf16[240,1024]{1,0:T(8,128)(2,1)S(1)}, bf16[240,1024]{1,0:T(8,128)(2,1)S(1)}, u32[]{:S(2)}, u32[]{:S(2)}) collective-permute-start(bf16[240,1024]{1,0:T(8,128)(2,1)S(1)} %get-tuple-element.158.refs_1_.refs_20_.refs_22_.refs_19_.refs_18_), channel_id=1, source_target_pairs={{0,2},{1,3},{2,0},{3,1},{4,6},{5,7},{6,4},{7,5},{8,10},{9,11},{10,... | collective-permute-start | bytes 1474568 | tf_op jit(solution)/shard_map/ppermute | solution.py:30
  63.6 13.9 %collective-permute-start.13 = (bf16[240,1024]{1,0:T(8,128)(2,1)S(1)}, bf16[240,1024]{1,0:T(8,128)(2,1)S(1)}, u32[]{:S(2)}, u32[]{:S(2)}) collective-permute-start(bf16[240,1024]{1,0:T(8,128)(2,1)S(1)} %get-tuple-element.175), channel_id=1, source_target_pairs={{0,1},{1,0},{2,3},{3,2},{4,5},{5,4},{6,7},{7,6},{8,9},{9,8},{10,11... | collective-permute-start | bytes 1474568 | tf_op jit(solution)/shard_map/ppermute | solution.py:30
  65.2 13.6 %collective-permute-start.14 = (bf16[240,1024]{1,0:T(8,128)(2,1)S(1)}, bf16[240,1024]{1,0:T(8,128)(2,1)S(1)}, u32[]{:S(2)}, u32[]{:S(2)}) collective-permute-start(bf16[240,1024]{1,0:T(8,128)(2,1)S(1)} %shard_map.265), channel_id=1, source_target_pairs={{0,2},{1,3},{2,0},{3,1},{4,6},{5,7},{6,4},{7,5},{8,10},{9,11},{10,... | collective-permute-start | bytes 1474568 | tf_op jit(solution)/shard_map/ppermute | solution.py:30
  72.5 25.2 %collective-permute-start.19 = (bf16[512,1024]{1,0:T(8,128)(2,1)S(1)}, bf16[512,1024]{1,0:T(8,128)(2,1)S(1)}, u32[]{:S(2)}, u32[]{:S(2)}) collective-permute-start(bf16[512,1024]{1,0:T(8,128)(2,1)S(1)} %shard_map.267), channel_id=1, source_target_pairs={{0,8},{4,12},{8,0},{12,4},{16,24},{20,28},{24,16},{28,20},{1,9},{5... | collective-permute-start | bytes 3145736 | tf_op jit(solution)/shard_map/ppermute | solution.py:30
  74.2 24.9 %collective-permute-start.15 = (bf16[512,1024]{1,0:T(8,128)(2,1)S(1)}, bf16[512,1024]{1,0:T(8,128)(2,1)S(1)}, u32[]{:S(2)}, u32[]{:S(2)}) collective-permute-start(bf16[512,1024]{1,0:T(8,128)(2,1)S(1)} %shard_map.266), channel_id=1, source_target_pairs={{0,4},{4,0},{8,12},{12,8},{16,20},{20,16},{24,28},{28,24},{1,5},{5... | collective-permute-start | bytes 3145736 | tf_op jit(solution)/shard_map/ppermute | solution.py:30
  77.4 17.6 %collective-permute-start.22 = (bf16[240,1024]{1,0:T(8,128)(2,1)S(1)}, bf16[240,1024]{1,0:T(8,128)(2,1)S(1)}, u32[]{:S(2)}, u32[]{:S(2)}) collective-permute-start(bf16[240,1024]{1,0:T(8,128)(2,1)S(1)} %get-tuple-element.195), channel_id=1, source_target_pairs={{0,1},{1,0},{2,3},{3,2},{4,5},{5,4},{6,7},{7,6},{8,9},{9,8},{10,11... | collective-permute-start | bytes 1474568 | tf_op jit(solution)/shard_map/ppermute | solution.py:30
  81.0 13.8 %collective-permute-start.16 = (bf16[240,1024]{1,0:T(8,128)(2,1)S(1)}, bf16[240,1024]{1,0:T(8,128)(2,1)S(1)}, u32[]{:S(2)}, u32[]{:S(2)}) collective-permute-start(bf16[240,1024]{1,0:T(8,128)(2,1)S(1)} %get-tuple-element.176.refs_30_.refs_1_.refs_24_.refs_19_.refs_21_.refs_16_.refs_15_.refs_8_), channel_id=1, source_target_pairs={{0,2},{1,3},{2,0},{3,1},{4,6},{5,7},{6,4},{7,5},{8,10},{9,11},{10,... | collective-permute-start | bytes 1474568 | tf_op jit(solution)/shard_map/ppermute | solution.py:30
  95.1 18.3 %collective-permute-start.23 = (bf16[240,1024]{1,0:T(8,128)(2,1)S(1)}, bf16[240,1024]{1,0:T(8,128)(2,1)S(1)}, u32[]{:S(2)}, u32[]{:S(2)}) collective-permute-start(bf16[240,1024]{1,0:T(8,128)(2,1)S(1)} %shard_map.276), channel_id=1, source_target_pairs={{0,2},{1,3},{2,0},{3,1},{4,6},{5,7},{6,4},{7,5},{8,10},{9,11},{10,... | collective-permute-start | bytes 1474568 | tf_op jit(solution)/shard_map/ppermute | solution.py:30
  99.4 12.8 %collective-permute-start.24 = (bf16[256,1024]{1,0:T(8,128)(2,1)S(1)}, bf16[256,1024]{1,0:T(8,128)(2,1)S(1)}, u32[]{:S(2)}, u32[]{:S(2)}) collective-permute-start(bf16[256,1024]{1,0:T(8,128)(2,1)S(1)} %get-tuple-element.188), channel_id=1, source_target_pairs={{0,4},{4,0},{8,12},{12,8},{16,20},{20,16},{24,28},{28,24},{1,5},{5... | collective-permute-start | bytes 1572872 | tf_op jit(solution)/shard_map/ppermute | solution.py:30
  101.0 12.5 %collective-permute-start.18 = (bf16[256,1024]{1,0:T(8,128)(2,1)S(1)}, bf16[256,1024]{1,0:T(8,128)(2,1)S(1)}, u32[]{:S(2)}, u32[]{:S(2)}) collective-permute-start(bf16[256,1024]{1,0:T(8,128)(2,1)S(1)} %get-tuple-element.186), channel_id=1, source_target_pairs={{0,8},{4,12},{8,0},{12,4},{16,24},{20,28},{24,16},{28,20},{1,9},{5... | collective-permute-start | bytes 1572872 | tf_op jit(solution)/shard_map/ppermute | solution.py:30
  113.8 32.3 %collective-permute-start.34 = (bf16[128,1024]{1,0:T(8,128)(2,1)S(1)}, bf16[128,1024]{1,0:T(8,128)(2,1)S(1)}, u32[]{:S(2)}, u32[]{:S(2)}) collective-permute-start(bf16[128,1024]{1,0:T(8,128)(2,1)S(1)} %get-tuple-element.205), channel_id=1, source_target_pairs={{0,16},{4,20},{8,24},{12,28},{16,0},{20,4},{24,8},{28,12},{1,17},{... | collective-permute-start | bytes 786440 | tf_op jit(solution)/shard_map/ppermute | solution.py:30
  116.5 21.6 %collective-permute-start.29 = (bf16[128,1024]{1,0:T(8,128)(2,1)S(1)}, bf16[128,1024]{1,0:T(8,128)(2,1)S(1)}, u32[]{:S(2)}, u32[]{:S(2)}) collective-permute-start(bf16[128,1024]{1,0:T(8,128)(2,1)S(1)} %get-tuple-element.202), channel_id=1, source_target_pairs={{0,16},{4,20},{8,24},{12,28},{16,0},{20,4},{24,8},{28,12},{1,17},{... | collective-permute-start | bytes 786440 | tf_op jit(solution)/shard_map/ppermute | solution.py:30
  122.4 23.6 %collective-permute-start.31 = (bf16[512,512]{1,0:T(8,128)(2,1)S(1)}, bf16[512,512]{1,0:T(8,128)(2,1)S(1)}, u32[]{:S(2)}, u32[]{:S(2)}) collective-permute-start(bf16[512,512]{1,0:T(8,128)(2,1)S(1)} %shard_map.282), channel_id=1, source_target_pairs={{0,8},{4,12},{8,0},{12,4},{16,24},{20,28},{24,16},{28,20},{1,9},{5... | collective-permute-start | bytes 1572872 | tf_op jit(solution)/shard_map/ppermute | solution.py:30
  125.1 14.8 %collective-permute-start.28 = (bf16[512,512]{1,0:T(8,128)(2,1)S(1)}, bf16[512,512]{1,0:T(8,128)(2,1)S(1)}, u32[]{:S(2)}, u32[]{:S(2)}) collective-permute-start(bf16[512,512]{1,0:T(8,128)(2,1)S(1)} %shard_map.281), channel_id=1, source_target_pairs={{0,4},{4,0},{8,12},{12,8},{16,20},{20,16},{24,28},{28,24},{1,5},{5... | collective-permute-start | bytes 1572872 | tf_op jit(solution)/shard_map/ppermute | solution.py:30
  138.8 18.4 %collective-permute-start.33 = (bf16[128,1024]{1,0:T(8,128)(2,1)S(1)}, bf16[128,1024]{1,0:T(8,128)(2,1)S(1)}, u32[]{:S(2)}, u32[]{:S(2)}) collective-permute-start(bf16[128,1024]{1,0:T(8,128)(2,1)S(1)} %shard_map.287), channel_id=1, source_target_pairs={{0,16},{4,20},{8,24},{12,28},{16,0},{20,4},{24,8},{28,12},{1,17},{... | collective-permute-start | bytes 786440 | tf_op jit(solution)/shard_map/ppermute | solution.py:30
  139.8 51.5 %collective-permute-start.27 = (bf16[240,1024]{1,0:T(8,128)(2,1)S(1)}, bf16[240,1024]{1,0:T(8,128)(2,1)S(1)}, u32[]{:S(2)}, u32[]{:S(2)}) collective-permute-start(bf16[240,1024]{1,0:T(8,128)(2,1)S(1)} %get-tuple-element.218), channel_id=1, source_target_pairs={{0,1},{1,0},{2,3},{3,2},{4,5},{5,4},{6,7},{7,6},{8,9},{9,8},{10,11... | collective-permute-start | bytes 1474568 | tf_op jit(solution)/shard_map/ppermute | solution.py:30
  146.0 17.3 %collective-permute-start.30 = (bf16[256,512]{1,0:T(8,128)(2,1)S(1)}, bf16[256,512]{1,0:T(8,128)(2,1)S(1)}, u32[]{:S(2)}, u32[]{:S(2)}) collective-permute-start(bf16[256,512]{1,0:T(8,128)(2,1)S(1)} %get-tuple-element.223), channel_id=1, source_target_pairs={{0,8},{4,12},{8,0},{12,4},{16,24},{20,28},{24,16},{28,20},{1,9},{5... | collective-permute-start | bytes 786440 | tf_op jit(solution)/shard_map/ppermute | solution.py:30
  146.1 11.2 %collective-permute-start.32 = (bf16[256,512]{1,0:T(8,128)(2,1)S(1)}, bf16[256,512]{1,0:T(8,128)(2,1)S(1)}, u32[]{:S(2)}, u32[]{:S(2)}) collective-permute-start(bf16[256,512]{1,0:T(8,128)(2,1)S(1)} %get-tuple-element.226), channel_id=1, source_target_pairs={{0,4},{4,0},{8,12},{12,8},{16,20},{20,16},{24,28},{28,24},{1,5},{5... | collective-permute-start | bytes 786440 | tf_op jit(solution)/shard_map/ppermute | solution.py:30
  147.0 20.8 %collective-permute-start.37 = (bf16[128,1024]{1,0:T(8,128)(2,1)S(1)}, bf16[128,1024]{1,0:T(8,128)(2,1)S(1)}, u32[]{:S(2)}, u32[]{:S(2)}) collective-permute-start(bf16[128,1024]{1,0:T(8,128)(2,1)S(1)} %shard_map.290), channel_id=1, source_target_pairs={{0,16},{4,20},{8,24},{12,28},{16,0},{20,4},{24,8},{28,12},{1,17},{... | collective-permute-start | bytes 786440 | tf_op jit(solution)/shard_map/ppermute | solution.py:30
  157.3 23.5 %collective-permute-start.43 = (bf16[256,1024]{1,0:T(8,128)(2,1)S(1)}, bf16[256,1024]{1,0:T(8,128)(2,1)S(1)}, u32[]{:S(2)}, u32[]{:S(2)}) collective-permute-start(bf16[256,1024]{1,0:T(8,128)(2,1)S(1)} %pad_maximum_fusion.2), channel_id=1, source_target_pairs={{0,8},{4,12},{8,0},{12,4},{16,24},{20,28},{24,16},{28,20},{1,9},{5... | collective-permute-start | bytes 1572872 | tf_op jit(solution)/shard_map/ppermute | solution.py:30
  157.4 17.1 %collective-permute-start.36 = (bf16[128,512]{1,0:T(8,128)(2,1)S(1)}, bf16[128,512]{1,0:T(8,128)(2,1)S(1)}, u32[]{:S(2)}, u32[]{:S(2)}) collective-permute-start(bf16[128,512]{1,0:T(8,128)(2,1)S(1)} %get-tuple-element.230), channel_id=1, source_target_pairs={{0,16},{4,20},{8,24},{12,28},{16,0},{20,4},{24,8},{28,12},{1,17},{... | collective-permute-start | bytes 393224 | tf_op jit(solution)/shard_map/ppermute | solution.py:30
  163.3 14.7 %collective-permute-start.35 = (bf16[128,512]{1,0:T(8,128)(2,1)S(1)}, bf16[128,512]{1,0:T(8,128)(2,1)S(1)}, u32[]{:S(2)}, u32[]{:S(2)}) collective-permute-start(bf16[128,512]{1,0:T(8,128)(2,1)S(1)} %get-tuple-element.234), channel_id=1, source_target_pairs={{0,16},{4,20},{8,24},{12,28},{16,0},{20,4},{24,8},{28,12},{1,17},{... | collective-permute-start | bytes 393224 | tf_op jit(solution)/shard_map/ppermute | solution.py:30
  167.9 13.1 %collective-permute-start.42 = (bf16[256,1024]{1,0:T(8,128)(2,1)S(1)}, bf16[256,1024]{1,0:T(8,128)(2,1)S(1)}, u32[]{:S(2)}, u32[]{:S(2)}) collective-permute-start(bf16[256,1024]{1,0:T(8,128)(2,1)S(1)} %pad_maximum_fusion.3), channel_id=1, source_target_pairs={{0,4},{4,0},{8,12},{12,8},{16,20},{20,16},{24,28},{28,24},{1,5},{5... | collective-permute-start | bytes 1572872 | tf_op jit(solution)/shard_map/ppermute | solution.py:30
  180.9 34.7 %collective-permute-start.49 = (bf16[512,1024]{1,0:T(8,128)(2,1)S(1)}, bf16[512,1024]{1,0:T(8,128)(2,1)S(1)}, u32[]{:S(2)}, u32[]{:S(2)}) collective-permute-start(bf16[512,1024]{1,0:T(8,128)(2,1)S(1)} %pad_maximum_fusion.refs_0_), channel_id=1, source_target_pairs={{0,4},{4,0},{8,12},{12,8},{16,20},{20,16},{24,28},{28,24},{1,5},{5... | collective-permute-start | bytes 3145736 | tf_op jit(solution)/shard_map/ppermute | solution.py:30
  184.6 14.7 %collective-permute-start.44 = (bf16[288,512]{1,0:T(8,128)(2,1)S(1)}, bf16[288,512]{1,0:T(8,128)(2,1)S(1)}, u32[]{:S(2)}, u32[]{:S(2)}) collective-permute-start(bf16[288,512]{1,0:T(8,128)(2,1)S(1)} %pad_maximum_fusion.6), channel_id=1, source_target_pairs={{0,8},{4,12},{8,0},{12,4},{16,24},{20,28},{24,16},{28,20},{1,9},{5... | collective-permute-start | bytes 884744 | tf_op jit(solution)/shard_map/ppermute | solution.py:30
  192.4 20.2 %collective-permute-start.46 = (bf16[256,512]{1,0:T(8,128)(2,1)S(1)}, bf16[256,512]{1,0:T(8,128)(2,1)S(1)}, u32[]{:S(2)}, u32[]{:S(2)}) collective-permute-start(bf16[256,512]{1,0:T(8,128)(2,1)S(1)} %pad_maximum_fusion.7), channel_id=1, source_target_pairs={{0,4},{4,0},{8,12},{12,8},{16,20},{20,16},{24,28},{28,24},{1,5},{5... | collective-permute-start | bytes 786440 | tf_op jit(solution)/shard_map/ppermute | solution.py:30
  192.4 25.8 %collective-permute-start.48 = (bf16[512,1024]{1,0:T(8,128)(2,1)S(1)}, bf16[512,1024]{1,0:T(8,128)(2,1)S(1)}, u32[]{:S(2)}, u32[]{:S(2)}) collective-permute-start(bf16[512,1024]{1,0:T(8,128)(2,1)S(1)} %pad_maximum_fusion.1.refs_0_), channel_id=1, source_target_pairs={{0,8},{4,12},{8,0},{12,4},{16,24},{20,28},{24,16},{28,20},{1,9},{5... | collective-permute-start | bytes 3145736 | tf_op jit(solution)/shard_map/ppermute | solution.py:30
  199.4 25.0 %collective-permute-start.45 = (bf16[544,512]{1,0:T(8,128)(2,1)S(1)}, bf16[544,512]{1,0:T(8,128)(2,1)S(1)}, u32[]{:S(2)}, u32[]{:S(2)}) collective-permute-start(bf16[544,512]{1,0:T(8,128)(2,1)S(1)} %get-tuple-element.260), channel_id=1, source_target_pairs={{0,4},{4,0},{8,12},{12,8},{16,20},{20,16},{24,28},{28,24},{1,5},{5... | collective-permute-start | bytes 1671176 | tf_op jit(solution)/shard_map/ppermute | solution.py:30
  212.7 11.7 %collective-permute-start.47 = (bf16[512,512]{1,0:T(8,128)(2,1)S(1)}, bf16[512,512]{1,0:T(8,128)(2,1)S(1)}, u32[]{:S(2)}, u32[]{:S(2)}) collective-permute-start(bf16[512,512]{1,0:T(8,128)(2,1)S(1)} %pad_maximum_fusion.4.second), channel_id=1, source_target_pairs={{0,8},{4,12},{8,0},{12,4},{16,24},{20,28},{24,16},{28,20},{1,9},{5... | collective-permute-start | bytes 1572872 | tf_op jit(solution)/shard_map/ppermute | solution.py:30
  (29 other events, 175.4 us)
